TPU v7x, 32 devices: a whole 2x2x4 slice. The times are simulated.
32 devices in a mesh: dp: 4 (over y, x), ctx: 8 (over z, core).
Axes of the slice: x: 2, y: 2, z: 4, core: 2. Of those that a mesh axis runs over, the one named last changes fastest.
Arguments:
- projections: bfloat16 [3072, 8192], P(None, ('dp', 'ctx')), may hold values from -6 to 6
- short_filter: bfloat16 [7, 3072], replicated, may hold values from -2 to 2
- long_filter: bfloat16 [256, 8192], P(('dp', 'ctx')), may hold values from -6 to 6
- out_grad: bfloat16 [1024, 8192], P(None, ('dp', 'ctx')), may hold values from -3 to 3
Outputs:
- mixed: bfloat16 [1024, 8192], P(None, ('dp', 'ctx'))
- proj_grad: bfloat16 [3072, 8192], P(None, ('dp', 'ctx'))
- filter_grad: float32 [256, 8192], P(('dp', 'ctx'))
All inputs are finite; a program needn't handle non-finite values.
Results may differ from a plain program's by a relative error of at most 0.01.
Values may be sent and summed in bfloat16 or wider, within the bound.
No kernel may reach another device: no remote copies, remote signals or barrier semaphores. Data moves between devices by JAX's collectives and lax.ppermute only.
A program may use at most 64 MiB of HBM per device.

v0:
```python
import math

import jax
import jax.numpy as jnp
from jax import lax
from jax.sharding import PartitionSpec as P

CPG = 4
TAPS = 7


def shifted(value, axis, steps):
    count = lax.axis_size(axis)
    first, last = (max(0, -steps), min(count, count - steps))
    return lax.ppermute(value, axis, [(source, source + steps) for source in range(first, last)])


def contract(form, first, second):
    return jnp.einsum(form, first, second, preferred_element_type=jnp.float32)


def dft_table(count_out, count_in, period):
    left_index = jnp.arange(count_out, dtype=jnp.int32)[:, None]
    right_index = jnp.arange(count_in, dtype=jnp.int32)[None, :]
    angle = (left_index * right_index % period).astype(jnp.float32) * (2.0 * math.pi / period)
    return (jnp.cos(angle), jnp.sin(angle))


def make_tables(seq_len):
    padded_len = 2 * seq_len
    inner_len = max(
        (
            divisor
            for divisor in range(1, seq_len + 1)
            if seq_len % divisor == 0 and divisor * divisor <= padded_len
        )
    )
    outer_len = padded_len // inner_len
    cos_outer, sin_outer = dft_table(outer_len, outer_len // 2, outer_len)
    cos_inner, sin_inner = dft_table(inner_len, inner_len, inner_len)
    return (
        (cos_outer.astype(jnp.bfloat16), sin_outer.astype(jnp.bfloat16)),
        dft_table(outer_len, inner_len, padded_len),
        (cos_inner.astype(jnp.bfloat16), sin_inner.astype(jnp.bfloat16)),
        padded_len,
    )


def forward_dft(signal, tables):
    (cos_outer, sin_outer), (cos_twist, sin_twist), (cos_inner, sin_inner), padded_len = tables
    count = signal.shape[0]
    folded = signal.reshape(count, cos_outer.shape[1], cos_inner.shape[0])
    first_re = contract("db,rba->rda", cos_outer, folded)
    first_im = -contract("db,rba->rda", sin_outer, folded)
    twist_re = (first_re * cos_twist + first_im * sin_twist).astype(jnp.bfloat16)
    twist_im = (first_im * cos_twist - first_re * sin_twist).astype(jnp.bfloat16)
    spec_re = contract("rda,ae->rde", twist_re, cos_inner) + contract(
        "rda,ae->rde", twist_im, sin_inner
    )
    spec_im = contract("rda,ae->rde", twist_im, cos_inner) - contract(
        "rda,ae->rde", twist_re, sin_inner
    )
    return (spec_re, spec_im)


def inverse_dft(spec_re, spec_im, tables):
    (cos_outer, sin_outer), (cos_twist, sin_twist), (cos_inner, sin_inner), padded_len = tables
    count = spec_re.shape[0]
    back_re = contract("rde,ea->rda", spec_re, cos_inner) - contract(
        "rde,ea->rda", spec_im, sin_inner
    )
    back_im = contract("rde,ea->rda", spec_im, cos_inner) + contract(
        "rde,ea->rda", spec_re, sin_inner
    )
    turn_re = (back_re * cos_twist - back_im * sin_twist).astype(jnp.bfloat16)
    turn_im = (back_im * cos_twist + back_re * sin_twist).astype(jnp.bfloat16)
    signal = contract("db,rda->rba", cos_outer, turn_re) - contract(
        "db,rda->rba", sin_outer, turn_im
    )
    return signal.reshape(count, -1) / padded_len


def shards(projections, short_filter, long_filter, out_grad):
    width = out_grad.shape[0]
    local_len = out_grad.shape[1]
    lanes_dp = lax.axis_size("dp")
    lanes_ctx = lax.axis_size("ctx")
    seq_len = local_len * lanes_dp * lanes_ctx
    groups = width // CPG
    local_groups = long_filter.shape[0]
    tables = make_tables(seq_len)
    weights = short_filter.astype(jnp.float32)
    rim_len = TAPS - 1
    earlier = shifted(projections[:, local_len - rim_len :], ("dp", "ctx"), 1)
    extended = jnp.concatenate([earlier, projections], axis=1).astype(jnp.float32)
    total = jnp.zeros(projections.shape, jnp.float32)
    for lag in range(TAPS):
        total = (
            total + weights[lag][:, None] * extended[:, rim_len - lag : rim_len - lag + local_len]
        )
    features = total.astype(jnp.bfloat16)
    query = features[:width].astype(jnp.float32)
    key_part = features[width : 2 * width].astype(jnp.float32)
    value_part = features[2 * width :].astype(jnp.float32)
    product = (key_part * value_part).astype(jnp.bfloat16)
    cotangent = out_grad.astype(jnp.float32)
    conv_grad = (cotangent * query).astype(jnp.bfloat16)
    scale = seq_len ** (-0.5)
    filt_re, filt_im = forward_dft(long_filter, tables)
    filt_re = filt_re[:, None]
    filt_im = filt_im[:, None]

    def spectra(whole):
        spec_re, spec_im = forward_dft(whole.reshape(-1, seq_len), tables)
        shape = (local_groups, CPG) + spec_re.shape[1:]
        return (spec_re.reshape(shape), spec_im.reshape(shape))

    def inverse_block(spec_re, spec_im):
        flat_shape = (-1,) + spec_re.shape[2:]
        signal = inverse_dft(spec_re.reshape(flat_shape), spec_im.reshape(flat_shape), tables)
        return signal.reshape(local_groups, CPG, seq_len).astype(jnp.bfloat16)

    def send_shape(block):
        return block.reshape(groups, CPG, 1, 1, local_len)

    def return_shape(block):
        return block.reshape(1, 1, local_groups, CPG, lanes_dp, lanes_ctx, local_len)

    prod_chan = lax.all_to_all(
        lax.all_to_all(send_shape(product), "dp", split_axis=0, concat_axis=2, tiled=True),
        "ctx",
        split_axis=0,
        concat_axis=3,
        tiled=True,
    )
    prod_re, prod_im = spectra(prod_chan)
    conv_re = ((filt_re * prod_re - filt_im * prod_im) * scale).astype(jnp.bfloat16)
    conv_im = ((filt_re * prod_im + filt_im * prod_re) * scale).astype(jnp.bfloat16)
    conv_chan = inverse_block(conv_re, conv_im)
    conv_tok = lax.all_to_all(
        lax.all_to_all(return_shape(conv_chan), "dp", split_axis=4, concat_axis=0, tiled=True),
        "ctx",
        split_axis=5,
        concat_axis=1,
        tiled=True,
    )
    grad_chan = lax.all_to_all(
        lax.all_to_all(send_shape(conv_grad), "dp", split_axis=0, concat_axis=2, tiled=True),
        "ctx",
        split_axis=0,
        concat_axis=3,
        tiled=True,
    )
    grad_re, grad_im = spectra(grad_chan)
    back_re = ((filt_re * grad_re + filt_im * grad_im) * scale).astype(jnp.bfloat16)
    back_im = ((filt_re * grad_im - filt_im * grad_re) * scale).astype(jnp.bfloat16)
    back_chan = inverse_block(back_re, back_im)
    back_tok = lax.all_to_all(
        lax.all_to_all(return_shape(back_chan), "dp", split_axis=4, concat_axis=0, tiled=True),
        "ctx",
        split_axis=5,
        concat_axis=1,
        tiled=True,
    )
    cross_re = jnp.sum(prod_re * grad_re + prod_im * grad_im, axis=1).astype(jnp.bfloat16)
    cross_im = jnp.sum(prod_re * grad_im - prod_im * grad_re, axis=1).astype(jnp.bfloat16)
    filter_grad = inverse_dft(cross_re, cross_im, tables) * scale
    conv = conv_tok.reshape(width, local_len).astype(jnp.float32)
    back = back_tok.reshape(width, local_len).astype(jnp.float32)
    mixed = (query * conv).astype(jnp.bfloat16)
    query_grad = (cotangent * conv).astype(jnp.bfloat16)
    key_grad = (back * value_part).astype(jnp.bfloat16)
    value_grad = (back * key_part).astype(jnp.bfloat16)
    feat_grad = jnp.concatenate([query_grad, key_grad, value_grad], axis=0)
    later = shifted(feat_grad[:, :rim_len], ("dp", "ctx"), -1)
    extended_grad = jnp.concatenate([feat_grad, later], axis=1).astype(jnp.float32)
    gathered = jnp.zeros(projections.shape, jnp.float32)
    for lag in range(TAPS):
        gathered = gathered + weights[lag][:, None] * extended_grad[:, lag : lag + local_len]
    proj_grad = gathered.astype(jnp.bfloat16)
    return (mixed, proj_grad, filter_grad)


def solution(mesh):
    placed = (P(None, ("dp", "ctx")), P(), P(("dp", "ctx"), None), P(None, ("dp", "ctx")))
    return jax.shard_map(
        shards,
        mesh=mesh,
        in_specs=placed,
        out_specs=(P(None, ("dp", "ctx")), P(None, ("dp", "ctx")), P(("dp", "ctx"), None)),
        check_vma=False,
    )
```

profile of v0, /device:TPU:1, one launch (start us, length us, event | category | flops | bytes accessed | tf_op | source)
XLA Modules:
  0.0 206.9 jit_solution(16455654542727587432)
XLA Ops:
  0.7 1.5 slice.86
  2.5 4.6 %collective-permute-start = (bf16[3072,6]{0,1:T(8,128)(2,1)S(1)}, bf16[3072,6]{0,1:T(8,128)(2,1)S(1)}, u32[]{:S(2)}, u32[]{:S(2)}) collective-permute-start(bf16[3072,6]{0,1:T(8,128)(2,1)S(1)} %copy.166), channel_id=1, source_target_pairs={{0,1},{1,2},{2,3},{3,4},{4,5},{5,6},{6,7},{7,8},{8,9},{9,10},{10,1... | collective-permute-start | bytes 110600 | tf_op jit(solution)/shard_map/ppermute | solution.py:15
  8.7 1.0 maximum_convert_fusion
  9.8 8.4 %fusion.8 = bf16[3072,256]{1,0:T(8,128)(2,1)S(1)} fusion(f32[3072,262]{1,0:T(8,128)S(1)} %maximum_convert_fusion, f32[3072]{0:T(1024)S(1)} %bitcast.265, f32[3072]{0:T(1024)S(1)} %bitcast.263, f32[3072]{0:T(1024)S(1)} %bitcast.261, f32[3072]{0:T(1024)S(1)} %bitcast.259, f32[3072]{0:T(1024)S(1)} %bitcast.257, f32[3072]{0:T(1024)S(1)} %bitcast.255, ...), kind=kLoop, calls=%fused_computation.24 | loop fusion | flops 11010048 | bytes 23678976 | tf_op jit(solution)/shard_map/convert_element_type | solution.py:101
  18.3 1.1 copy-done.3
  19.5 0.9 reshape.141
  20.4 3.5 %all-to-all-start.4 = ((bf16[256,4,1,1,256]{4,1,3,2,0:T(4,128)(2,1)}), bf16[256,4,1,1,256]{4,1,3,2,0:T(4,128)(2,1)S(1)}, u32[]{:S(2)}, u32[]{:S(2)}) async-start(bf16[256,4,1,1,256]{4,1,3,2,0:T(4,128)(2,1)} %bitcast.30), calls=%async_computation.4 | async-start | bytes 1048576 | tf_op jit(solution)/shard_map/all_to_all | solution.py:148
  24.8 4.6 %all-to-all-done.4 = bf16[256,4,1,1,256]{4,1,3,2,0:T(4,128)(2,1)S(1)} async-done(((bf16[256,4,1,1,256]{4,1,3,2,0:T(4,128)(2,1)}), bf16[256,4,1,1,256]{4,1,3,2,0:T(4,128)(2,1)S(1)}, u32[]{:S(2)}, u32[]{:S(2)}) %all-to-all-start.4) | async-done | bytes 524320 | tf_op jit(solution)/shard_map/all_to_all | solution.py:148
  29.4 1.5 copy.180
  30.8 8.8 %all-to-all-start.5 = ((bf16[64,4,4,1,256]{4,2,1,3,0:T(4,128)(2,1)}), bf16[64,4,4,1,256]{4,2,1,3,0:T(4,128)(2,1)S(1)}, u32[]{:S(2)}, u32[]{:S(2)}) async-start(bf16[64,4,4,1,256]{4,2,1,3,0:T(4,128)(2,1)} %bitcast.238), calls=%async_computation.5 | async-start | bytes 1048576 | tf_op jit(solution)/shard_map/all_to_all | solution.py:147
  41.4 12.7 %all-to-all-done.5 = bf16[64,4,4,1,256]{4,2,1,3,0:T(4,128)(2,1)S(1)} async-done(((bf16[64,4,4,1,256]{4,2,1,3,0:T(4,128)(2,1)}), bf16[64,4,4,1,256]{4,2,1,3,0:T(4,128)(2,1)S(1)}, u32[]{:S(2)}, u32[]{:S(2)}) %all-to-all-start.5) | async-done | bytes 524320 | tf_op jit(solution)/shard_map/all_to_all | solution.py:147
  55.2 0.9 fusion.27
  58.2 2.6 %fusion.22 = (bf16[32,128,128]{2,1,0:T(8,128)(2,1)S(1)}, bf16[32,128,128]{2,1,0:T(8,128)(2,1)S(1)}, f32[32,128,128]{2,1,0:T(8,128)}) fusion(f32[32,128,128]{2,1,0:T(8,128)S(1)} %convolution_subtract_fusion.1, f32[8,128,128]{2,1,0:T(8,128)S(1)} %convolution_subtract_fusion.7, f32[8,128,128]{2,1,0:T(8,128)S(1)} %convolution_add_fusion.5, ...), kind=kOutput, calls=%fused_computation.46 | convolution fusion | flops 140230656 | bytes 10485760 | tf_op jit(solution)/shard_map/rda,ae->rde/dot_general | solution.py:19
  62.2 0.7 convolution_subtract_fusion
  64.3 1.5 fusion.38
  65.9 2.0 convert_element_type.414
  67.9 1.1 copy.141
  69.0 9.6 %all_to_all.120 = bf16[1,1,8,4,4,8,256]{6,5,3,2,1,0,4:T(8,128)(2,1)S(1)} all-to-all(bf16[1,1,8,4,4,8,256]{6,5,3,2,1,0,4:T(8,128)(2,1)S(1)} %copy.141), channel_id=1, replica_groups=mesh['dp'=4,'ctx'=8] {'dp'}, dimensions={4} | all-to-all | bytes 1048576 | tf_op jit(solution)/shard_map/all_to_all | solution.py:159
  79.0 19.3 %all_to_all.121 = bf16[4,1,8,4,1,8,256]{6,0,3,2,4,1,5:T(4,128)(2,1)S(1)} all-to-all(bf16[4,1,8,4,1,8,256]{6,0,3,2,4,1,5:T(4,128)(2,1)S(1)} %copy.142), channel_id=1, replica_groups=mesh['dp'=4,'ctx'=8] {'ctx'}, dimensions={5} | all-to-all | bytes 1048576 | tf_op jit(solution)/shard_map/all_to_all | solution.py:158
  98.6 1.3 copy.143
  99.9 2.6 %reshape.143 = f32[1024,256]{1,0:T(8,128)} reshape(f32[4,8,1,8,4,1,1,256]{7,4,3,1,0,6,5,2:T(4,128)} %copy.143) | data formatting | bytes 2097152 | tf_op jit(solution)/shard_map/convert_element_type | solution.py:169
  102.5 3.0 %fusion.45 = (bf16[1024,256]{1,0:T(8,128)(2,1)}, bf16[1024,256]{1,0:T(8,128)(2,1)}, bf16[1024,256]{1,0:T(8,128)(2,1)}) fusion(f32[1024,256]{1,0:T(8,128)} %reshape.143, bf16[3072,256]{1,0:T(8,128)(2,1)} %copy-done.3), kind=kLoop, calls=%fused_computation.107 | loop fusion | flops 2097152 | bytes 3670016 | tf_op jit(solution)/shard_map/convert_element_type | solution.py:172
  105.5 2.0 reshape.140
  107.5 10.6 %all_to_all.122 = bf16[256,4,1,1,256]{4,1,3,2,0:T(4,128)(2,1)S(1)} all-to-all(bf16[256,4,1,1,256]{4,1,3,2,0:T(4,128)(2,1)} %bitcast.248), channel_id=1, replica_groups=mesh['dp'=4,'ctx'=8] {'dp'}, dimensions={0} | all-to-all | bytes 1048576 | tf_op jit(solution)/shard_map/all_to_all | solution.py:130
  118.7 19.6 %all_to_all.123 = bf16[64,4,4,1,256]{4,2,1,3,0:T(4,128)(2,1)S(1)} all-to-all(bf16[64,4,4,1,256]{4,2,1,3,0:T(4,128)(2,1)S(1)} %bitcast.250), channel_id=1, replica_groups=mesh['dp'=4,'ctx'=8] {'ctx'}, dimensions={0} | all-to-all | bytes 1048576 | tf_op jit(solution)/shard_map/all_to_all | solution.py:129
  138.5 0.9 copy.111
  139.4 2.0 reshape_reshape.6
  141.4 1.7 fusion.136
  143.1 0.9 fusion.31
  146.1 2.7 %fusion.16 = (bf16[32,128,128]{2,1,0:T(8,128)(2,1)S(1)}, bf16[32,128,128]{2,1,0:T(8,128)(2,1)S(1)}, f32[32,128,128]{2,1,0:T(8,128)}) fusion(f32[32,128,128]{2,1,0:T(8,128)S(1)} %convolution_subtract_fusion.3, f32[8,128,128]{2,1,0:T(8,128)S(1)} %convolution_subtract_fusion.7, f32[8,128,128]{2,1,0:T(8,128)S(1)} %convolution_add_fusion.5, ...), kind=kOutput, calls=%fused_computation.40 | convolution fusion | flops 140230656 | bytes 10485760 | tf_op jit(solution)/shard_map/rda,ae->rde/dot_general | solution.py:19
  150.2 0.7 convolution_subtract_fusion.2
  150.9 0.7 convolution_add_fusion.2
  152.3 0.7 fusion.39
  153.2 0.9 copy.124
  154.1 3.7 %all-to-all-start.2 = ((bf16[1,1,8,4,4,8,256]{6,5,3,2,1,0,4:T(8,128)(2,1)}), bf16[1,1,8,4,4,8,256]{6,5,3,2,1,0,4:T(8,128)(2,1)S(1)}, u32[]{:S(2)}, u32[]{:S(2)}) async-start(bf16[1,1,8,4,4,8,256]{6,5,3,2,1,0,4:T(8,128)(2,1)} %copy.124), calls=%async_computation.2 | async-start | bytes 1048576 | tf_op jit(solution)/shard_map/all_to_all | solution.py:141
  157.8 3.9 %bitcast_reduce_fusion.1 = (bf16[8,128,128]{2,1,0:T(8,128)(2,1)S(1)}, bf16[8,128,128]{2,1,0:T(8,128)(2,1)S(1)}) fusion(f32[32,128,128]{2,1,0:T(8,128)} %copy-done.2, f32[32,128,128]{2,1,0:T(8,128)S(1)} %convolution_subtract_fusion.1, f32[32,128,128]{2,1,0:T(8,128)} %get-tuple-element.31, f32[32,128,128]{2,1,0:T(8,128)} %get-tuple-element.30), kind=kLoop, calls=%fused_computation.51 | loop fusion | flops 3932160 | bytes 8912896 | tf_op jit(solution)/shard_map/reduce_sum | solution.py:165
  162.1 2.4 %all-to-all-done.2 = bf16[1,1,8,4,4,8,256]{6,5,3,2,1,0,4:T(8,128)(2,1)S(1)} async-done(((bf16[1,1,8,4,4,8,256]{6,5,3,2,1,0,4:T(8,128)(2,1)}), bf16[1,1,8,4,4,8,256]{6,5,3,2,1,0,4:T(8,128)(2,1)S(1)}, u32[]{:S(2)}, u32[]{:S(2)}) %all-to-all-start.2) | async-done | bytes 524320 | tf_op jit(solution)/shard_map/all_to_all | solution.py:141
  164.6 1.2 copy.125
  165.8 5.3 %all-to-all-start.3 = ((bf16[4,1,8,4,1,8,256]{6,0,3,2,4,1,5:T(4,128)(2,1)}), bf16[4,1,8,4,1,8,256]{6,0,3,2,4,1,5:T(4,128)(2,1)S(1)}, u32[]{:S(2)}, u32[]{:S(2)}) async-start(bf16[4,1,8,4,1,8,256]{6,0,3,2,4,1,5:T(4,128)(2,1)} %copy.125), calls=%async_computation.3 | async-start | bytes 1048576 | tf_op jit(solution)/shard_map/all_to_all | solution.py:140
  172.5 1.0 fusion.60
  173.5 12.1 %all-to-all-done.3 = bf16[4,1,8,4,1,8,256]{6,0,3,2,4,1,5:T(4,128)(2,1)S(1)} async-done(((bf16[4,1,8,4,1,8,256]{6,0,3,2,4,1,5:T(4,128)(2,1)}), bf16[4,1,8,4,1,8,256]{6,0,3,2,4,1,5:T(4,128)(2,1)S(1)}, u32[]{:S(2)}, u32[]{:S(2)}) %all-to-all-start.3) | async-done | bytes 524320 | tf_op jit(solution)/shard_map/all_to_all | solution.py:140
  186.2 1.4 reshape.142
  187.6 2.4 %fusion.46 = (bf16[1024,256]{1,0:T(8,128)(2,1)S(1)}, bf16[1024,256]{1,0:T(8,128)(2,1)}) fusion(f32[1024,256]{1,0:T(8,128)} %reshape.142, bf16[1024,256]{1,0:T(8,128)(2,1)S(1)} %copy-done.9, bf16[3072,256]{1,0:T(8,128)(2,1)} %copy-done.3), kind=kLoop, calls=%fused_computation.108 | loop fusion | flops 1572864 | bytes 3145728 | tf_op jit(solution)/shard_map/convert_element_type | solution.py:171
  190.1 0.9 copy.144
  191.0 2.8 %collective-permute-start.1 = (bf16[3072,6]{0,1:T(8,128)(2,1)}, bf16[3072,6]{0,1:T(8,128)(2,1)S(1)}, u32[]{:S(2)}, u32[]{:S(2)}) collective-permute-start(bf16[3072,6]{0,1:T(8,128)(2,1)} %copy.144), channel_id=1, source_target_pairs={{1,0},{2,1},{3,2},{4,3},{5,4},{6,5},{7,6},{8,7},{9,8},{10,9},{11,1... | collective-permute-start | bytes 110600 | tf_op jit(solution)/shard_map/ppermute | solution.py:15
  193.8 1.3 fusion.41
  195.1 0.9 copy.183
  197.8 9.1 %fusion.1 = bf16[3072,256]{1,0:T(8,128)(2,1)} fusion(f32[3072,262]{1,0:T(8,128)S(1)} %maximum_convert_fusion.1, f32[3072]{0:T(1024)S(1)} %bitcast.266, f32[3072]{0:T(1024)S(1)} %bitcast.264, f32[3072]{0:T(1024)S(1)} %bitcast.262, f32[3072]{0:T(1024)S(1)} %bitcast.260, f32[3072]{0:T(1024)S(1)} %bitcast.258, f32[3072]{0:T(1024)S(1)} %bitcast.256, ...), kind=kLoop, calls=%fused_computation.10 | loop fusion | flops 11010048 | bytes 23678976 | tf_op jit(solution)/shard_map/convert_element_type | solution.py:180
  (99 shorter events, 20.5 us)
Async XLA Ops:
  0.6 23.3 %copy-start = (bf16[8,8192]{1,0:T(8,128)(2,1)S(1)}, bf16[8,8192]{1,0:T(8,128)(2,1)}, u32[]{:S(2)}) copy-start(bf16[8,8192]{1,0:T(8,128)(2,1)} %param.6) | copy-start | bytes 393220
  0.6 8.1 %copy-start.7 = (bf16[3072,256]{1,0:T(8,128)(2,1)S(1)}, bf16[3072,256]{1,0:T(8,128)(2,1)}, u32[]{:S(2)}) copy-start(bf16[3072,256]{1,0:T(8,128)(2,1)} %param.4) | copy-start | bytes 4718596
  0.7 6.5 %copy-start.14 = (bf16[7,3072]{1,0:T(8,128)(2,1)S(1)}, bf16[7,3072]{1,0:T(8,128)(2,1)}, u32[]{:S(2)}) copy-start(bf16[7,3072]{1,0:T(8,128)(2,1)} %param.5) | copy-start | bytes 129028
  2.5 5.8 %collective-permute-start = (bf16[3072,6]{0,1:T(8,128)(2,1)S(1)}, bf16[3072,6]{0,1:T(8,128)(2,1)S(1)}, u32[]{:S(2)}, u32[]{:S(2)}) collective-permute-start(bf16[3072,6]{0,1:T(8,128)(2,1)S(1)} %copy.166), channel_id=1, source_target_pairs={{0,1},{1,2},{2,3},{3,4},{4,5},{5,6},{6,7},{7,8},{8,9},{9,10},{10,1... | collective-permute-start | bytes 110600 | tf_op jit(solution)/shard_map/ppermute | solution.py:15
  7.2 2.5 %copy-start.15 = (f32[1,3072]{1,0:T(1,128)}, f32[1,3072]{1,0:T(1,128)S(1)}, u32[]{:S(2)}) copy-start(f32[1,3072]{1,0:T(1,128)S(1)} %get-tuple-element.24) | copy-start | bytes 36868
  7.2 2.5 %copy-start.17 = (f32[1,3072]{1,0:T(1,128)}, f32[1,3072]{1,0:T(1,128)S(1)}, u32[]{:S(2)}) copy-start(f32[1,3072]{1,0:T(1,128)S(1)} %get-tuple-element.25) | copy-start | bytes 36868
  7.2 2.5 %copy-start.19 = (f32[1,3072]{1,0:T(1,128)}, f32[1,3072]{1,0:T(1,128)S(1)}, u32[]{:S(2)}) copy-start(f32[1,3072]{1,0:T(1,128)S(1)} %get-tuple-element.26) | copy-start | bytes 36868
  7.2 2.5 %copy-start.21 = (f32[1,3072]{1,0:T(1,128)}, f32[1,3072]{1,0:T(1,128)S(1)}, u32[]{:S(2)}) copy-start(f32[1,3072]{1,0:T(1,128)S(1)} %get-tuple-element.27) | copy-start | bytes 36868
  7.2 2.5 %copy-start.23 = (f32[1,3072]{1,0:T(1,128)}, f32[1,3072]{1,0:T(1,128)S(1)}, u32[]{:S(2)}) copy-start(f32[1,3072]{1,0:T(1,128)S(1)} %get-tuple-element.28) | copy-start | bytes 36868
  7.3 2.5 %copy-start.25 = (f32[1,3072]{1,0:T(1,128)}, f32[1,3072]{1,0:T(1,128)S(1)}, u32[]{:S(2)}) copy-start(f32[1,3072]{1,0:T(1,128)S(1)} %get-tuple-element.29) | copy-start | bytes 36868
  7.5 164.9 %copy-start.10 = (f32[128,128]{1,0:T(8,128)}, f32[128,128]{1,0:T(8,128)S(1)}, u32[]{:S(2)}) copy-start(f32[128,128]{1,0:T(8,128)S(1)} %get-tuple-element.32) | copy-start | bytes 196612
  7.6 164.9 %copy-start.12 = (f32[128,128]{1,0:T(8,128)}, f32[128,128]{1,0:T(8,128)S(1)}, u32[]{:S(2)}) copy-start(f32[128,128]{1,0:T(8,128)S(1)} %get-tuple-element.33) | copy-start | bytes 196612
  9.8 9.6 %copy-start.8 = (bf16[1024,256]{1,0:T(8,128)(2,1)S(1)}, bf16[1024,256]{1,0:T(8,128)(2,1)}, u32[]{:S(2)}) copy-start(bf16[1024,256]{1,0:T(8,128)(2,1)} %param.7) | copy-start | bytes 1572868
  18.2 1.1 copy-start.3
  20.4 8.9 %all-to-all-start.4 = ((bf16[256,4,1,1,256]{4,1,3,2,0:T(4,128)(2,1)}), bf16[256,4,1,1,256]{4,1,3,2,0:T(4,128)(2,1)S(1)}, u32[]{:S(2)}, u32[]{:S(2)}) async-start(bf16[256,4,1,1,256]{4,1,3,2,0:T(4,128)(2,1)} %bitcast.30), calls=%async_computation.4 | async-start | bytes 1048576 | tf_op jit(solution)/shard_map/all_to_all | solution.py:148
  30.8 23.3 %all-to-all-start.5 = ((bf16[64,4,4,1,256]{4,2,1,3,0:T(4,128)(2,1)}), bf16[64,4,4,1,256]{4,2,1,3,0:T(4,128)(2,1)S(1)}, u32[]{:S(2)}, u32[]{:S(2)}) async-start(bf16[64,4,4,1,256]{4,2,1,3,0:T(4,128)(2,1)} %bitcast.238), calls=%async_computation.5 | async-start | bytes 1048576 | tf_op jit(solution)/shard_map/all_to_all | solution.py:147
  141.4 1.7 copy-start.4
  146.1 2.7 %copy-start.2 = (f32[32,128,128]{2,1,0:T(8,128)}, f32[32,128,128]{2,1,0:T(8,128)S(1)}, u32[]{:S(2)}) copy-start(f32[32,128,128]{2,1,0:T(8,128)S(1)} %convolution_subtract_fusion.3) | copy-start | bytes 6291460
  154.1 10.5 %all-to-all-start.2 = ((bf16[1,1,8,4,4,8,256]{6,5,3,2,1,0,4:T(8,128)(2,1)}), bf16[1,1,8,4,4,8,256]{6,5,3,2,1,0,4:T(8,128)(2,1)S(1)}, u32[]{:S(2)}, u32[]{:S(2)}) async-start(bf16[1,1,8,4,4,8,256]{6,5,3,2,1,0,4:T(8,128)(2,1)} %copy.124), calls=%async_computation.2 | async-start | bytes 1048576 | tf_op jit(solution)/shard_map/all_to_all | solution.py:141
  165.8 19.8 %all-to-all-start.3 = ((bf16[4,1,8,4,1,8,256]{6,0,3,2,4,1,5:T(4,128)(2,1)}), bf16[4,1,8,4,1,8,256]{6,0,3,2,4,1,5:T(4,128)(2,1)S(1)}, u32[]{:S(2)}, u32[]{:S(2)}) async-start(bf16[4,1,8,4,1,8,256]{6,0,3,2,4,1,5:T(4,128)(2,1)} %copy.125), calls=%async_computation.3 | async-start | bytes 1048576 | tf_op jit(solution)/shard_map/all_to_all | solution.py:140
  185.9 1.6 copy-start.9
  187.5 2.4 %copy-start.5 = (bf16[1024,256]{1,0:T(8,128)(2,1)S(1)}, bf16[1024,256]{1,0:T(8,128)(2,1)}, u32[]{:S(2)}) copy-start(bf16[1024,256]{1,0:T(8,128)(2,1)} %get-tuple-element.16) | copy-start | bytes 1572868
  187.5 2.4 %copy-start.6 = (bf16[1024,256]{1,0:T(8,128)(2,1)S(1)}, bf16[1024,256]{1,0:T(8,128)(2,1)}, u32[]{:S(2)}) copy-start(bf16[1024,256]{1,0:T(8,128)(2,1)} %get-tuple-element.17) | copy-start | bytes 1572868
  190.0 3.8 %copy-start.11 = (f32[128,128]{1,0:T(8,128)S(1)}, f32[128,128]{1,0:T(8,128)}, u32[]{:S(2)}) copy-start(f32[128,128]{1,0:T(8,128)} %copy-done.10) | copy-start | bytes 196612
  190.0 3.8 %copy-start.13 = (f32[128,128]{1,0:T(8,128)S(1)}, f32[128,128]{1,0:T(8,128)}, u32[]{:S(2)}) copy-start(f32[128,128]{1,0:T(8,128)} %copy-done.12) | copy-start | bytes 196612
  191.0 5.6 %collective-permute-start.1 = (bf16[3072,6]{0,1:T(8,128)(2,1)}, bf16[3072,6]{0,1:T(8,128)(2,1)S(1)}, u32[]{:S(2)}, u32[]{:S(2)}) collective-permute-start(bf16[3072,6]{0,1:T(8,128)(2,1)} %copy.144), channel_id=1, source_target_pairs={{1,0},{2,1},{3,2},{4,3},{5,4},{6,5},{7,6},{8,7},{9,8},{10,9},{11,1... | collective-permute-start | bytes 110600 | tf_op jit(solution)/shard_map/ppermute | solution.py:15
  197.0 0.7 copy-start.16
  197.0 0.7 copy-start.18
  197.0 0.7 copy-start.20
  197.0 0.7 copy-start.22
  197.0 0.7 copy-start.24
  197.1 0.7 copy-start.26
  197.8 9.1 %copy-start.1 = (bf16[8,8192]{1,0:T(8,128)(2,1)S(1)}, bf16[8,8192]{1,0:T(8,128)(2,1)}, u32[]{:S(2)}) copy-start(bf16[8,8192]{1,0:T(8,128)(2,1)} %param.6) | copy-start | bytes 393220
where the time goes:
time: 209 us; the launch traced here: 207 us
  blocking collectives  59.1 us (28%)
  waiting for transfers between devices  32.9 us (16%)
  matrix products  29.6 us (14%)
  other arithmetic  29.2 us (14%)
  starting transfers between devices  28.7 us (14%)
  local copies, waits for them, and re-layouts  26.1 us (12%)
    dot_general x36, matrix products, contract(): return jnp.einsum(form, first, second, preferred_element_type=jnp.float32)  29.6 us
    all_to_all x1, blocking collectives, shards(): lax.all_to_all(lax.all_to_all(send_shape(product), 'dp', split_axis=0, co...  19.6 us
    all_to_all x1, blocking collectives, shards(): lax.all_to_all(lax.all_to_all(return_shape(back_chan), 'dp', split_axis=4...  19.3 us
    all_to_all x1, waiting for transfers between devices, shards(): lax.all_to_all(lax.all_to_all(send_shape(conv_grad), 'dp', split_axis=0,...  12.7 us
    all_to_all x1, waiting for transfers between devices, shards(): lax.all_to_all(lax.all_to_all(return_shape(conv_chan), 'dp', split_axis=4...  12.1 us
    all_to_all x1, blocking collectives, shards(): lax.all_to_all(send_shape(product), 'dp', split_axis=0, concat_axis=2, ti...  10.6 us
    all_to_all x1, blocking collectives, shards(): lax.all_to_all(return_shape(back_chan), 'dp', split_axis=4, concat_axis=0...  9.62 us
    convert_element_type x1, other arithmetic, shards(): proj_grad = gathered.astype(jnp.bfloat16)  9.09 us
  transfers between devices with their start and end apart: 6, of which 6 were waited for; matrix products, arithmetic and copies ran while one was open for 6% of the time, Pallas kernels for 0%

commit v1 on v0

--- a/solution.py
+++ b/solution.py
@@ -120,48 +120,31 @@
         signal = inverse_dft(spec_re.reshape(flat_shape), spec_im.reshape(flat_shape), tables)
         return signal.reshape(local_groups, CPG, seq_len).astype(jnp.bfloat16)
 
-    def send_shape(block):
-        return block.reshape(groups, CPG, 1, 1, local_len)
+    devices = lanes_dp * lanes_ctx
+    owned = local_groups * CPG
+    everyone = ("dp", "ctx")
 
-    def return_shape(block):
-        return block.reshape(1, 1, local_groups, CPG, lanes_dp, lanes_ctx, local_len)
+    def to_owners(block):
+        pieces = block.reshape(devices, owned, local_len)
+        arrived = lax.all_to_all(pieces, everyone, split_axis=0, concat_axis=0, tiled=True)
+        return arrived.transpose(1, 0, 2)
 
-    prod_chan = lax.all_to_all(
-        lax.all_to_all(send_shape(product), "dp", split_axis=0, concat_axis=2, tiled=True),
-        "ctx",
-        split_axis=0,
-        concat_axis=3,
-        tiled=True,
-    )
+    def to_positions(block):
+        pieces = block.reshape(owned, devices, local_len).transpose(1, 0, 2)
+        return lax.all_to_all(pieces, everyone, split_axis=0, concat_axis=0, tiled=True)
+
+    prod_chan = to_owners(product)
     prod_re, prod_im = spectra(prod_chan)
     conv_re = ((filt_re * prod_re - filt_im * prod_im) * scale).astype(jnp.bfloat16)
     conv_im = ((filt_re * prod_im + filt_im * prod_re) * scale).astype(jnp.bfloat16)
     conv_chan = inverse_block(conv_re, conv_im)
-    conv_tok = lax.all_to_all(
-        lax.all_to_all(return_shape(conv_chan), "dp", split_axis=4, concat_axis=0, tiled=True),
-        "ctx",
-        split_axis=5,
-        concat_axis=1,
-        tiled=True,
-    )
-    grad_chan = lax.all_to_all(
-        lax.all_to_all(send_shape(conv_grad), "dp", split_axis=0, concat_axis=2, tiled=True),
-        "ctx",
-        split_axis=0,
-        concat_axis=3,
-        tiled=True,
-    )
+    conv_tok = to_positions(conv_chan)
+    grad_chan = to_owners(conv_grad)
     grad_re, grad_im = spectra(grad_chan)
     back_re = ((filt_re * grad_re + filt_im * grad_im) * scale).astype(jnp.bfloat16)
     back_im = ((filt_re * grad_im - filt_im * grad_re) * scale).astype(jnp.bfloat16)
     back_chan = inverse_block(back_re, back_im)
-    back_tok = lax.all_to_all(
-        lax.all_to_all(return_shape(back_chan), "dp", split_axis=4, concat_axis=0, tiled=True),
-        "ctx",
-        split_axis=5,
-        concat_axis=1,
-        tiled=True,
-    )
+    back_tok = to_positions(back_chan)
     cross_re = jnp.sum(prod_re * grad_re + prod_im * grad_im, axis=1).astype(jnp.bfloat16)
     cross_im = jnp.sum(prod_re * grad_im - prod_im * grad_re, axis=1).astype(jnp.bfloat16)
     filter_grad = inverse_dft(cross_re, cross_im, tables) * scale

time: 209 us -> 150 us (0.72)
  blocking collectives: 59.1 us -> 37.3 us
  other arithmetic: 29.2 us -> 17.1 us
  starting transfers between devices: 28.7 us -> 17.1 us
  local copies, waits for them, and re-layouts: 26.1 us -> 20.5 us
  matrix products: 29.6 us -> 25.7 us
  waiting for transfers between devices: 32.9 us -> 29.6 us
    all_to_all x4 -> x2, blocking collectives: 59.1 us -> 37.3 us  [the longest x1 19 us: to_owners(): lax.all_to_all(pieces, everyone, split_axis=0, concat_axis=0, tiled=True)]
    all_to_all x4 -> x2, starting transfers between devices: 21.3 us -> 10.2 us  [the longest x1 6.65 us: to_owners(): lax.all_to_all(pieces, everyone, split_axis=0, concat_axis=0, tiled=True)]
    convert_element_type x1, other arithmetic: 9.09 us -> 2.64 us  [shards(): proj_grad = gathered.astype(jnp.bfloat16)]
    convert_element_type x1, other arithmetic: 8.44 us -> 2.64 us  [shards(): features = total.astype(jnp.bfloat16)]
    all_to_all x8 -> x0, local copies, waits for them, and re-layouts: 5.09 us -> none  [the longest x1 1.47 us: shards(): lax.all_to_all(send_shape(conv_grad), 'dp', split_axis=0, concat_axis=2,...]
    unnamed x56 -> x67, local copies, waits for them, and re-layouts: 2.79 us -> 7.44 us
    dot_general x36, matrix products: 29.6 us -> 25.7 us  [contract(): return jnp.einsum(form, first, second, preferred_element_type=jnp.float32)]
    all_to_all x4 -> x2, waiting for transfers between devices: 31.7 us -> 28.1 us  [the longest x1 14.5 us: to_positions(): lax.all_to_all(pieces, everyone, split_axis=0, concat_axis=0, tiled=True)]
  transfers between devices with their start and end apart: 6 -> 4, of which waited for: 6 -> 4; matrix products, arithmetic and copies ran while one was open for 6% -> 5% of each run, Pallas kernels for 0% -> 0%
where the time goes in v1:
time: 150 us; the launch traced here: 149 us
  blocking collectives  37.3 us (25%)
  waiting for transfers between devices  29.6 us (20%)
  matrix products  25.7 us (17%)
  local copies, waits for them, and re-layouts  20.5 us (14%)
  starting transfers between devices  17.1 us (11%)
  other arithmetic  17.1 us (11%)
    dot_general x36, matrix products, contract(): return jnp.einsum(form, first, second, preferred_element_type=jnp.float32)  25.7 us
    all_to_all x1, blocking collectives, to_owners(): lax.all_to_all(pieces, everyone, split_axis=0, concat_axis=0, tiled=True)  19 us
    all_to_all x1, blocking collectives, to_positions(): lax.all_to_all(pieces, everyone, split_axis=0, concat_axis=0, tiled=True)  18.4 us
    all_to_all x1, waiting for transfers between devices, to_positions(): lax.all_to_all(pieces, everyone, split_axis=0, concat_axis=0, tiled=True)  14.5 us
    all_to_all x1, waiting for transfers between devices, to_owners(): lax.all_to_all(pieces, everyone, split_axis=0, concat_axis=0, tiled=True)  13.6 us
    unnamed x67, local copies, waits for them, and re-layouts  7.44 us
    ppermute x2, starting transfers between devices, shifted(): lax.ppermute(value, axis, [(source, source + steps) for source in range(f...  6.98 us
    all_to_all x1, starting transfers between devices, to_owners(): lax.all_to_all(pieces, everyone, split_axis=0, concat_axis=0, tiled=True)  6.65 us
  transfers between devices with their start and end apart: 4, of which 4 were waited for; matrix products, arithmetic and copies ran while one was open for 5% of the time, Pallas kernels for 0%

profile of v1, /device:TPU:1, one launch (start us, length us, event | category | flops | bytes accessed | tf_op | source)
XLA Modules:
  0.0 148.7 jit_solution(2795070763387493813)
XLA Ops:
  0.7 1.8 %copy.35 = bf16[3072,256]{0,1:T(8,128)(2,1)S(1)} copy(bf16[3072,256]{1,0:T(8,128)(2,1)} %param.4) | data formatting | bytes 3145728 | tf_op args[0]
  3.1 4.6 %collective-permute-start = (bf16[3072,6]{0,1:T(8,128)(2,1)}, bf16[3072,6]{0,1:T(8,128)(2,1)S(1)}, u32[]{:S(2)}, u32[]{:S(2)}) collective-permute-start(bf16[3072,6]{0,1:T(8,128)(2,1)} %slice.112), channel_id=1, source_target_pairs={{0,1},{1,2},{2,3},{3,4},{4,5},{5,6},{6,7},{7,8},{8,9},{9,10},{10,1... | collective-permute-start | bytes 110600 | tf_op jit(solution)/shard_map/ppermute | solution.py:15
  9.7 2.6 %fusion.8 = bf16[3072,256]{0,1:T(8,128)(2,1)S(1)} fusion(f32[3072,262]{0,1:T(8,128)S(1)} %maximum_convert_fusion, f32[3072]{0:T(1024)S(1)} %bitcast.221, f32[3072]{0:T(1024)S(1)} %bitcast.219, f32[3072]{0:T(1024)S(1)} %bitcast.217, f32[3072]{0:T(1024)S(1)} %bitcast.215, f32[3072]{0:T(1024)S(1)} %bitcast.213, f32[3072]{0:T(1024)S(1)} %bitcast.211, ...), kind=kLoop, calls=%fused_computation.24 | loop fusion | flops 11010048 | bytes 23678976 | tf_op jit(solution)/shard_map/convert_element_type | solution.py:101
  12.3 1.1 copy-done.2
  13.7 1.0 copy.57
  14.7 6.6 %all-to-all-start.2 = ((bf16[32,32,256]{2,1,0:T(8,128)(2,1)}), bf16[32,32,256]{2,1,0:T(8,128)(2,1)S(1)}, u32[]{:S(2)}, u32[]{:S(2)}) async-start(bf16[32,32,256]{2,1,0:T(8,128)(2,1)} %bitcast.24), calls=%async_computation.2 | async-start | bytes 1048576 | tf_op jit(solution)/shard_map/all_to_all | solution.py:129
  23.9 13.6 %all-to-all-done.2 = bf16[32,32,256]{2,1,0:T(8,128)(2,1)S(1)} async-done(((bf16[32,32,256]{2,1,0:T(8,128)(2,1)}), bf16[32,32,256]{2,1,0:T(8,128)(2,1)S(1)}, u32[]{:S(2)}, u32[]{:S(2)}) %all-to-all-start.2) | async-done | bytes 524320 | tf_op jit(solution)/shard_map/all_to_all | solution.py:129
  38.5 0.9 fusion.27
  39.4 0.7 fusion.110
  40.1 0.7 fusion.108
  40.8 0.7 convolution_subtract_fusion.1
  41.5 2.6 %fusion.22 = (bf16[32,128,128]{2,1,0:T(8,128)(2,1)S(1)}, bf16[32,128,128]{2,1,0:T(8,128)(2,1)S(1)}, f32[32,128,128]{2,1,0:T(8,128)}) fusion(f32[32,128,128]{2,1,0:T(8,128)S(1)} %convolution_subtract_fusion.1, f32[8,128,128]{2,1,0:T(8,128)S(1)} %convolution_subtract_fusion.7, f32[8,128,128]{2,1,0:T(8,128)S(1)} %convolution_add_fusion.5, ...), kind=kOutput, calls=%fused_computation.44 | convolution fusion | flops 140230656 | bytes 10485760 | tf_op jit(solution)/shard_map/rda,ae->rde/dot_general | solution.py:19
  44.2 0.7 fusion.106
  44.9 0.7 fusion.104
  45.6 0.7 convolution_subtract_fusion
  46.3 0.7 convolution_add_fusion
  47.7 0.7 fusion.38
  48.9 18.4 %all_to_all.20 = bf16[32,32,256]{2,1,0:T(8,128)(2,1)S(1)} all-to-all(bf16[32,32,256]{2,1,0:T(8,128)(2,1)S(1)} %bitcast.205), channel_id=1, replica_groups=mesh['dp'=4,'ctx'=8] {'dp','ctx'}, dimensions={0} | all-to-all | bytes 1048576 | tf_op jit(solution)/shard_map/all_to_all | solution.py:134
  67.4 1.3 copy.70
  68.7 2.7 %fusion.45 = (bf16[1024,256]{0,1:T(8,128)(2,1)S(1)}, bf16[1024,256]{0,1:T(8,128)(2,1)S(1)}, bf16[1024,256]{0,1:T(8,128)(2,1)}) fusion(f32[1024,256]{0,1:T(8,128)} %copy.70, bf16[3072,256]{0,1:T(8,128)(2,1)} %copy-done.2), kind=kLoop, calls=%fused_computation.107 | loop fusion | flops 2097152 | bytes 3670016 | tf_op jit(solution)/shard_map/convert_element_type | solution.py:155
  71.4 2.0 %copy.39 = bf16[1024,256]{1,0:T(8,128)(2,1)} copy(bf16[1024,256]{0,1:T(8,128)(2,1)} %get-tuple-element.18) | data formatting | bytes 1048576 | tf_op jit(solution)/shard_map/convert_element_type | solution.py:105
  73.4 19.0 %all_to_all.21 = bf16[32,32,256]{2,1,0:T(8,128)(2,1)S(1)} all-to-all(bf16[32,32,256]{2,1,0:T(8,128)(2,1)} %bitcast.206), channel_id=1, replica_groups=mesh['dp'=4,'ctx'=8] {'dp','ctx'}, dimensions={0} | all-to-all | bytes 1048576 | tf_op jit(solution)/shard_map/all_to_all | solution.py:129
  92.4 1.1 copy.40
  93.5 2.0 %reshape_reshape.6 = bf16[32,64,128]{2,1,0:T(8,128)(2,1)} reshape(bf16[32,32,256]{2,1,0:T(8,128)(2,1)} %copy.40) | data formatting | bytes 1048576 | tf_op jit(solution)/shard_map/reshape;reshape | solution.py:52
  95.5 1.7 %fusion.136 = f32[32,128,128]{2,1,0:T(8,128)S(1)} fusion(bf16[32,64,128]{2,1,0:T(8,128)(2,1)} %reshape_reshape.6), kind=kOutput, calls=%fused_computation.194 | convolution fusion | flops 67231744 | bytes 2621440 | tf_op jit(solution)/shard_map/db,rba->rda/dot_general | solution.py:19
  97.2 0.9 fusion.31
  98.2 0.7 fusion.120
  98.8 0.7 fusion.116
  100.7 1.3 fusion.16
  102.3 1.7 %bitcast_reduce_fusion.1 = (bf16[8,128,128]{2,1,0:T(8,128)(2,1)S(1)}, bf16[8,128,128]{2,1,0:T(8,128)(2,1)}) fusion(f32[32,128,128]{2,1,0:T(8,128)S(1)} %convolution_subtract_fusion.3, f32[32,128,128]{2,1,0:T(8,128)S(1)} %convolution_subtract_fusion.1, f32[32,128,128]{2,1,0:T(8,128)S(1)} %get-tuple-element.31, f32[32,128,128]{2,1,0:T(8,128)S(1)} %copy-done.3), kind=kLoop, calls=%fused_computation.49 | loop fusion | flops 3932160 | bytes 8912896 | tf_op jit(solution)/shard_map/reduce_sum | solution.py:148
  104.5 0.7 fusion.114
  105.2 0.7 fusion.112
  105.9 0.7 convolution_subtract_fusion.2
  106.6 0.7 convolution_add_fusion.2
  108.0 0.7 fusion.39
  108.9 1.1 copy.105
  110.0 3.5 %all-to-all-start.1 = ((bf16[32,32,256]{2,1,0:T(8,128)(2,1)}), bf16[32,32,256]{2,1,0:T(8,128)(2,1)}, u32[]{:S(2)}, u32[]{:S(2)}) async-start(bf16[32,32,256]{2,1,0:T(8,128)(2,1)} %bitcast.200), calls=%async_computation.1 | async-start | bytes 1048576 | tf_op jit(solution)/shard_map/all_to_all | solution.py:134
  115.3 14.5 %all-to-all-done.1 = bf16[32,32,256]{2,1,0:T(8,128)(2,1)} async-done(((bf16[32,32,256]{2,1,0:T(8,128)(2,1)}), bf16[32,32,256]{2,1,0:T(8,128)(2,1)}, u32[]{:S(2)}, u32[]{:S(2)}) %all-to-all-start.1) | async-done | bytes 524320 | tf_op jit(solution)/shard_map/all_to_all | solution.py:134
  129.8 2.1 %bitcast_convert_fusion.1 = f32[1024,256]{1,0:T(8,128)} fusion(bf16[32,32,256]{2,1,0:T(8,128)(2,1)} %all-to-all-done.1), kind=kLoop, calls=%fused_computation.121 | loop fusion | flops 262144 | bytes 1572864 | tf_op jit(solution)/shard_map/convert_element_type | solution.py:151
  131.9 2.5 %copy.54 = f32[1024,256]{0,1:T(8,128)} copy(f32[1024,256]{1,0:T(8,128)} %bitcast_convert_fusion.1) | data formatting | bytes 2097152 | tf_op jit(solution)/shard_map/convert_element_type | solution.py:151
  134.4 2.4 %fusion.46 = (bf16[1024,256]{0,1:T(8,128)(2,1)S(1)}, bf16[1024,256]{0,1:T(8,128)(2,1)}) fusion(f32[1024,256]{0,1:T(8,128)} %copy.54, bf16[1024,256]{0,1:T(8,128)(2,1)S(1)} %copy-done.10, bf16[3072,256]{0,1:T(8,128)(2,1)} %copy-done.2), kind=kLoop, calls=%fused_computation.108 | loop fusion | flops 1572864 | bytes 3145728 | tf_op jit(solution)/shard_map/convert_element_type | solution.py:154
  137.5 2.4 %collective-permute-start.1 = (bf16[3072,6]{0,1:T(8,128)(2,1)}, bf16[3072,6]{0,1:T(8,128)(2,1)}, u32[]{:S(2)}, u32[]{:S(2)}) collective-permute-start(bf16[3072,6]{0,1:T(8,128)(2,1)} %pad_maximum_fusion), channel_id=1, source_target_pairs={{1,0},{2,1},{3,2},{4,3},{5,4},{6,5},{7,6},{8,7},{9,8},{10,9},{11,1... | collective-permute-start | bytes 110600 | tf_op jit(solution)/shard_map/ppermute | solution.py:15
  140.3 0.9 copy.106
  141.1 1.0 copy.72
  142.2 1.1 collective-permute-done.1
  143.2 1.2 maximum_convert_fusion.1
  144.5 2.6 %fusion.1 = bf16[3072,256]{0,1:T(8,128)(2,1)S(1)} fusion(f32[3072,262]{0,1:T(8,128)S(1)} %maximum_convert_fusion.1, f32[3072]{0:T(1024)S(1)} %bitcast.222, f32[3072]{0:T(1024)S(1)} %bitcast.220, f32[3072]{0:T(1024)S(1)} %bitcast.218, f32[3072]{0:T(1024)S(1)} %bitcast.216, f32[3072]{0:T(1024)S(1)} %bitcast.214, f32[3072]{0:T(1024)S(1)} %bitcast.212, ...), kind=kLoop, calls=%fused_computation.10 | loop fusion | flops 11010048 | bytes 23678976 | tf_op jit(solution)/shard_map/convert_element_type | solution.py:163
  147.1 1.6 %copy.73 = bf16[3072,256]{1,0:T(8,128)(2,1)} copy(bf16[3072,256]{0,1:T(8,128)(2,1)S(1)} %fusion.1) | data formatting | bytes 3145728
  (93 shorter events, 12.8 us)
Async XLA Ops:
  0.6 7.1 %copy-start = (bf16[8,8192]{1,0:T(8,128)(2,1)S(1)}, bf16[8,8192]{1,0:T(8,128)(2,1)}, u32[]{:S(2)}) copy-start(bf16[8,8192]{1,0:T(8,128)(2,1)} %param.6) | copy-start | bytes 393220
  0.6 7.0 %copy-start.18 = (bf16[7,3072]{1,0:T(8,128)(2,1)S(1)}, bf16[7,3072]{1,0:T(8,128)(2,1)}, u32[]{:S(2)}) copy-start(bf16[7,3072]{1,0:T(8,128)(2,1)} %param.5) | copy-start | bytes 129028
  0.7 7.8 %copy-start.17 = (bf16[1024,256]{1,0:T(8,128)(2,1)S(1)}, bf16[1024,256]{1,0:T(8,128)(2,1)}, u32[]{:S(2)}) copy-start(bf16[1024,256]{1,0:T(8,128)(2,1)} %param.7) | copy-start | bytes 1572868
  3.1 6.1 %collective-permute-start = (bf16[3072,6]{0,1:T(8,128)(2,1)}, bf16[3072,6]{0,1:T(8,128)(2,1)S(1)}, u32[]{:S(2)}, u32[]{:S(2)}) collective-permute-start(bf16[3072,6]{0,1:T(8,128)(2,1)} %slice.112), channel_id=1, source_target_pairs={{0,1},{1,2},{2,3},{3,4},{4,5},{5,6},{6,7},{7,8},{8,9},{9,10},{10,1... | collective-permute-start | bytes 110600 | tf_op jit(solution)/shard_map/ppermute | solution.py:15
  7.8 1.8 %copy-start.19 = (f32[1,3072]{1,0:T(1,128)}, f32[1,3072]{1,0:T(1,128)S(1)}, u32[]{:S(2)}) copy-start(f32[1,3072]{1,0:T(1,128)S(1)} %get-tuple-element.24) | copy-start | bytes 36868
  7.8 1.8 %copy-start.21 = (f32[1,3072]{1,0:T(1,128)}, f32[1,3072]{1,0:T(1,128)S(1)}, u32[]{:S(2)}) copy-start(f32[1,3072]{1,0:T(1,128)S(1)} %get-tuple-element.25) | copy-start | bytes 36868
  7.8 1.8 %copy-start.23 = (f32[1,3072]{1,0:T(1,128)}, f32[1,3072]{1,0:T(1,128)S(1)}, u32[]{:S(2)}) copy-start(f32[1,3072]{1,0:T(1,128)S(1)} %get-tuple-element.26) | copy-start | bytes 36868
  7.8 1.8 %copy-start.25 = (f32[1,3072]{1,0:T(1,128)}, f32[1,3072]{1,0:T(1,128)S(1)}, u32[]{:S(2)}) copy-start(f32[1,3072]{1,0:T(1,128)S(1)} %get-tuple-element.27) | copy-start | bytes 36868
  7.8 1.8 %copy-start.27 = (f32[1,3072]{1,0:T(1,128)}, f32[1,3072]{1,0:T(1,128)S(1)}, u32[]{:S(2)}) copy-start(f32[1,3072]{1,0:T(1,128)S(1)} %get-tuple-element.28) | copy-start | bytes 36868
  7.8 1.8 %copy-start.29 = (f32[1,3072]{1,0:T(1,128)}, f32[1,3072]{1,0:T(1,128)S(1)}, u32[]{:S(2)}) copy-start(f32[1,3072]{1,0:T(1,128)S(1)} %get-tuple-element.29) | copy-start | bytes 36868
  8.5 13.3 %copy-start.13 = (f32[128,128]{1,0:T(8,128)}, f32[128,128]{1,0:T(8,128)S(1)}, u32[]{:S(2)}) copy-start(f32[128,128]{1,0:T(8,128)S(1)} %get-tuple-element.32) | copy-start | bytes 196612
  8.5 13.4 %copy-start.15 = (f32[128,128]{1,0:T(8,128)}, f32[128,128]{1,0:T(8,128)S(1)}, u32[]{:S(2)}) copy-start(f32[128,128]{1,0:T(8,128)S(1)} %get-tuple-element.33) | copy-start | bytes 196612
  8.7 3.6 %copy-start.9 = (bf16[1024,256]{0,1:T(8,128)(2,1)}, bf16[1024,256]{0,1:T(8,128)(2,1)S(1)}, u32[]{:S(2)}) copy-start(bf16[1024,256]{0,1:T(8,128)(2,1)S(1)} %copy.55) | copy-start | bytes 1572868
  12.3 1.1 copy-start.2
  14.7 22.8 %all-to-all-start.2 = ((bf16[32,32,256]{2,1,0:T(8,128)(2,1)}), bf16[32,32,256]{2,1,0:T(8,128)(2,1)S(1)}, u32[]{:S(2)}, u32[]{:S(2)}) async-start(bf16[32,32,256]{2,1,0:T(8,128)(2,1)} %bitcast.24), calls=%async_computation.2 | async-start | bytes 1048576 | tf_op jit(solution)/shard_map/all_to_all | solution.py:129
  23.4 18.1 %copy-start.4 = (f32[8,128,128]{2,1,0:T(8,128)}, f32[8,128,128]{2,1,0:T(8,128)S(1)}, u32[]{:S(2)}) copy-start(f32[8,128,128]{2,1,0:T(8,128)S(1)} %convolution_add_fusion.5) | copy-start | bytes 1572868
  23.8 17.7 %copy-start.6 = (f32[8,128,128]{2,1,0:T(8,128)}, f32[8,128,128]{2,1,0:T(8,128)S(1)}, u32[]{:S(2)}) copy-start(f32[8,128,128]{2,1,0:T(8,128)S(1)} %convolution_subtract_fusion.7) | copy-start | bytes 1572868
  95.5 1.7 %copy-start.8 = (bf16[32,64,128]{2,1,0:T(8,128)(2,1)S(1)}, bf16[32,64,128]{2,1,0:T(8,128)(2,1)}, u32[]{:S(2)}) copy-start(bf16[32,64,128]{2,1,0:T(8,128)(2,1)} %reshape_reshape.6) | copy-start | bytes 1572868
  99.5 1.0 copy-start.5
  99.5 1.2 copy-start.7
  100.7 1.6 %copy-start.3 = (f32[32,128,128]{2,1,0:T(8,128)S(1)}, f32[32,128,128]{2,1,0:T(8,128)}, u32[]{:S(2)}) copy-start(f32[32,128,128]{2,1,0:T(8,128)} %get-tuple-element.30) | copy-start | bytes 6291460
  108.7 4.8 %copy-start.11 = (bf16[8,128,128]{2,1,0:T(8,128)(2,1)S(1)}, bf16[8,128,128]{2,1,0:T(8,128)(2,1)}, u32[]{:S(2)}) copy-start(bf16[8,128,128]{2,1,0:T(8,128)(2,1)} %get-tuple-element.7) | copy-start | bytes 786436
  110.0 4.9 %copy-start.14 = (f32[128,128]{1,0:T(8,128)S(1)}, f32[128,128]{1,0:T(8,128)}, u32[]{:S(2)}) copy-start(f32[128,128]{1,0:T(8,128)} %copy-done.13) | copy-start | bytes 196612
  110.0 4.9 %copy-start.16 = (f32[128,128]{1,0:T(8,128)S(1)}, f32[128,128]{1,0:T(8,128)}, u32[]{:S(2)}) copy-start(f32[128,128]{1,0:T(8,128)} %copy-done.15) | copy-start | bytes 196612
  110.0 19.8 %all-to-all-start.1 = ((bf16[32,32,256]{2,1,0:T(8,128)(2,1)}), bf16[32,32,256]{2,1,0:T(8,128)(2,1)}, u32[]{:S(2)}, u32[]{:S(2)}) async-start(bf16[32,32,256]{2,1,0:T(8,128)(2,1)} %bitcast.200), calls=%async_computation.1 | async-start | bytes 1048576 | tf_op jit(solution)/shard_map/all_to_all | solution.py:134
  115.3 19.2 %copy-start.10 = (bf16[1024,256]{0,1:T(8,128)(2,1)S(1)}, bf16[1024,256]{0,1:T(8,128)(2,1)}, u32[]{:S(2)}) copy-start(bf16[1024,256]{0,1:T(8,128)(2,1)} %copy-done.9) | copy-start | bytes 1572868
  136.9 4.2 %copy-start.12 = (bf16[1024,256]{0,1:T(8,128)(2,1)S(1)}, bf16[1024,256]{0,1:T(8,128)(2,1)}, u32[]{:S(2)}) copy-start(bf16[1024,256]{0,1:T(8,128)(2,1)} %get-tuple-element.22) | copy-start | bytes 1572868
  137.5 5.7 %collective-permute-start.1 = (bf16[3072,6]{0,1:T(8,128)(2,1)}, bf16[3072,6]{0,1:T(8,128)(2,1)}, u32[]{:S(2)}, u32[]{:S(2)}) collective-permute-start(bf16[3072,6]{0,1:T(8,128)(2,1)} %pad_maximum_fusion), channel_id=1, source_target_pairs={{1,0},{2,1},{3,2},{4,3},{5,4},{6,5},{7,6},{8,7},{9,8},{10,9},{11,1... | collective-permute-start | bytes 110600 | tf_op jit(solution)/shard_map/ppermute | solution.py:15
  142.1 2.3 %copy-start.20 = (f32[1,3072]{1,0:T(1,128)S(1)}, f32[1,3072]{1,0:T(1,128)}, u32[]{:S(2)}) copy-start(f32[1,3072]{1,0:T(1,128)} %copy-done.19) | copy-start | bytes 36868
  142.1 2.3 %copy-start.22 = (f32[1,3072]{1,0:T(1,128)S(1)}, f32[1,3072]{1,0:T(1,128)}, u32[]{:S(2)}) copy-start(f32[1,3072]{1,0:T(1,128)} %copy-done.21) | copy-start | bytes 36868
  142.1 2.3 %copy-start.24 = (f32[1,3072]{1,0:T(1,128)S(1)}, f32[1,3072]{1,0:T(1,128)}, u32[]{:S(2)}) copy-start(f32[1,3072]{1,0:T(1,128)} %copy-done.23) | copy-start | bytes 36868
  142.1 2.3 %copy-start.26 = (f32[1,3072]{1,0:T(1,128)S(1)}, f32[1,3072]{1,0:T(1,128)}, u32[]{:S(2)}) copy-start(f32[1,3072]{1,0:T(1,128)} %copy-done.25) | copy-start | bytes 36868
  142.1 2.3 %copy-start.28 = (f32[1,3072]{1,0:T(1,128)S(1)}, f32[1,3072]{1,0:T(1,128)}, u32[]{:S(2)}) copy-start(f32[1,3072]{1,0:T(1,128)} %copy-done.27) | copy-start | bytes 36868
  142.1 2.3 %copy-start.30 = (f32[1,3072]{1,0:T(1,128)S(1)}, f32[1,3072]{1,0:T(1,128)}, u32[]{:S(2)}) copy-start(f32[1,3072]{1,0:T(1,128)} %copy-done.29) | copy-start | bytes 36868
  144.5 4.2 %copy-start.1 = (bf16[8,8192]{1,0:T(8,128)(2,1)S(1)}, bf16[8,8192]{1,0:T(8,128)(2,1)}, u32[]{:S(2)}) copy-start(bf16[8,8192]{1,0:T(8,128)(2,1)} %param.6) | copy-start | bytes 393220

commit v2 on v1

v2 whole, which is shorter than its diff:
```python
import math

import jax
import jax.numpy as jnp
import numpy as np
from jax import lax
from jax.experimental import pallas as pl
from jax.experimental.pallas import tpu as pltpu
from jax.sharding import PartitionSpec as P

CPG = 4
TAPS = 7
PAIRS = CPG // 2
EVERYONE = ("dp", "ctx")
VMEM_LIMIT = 40 * 1024 * 1024


def shifted(value, axis, steps):
    count = lax.axis_size(axis)
    first, last = (max(0, -steps), min(count, count - steps))
    return lax.ppermute(value, axis, [(source, source + steps) for source in range(first, last)])


def sizes_of(seq_len):
    padded = 2 * seq_len
    inner = max(d for d in range(1, seq_len + 1) if seq_len % d == 0 and d * d <= padded)
    return padded, inner, padded // inner


def table(count_out, count_in, period):
    turns = np.arange(count_out, dtype=np.int64)[:, None] * np.arange(count_in, dtype=np.int64)
    angle = (turns % period).astype(np.float64) * (2.0 * math.pi / period)
    return np.cos(angle), np.sin(angle)


def make_tables(seq_len, sources):
    padded, inner, outer = sizes_of(seq_len)
    half = outer // 2
    fold = half // sources
    order = np.arange(half).reshape(sources, fold).T.reshape(-1)
    cos_o, sin_o = table(outer, half, outer)
    cos_i, sin_i = table(inner, inner, inner)
    cos_p, sin_p = cos_o[:, order], sin_o[:, order]
    narrow = lambda blocks: jnp.asarray(np.block(blocks).astype(np.float32)).astype(jnp.bfloat16)
    twist = [jnp.asarray(t.astype(np.float32)) for t in table(outer, inner, padded)]
    return {
        "first": narrow([[cos_p, sin_p], [-sin_p, cos_p]]),
        "second": narrow([[cos_i, -sin_i], [sin_i, cos_i]]),
        "third": narrow([[cos_i, sin_i], [-sin_i, cos_i]]),
        "fourth": narrow([[cos_p.T, -sin_p.T], [sin_p.T, cos_p.T]]),
        "first_real": narrow([[cos_o], [-sin_o]]),
        "fourth_real": narrow([[cos_o.T, -sin_o.T]]),
        "twist_re": twist[0],
        "twist_im": twist[1],
    }


LANES = 128


def spread(tall, count, stride, first, height, width):
    tiles = [tall[pl.ds(t * height + first, count, stride=stride), :] for t in range(width[0] // LANES, width[1] // LANES)]
    return tiles[0] if len(tiles) == 1 else jnp.concatenate(tiles, axis=1)


def put_spread(tall, values, stride, first, height, width):
    for i, t in enumerate(range(width[0] // LANES, width[1] // LANES)):
        tall[pl.ds(t * height + first, values.shape[0], stride=stride), :] = values[:, i * LANES : (i + 1) * LANES]


def dot(left, right):
    return jnp.dot(left, right, preferred_element_type=jnp.float32)


def transform_filters(long_filter, tables, seq_len):
    padded, inner, outer = sizes_of(seq_len)
    half = outer // 2
    groups = long_filter.shape[0]
    scale = seq_len ** -0.5

    def kernel(x_ref, first_ref, second_ref, tr_ref, ti_ref, out_ref, tall):
        height = half * groups
        for b in range(half):
            for t in range(inner // LANES):
                at = t * height + b * groups
                lanes = slice(b * inner + t * LANES, b * inner + (t + 1) * LANES)
                tall[at : at + groups, :] = x_ref[:, lanes].astype(jnp.float32)
        for g in range(groups):
            x = spread(tall, half, groups, g, height, (0, inner)).astype(jnp.bfloat16)
            f = dot(first_ref[...], x)
            f_re, f_im = f[:outer], f[outer:]
            g_re = (f_re * tr_ref[...] + f_im * ti_ref[...]).astype(jnp.bfloat16)
            g_im = (f_im * tr_ref[...] - f_re * ti_ref[...]).astype(jnp.bfloat16)
            spec = dot(g_re, second_ref[:inner]) + dot(g_im, second_ref[inner:])
            out_ref[g * outer : (g + 1) * outer, :] = spec * scale

    return pl.pallas_call(
        kernel,
        name="filter_dft",
        out_shape=jax.ShapeDtypeStruct((groups * outer, 2 * inner), jnp.float32),
        scratch_shapes=[pltpu.VMEM((half * groups * inner // LANES, LANES), jnp.float32)],
        compiler_params=pltpu.CompilerParams(vmem_limit_bytes=VMEM_LIMIT),
        cost_estimate=pl.CostEstimate(flops=200_000_000, bytes_accessed=2_000_000, transcendentals=0),
    )(long_filter, tables["first_real"], tables["second"], tables["twist_re"], tables["twist_im"])


def filtered(arrived, filters, tables, seq_len, other=None):
    padded, inner, outer = sizes_of(seq_len)
    half = outer // 2
    sources, channels, local = arrived.shape
    fold = local // inner
    groups = channels // CPG
    backward = other is not None

    def kernel(*refs):
        if backward:
            (x_ref, f_ref, k_ref, first_ref, second_ref, third_ref, fourth_ref, tr_ref, ti_ref,
             y_ref, cross_ref, tall, wide, stage, turn) = refs
        else:
            (x_ref, f_ref, first_ref, second_ref, third_ref, fourth_ref, tr_ref, ti_ref,
             y_ref, z_ref, tall, wide, stage, turn) = refs
        height = sources * channels
        for t in range(local // LANES):
            block = x_ref[:, :, t * LANES : (t + 1) * LANES].astype(jnp.float32)
            tall[t * height : (t + 1) * height, :] = block.reshape(height, LANES)
        for c in range(channels):
            pair, part = divmod(c, 2)
            for h in range(fold):
                rows = spread(tall, sources, channels, c, height, (h * inner, (h + 1) * inner))
                at = part * half + h * sources
                wide[at : at + sources, pair * inner : (pair + 1) * inner] = rows.astype(jnp.bfloat16)
        for g in range(groups):
            span = PAIRS * inner
            f = dot(first_ref[...], wide[:, g * span : (g + 1) * span])
            for p in range(PAIRS):
                f_re = f[:outer, p * inner : (p + 1) * inner]
                f_im = f[outer:, p * inner : (p + 1) * inner]
                at = (g * PAIRS + p) * outer
                stage[at : at + outer, :inner] = (f_re * tr_ref[...] + f_im * ti_ref[...]).astype(jnp.bfloat16)
                stage[at : at + outer, inner:] = (f_im * tr_ref[...] - f_re * ti_ref[...]).astype(jnp.bfloat16)
        for g in range(groups):
            s_re = f_ref[g * outer : (g + 1) * outer, :inner]
            s_im = f_ref[g * outer : (g + 1) * outer, inner:]
            cross_re = cross_im = None
            for p in range(PAIRS):
                at = (g * PAIRS + p) * outer
                z = dot(stage[at : at + outer, :], second_ref[...])
                z_re, z_im = z[:, :inner], z[:, inner:]
                if backward:
                    k_re = k_ref[at : at + outer, :inner].astype(jnp.float32)
                    k_im = k_ref[at : at + outer, inner:].astype(jnp.float32)
                    part_re = k_re * z_re + k_im * z_im
                    part_im = k_re * z_im - k_im * z_re
                    cross_re = part_re if cross_re is None else cross_re + part_re
                    cross_im = part_im if cross_im is None else cross_im + part_im
                    o_re = s_re * z_re + s_im * z_im
                    o_im = s_re * z_im - s_im * z_re
                else:
                    z_ref[at : at + outer, :] = z
                    o_re = s_re * z_re - s_im * z_im
                    o_im = s_re * z_im + s_im * z_re
                stage[at : at + outer, :inner] = o_re.astype(jnp.bfloat16)
                stage[at : at + outer, inner:] = o_im.astype(jnp.bfloat16)
            if backward:
                cross_ref[g * outer : (g + 1) * outer, :inner] = cross_re.astype(jnp.bfloat16)
                cross_ref[g * outer : (g + 1) * outer, inner:] = cross_im.astype(jnp.bfloat16)
        for pair in range(groups * PAIRS):
            at = pair * outer
            h = dot(stage[at : at + outer, :], third_ref[...])
            h_re, h_im = h[:, :inner], h[:, inner:]
            lanes = slice(pair * inner, (pair + 1) * inner)
            turn[:outer, lanes] = (h_re * tr_ref[...] - h_im * ti_ref[...]).astype(jnp.bfloat16)
            turn[outer:, lanes] = (h_im * tr_ref[...] + h_re * ti_ref[...]).astype(jnp.bfloat16)
        for g in range(groups):
            span = PAIRS * inner
            y = dot(fourth_ref[...], turn[:, g * span : (g + 1) * span]) * (1.0 / padded)
            for p in range(PAIRS):
                for part in range(2):
                    c = (g * PAIRS + p) * 2 + part
                    for h in range(fold):
                        at = part * half + h * sources
                        rows = y[at : at + sources, p * inner : (p + 1) * inner]
                        put_spread(tall, rows, channels, c, height, (h * inner, (h + 1) * inner))
        for t in range(local // LANES):
            block = tall[t * height : (t + 1) * height, :].reshape(sources, channels, LANES)
            y_ref[:, :, t * LANES : (t + 1) * LANES] = block.astype(jnp.bfloat16)

    pairs = groups * PAIRS
    if backward:
        extra = jax.ShapeDtypeStruct((groups * outer, 2 * inner), jnp.bfloat16)
    else:
        extra = jax.ShapeDtypeStruct((pairs * outer, 2 * inner), jnp.float32)
    operands = [arrived, filters] + ([other] if backward else [])
    operands += [tables[n] for n in ("first", "second", "third", "fourth", "twist_re", "twist_im")]
    return pl.pallas_call(
        kernel,
        name="correlate" if backward else "convolve",
        out_shape=(jax.ShapeDtypeStruct(arrived.shape, jnp.bfloat16), extra),
        scratch_shapes=[
            pltpu.VMEM((sources * channels * local // LANES, LANES), jnp.float32),
            pltpu.VMEM((outer, pairs * inner), jnp.bfloat16),
            pltpu.VMEM((pairs * outer, 2 * inner), jnp.bfloat16),
            pltpu.VMEM((2 * outer, pairs * inner), jnp.bfloat16),
        ],
        compiler_params=pltpu.CompilerParams(vmem_limit_bytes=VMEM_LIMIT),
        cost_estimate=pl.CostEstimate(flops=2_000_000_000, bytes_accessed=5_000_000, transcendentals=0),
    )(*operands)


def filter_gradient(cross, tables, seq_len):
    padded, inner, outer = sizes_of(seq_len)
    half = outer // 2
    groups = cross.shape[0] // outer
    scale = seq_len ** -0.5 / padded

    def kernel(s_ref, third_ref, fourth_ref, tr_ref, ti_ref, out_ref, tall, turn):
        for g in range(groups):
            h = dot(s_ref[g * outer : (g + 1) * outer, :], third_ref[...])
            h_re, h_im = h[:, :inner], h[:, inner:]
            turn[:outer, g * inner : (g + 1) * inner] = (h_re * tr_ref[...] - h_im * ti_ref[...]).astype(jnp.bfloat16)
            turn[outer:, g * inner : (g + 1) * inner] = (h_im * tr_ref[...] + h_re * ti_ref[...]).astype(jnp.bfloat16)
        for g in range(groups):
            y = dot(fourth_ref[...], turn[:, g * inner : (g + 1) * inner]) * scale
            put_spread(tall, y, groups, g, half * groups, (0, inner))
        for b in range(half):
            for t in range(inner // LANES):
                at = (t * half + b) * groups
                out_ref[:, b * inner + t * LANES : b * inner + (t + 1) * LANES] = tall[at : at + groups, :]

    return pl.pallas_call(
        kernel,
        name="filter_gradient",
        out_shape=jax.ShapeDtypeStruct((groups, seq_len), jnp.float32),
        scratch_shapes=[
            pltpu.VMEM((half * groups * inner // LANES, LANES), jnp.float32),
            pltpu.VMEM((2 * outer, groups * inner), jnp.bfloat16),
        ],
        compiler_params=pltpu.CompilerParams(vmem_limit_bytes=VMEM_LIMIT),
        cost_estimate=pl.CostEstimate(flops=200_000_000, bytes_accessed=2_000_000, transcendentals=0),
    )(cross, tables["third"], tables["fourth_real"], tables["twist_re"], tables["twist_im"])


def shards(projections, short_filter, long_filter, out_grad):
    width, local_len = out_grad.shape
    devices = lax.axis_size(EVERYONE)
    seq_len = local_len * devices
    owned = width // devices
    tables = make_tables(seq_len, devices)
    weights = short_filter.astype(jnp.float32)
    rim_len = TAPS - 1
    earlier = shifted(projections[:, local_len - rim_len :], EVERYONE, 1)
    extended = jnp.concatenate([earlier, projections], axis=1).astype(jnp.float32)
    total = jnp.zeros(projections.shape, jnp.float32)
    for lag in range(TAPS):
        total = (
            total + weights[lag][:, None] * extended[:, rim_len - lag : rim_len - lag + local_len]
        )
    features = total.astype(jnp.bfloat16)
    query = features[:width].astype(jnp.float32)
    key_part = features[width : 2 * width].astype(jnp.float32)
    value_part = features[2 * width :].astype(jnp.float32)
    product = (key_part * value_part).astype(jnp.bfloat16)
    cotangent = out_grad.astype(jnp.float32)
    conv_grad = (cotangent * query).astype(jnp.bfloat16)

    def exchange(block):
        pieces = block.reshape(devices, owned, local_len)
        return lax.all_to_all(pieces, EVERYONE, split_axis=0, concat_axis=0, tiled=True)

    filters = transform_filters(long_filter, tables, seq_len)
    prod_chan = exchange(product)
    conv_grad, prod_chan = lax.optimization_barrier((conv_grad, prod_chan))
    grad_chan = exchange(conv_grad)
    conv_chan, prod_spec = filtered(prod_chan, filters, tables, seq_len)
    conv_chan, grad_chan = lax.optimization_barrier((conv_chan, grad_chan))
    conv_tok = exchange(conv_chan)
    back_chan, cross = filtered(grad_chan, filters, tables, seq_len, prod_spec)
    back_chan, conv_tok = lax.optimization_barrier((back_chan, conv_tok))
    back_tok = exchange(back_chan)
    filter_grad = filter_gradient(cross, tables, seq_len)

    conv = conv_tok.reshape(width, local_len).astype(jnp.float32)
    back = back_tok.reshape(width, local_len).astype(jnp.float32)
    mixed = (query * conv).astype(jnp.bfloat16)
    query_grad = (cotangent * conv).astype(jnp.bfloat16)
    key_grad = (back * value_part).astype(jnp.bfloat16)
    value_grad = (back * key_part).astype(jnp.bfloat16)
    feat_grad = jnp.concatenate([query_grad, key_grad, value_grad], axis=0)
    later = shifted(feat_grad[:, :rim_len], EVERYONE, -1)
    extended_grad = jnp.concatenate([feat_grad, later], axis=1).astype(jnp.float32)
    gathered = jnp.zeros(projections.shape, jnp.float32)
    for lag in range(TAPS):
        gathered = gathered + weights[lag][:, None] * extended_grad[:, lag : lag + local_len]
    proj_grad = gathered.astype(jnp.bfloat16)
    return (mixed, proj_grad, filter_grad)


def solution(mesh):
    placed = (P(None, EVERYONE), P(), P(EVERYONE, None), P(None, EVERYONE))
    return jax.shard_map(
        shards,
        mesh=mesh,
        in_specs=placed,
        out_specs=(P(None, EVERYONE), P(None, EVERYONE), P(EVERYONE, None)),
        check_vma=False,
    )
```

time: 150 us -> 113 us (0.75)
  matrix products: 25.7 us -> 0 us
  blocking collectives: 37.3 us -> 22.7 us
  Pallas kernels: 0 us -> 9.89 us
  waiting for transfers between devices: 29.6 us -> 36.5 us
  local copies, waits for them, and re-layouts: 20.5 us -> 14.5 us
  other arithmetic: 17.1 us -> 11.8 us
    dot_general x36 -> x0, matrix products: 25.7 us -> none  [contract(): return jnp.einsum(form, first, second, preferred_element_type=jnp.float32)]
    all_to_all x2 -> x1, blocking collectives: 37.3 us -> 22.7 us  [exchange(): lax.all_to_all(pieces, EVERYONE, split_axis=0, concat_axis=0, tiled=True)]
    pallas_call x0 -> x4, Pallas kernels: none -> 9.89 us  [the longest x2 7.55 us: filtered(): pl.pallas_call(kernel, name='correlate' if backward else 'convolve', out_...]
    all_to_all x2 -> x3, waiting for transfers between devices: 28.1 us -> 35.7 us  [exchange(): lax.all_to_all(pieces, EVERYONE, split_axis=0, concat_axis=0, tiled=True)]
    unnamed x67 -> x62, local copies, waits for them, and re-layouts: 7.44 us -> 10.6 us
    convert_element_type x5 -> x0, local copies, waits for them, and re-layouts: 2.73 us -> none  [the longest x4 1.73 us: inverse_block(): return signal.reshape(local_groups, CPG, seq_len).astype(jnp.bfloat16)]
    convert_element_type x2 -> x1, other arithmetic: 2.64 us -> 0.4 us  [shards(): product = (key_part * value_part).astype(jnp.bfloat16)]
    another operation x2 -> x0, local copies, waits for them, and re-layouts: 2.19 us -> none  [forward_dft(): folded = signal.reshape(count, cos_outer.shape[1], cos_inner.shape[0])]
  transfers between devices with their start and end apart: 4 -> 5, of which waited for: 4 -> 4; matrix products, arithmetic and copies ran while one was open for 5% -> 3% of each run, Pallas kernels for 0% -> 9%
where the time goes in v2:
time: 113 us; the launch traced here: 112 us
  waiting for transfers between devices  36.5 us (32%)
  blocking collectives  22.7 us (20%)
  starting transfers between devices  15.9 us (14%)
  local copies, waits for them, and re-layouts  14.5 us (13%)
  other arithmetic  11.8 us (10%)
  Pallas kernels  9.89 us (9%)
    all_to_all x3, waiting for transfers between devices, exchange(): lax.all_to_all(pieces, EVERYONE, split_axis=0, concat_axis=0, tiled=True)  35.7 us
    all_to_all x1, blocking collectives, exchange(): lax.all_to_all(pieces, EVERYONE, split_axis=0, concat_axis=0, tiled=True)  22.7 us
    unnamed x62, local copies, waits for them, and re-layouts  10.6 us
    all_to_all x3, starting transfers between devices, exchange(): lax.all_to_all(pieces, EVERYONE, split_axis=0, concat_axis=0, tiled=True)  8.77 us
    pallas_call x2, Pallas kernels, filtered(): pl.pallas_call(kernel, name='correlate' if backward else 'convolve', out_...  7.55 us
    ppermute x2, starting transfers between devices, shifted(): lax.ppermute(value, axis, [(source, source + steps) for source in range(f...  7.17 us
    convert_element_type x1, other arithmetic, shards(): key_grad = (back * value_part).astype(jnp.bfloat16)  3.06 us
    convert_element_type x1, other arithmetic, shards(): proj_grad = gathered.astype(jnp.bfloat16)  2.64 us
  transfers between devices with their start and end apart: 5, of which 4 were waited for; matrix products, arithmetic and copies ran while one was open for 3% of the time, Pallas kernels for 9%

profile of v2, /device:TPU:1, one launch (start us, length us, event | category | flops | bytes accessed | tf_op | source)
XLA Modules:
  0.0 112.5 jit_solution(16118200544900614203)
XLA Ops:
  0.6 0.0 copy-start.16
  0.6 0.0 copy-start.15
  0.7 1.8 %copy.15 = bf16[3072,256]{0,1:T(8,128)(2,1)S(1)} copy(bf16[3072,256]{1,0:T(8,128)(2,1)} %param.12) | data formatting | bytes 3145728 | tf_op args[0]
  2.5 4.6 %collective-permute-start = (bf16[3072,6]{0,1:T(8,128)(2,1)S(1)}, bf16[3072,6]{0,1:T(8,128)(2,1)S(1)}, u32[]{:S(2)}, u32[]{:S(2)}) collective-permute-start(bf16[3072,6]{0,1:T(8,128)(2,1)S(1)} %slice.112), channel_id=1, source_target_pairs={{0,1},{1,2},{2,3},{3,4},{4,5},{5,6},{6,7},{7,8},{8,9},{9,10},{10,1... | collective-permute-start | bytes 110600 | tf_op jit(solution)/shard_map/ppermute | solution.py:21
  7.1 0.0 copy-done.16
  7.1 0.1 fusion.20
  7.1 0.0 copy-done.15
  7.1 0.0 copy-start.17
  7.2 0.0 copy-start.19
  7.2 0.2 copy.17
  7.4 0.8 collective-permute-done
  8.2 0.4 maximum_convert_fusion
  8.7 2.6 %fusion.8 = bf16[3072,256]{0,1:T(8,128)(2,1)S(1)} fusion(f32[3072,262]{0,1:T(8,128)S(1)} %maximum_convert_fusion, f32[3072]{0:T(1024)S(1)} %bitcast.28, f32[3072]{0:T(1024)S(1)} %bitcast.26, f32[3072]{0:T(1024)S(1)} %bitcast.24, f32[3072]{0:T(1024)S(1)} %bitcast.22, f32[3072]{0:T(1024)S(1)} %bitcast.20, f32[3072]{0:T(1024)S(1)} %bitcast.18, f32[3072]{0:T(1024)S(1)} %bitcast.16), kind=kLoop, calls=%fused_computation.16 | loop fusion | flops 11010048 | bytes 23678976 | tf_op jit(solution)/shard_map/convert_element_type | solution.py:258
  11.4 0.0 copy-start.11
  11.4 1.1 %copy-done.11 = bf16[3072,256]{0,1:T(8,128)(2,1)} copy-done((bf16[3072,256]{0,1:T(8,128)(2,1)}, bf16[3072,256]{0,1:T(8,128)(2,1)S(1)}, u32[]{:S(2)}) %copy-start.11) | copy-done | bytes 1572888
  12.5 0.0 copy-start.5
  12.6 0.4 fusion.18
  13.0 0.0 copy-start.3
  13.0 0.0 copy-start.7
  13.0 0.0 copy-start.8
  13.0 0.2 copy.18
  13.2 22.7 %all_to_all.20.refs_0_ = bf16[32,32,256]{2,1,0:T(8,128)(2,1)S(1)} all-to-all(bf16[32,32,256]{2,1,0:T(8,128)(2,1)S(1)} %bitcast.15), channel_id=1, replica_groups=mesh['dp'=4,'ctx'=8] {'dp','ctx'}, dimensions={0} | all-to-all | bytes 1048576 | tf_op jit(solution)/shard_map/all_to_all | solution.py:268
  35.9 1.0 copy.19
  36.9 2.7 %all-to-all-start.1 = ((bf16[32,32,256]{2,1,0:T(8,128)(2,1)}), bf16[32,32,256]{2,1,0:T(8,128)(2,1)S(1)}, u32[]{:S(2)}, u32[]{:S(2)}) async-start(bf16[32,32,256]{2,1,0:T(8,128)(2,1)} %bitcast.8), calls=%async_computation.1 | async-start | bytes 1048576 | tf_op jit(solution)/shard_map/all_to_all | solution.py:268
  39.6 1.1 filter_dft.1.refs_1_
  40.7 3.6 %convolve.1 = (bf16[32,32,256]{2,1,0:T(8,128)(2,1)}, f32[2048,256]{1,0:T(8,128)S(1)}) custom-call(bf16[32,32,256]{2,1,0:T(8,128)(2,1)S(1)} %all_to_all.20.refs_0_, f32[1024,256]{1,0:T(8,128)S(1)} %filter_dft.1.refs_1_, bf16[256,128]{1,0:T(8,128)(2,1)S(1)} %copy-done.8, bf16[256,256]{1,0:T(8,128)(2,1)S(1)} %copy-done.4, bf16[256,256]{1,0:T(8,128)(2,1)S(1)} %copy-done.3, ...), custom_call_target="tpu_custom_call" | custom-call | flops 2000000000 | bytes 5000000 | tf_op jit(solution)/shard_map/convolve/pallas_call | solution.py:195
  44.4 1.4 %copy-done.9 = f32[2048,256]{1,0:T(8,128)} copy-done((f32[2048,256]{1,0:T(8,128)}, f32[2048,256]{1,0:T(8,128)S(1)}, u32[]{:S(2)}) %copy-start.9) | copy-done | bytes 2097176
  45.7 10.1 %all-to-all-done.1.refs_0_ = bf16[32,32,256]{2,1,0:T(8,128)(2,1)S(1)} async-done(((bf16[32,32,256]{2,1,0:T(8,128)(2,1)}), bf16[32,32,256]{2,1,0:T(8,128)(2,1)S(1)}, u32[]{:S(2)}, u32[]{:S(2)}) %all-to-all-start.1) | async-done | bytes 524320 | tf_op jit(solution)/shard_map/all_to_all | solution.py:268
  55.8 2.7 %all-to-all-start.2 = ((bf16[32,32,256]{2,1,0:T(8,128)(2,1)}), bf16[32,32,256]{2,1,0:T(8,128)(2,1)S(1)}, u32[]{:S(2)}, u32[]{:S(2)}) async-start(bf16[32,32,256]{2,1,0:T(8,128)(2,1)} %get-tuple-element.19), calls=%async_computation.2 | async-start | bytes 1048576 | tf_op jit(solution)/shard_map/all_to_all | solution.py:268
  58.6 1.6 %copy-done.10 = f32[2048,256]{1,0:T(8,128)S(1)} copy-done((f32[2048,256]{1,0:T(8,128)S(1)}, f32[2048,256]{1,0:T(8,128)}, u32[]{:S(2)}) %copy-start.10) | copy-done | bytes 2097176
  60.1 3.9 %correlate.1 = (bf16[32,32,256]{2,1,0:T(8,128)(2,1)}, bf16[1024,256]{1,0:T(8,128)(2,1)S(1)}) custom-call(bf16[32,32,256]{2,1,0:T(8,128)(2,1)S(1)} %all-to-all-done.1.refs_0_, f32[1024,256]{1,0:T(8,128)S(1)} %filter_dft.1.refs_1_, f32[2048,256]{1,0:T(8,128)S(1)} %copy-done.10, bf16[256,128]{1,0:T(8,128)(2,1)S(1)} %copy-done.8, ...), custom_call_target="tpu_custom_call" | custom-call | flops 2000000000 | bytes 5000000 | tf_op jit(solution)/shard_map/correlate/pallas_call | solution.py:195
  64.1 10.7 %all-to-all-done.2 = bf16[32,32,256]{2,1,0:T(8,128)(2,1)S(1)} async-done(((bf16[32,32,256]{2,1,0:T(8,128)(2,1)}), bf16[32,32,256]{2,1,0:T(8,128)(2,1)S(1)}, u32[]{:S(2)}, u32[]{:S(2)}) %all-to-all-start.2) | async-done | bytes 524320 | tf_op jit(solution)/shard_map/all_to_all | solution.py:268
  74.8 3.4 %all-to-all-start.3 = ((bf16[32,32,256]{2,1,0:T(8,128)(2,1)}), bf16[32,32,256]{2,1,0:T(8,128)(2,1)}, u32[]{:S(2)}, u32[]{:S(2)}) async-start(bf16[32,32,256]{2,1,0:T(8,128)(2,1)} %get-tuple-element.21), calls=%async_computation.3 | async-start | bytes 1048576 | tf_op jit(solution)/shard_map/all_to_all | solution.py:268
  78.2 0.1 bitcast_convert_fusion.1
  78.3 0.0 copy-start.12
  78.3 1.3 %copy.20 = f32[1024,256]{0,1:T(8,128)} copy(f32[1024,256]{1,0:T(8,128)S(1)} %bitcast_convert_fusion.1) | data formatting | bytes 2097152 | tf_op jit(solution)/shard_map/convert_element_type | solution.py:282
  79.6 14.8 %all-to-all-done.3 = bf16[32,32,256]{2,1,0:T(8,128)(2,1)} async-done(((bf16[32,32,256]{2,1,0:T(8,128)(2,1)}), bf16[32,32,256]{2,1,0:T(8,128)(2,1)}, u32[]{:S(2)}, u32[]{:S(2)}) %all-to-all-start.3) | async-done | bytes 524320 | tf_op jit(solution)/shard_map/all_to_all | solution.py:268
  94.5 1.1 bitcast_convert_fusion
  95.6 1.3 %copy.22 = f32[1024,256]{0,1:T(8,128)} copy(f32[1024,256]{1,0:T(8,128)S(1)} %bitcast_convert_fusion) | data formatting | bytes 2097152 | tf_op jit(solution)/shard_map/convert_element_type | solution.py:283
  96.9 3.1 %fusion.19 = (bf16[1024,256]{0,1:T(8,128)(2,1)S(1)}, bf16[1024,256]{0,1:T(8,128)(2,1)S(1)}, bf16[1024,256]{0,1:T(8,128)(2,1)}, bf16[1024,256]{0,1:T(8,128)(2,1)S(1)}) fusion(f32[1024,256]{0,1:T(8,128)} %copy.22, bf16[3072,256]{0,1:T(8,128)(2,1)S(1)} %copy-done.12, f32[1024,256]{0,1:T(8,128)} %copy.20, bf16[1024,256]{0,1:T(8,128)(2,1)} %copy-done.14), kind=kLoop, calls=%fused_computation.41 | loop fusion | flops 3145728 | bytes 6291456 | tf_op jit(solution)/shard_map/convert_element_type | solution.py:286
  100.0 0.8 copy-done.13
  100.7 2.6 %collective-permute-start.1 = (bf16[3072,6]{0,1:T(8,128)(2,1)S(1)}, bf16[3072,6]{0,1:T(8,128)(2,1)S(1)}, u32[]{:S(2)}, u32[]{:S(2)}) collective-permute-start(bf16[3072,6]{0,1:T(8,128)(2,1)S(1)} %pad_maximum_fusion), channel_id=1, source_target_pairs={{1,0},{2,1},{3,2},{4,3},{5,4},{6,5},{7,6},{8,7},{9,8},{10,9},{11,1... | collective-permute-start | bytes 110600 | tf_op jit(solution)/shard_map/ppermute | solution.py:21
  103.3 1.3 %filter_gradient.1 = f32[8,8192]{1,0:T(8,128)} custom-call(bf16[1024,256]{1,0:T(8,128)(2,1)S(1)} %get-tuple-element.22.s_ref, bf16[256,256]{1,0:T(8,128)(2,1)S(1)} %copy-done.3, bf16[64,256]{1,0:T(8,128)(2,1)S(1)} %copy-done.6, f32[128,128]{1,0:T(8,128)S(1)} %copy-done.1, f32[128,128]{1,0:T(8,128)S(1)} %copy-done), custom_call_target="tpu_custom_call" | custom-call | flops 200000000 | bytes 2000000 | tf_op jit(solution)/shard_map/filter_gradient/pallas_call | solution.py:230
  104.7 2.1 %copy.24 = bf16[1024,256]{1,0:T(8,128)(2,1)} copy(bf16[1024,256]{0,1:T(8,128)(2,1)} %get-tuple-element.28) | data formatting | bytes 1048576
  106.8 0.0 collective-permute-done.1
  106.8 1.4 %maximum_convert_fusion.1 = f32[3072,262]{0,1:T(8,128)S(1)} fusion(bf16[3072,6]{0,1:T(8,128)(2,1)S(1)} %collective-permute-done.1, bf16[1024,256]{0,1:T(8,128)(2,1)S(1)} %get-tuple-element.27, bf16[1024,256]{0,1:T(8,128)(2,1)S(1)} %get-tuple-element.26, bf16[1024,256]{0,1:T(8,128)(2,1)} %copy-done.13), kind=kLoop, calls=%fused_computation.29 | loop fusion | flops 6438912 | bytes 4829184 | tf_op jit(solution)/shard_map/convert_element_type | solution.py:290
  108.2 2.6 %fusion.1 = bf16[3072,256]{0,1:T(8,128)(2,1)S(1)} fusion(f32[3072,262]{0,1:T(8,128)S(1)} %maximum_convert_fusion.1, f32[3072]{0:T(1024)S(1)} %bitcast.29, f32[3072]{0:T(1024)S(1)} %bitcast.27, f32[3072]{0:T(1024)S(1)} %bitcast.25, f32[3072]{0:T(1024)S(1)} %bitcast.23, f32[3072]{0:T(1024)S(1)} %bitcast.21, f32[3072]{0:T(1024)S(1)} %bitcast.19, ...), kind=kLoop, calls=%fused_computation.2 | loop fusion | flops 11010048 | bytes 23678976 | tf_op jit(solution)/shard_map/convert_element_type | solution.py:294
  110.9 1.6 %copy.25 = bf16[3072,256]{1,0:T(8,128)(2,1)} copy(bf16[3072,256]{0,1:T(8,128)(2,1)S(1)} %fusion.1) | data formatting | bytes 3145728
  (44 shorter events, 0.1 us)
Async XLA Ops:
  0.6 6.4 %copy-start.16 = (bf16[7,3072]{1,0:T(8,128)(2,1)S(1)}, bf16[7,3072]{1,0:T(8,128)(2,1)}, u32[]{:S(2)}) copy-start(bf16[7,3072]{1,0:T(8,128)(2,1)} %param.13) | copy-start | bytes 129028
  0.6 6.5 %copy-start.15 = (bf16[1024,256]{1,0:T(8,128)(2,1)S(1)}, bf16[1024,256]{1,0:T(8,128)(2,1)}, u32[]{:S(2)}) copy-start(bf16[1024,256]{1,0:T(8,128)(2,1)} %param.15) | copy-start | bytes 1572868
  2.5 5.8 %collective-permute-start = (bf16[3072,6]{0,1:T(8,128)(2,1)S(1)}, bf16[3072,6]{0,1:T(8,128)(2,1)S(1)}, u32[]{:S(2)}, u32[]{:S(2)}) collective-permute-start(bf16[3072,6]{0,1:T(8,128)(2,1)S(1)} %slice.112), channel_id=1, source_target_pairs={{0,1},{1,2},{2,3},{3,4},{4,5},{5,6},{6,7},{7,8},{8,9},{9,10},{10,1... | collective-permute-start | bytes 110600 | tf_op jit(solution)/shard_map/ppermute | solution.py:21
  7.1 1.5 %copy-start.17 = (f32[1,3072]{1,0:T(1,128)}, f32[1,3072]{1,0:T(1,128)S(1)}, u32[]{:S(2)}) copy-start(f32[1,3072]{1,0:T(1,128)S(1)} %get-tuple-element.33) | copy-start | bytes 36868
  7.2 1.5 %copy-start.19 = (f32[1,3072]{1,0:T(1,128)}, f32[1,3072]{1,0:T(1,128)S(1)}, u32[]{:S(2)}) copy-start(f32[1,3072]{1,0:T(1,128)S(1)} %get-tuple-element.34) | copy-start | bytes 36868
  7.2 1.5 %copy-start.21 = (f32[1,3072]{1,0:T(1,128)}, f32[1,3072]{1,0:T(1,128)S(1)}, u32[]{:S(2)}) copy-start(f32[1,3072]{1,0:T(1,128)S(1)} %get-tuple-element.35) | copy-start | bytes 36868
  7.2 1.5 %copy-start.23 = (f32[1,3072]{1,0:T(1,128)}, f32[1,3072]{1,0:T(1,128)S(1)}, u32[]{:S(2)}) copy-start(f32[1,3072]{1,0:T(1,128)S(1)} %get-tuple-element.36) | copy-start | bytes 36868
  7.2 1.5 %copy-start.25 = (f32[1,3072]{1,0:T(1,128)}, f32[1,3072]{1,0:T(1,128)S(1)}, u32[]{:S(2)}) copy-start(f32[1,3072]{1,0:T(1,128)S(1)} %get-tuple-element.37) | copy-start | bytes 36868
  7.2 1.5 %copy-start.27 = (f32[1,3072]{1,0:T(1,128)}, f32[1,3072]{1,0:T(1,128)S(1)}, u32[]{:S(2)}) copy-start(f32[1,3072]{1,0:T(1,128)S(1)} %get-tuple-element.38) | copy-start | bytes 36868
  7.4 4.0 %copy-start.14 = (bf16[1024,256]{0,1:T(8,128)(2,1)}, bf16[1024,256]{0,1:T(8,128)(2,1)S(1)}, u32[]{:S(2)}) copy-start(bf16[1024,256]{0,1:T(8,128)(2,1)S(1)} %copy.17) | copy-start | bytes 1572868
  11.4 1.1 %copy-start.11 = (bf16[3072,256]{0,1:T(8,128)(2,1)}, bf16[3072,256]{0,1:T(8,128)(2,1)S(1)}, u32[]{:S(2)}) copy-start(bf16[3072,256]{0,1:T(8,128)(2,1)S(1)} %fusion.8) | copy-start | bytes 4718596
  12.5 27.1 %copy-start = (f32[128,128]{1,0:T(8,128)S(1)}, f32[128,128]{1,0:T(8,128)}, u32[]{:S(2)}) copy-start(f32[128,128]{1,0:T(8,128)} %constant.17.clone.ti_ref.refs_7_.refs_8_) | copy-start | bytes 196612
  12.5 27.1 %copy-start.1 = (f32[128,128]{1,0:T(8,128)S(1)}, f32[128,128]{1,0:T(8,128)}, u32[]{:S(2)}) copy-start(f32[128,128]{1,0:T(8,128)} %constant.16.clone.tr_ref.refs_6_.refs_7_) | copy-start | bytes 196612
  12.5 27.1 %copy-start.2 = (bf16[8,8192]{1,0:T(8,128)(2,1)S(1)}, bf16[8,8192]{1,0:T(8,128)(2,1)}, u32[]{:S(2)}) copy-start(bf16[8,8192]{1,0:T(8,128)(2,1)} %x_ref.1) | copy-start | bytes 393220
  12.5 27.1 %copy-start.4 = (bf16[256,256]{1,0:T(8,128)(2,1)S(1)}, bf16[256,256]{1,0:T(8,128)(2,1)}, u32[]{:S(2)}) copy-start(bf16[256,256]{1,0:T(8,128)(2,1)} %constant.26.second_ref.refs_3_.refs_4_) | copy-start | bytes 393220
  12.5 27.1 %copy-start.5 = (bf16[256,64]{1,0:T(8,128)(2,1)S(1)}, bf16[256,64]{1,0:T(8,128)(2,1)}, u32[]{:S(2)}) copy-start(bf16[256,64]{1,0:T(8,128)(2,1)} %constant.25.first_ref) | copy-start | bytes 98308
  13.0 27.7 %copy-start.3 = (bf16[256,256]{1,0:T(8,128)(2,1)S(1)}, bf16[256,256]{1,0:T(8,128)(2,1)}, u32[]{:S(2)}) copy-start(bf16[256,256]{1,0:T(8,128)(2,1)} %constant.28.refs_4_.refs_5_.third_ref) | copy-start | bytes 393220
  13.0 27.7 %copy-start.7 = (bf16[128,256]{1,0:T(8,128)(2,1)S(1)}, bf16[128,256]{1,0:T(8,128)(2,1)}, u32[]{:S(2)}) copy-start(bf16[128,256]{1,0:T(8,128)(2,1)} %constant.29.refs_5_.refs_6_) | copy-start | bytes 196612
  13.0 27.7 %copy-start.8 = (bf16[256,128]{1,0:T(8,128)(2,1)S(1)}, bf16[256,128]{1,0:T(8,128)(2,1)}, u32[]{:S(2)}) copy-start(bf16[256,128]{1,0:T(8,128)(2,1)} %constant.27.refs_2_.refs_3_) | copy-start | bytes 196612
  36.9 19.0 %all-to-all-start.1 = ((bf16[32,32,256]{2,1,0:T(8,128)(2,1)}), bf16[32,32,256]{2,1,0:T(8,128)(2,1)S(1)}, u32[]{:S(2)}, u32[]{:S(2)}) async-start(bf16[32,32,256]{2,1,0:T(8,128)(2,1)} %bitcast.8), calls=%async_computation.1 | async-start | bytes 1048576 | tf_op jit(solution)/shard_map/all_to_all | solution.py:268
  44.4 1.4 %copy-start.9 = (f32[2048,256]{1,0:T(8,128)}, f32[2048,256]{1,0:T(8,128)S(1)}, u32[]{:S(2)}) copy-start(f32[2048,256]{1,0:T(8,128)S(1)} %get-tuple-element.17.refs_2_) | copy-start | bytes 6291460
  55.8 19.0 %all-to-all-start.2 = ((bf16[32,32,256]{2,1,0:T(8,128)(2,1)}), bf16[32,32,256]{2,1,0:T(8,128)(2,1)S(1)}, u32[]{:S(2)}, u32[]{:S(2)}) async-start(bf16[32,32,256]{2,1,0:T(8,128)(2,1)} %get-tuple-element.19), calls=%async_computation.2 | async-start | bytes 1048576 | tf_op jit(solution)/shard_map/all_to_all | solution.py:268
  58.5 1.6 %copy-start.10 = (f32[2048,256]{1,0:T(8,128)S(1)}, f32[2048,256]{1,0:T(8,128)}, u32[]{:S(2)}) copy-start(f32[2048,256]{1,0:T(8,128)} %copy-done.9) | copy-start | bytes 6291460
  74.8 19.7 %all-to-all-start.3 = ((bf16[32,32,256]{2,1,0:T(8,128)(2,1)}), bf16[32,32,256]{2,1,0:T(8,128)(2,1)}, u32[]{:S(2)}, u32[]{:S(2)}) async-start(bf16[32,32,256]{2,1,0:T(8,128)(2,1)} %get-tuple-element.21), calls=%async_computation.3 | async-start | bytes 1048576 | tf_op jit(solution)/shard_map/all_to_all | solution.py:268
  78.3 18.6 %copy-start.12 = (bf16[3072,256]{0,1:T(8,128)(2,1)S(1)}, bf16[3072,256]{0,1:T(8,128)(2,1)}, u32[]{:S(2)}) copy-start(bf16[3072,256]{0,1:T(8,128)(2,1)} %copy-done.11) | copy-start | bytes 4718596
  96.9 6.4 %copy-start.6 = (bf16[64,256]{1,0:T(8,128)(2,1)S(1)}, bf16[64,256]{1,0:T(8,128)(2,1)}, u32[]{:S(2)}) copy-start(bf16[64,256]{1,0:T(8,128)(2,1)} %constant.30.fourth_ref) | copy-start | bytes 98308
  100.0 0.8 copy-start.13
  100.7 6.0 %collective-permute-start.1 = (bf16[3072,6]{0,1:T(8,128)(2,1)S(1)}, bf16[3072,6]{0,1:T(8,128)(2,1)S(1)}, u32[]{:S(2)}, u32[]{:S(2)}) collective-permute-start(bf16[3072,6]{0,1:T(8,128)(2,1)S(1)} %pad_maximum_fusion), channel_id=1, source_target_pairs={{1,0},{2,1},{3,2},{4,3},{5,4},{6,5},{7,6},{8,7},{9,8},{10,9},{11,1... | collective-permute-start | bytes 110600 | tf_op jit(solution)/shard_map/ppermute | solution.py:21
  104.6 3.6 %copy-start.18 = (f32[1,3072]{1,0:T(1,128)S(1)}, f32[1,3072]{1,0:T(1,128)}, u32[]{:S(2)}) copy-start(f32[1,3072]{1,0:T(1,128)} %copy-done.17) | copy-start | bytes 36868
  104.6 3.6 %copy-start.20 = (f32[1,3072]{1,0:T(1,128)S(1)}, f32[1,3072]{1,0:T(1,128)}, u32[]{:S(2)}) copy-start(f32[1,3072]{1,0:T(1,128)} %copy-done.19) | copy-start | bytes 36868
  104.6 3.6 %copy-start.22 = (f32[1,3072]{1,0:T(1,128)S(1)}, f32[1,3072]{1,0:T(1,128)}, u32[]{:S(2)}) copy-start(f32[1,3072]{1,0:T(1,128)} %copy-done.21) | copy-start | bytes 36868
  104.6 3.6 %copy-start.24 = (f32[1,3072]{1,0:T(1,128)S(1)}, f32[1,3072]{1,0:T(1,128)}, u32[]{:S(2)}) copy-start(f32[1,3072]{1,0:T(1,128)} %copy-done.23) | copy-start | bytes 36868
  104.6 3.6 %copy-start.26 = (f32[1,3072]{1,0:T(1,128)S(1)}, f32[1,3072]{1,0:T(1,128)}, u32[]{:S(2)}) copy-start(f32[1,3072]{1,0:T(1,128)} %copy-done.25) | copy-start | bytes 36868
  104.6 3.6 %copy-start.28 = (f32[1,3072]{1,0:T(1,128)S(1)}, f32[1,3072]{1,0:T(1,128)}, u32[]{:S(2)}) copy-start(f32[1,3072]{1,0:T(1,128)} %copy-done.27) | copy-start | bytes 36868

commit v3 on v2

--- a/solution.py
+++ b/solution.py
@@ -240,28 +240,208 @@
     )(cross, tables["third"], tables["fourth_real"], tables["twist_re"], tables["twist_im"])
 
 
+RIM = 8
+ROWS = 256
+
+
+def rims(arrays, first):
+    kind, rows_all, local = arrays[0].shape[0], arrays[0].shape[1], arrays[0].shape[2]
+    start = 0 if first else LANES - RIM
+    pick = np.zeros((RIM, LANES), np.float32)
+    pick[np.arange(RIM), start + np.arange(RIM)] = 1.0
+
+    def kernel(pick_ref, *refs):
+        out_ref = refs[-1]
+        value = refs[0][0]
+        for ref in refs[1:-1]:
+            value = (value.astype(jnp.float32) * ref[0].astype(jnp.float32)).astype(jnp.bfloat16)
+        out_ref[...] = lax.dot_general(
+            pick_ref[...], value, (((1,), (1,)), ((), ())), preferred_element_type=jnp.float32
+        ).astype(jnp.bfloat16)
+
+    tile = 0 if first else local // LANES - 1
+    return kernel, pick, tile
+
+
+def call_rims(name, count, width, tile, pick, kernel, operands, maps):
+    return pl.pallas_call(
+        kernel,
+        name=name,
+        grid=(count,),
+        in_specs=[pl.BlockSpec((RIM, LANES), lambda i: (0, 0))]
+        + [pl.BlockSpec((1, width, LANES), m) for m in maps],
+        out_specs=pl.BlockSpec((RIM, width), lambda i: (0, i)),
+        out_shape=jax.ShapeDtypeStruct((RIM, count * width), jnp.bfloat16),
+        cost_estimate=pl.CostEstimate(flops=10_000_000, bytes_accessed=1_000_000, transcendentals=0),
+    )(jnp.asarray(pick).astype(jnp.bfloat16), *operands)
+
+
+def edge_columns(rim, weights, forward):
+    spot = lax.broadcasted_iota(jnp.int32, (RIM, LANES), 0)
+    added = jnp.zeros((RIM, LANES), jnp.float32)
+    for lag in range(1, TAPS):
+        moved = pltpu.roll(rim, lag if forward else RIM - lag, 0)
+        inside = spot < lag if forward else spot >= RIM - lag
+        added = added + jnp.where(inside, moved, 0.0) * weights[lag : lag + 1]
+    taps = jnp.concatenate([weights, jnp.zeros((RIM - TAPS, LANES), jnp.float32)], axis=0)
+    rest = jnp.zeros((LANES - 2 * RIM, LANES), jnp.float32)
+    rows = [added, taps, rest] if forward else [taps, rest, added]
+    return jnp.concatenate(rows, axis=0).T
+
+
+def seven_taps(tiles, rim, weights, forward):
+    columns = edge_columns(rim, weights, forward)
+    lane = lax.broadcasted_iota(jnp.int32, (LANES, LANES), 1)
+    offset = RIM if forward else 0
+    edge = jnp.where(lane < RIM, columns, 0.0) if forward else jnp.where(lane >= LANES - RIM, columns, 0.0)
+    tap = [columns[:, offset + lag : offset + lag + 1] for lag in range(TAPS)]
+    total = [tile * tap[0] for tile in tiles]
+    last = len(tiles) - 1
+    for lag in range(1, TAPS):
+        if forward:
+            moved = [pltpu.roll(tile, lag, 1) for tile in tiles]
+            inside = lane >= lag
+            for t in range(len(tiles)):
+                total[t] = total[t] + tap[lag] * jnp.where(inside, moved[t], moved[t - 1] if t else 0.0)
+        else:
+            moved = [pltpu.roll(tile, LANES - lag, 1) for tile in tiles]
+            inside = lane < LANES - lag
+            for t in range(len(tiles)):
+                total[t] = total[t] + tap[lag] * jnp.where(inside, moved[t], moved[t + 1] if t < last else 0.0)
+    if forward:
+        total[0] = total[0] + edge
+    else:
+        total[last] = total[last] + edge
+    return total
+
+
+def features_of(projections, rim, short_filter, out_grad):
+    width, local = out_grad.shape
+    steps = width // ROWS
+
+    def kernel(x_ref, rim_q, rim_k, rim_v, w_q, w_k, w_v, og_ref, f_ref, kv_ref, dconv_ref):
+        for r in range(ROWS // LANES):
+            rows = slice(r * LANES, (r + 1) * LANES)
+            made = []
+            for part, (rim_ref, w_ref) in enumerate(((rim_q, w_q), (rim_k, w_k), (rim_v, w_v))):
+                tiles = [
+                    x_ref[part, rows, t * LANES : (t + 1) * LANES].astype(jnp.float32)
+                    for t in range(local // LANES)
+                ]
+                total = seven_taps(
+                    tiles, rim_ref[:, rows].astype(jnp.float32), w_ref[:, rows].astype(jnp.float32), True
+                )
+                total = [value.astype(jnp.bfloat16) for value in total]
+                for t, value in enumerate(total):
+                    f_ref[part, rows, t * LANES : (t + 1) * LANES] = value
+                made.append([value.astype(jnp.float32) for value in total])
+            for t in range(local // LANES):
+                lanes = slice(t * LANES, (t + 1) * LANES)
+                kv_ref[rows, lanes] = (made[1][t] * made[2][t]).astype(jnp.bfloat16)
+                og = og_ref[rows, lanes].astype(jnp.float32)
+                dconv_ref[rows, lanes] = (og * made[0][t]).astype(jnp.bfloat16)
+
+    third = lambda part: (lambda i: (0, part * steps + i))
+    pair = pl.BlockSpec((ROWS, local), lambda i: (i, 0))
+    triple = pl.BlockSpec((3, ROWS, local), lambda i: (0, i, 0))
+    return pl.pallas_call(
+        kernel,
+        name="features",
+        grid=(steps,),
+        in_specs=[triple]
+        + [pl.BlockSpec((RIM, ROWS), third(p)) for p in range(3)]
+        + [pl.BlockSpec((TAPS, ROWS), third(p)) for p in range(3)]
+        + [pair],
+        out_specs=(triple, pair, pair),
+        out_shape=(
+            jax.ShapeDtypeStruct((3, width, local), jnp.bfloat16),
+            jax.ShapeDtypeStruct((width, local), jnp.bfloat16),
+            jax.ShapeDtypeStruct((width, local), jnp.bfloat16),
+        ),
+        cost_estimate=pl.CostEstimate(flops=20_000_000, bytes_accessed=5_000_000, transcendentals=0),
+    )(projections, rim, rim, rim, short_filter, short_filter, short_filter, out_grad)
+
+
+def query_side(feats, conv, out_grad, rim, short_filter):
+    width, local = out_grad.shape
+    steps = width // ROWS
+
+    def kernel(q_ref, conv_ref, og_ref, rim_ref, w_ref, mixed_ref, grad_ref):
+        for r in range(ROWS // LANES):
+            rows = slice(r * LANES, (r + 1) * LANES)
+            tiles = []
+            for t in range(local // LANES):
+                lanes = slice(t * LANES, (t + 1) * LANES)
+                conv_here = conv_ref[0, rows, lanes].astype(jnp.float32)
+                mixed_ref[rows, lanes] = (q_ref[0, rows, lanes].astype(jnp.float32) * conv_here).astype(jnp.bfloat16)
+                grad = (og_ref[rows, lanes].astype(jnp.float32) * conv_here).astype(jnp.bfloat16)
+                tiles.append(grad.astype(jnp.float32))
+            total = seven_taps(tiles, rim_ref[:, rows].astype(jnp.float32), w_ref[:, rows].astype(jnp.float32), False)
+            for t, value in enumerate(total):
+                grad_ref[0, rows, t * LANES : (t + 1) * LANES] = value.astype(jnp.bfloat16)
+
+    pair = pl.BlockSpec((ROWS, local), lambda i: (i, 0))
+    one = pl.BlockSpec((1, ROWS, local), lambda i: (0, i, 0))
+    return pl.pallas_call(
+        kernel,
+        name="query_side",
+        grid=(steps,),
+        in_specs=[one, one, pair, pl.BlockSpec((RIM, ROWS), lambda i: (0, i)), pl.BlockSpec((TAPS, ROWS), lambda i: (0, i))],
+        out_specs=(pair, one),
+        out_shape=(
+            jax.ShapeDtypeStruct((width, local), jnp.bfloat16),
+            jax.ShapeDtypeStruct((3, width, local), jnp.bfloat16),
+        ),
+        cost_estimate=pl.CostEstimate(flops=10_000_000, bytes_accessed=3_000_000, transcendentals=0),
+    )(feats, conv, out_grad, rim, short_filter)
+
+
+def key_value_side(grad, feats, back, rim, short_filter):
+    width, local = back.shape[1:]
+    steps = width // ROWS
+
+    def kernel(_, f_ref, back_ref, rim_ref, w_ref, grad_ref):
+        for r in range(ROWS // LANES):
+            rows = slice(r * LANES, (r + 1) * LANES)
+            tiles = []
+            for t in range(local // LANES):
+                lanes = slice(t * LANES, (t + 1) * LANES)
+                value = back_ref[0, rows, lanes].astype(jnp.float32) * f_ref[0, rows, lanes].astype(jnp.float32)
+                tiles.append(value.astype(jnp.bfloat16).astype(jnp.float32))
+            total = seven_taps(tiles, rim_ref[:, rows].astype(jnp.float32), w_ref[:, rows].astype(jnp.float32), False)
+            for t, value in enumerate(total):
+                grad_ref[0, rows, t * LANES : (t + 1) * LANES] = value.astype(jnp.bfloat16)
+
+    return pl.pallas_call(
+        kernel,
+        name="key_value_side",
+        grid=(2, steps),
+        in_specs=[
+            pl.BlockSpec(memory_space=pl.ANY),
+            pl.BlockSpec((1, ROWS, local), lambda p, i: (2 - p, i, 0)),
+            pl.BlockSpec((1, ROWS, local), lambda p, i: (0, i, 0)),
+            pl.BlockSpec((RIM, ROWS), lambda p, i: (0, p * steps + i)),
+            pl.BlockSpec((TAPS, ROWS), lambda p, i: (0, (1 + p) * steps + i)),
+        ],
+        out_specs=pl.BlockSpec((1, ROWS, local), lambda p, i: (1 + p, i, 0)),
+        out_shape=jax.ShapeDtypeStruct((3, width, local), jnp.bfloat16),
+        input_output_aliases={0: 0},
+        cost_estimate=pl.CostEstimate(flops=20_000_000, bytes_accessed=4_000_000, transcendentals=0),
+    )(grad, feats, back, rim, short_filter)
+
+
 def shards(projections, short_filter, long_filter, out_grad):
     width, local_len = out_grad.shape
     devices = lax.axis_size(EVERYONE)
     seq_len = local_len * devices
     owned = width // devices
     tables = make_tables(seq_len, devices)
-    weights = short_filter.astype(jnp.float32)
-    rim_len = TAPS - 1
-    earlier = shifted(projections[:, local_len - rim_len :], EVERYONE, 1)
-    extended = jnp.concatenate([earlier, projections], axis=1).astype(jnp.float32)
-    total = jnp.zeros(projections.shape, jnp.float32)
-    for lag in range(TAPS):
-        total = (
-            total + weights[lag][:, None] * extended[:, rim_len - lag : rim_len - lag + local_len]
-        )
-    features = total.astype(jnp.bfloat16)
-    query = features[:width].astype(jnp.float32)
-    key_part = features[width : 2 * width].astype(jnp.float32)
-    value_part = features[2 * width :].astype(jnp.float32)
-    product = (key_part * value_part).astype(jnp.bfloat16)
-    cotangent = out_grad.astype(jnp.float32)
-    conv_grad = (cotangent * query).astype(jnp.bfloat16)
+    tripled = projections.reshape(3, width, local_len)
+
+    kernel, pick, tile = rims([tripled], False)
+    own_rim = call_rims("last_positions", 3, width, tile, pick, kernel, [tripled], [lambda i: (i, 0, tile)])
+    left_rim = shifted(own_rim, EVERYONE, 1)
+    feats, product, conv_grad = features_of(tripled, left_rim, short_filter, out_grad)
 
     def exchange(block):
         pieces = block.reshape(devices, owned, local_len)
@@ -279,20 +459,22 @@
     back_tok = exchange(back_chan)
     filter_grad = filter_gradient(cross, tables, seq_len)
 
-    conv = conv_tok.reshape(width, local_len).astype(jnp.float32)
-    back = back_tok.reshape(width, local_len).astype(jnp.float32)
-    mixed = (query * conv).astype(jnp.bfloat16)
-    query_grad = (cotangent * conv).astype(jnp.bfloat16)
-    key_grad = (back * value_part).astype(jnp.bfloat16)
-    value_grad = (back * key_part).astype(jnp.bfloat16)
-    feat_grad = jnp.concatenate([query_grad, key_grad, value_grad], axis=0)
-    later = shifted(feat_grad[:, :rim_len], EVERYONE, -1)
-    extended_grad = jnp.concatenate([feat_grad, later], axis=1).astype(jnp.float32)
-    gathered = jnp.zeros(projections.shape, jnp.float32)
-    for lag in range(TAPS):
-        gathered = gathered + weights[lag][:, None] * extended_grad[:, lag : lag + local_len]
-    proj_grad = gathered.astype(jnp.bfloat16)
-    return (mixed, proj_grad, filter_grad)
+    conv = conv_tok.reshape(1, width, local_len)
+    cotangent = out_grad.reshape(1, width, local_len)
+    here = lambda i: (0, 0, 0)
+    kernel, pick, tile = rims([conv, cotangent], True)
+    query_rim = call_rims("query_rim", 1, width, tile, pick, kernel, [conv, cotangent], [here, here])
+    query_rim = shifted(query_rim, EVERYONE, -1)
+    mixed, grad = query_side(feats, conv, out_grad, query_rim, short_filter)
+
+    back = back_tok.reshape(1, width, local_len)
+    kernel, pick, tile = rims([back, feats], True)
+    side_rim = call_rims(
+        "key_value_rim", 2, width, tile, pick, kernel, [back, feats], [here, lambda i: (2 - i, 0, 0)]
+    )
+    side_rim = shifted(side_rim, EVERYONE, -1)
+    grad = key_value_side(grad, feats, back, side_rim, short_filter)
+    return (mixed, grad.reshape(3 * width, local_len), filter_grad)
 
 
 def solution(mesh):

time: 113 us -> 127 us (1.12)
  Pallas kernels: 9.89 us -> 38.7 us
  blocking collectives: 22.7 us -> 41.5 us
  other arithmetic: 11.8 us -> 0 us
  waiting for transfers between devices: 36.5 us -> 25.2 us
  local copies, waits for them, and re-layouts: 14.5 us -> 4.8 us
    pallas_call x0 -> x6, Pallas kernels: none -> 29.6 us  [the longest x1 9.91 us: features_of(): pl.pallas_call(kernel, name='features', grid=(steps,), in_specs=[triple]...]
    all_to_all x1 -> x2, blocking collectives: 22.7 us -> 41.5 us  [exchange(): lax.all_to_all(pieces, EVERYONE, split_axis=0, concat_axis=0, tiled=True)]
    all_to_all x3 -> x2, waiting for transfers between devices: 35.7 us -> 21.7 us  [exchange(): lax.all_to_all(pieces, EVERYONE, split_axis=0, concat_axis=0, tiled=True)]
    convert_element_type x8 -> x0, other arithmetic: 11.8 us -> none  [the longest x1 3.06 us: shards(): key_grad = (back * value_part).astype(jnp.bfloat16)]
    unnamed x62 -> x28, local copies, waits for them, and re-layouts: 10.6 us -> 4.8 us
    convert_element_type x3 -> x0, local copies, waits for them, and re-layouts: 2.83 us -> none  [the longest x1 1.33 us: shards(): conv = conv_tok.reshape(width, local_len).astype(jnp.float32)]
    ppermute x2 -> x3, waiting for transfers between devices: 0.79 us -> 3.52 us  [shifted(): lax.ppermute(value, axis, [(source, source + steps) for source in range(f...]
    all_to_all x3 -> x2, starting transfers between devices: 8.77 us -> 6.07 us  [exchange(): lax.all_to_all(pieces, EVERYONE, split_axis=0, concat_axis=0, tiled=True)]
  transfers between devices with their start and end apart: 5 -> 5, of which waited for: 4 -> 4; matrix products, arithmetic and copies ran while one was open for 3% -> 0% of each run, Pallas kernels for 9% -> 12%
where the time goes in v3:
time: 127 us; the launch traced here: 126 us
  blocking collectives  41.5 us (33%)
  Pallas kernels  38.7 us (30%)
  waiting for transfers between devices  25.2 us (20%)
  starting transfers between devices  15 us (12%)
  local copies, waits for them, and re-layouts  4.8 us (4%)
    all_to_all x2, blocking collectives, exchange(): lax.all_to_all(pieces, EVERYONE, split_axis=0, concat_axis=0, tiled=True)  41.5 us
    all_to_all x2, waiting for transfers between devices, exchange(): lax.all_to_all(pieces, EVERYONE, split_axis=0, concat_axis=0, tiled=True)  21.7 us
    pallas_call x1, Pallas kernels, features_of(): pl.pallas_call(kernel, name='features', grid=(steps,), in_specs=[triple]...  9.91 us
    ppermute x3, starting transfers between devices, shifted(): lax.ppermute(value, axis, [(source, source + steps) for source in range(f...  8.88 us
    pallas_call x1, Pallas kernels, key_value_side(): pl.pallas_call(kernel, name='key_value_side', grid=(2, steps), in_specs=[...  8.14 us
    pallas_call x3, Pallas kernels, call_rims(): pl.pallas_call(kernel, name=name, grid=(count,), in_specs=[pl.BlockSpec((...  6.76 us
    pallas_call x2, Pallas kernels, filtered(): pl.pallas_call(kernel, name='correlate' if backward else 'convolve', out_...  6.74 us
    all_to_all x2, starting transfers between devices, exchange(): lax.all_to_all(pieces, EVERYONE, split_axis=0, concat_axis=0, tiled=True)  6.07 us
  transfers between devices with their start and end apart: 5, of which 4 were waited for; matrix products, arithmetic and copies ran while one was open for 0% of the time, Pallas kernels for 12%

profile of v3, /device:TPU:1, one launch (start us, length us, event | category | flops | bytes accessed | tf_op | source)
XLA Modules:
  0.0 126.0 jit_solution(3436208759457845613)
XLA Ops:
  0.6 2.9 %last_positions.1 = bf16[8,3072]{1,0:T(8,128)(2,1)} custom-call(bf16[8,128]{1,0:T(8,128)(2,1)} %constant.31.pick_ref, bf16[3,1024,256]{2,1,0:T(8,128)(2,1)} %bitcast.7), custom_call_target="tpu_custom_call" | custom-call | flops 10000000 | bytes 1000000 | tf_op jit(solution)/shard_map/last_positions/pallas_call | solution.py:267
  3.5 4.6 %collective-permute-start = (bf16[8,3072]{1,0:T(8,128)(2,1)}, bf16[8,3072]{1,0:T(8,128)(2,1)S(1)}, u32[]{:S(2)}, u32[]{:S(2)}) collective-permute-start(bf16[8,3072]{1,0:T(8,128)(2,1)} %last_positions.1), channel_id=1, source_target_pairs={{0,1},{1,2},{2,3},{3,4},{4,5},{5,6},{6,7},{7,8},{8,9},{9,10},{10,1... | collective-permute-start | bytes 147464 | tf_op jit(solution)/shard_map/ppermute | solution.py:21
  8.1 1.5 %collective-permute-done.rim_q.rim_k.rim_v = bf16[8,3072]{1,0:T(8,128)(2,1)S(1)} collective-permute-done((bf16[8,3072]{1,0:T(8,128)(2,1)}, bf16[8,3072]{1,0:T(8,128)(2,1)S(1)}, u32[]{:S(2)}, u32[]{:S(2)}) %collective-permute-start) | collective-permute-done | bytes 49184 | tf_op jit(solution)/shard_map/ppermute | solution.py:21
  9.6 0.0 copy-start.11
  9.6 0.6 copy-done.11
  10.2 9.9 %features.1 = (bf16[3,1024,256]{2,1,0:T(8,128)(2,1)}, bf16[1024,256]{1,0:T(8,128)(2,1)}, bf16[1024,256]{1,0:T(8,128)(2,1)}) custom-call(bf16[3,1024,256]{2,1,0:T(8,128)(2,1)} %bitcast.8, bf16[8,3072]{1,0:T(8,128)(2,1)} %copy-done.11, bf16[8,3072]{1,0:T(8,128)(2,1)} %copy-done.11, bf16[8,3072]{1,0:T(8,128)(2,1)} %copy-done.11, bf16[7,3072]{1,0:T(8,128)(2,1)} %w_ref.3, ...), custom_call_target="tpu_custom_call" | custom-call | flops 20000000 | bytes 5000000 | tf_op jit(solution)/shard_map/features/pallas_call | solution.py:347
  20.1 0.0 copy-start
  20.1 0.0 copy-start.1
  20.1 0.0 copy-start.2
  20.2 0.0 copy-start.4
  20.2 0.0 copy-start.5
  20.2 0.0 copy-start.3
  20.2 0.0 copy-start.7
  20.2 0.0 copy-start.8
  20.2 22.8 %all_to_all.20.refs_0_ = bf16[32,32,256]{2,1,0:T(8,128)(2,1)S(1)} all-to-all(bf16[32,32,256]{2,1,0:T(8,128)(2,1)} %bitcast.14), channel_id=1, replica_groups=mesh['dp'=4,'ctx'=8] {'dp','ctx'}, dimensions={0} | all-to-all | bytes 1048576 | tf_op jit(solution)/shard_map/all_to_all | solution.py:448
  43.0 2.7 %all-to-all-start.1 = ((bf16[32,32,256]{2,1,0:T(8,128)(2,1)}), bf16[32,32,256]{2,1,0:T(8,128)(2,1)S(1)}, u32[]{:S(2)}, u32[]{:S(2)}) async-start(bf16[32,32,256]{2,1,0:T(8,128)(2,1)} %bitcast.13), calls=%async_computation.1 | async-start | bytes 1048576 | tf_op jit(solution)/shard_map/all_to_all | solution.py:448
  45.7 0.0 copy-done
  45.7 0.0 copy-done.1
  45.7 0.0 copy-done.2
  45.7 0.0 copy-done.4
  45.7 0.0 copy-done.5
  45.8 1.1 filter_dft.1.refs_1_
  46.8 0.0 copy-done.3
  46.8 0.0 copy-done.7
  46.8 0.0 copy-done.8
  46.8 3.6 %convolve.1 = (bf16[32,32,256]{2,1,0:T(8,128)(2,1)}, f32[2048,256]{1,0:T(8,128)S(1)}) custom-call(bf16[32,32,256]{2,1,0:T(8,128)(2,1)S(1)} %all_to_all.20.refs_0_, f32[1024,256]{1,0:T(8,128)S(1)} %filter_dft.1.refs_1_, bf16[256,128]{1,0:T(8,128)(2,1)S(1)} %copy-done.8, bf16[256,256]{1,0:T(8,128)(2,1)S(1)} %copy-done.4, bf16[256,256]{1,0:T(8,128)(2,1)S(1)} %copy-done.3, ...), custom_call_target="tpu_custom_call" | custom-call | flops 2000000000 | bytes 5000000 | tf_op jit(solution)/shard_map/convolve/pallas_call | solution.py:195
  50.5 0.0 copy-start.9
  50.5 1.3 %copy-done.9 = f32[2048,256]{1,0:T(8,128)} copy-done((f32[2048,256]{1,0:T(8,128)}, f32[2048,256]{1,0:T(8,128)S(1)}, u32[]{:S(2)}) %copy-start.9) | copy-done | bytes 2097176
  51.8 10.1 %all-to-all-done.1.refs_0_ = bf16[32,32,256]{2,1,0:T(8,128)(2,1)S(1)} async-done(((bf16[32,32,256]{2,1,0:T(8,128)(2,1)}), bf16[32,32,256]{2,1,0:T(8,128)(2,1)S(1)}, u32[]{:S(2)}, u32[]{:S(2)}) %all-to-all-start.1) | async-done | bytes 524320 | tf_op jit(solution)/shard_map/all_to_all | solution.py:448
  62.0 3.4 %all-to-all-start.2 = ((bf16[32,32,256]{2,1,0:T(8,128)(2,1)}), bf16[32,32,256]{2,1,0:T(8,128)(2,1)}, u32[]{:S(2)}, u32[]{:S(2)}) async-start(bf16[32,32,256]{2,1,0:T(8,128)(2,1)} %get-tuple-element.27), calls=%async_computation.2 | async-start | bytes 1048576 | tf_op jit(solution)/shard_map/all_to_all | solution.py:448
  65.3 0.0 copy-start.10
  65.3 1.6 %copy-done.10 = f32[2048,256]{1,0:T(8,128)S(1)} copy-done((f32[2048,256]{1,0:T(8,128)S(1)}, f32[2048,256]{1,0:T(8,128)}, u32[]{:S(2)}) %copy-start.10) | copy-done | bytes 2097176
  66.9 3.1 %correlate.1 = (bf16[32,32,256]{2,1,0:T(8,128)(2,1)S(1)}, bf16[1024,256]{1,0:T(8,128)(2,1)S(1)}) custom-call(bf16[32,32,256]{2,1,0:T(8,128)(2,1)S(1)} %all-to-all-done.1.refs_0_, f32[1024,256]{1,0:T(8,128)S(1)} %filter_dft.1.refs_1_, f32[2048,256]{1,0:T(8,128)S(1)} %copy-done.10, bf16[256,128]{1,0:T(8,128)(2,1)S(1)} %copy-done.8, ...), custom_call_target="tpu_custom_call" | custom-call | flops 2000000000 | bytes 5000000 | tf_op jit(solution)/shard_map/correlate/pallas_call | solution.py:195
  70.0 11.6 %all-to-all-done.2 = bf16[32,32,256]{2,1,0:T(8,128)(2,1)} async-done(((bf16[32,32,256]{2,1,0:T(8,128)(2,1)}), bf16[32,32,256]{2,1,0:T(8,128)(2,1)}, u32[]{:S(2)}, u32[]{:S(2)}) %all-to-all-start.2) | async-done | bytes 524320 | tf_op jit(solution)/shard_map/all_to_all | solution.py:448
  81.6 18.7 %all_to_all.21 = bf16[32,32,256]{2,1,0:T(8,128)(2,1)} all-to-all(bf16[32,32,256]{2,1,0:T(8,128)(2,1)S(1)} %get-tuple-element.31), channel_id=1, replica_groups=mesh['dp'=4,'ctx'=8] {'dp','ctx'}, dimensions={0} | all-to-all | bytes 1048576 | tf_op jit(solution)/shard_map/all_to_all | solution.py:448
  100.4 0.0 copy-start.6
  100.4 2.0 %key_value_rim.1 = bf16[8,2048]{1,0:T(8,128)(2,1)} custom-call(bf16[8,128]{1,0:T(8,128)(2,1)} %constant.37.pick_ref, bf16[1,1024,256]{2,1,0:T(8,128)(2,1)} %bitcast.10, bf16[3,1024,256]{2,1,0:T(8,128)(2,1)} %get-tuple-element.18.q_ref.refs_1_.f_ref), custom_call_target="tpu_custom_call" | custom-call | flops 10000000 | bytes 1000000 | tf_op jit(solution)/shard_map/key_value_rim/pallas_call | solution.py:267
  102.4 2.4 %collective-permute-start.2 = (bf16[8,2048]{1,0:T(8,128)(2,1)}, bf16[8,2048]{1,0:T(8,128)(2,1)S(1)}, u32[]{:S(2)}, u32[]{:S(2)}) collective-permute-start(bf16[8,2048]{1,0:T(8,128)(2,1)} %key_value_rim.1), channel_id=1, source_target_pairs={{1,0},{2,1},{3,2},{4,3},{5,4},{6,5},{7,6},{8,7},{9,8},{10,9},{11,1... | collective-permute-start | bytes 98312 | tf_op jit(solution)/shard_map/ppermute | solution.py:21
  104.8 1.8 %query_rim.1 = bf16[8,1024]{1,0:T(8,128)(2,1)} custom-call(bf16[8,128]{1,0:T(8,128)(2,1)} %constant.37.pick_ref, bf16[1,1024,256]{2,1,0:T(8,128)(2,1)} %bitcast.3.refs_0_.conv_ref, bf16[1,1024,256]{2,1,0:T(8,128)(2,1)} %bitcast.9), custom_call_target="tpu_custom_call" | custom-call | flops 10000000 | bytes 1000000 | tf_op jit(solution)/shard_map/query_rim/pallas_call | solution.py:267
  106.6 1.9 %collective-permute-start.1 = (bf16[8,1024]{1,0:T(8,128)(2,1)}, bf16[8,1024]{1,0:T(8,128)(2,1)S(1)}, u32[]{:S(2)}, u32[]{:S(2)}) collective-permute-start(bf16[8,1024]{1,0:T(8,128)(2,1)} %query_rim.1), channel_id=1, source_target_pairs={{1,0},{2,1},{3,2},{4,3},{5,4},{6,5},{7,6},{8,7},{9,8},{10,9},{11,1... | collective-permute-start | bytes 49160 | tf_op jit(solution)/shard_map/ppermute | solution.py:21
  108.5 0.0 copy-done.6
  108.6 1.3 %filter_gradient.1 = f32[8,8192]{1,0:T(8,128)} custom-call(bf16[1024,256]{1,0:T(8,128)(2,1)S(1)} %get-tuple-element.32.s_ref, bf16[256,256]{1,0:T(8,128)(2,1)S(1)} %copy-done.3, bf16[64,256]{1,0:T(8,128)(2,1)S(1)} %copy-done.6, f32[128,128]{1,0:T(8,128)S(1)} %copy-done.1, f32[128,128]{1,0:T(8,128)S(1)} %copy-done), custom_call_target="tpu_custom_call" | custom-call | flops 200000000 | bytes 2000000 | tf_op jit(solution)/shard_map/filter_gradient/pallas_call | solution.py:230
  109.8 2.0 %collective-permute-done.1.rim_ref = bf16[8,1024]{1,0:T(8,128)(2,1)S(1)} collective-permute-done((bf16[8,1024]{1,0:T(8,128)(2,1)}, bf16[8,1024]{1,0:T(8,128)(2,1)S(1)}, u32[]{:S(2)}, u32[]{:S(2)}) %collective-permute-start.1) | collective-permute-done | bytes 16416 | tf_op jit(solution)/shard_map/ppermute | solution.py:21
  111.9 0.6 copy-done.13
  112.5 4.8 %query_side.1 = (bf16[1024,256]{1,0:T(8,128)(2,1)}, bf16[3,1024,256]{2,1,0:T(8,128)(2,1)}) custom-call(bf16[3,1024,256]{2,1,0:T(8,128)(2,1)} %get-tuple-element.18.q_ref.refs_1_.f_ref, bf16[1,1024,256]{2,1,0:T(8,128)(2,1)} %bitcast.3.refs_0_.conv_ref, bf16[1024,256]{1,0:T(8,128)(2,1)} %og_ref.3, bf16[8,1024]{1,0:T(8,128)(2,1)} %copy-done.13, ...), custom_call_target="tpu_custom_call" | custom-call | flops 10000000 | bytes 3000000 | tf_op jit(solution)/shard_map/query_side/pallas_call | solution.py:385
  117.3 0.0 collective-permute-done.2.rim_ref
  117.3 0.6 copy-done.12
  117.9 8.1 %key_value_side.1 = bf16[3,1024,256]{2,1,0:T(8,128)(2,1)} custom-call(bf16[3,1024,256]{2,1,0:T(8,128)(2,1)} %get-tuple-element.30._, bf16[3,1024,256]{2,1,0:T(8,128)(2,1)} %get-tuple-element.18.q_ref.refs_1_.f_ref, bf16[1,1024,256]{2,1,0:T(8,128)(2,1)} %bitcast.11, bf16[8,2048]{1,0:T(8,128)(2,1)} %copy-done.12, ...), custom_call_target="tpu_custom_call", output_to_operand_aliasing={{}: (0, {})} | custom-call | flops 20000000 | bytes 4000000 | tf_op jit(solution)/shard_map/key_value_side/pallas_call | solution.py:415
  (2 shorter events, 0.0 us)
Async XLA Ops:
  3.5 6.1 %collective-permute-start = (bf16[8,3072]{1,0:T(8,128)(2,1)}, bf16[8,3072]{1,0:T(8,128)(2,1)S(1)}, u32[]{:S(2)}, u32[]{:S(2)}) collective-permute-start(bf16[8,3072]{1,0:T(8,128)(2,1)} %last_positions.1), channel_id=1, source_target_pairs={{0,1},{1,2},{2,3},{3,4},{4,5},{5,6},{6,7},{7,8},{8,9},{9,10},{10,1... | collective-permute-start | bytes 147464 | tf_op jit(solution)/shard_map/ppermute | solution.py:21
  9.6 0.6 copy-start.11
  20.1 25.6 %copy-start = (f32[128,128]{1,0:T(8,128)S(1)}, f32[128,128]{1,0:T(8,128)}, u32[]{:S(2)}) copy-start(f32[128,128]{1,0:T(8,128)} %constant.21.clone.ti_ref.refs_7_.refs_8_) | copy-start | bytes 196612
  20.1 25.6 %copy-start.1 = (f32[128,128]{1,0:T(8,128)S(1)}, f32[128,128]{1,0:T(8,128)}, u32[]{:S(2)}) copy-start(f32[128,128]{1,0:T(8,128)} %constant.20.clone.tr_ref.refs_6_.refs_7_) | copy-start | bytes 196612
  20.1 25.6 %copy-start.2 = (bf16[8,8192]{1,0:T(8,128)(2,1)S(1)}, bf16[8,8192]{1,0:T(8,128)(2,1)}, u32[]{:S(2)}) copy-start(bf16[8,8192]{1,0:T(8,128)(2,1)} %x_ref.1) | copy-start | bytes 393220
  20.2 25.6 %copy-start.4 = (bf16[256,256]{1,0:T(8,128)(2,1)S(1)}, bf16[256,256]{1,0:T(8,128)(2,1)}, u32[]{:S(2)}) copy-start(bf16[256,256]{1,0:T(8,128)(2,1)} %constant.33.second_ref.refs_3_.refs_4_) | copy-start | bytes 393220
  20.2 25.6 %copy-start.5 = (bf16[256,64]{1,0:T(8,128)(2,1)S(1)}, bf16[256,64]{1,0:T(8,128)(2,1)}, u32[]{:S(2)}) copy-start(bf16[256,64]{1,0:T(8,128)(2,1)} %constant.32.first_ref) | copy-start | bytes 98308
  20.2 26.6 %copy-start.3 = (bf16[256,256]{1,0:T(8,128)(2,1)S(1)}, bf16[256,256]{1,0:T(8,128)(2,1)}, u32[]{:S(2)}) copy-start(bf16[256,256]{1,0:T(8,128)(2,1)} %constant.35.refs_4_.refs_5_.third_ref) | copy-start | bytes 393220
  20.2 26.6 %copy-start.7 = (bf16[128,256]{1,0:T(8,128)(2,1)S(1)}, bf16[128,256]{1,0:T(8,128)(2,1)}, u32[]{:S(2)}) copy-start(bf16[128,256]{1,0:T(8,128)(2,1)} %constant.36.refs_5_.refs_6_) | copy-start | bytes 196612
  20.2 26.6 %copy-start.8 = (bf16[256,128]{1,0:T(8,128)(2,1)S(1)}, bf16[256,128]{1,0:T(8,128)(2,1)}, u32[]{:S(2)}) copy-start(bf16[256,128]{1,0:T(8,128)(2,1)} %constant.34.refs_2_.refs_3_) | copy-start | bytes 196612
  43.0 19.0 %all-to-all-start.1 = ((bf16[32,32,256]{2,1,0:T(8,128)(2,1)}), bf16[32,32,256]{2,1,0:T(8,128)(2,1)S(1)}, u32[]{:S(2)}, u32[]{:S(2)}) async-start(bf16[32,32,256]{2,1,0:T(8,128)(2,1)} %bitcast.13), calls=%async_computation.1 | async-start | bytes 1048576 | tf_op jit(solution)/shard_map/all_to_all | solution.py:448
  50.5 1.3 %copy-start.9 = (f32[2048,256]{1,0:T(8,128)}, f32[2048,256]{1,0:T(8,128)S(1)}, u32[]{:S(2)}) copy-start(f32[2048,256]{1,0:T(8,128)S(1)} %get-tuple-element.25.refs_2_) | copy-start | bytes 6291460
  62.0 19.7 %all-to-all-start.2 = ((bf16[32,32,256]{2,1,0:T(8,128)(2,1)}), bf16[32,32,256]{2,1,0:T(8,128)(2,1)}, u32[]{:S(2)}, u32[]{:S(2)}) async-start(bf16[32,32,256]{2,1,0:T(8,128)(2,1)} %get-tuple-element.27), calls=%async_computation.2 | async-start | bytes 1048576 | tf_op jit(solution)/shard_map/all_to_all | solution.py:448
  65.3 1.6 %copy-start.10 = (f32[2048,256]{1,0:T(8,128)S(1)}, f32[2048,256]{1,0:T(8,128)}, u32[]{:S(2)}) copy-start(f32[2048,256]{1,0:T(8,128)} %copy-done.9) | copy-start | bytes 6291460
  100.4 8.2 %copy-start.6 = (bf16[64,256]{1,0:T(8,128)(2,1)S(1)}, bf16[64,256]{1,0:T(8,128)(2,1)}, u32[]{:S(2)}) copy-start(bf16[64,256]{1,0:T(8,128)(2,1)} %constant.38.fourth_ref) | copy-start | bytes 98308
  102.4 14.9 %collective-permute-start.2 = (bf16[8,2048]{1,0:T(8,128)(2,1)}, bf16[8,2048]{1,0:T(8,128)(2,1)S(1)}, u32[]{:S(2)}, u32[]{:S(2)}) collective-permute-start(bf16[8,2048]{1,0:T(8,128)(2,1)} %key_value_rim.1), channel_id=1, source_target_pairs={{1,0},{2,1},{3,2},{4,3},{5,4},{6,5},{7,6},{8,7},{9,8},{10,9},{11,1... | collective-permute-start | bytes 98312 | tf_op jit(solution)/shard_map/ppermute | solution.py:21
  106.6 5.3 %collective-permute-start.1 = (bf16[8,1024]{1,0:T(8,128)(2,1)}, bf16[8,1024]{1,0:T(8,128)(2,1)S(1)}, u32[]{:S(2)}, u32[]{:S(2)}) collective-permute-start(bf16[8,1024]{1,0:T(8,128)(2,1)} %query_rim.1), channel_id=1, source_target_pairs={{1,0},{2,1},{3,2},{4,3},{5,4},{6,5},{7,6},{8,7},{9,8},{10,9},{11,1... | collective-permute-start | bytes 49160 | tf_op jit(solution)/shard_map/ppermute | solution.py:21
  111.9 0.6 copy-start.13
  117.3 0.6 copy-start.12

commit v4 on v2

--- a/solution.py
+++ b/solution.py
@@ -240,28 +240,184 @@
     )(cross, tables["third"], tables["fourth_real"], tables["twist_re"], tables["twist_im"])
 
 
+RIM = 8
+
+
+def seven_taps(tall, value, rim, weights, forward):
+    count = value.shape[0]
+    if forward:
+        tall[:RIM, :] = rim
+        tall[RIM : RIM + count, :] = value
+    else:
+        tall[:count, :] = value
+        tall[count : count + RIM, :] = rim
+    total = value * weights[:1]
+    for lag in range(1, TAPS):
+        first = RIM - lag if forward else lag
+        total = total + tall[first : first + count, :] * weights[lag : lag + 1]
+    return total
+
+
+def lane_block(i, offset=0):
+    return pl.ds(pl.multiple_of(i * LANES + offset, LANES), LANES)
+
+
+def whole_call(kernel, name, out_shape, operands, scratch=(), flops=10_000_000, **kwargs):
+    return pl.pallas_call(
+        kernel,
+        name=name,
+        out_shape=out_shape,
+        scratch_shapes=list(scratch),
+        compiler_params=pltpu.CompilerParams(vmem_limit_bytes=VMEM_LIMIT),
+        cost_estimate=pl.CostEstimate(flops=flops, bytes_accessed=4_000_000, transcendentals=0),
+        **kwargs,
+    )(*operands)
+
+
+def narrow_shape(*shape):
+    return jax.ShapeDtypeStruct(shape, jnp.bfloat16)
+
+
+def features_of(turned, rim, short_filter, cotangent):
+    local, width = cotangent.shape
+
+    def kernel(x_ref, rim_ref, w_ref, og_ref, f_ref, kv_ref, dconv_ref, tall):
+        @pl.loop(0, width // LANES)
+        def _(i):
+            made = []
+            for part in range(3):
+                lanes = lane_block(i, part * width)
+                total = seven_taps(
+                    tall.at[part],
+                    x_ref[:, lanes].astype(jnp.float32),
+                    rim_ref[:, lanes].astype(jnp.float32),
+                    w_ref[:, lanes].astype(jnp.float32),
+                    True,
+                ).astype(jnp.bfloat16)
+                f_ref[:, lanes] = total
+                made.append(total.astype(jnp.float32))
+            rows = lane_block(i)
+            kv_ref[rows, :] = (made[1] * made[2]).astype(jnp.bfloat16).T
+            og = og_ref[:, rows].astype(jnp.float32)
+            dconv_ref[rows, :] = (og * made[0]).astype(jnp.bfloat16).T
+
+    return whole_call(
+        kernel,
+        "features",
+        (narrow_shape(local, 3 * width), narrow_shape(width, local), narrow_shape(width, local)),
+        (turned, rim, short_filter, cotangent),
+        [pltpu.VMEM((3, local + RIM, LANES), jnp.float32)],
+    )
+
+
+def query_products(feats, conv, cotangent):
+    width, local = conv.shape
+
+    def kernel(f_ref, conv_ref, og_ref, mixed_ref, dq_ref, rim_ref):
+        @pl.loop(0, width // LANES)
+        def _(i):
+            lanes = lane_block(i)
+            here = conv_ref[lanes, :].T.astype(jnp.float32)
+            mixed_ref[lanes, :] = (f_ref[:, lanes].astype(jnp.float32) * here).astype(jnp.bfloat16).T
+            dq = (og_ref[:, lanes].astype(jnp.float32) * here).astype(jnp.bfloat16)
+            dq_ref[:, lanes] = dq
+            rim_ref[:, lanes] = dq[:RIM]
+
+    return whole_call(
+        kernel,
+        "query_products",
+        (narrow_shape(width, local), narrow_shape(local, width), narrow_shape(RIM, width)),
+        (feats, conv, cotangent),
+    )
+
+
+def key_value_products(feats, back):
+    width, local = back.shape
+
+    def kernel(f_ref, back_ref, d_ref, rim_ref):
+        @pl.loop(0, width // LANES)
+        def _(i):
+            here = back_ref[lane_block(i), :].T.astype(jnp.float32)
+            for part in range(2):
+                other = f_ref[:, lane_block(i, (2 - part) * width)].astype(jnp.float32)
+                grad = (here * other).astype(jnp.bfloat16)
+                d_ref[:, lane_block(i, part * width)] = grad
+                rim_ref[:, lane_block(i, part * width)] = grad[:RIM]
+
+    return whole_call(
+        kernel,
+        "key_value_products",
+        (narrow_shape(local, 2 * width), narrow_shape(RIM, 2 * width)),
+        (feats, back),
+    )
+
+
+def query_gradient(grad, rim, short_filter):
+    local, width = grad.shape
+    steps = width // GRAD_ROWS
+
+    def kernel(d_ref, rim_ref, w_ref, out_ref, tall):
+        gradient_block(d_ref, rim_ref, w_ref, out_ref, tall)
+
+    return gradient_call(kernel, "query_gradient", (), grad, rim, short_filter, 1, 0)
+
+
+def key_value_gradient(whole, grad, rim, short_filter):
+    def kernel(_, d_ref, rim_ref, w_ref, out_ref, tall):
+        gradient_block(d_ref, rim_ref, w_ref, out_ref, tall)
+
+    return gradient_call(kernel, "key_value_gradient", (whole,), grad, rim, short_filter, 2, 1)
+
+
+GRAD_ROWS = 512
+
+
+def gradient_block(d_ref, rim_ref, w_ref, out_ref, tall):
+    for c in range(GRAD_ROWS // LANES):
+        lanes = slice(c * LANES, (c + 1) * LANES)
+        total = seven_taps(
+            tall.at[c],
+            d_ref[:, lanes].astype(jnp.float32),
+            rim_ref[:, lanes].astype(jnp.float32),
+            w_ref[:, lanes].astype(jnp.float32),
+            False,
+        )
+        out_ref[lanes, :] = total.astype(jnp.bfloat16).T
+
+
+def gradient_call(kernel, name, whole, grad, rim, short_filter, parts, first):
+    local, lanes = grad.shape
+    width = lanes // parts
+    steps = width // GRAD_ROWS
+    return pl.pallas_call(
+        kernel,
+        name=name,
+        grid=(parts * steps,),
+        in_specs=[pl.BlockSpec(memory_space=pl.ANY)] * len(whole)
+        + [
+            pl.BlockSpec((local, GRAD_ROWS), lambda i: (0, i)),
+            pl.BlockSpec((RIM, GRAD_ROWS), lambda i: (0, i)),
+            pl.BlockSpec((TAPS, GRAD_ROWS), lambda i: (0, first * steps + i)),
+        ],
+        out_specs=pl.BlockSpec((GRAD_ROWS, local), lambda i: (first * steps + i, 0)),
+        out_shape=narrow_shape(3 * width, local),
+        scratch_shapes=[pltpu.VMEM((GRAD_ROWS // LANES, local + RIM, LANES), jnp.float32)],
+        input_output_aliases={0: 0} if whole else {},
+        cost_estimate=pl.CostEstimate(flops=20_000_000, bytes_accessed=4_000_000, transcendentals=0),
+    )(*whole, grad, rim, short_filter)
+
+
 def shards(projections, short_filter, long_filter, out_grad):
     width, local_len = out_grad.shape
     devices = lax.axis_size(EVERYONE)
     seq_len = local_len * devices
     owned = width // devices
     tables = make_tables(seq_len, devices)
-    weights = short_filter.astype(jnp.float32)
-    rim_len = TAPS - 1
-    earlier = shifted(projections[:, local_len - rim_len :], EVERYONE, 1)
-    extended = jnp.concatenate([earlier, projections], axis=1).astype(jnp.float32)
-    total = jnp.zeros(projections.shape, jnp.float32)
-    for lag in range(TAPS):
-        total = (
-            total + weights[lag][:, None] * extended[:, rim_len - lag : rim_len - lag + local_len]
-        )
-    features = total.astype(jnp.bfloat16)
-    query = features[:width].astype(jnp.float32)
-    key_part = features[width : 2 * width].astype(jnp.float32)
-    value_part = features[2 * width :].astype(jnp.float32)
-    product = (key_part * value_part).astype(jnp.bfloat16)
-    cotangent = out_grad.astype(jnp.float32)
-    conv_grad = (cotangent * query).astype(jnp.bfloat16)
+
+    turned = projections.T
+    cotangent = out_grad.T
+    rim = shifted(turned[local_len - RIM :], EVERYONE, 1)
+    feats, product, conv_grad = features_of(turned, rim, short_filter, cotangent)
 
     def exchange(block):
         pieces = block.reshape(devices, owned, local_len)
@@ -277,22 +433,15 @@
     back_chan, cross = filtered(grad_chan, filters, tables, seq_len, prod_spec)
     back_chan, conv_tok = lax.optimization_barrier((back_chan, conv_tok))
     back_tok = exchange(back_chan)
+
     filter_grad = filter_gradient(cross, tables, seq_len)
-
-    conv = conv_tok.reshape(width, local_len).astype(jnp.float32)
-    back = back_tok.reshape(width, local_len).astype(jnp.float32)
-    mixed = (query * conv).astype(jnp.bfloat16)
-    query_grad = (cotangent * conv).astype(jnp.bfloat16)
-    key_grad = (back * value_part).astype(jnp.bfloat16)
-    value_grad = (back * key_part).astype(jnp.bfloat16)
-    feat_grad = jnp.concatenate([query_grad, key_grad, value_grad], axis=0)
-    later = shifted(feat_grad[:, :rim_len], EVERYONE, -1)
-    extended_grad = jnp.concatenate([feat_grad, later], axis=1).astype(jnp.float32)
-    gathered = jnp.zeros(projections.shape, jnp.float32)
-    for lag in range(TAPS):
-        gathered = gathered + weights[lag][:, None] * extended_grad[:, lag : lag + local_len]
-    proj_grad = gathered.astype(jnp.bfloat16)
-    return (mixed, proj_grad, filter_grad)
+    mixed, grad_q, rim_q = query_products(feats, conv_tok.reshape(width, local_len), cotangent)
+    grad = query_gradient(grad_q, shifted(rim_q, EVERYONE, -1), short_filter)
+    filter_grad, mixed, grad, back_tok = lax.optimization_barrier((filter_grad, mixed, grad, back_tok))
+
+    grad_kv, rim_kv = key_value_products(feats, back_tok.reshape(width, local_len))
+    grad = key_value_gradient(grad, grad_kv, shifted(rim_kv, EVERYONE, -1), short_filter)
+    return (mixed, grad, filter_grad)
 
 
 def solution(mesh):

time: 113 us -> 105 us (0.929)
  other arithmetic: 11.8 us -> 0 us
  Pallas kernels: 9.89 us -> 21.1 us
  waiting for transfers between devices: 36.5 us -> 26 us
  starting transfers between devices: 15.9 us -> 17.4 us
    all_to_all x3, waiting for transfers between devices: 35.7 us -> 21.2 us  [exchange(): lax.all_to_all(pieces, EVERYONE, split_axis=0, concat_axis=0, tiled=True)]
    pallas_call x0 -> x5, Pallas kernels: none -> 12 us  [the longest x2 6.43 us: gradient_call(): pl.pallas_call(kernel, name=name, grid=(parts * steps,), in_specs=[pl.Blo...]
    convert_element_type x8 -> x0, other arithmetic: 11.8 us -> none  [the longest x1 3.06 us: shards(): key_grad = (back * value_part).astype(jnp.bfloat16)]
    unnamed x62 -> x56, local copies, waits for them, and re-layouts: 10.6 us -> 15.3 us
    ppermute x2 -> x3, waiting for transfers between devices: 0.79 us -> 4.87 us  [shifted(): lax.ppermute(value, axis, [(source, source + steps) for source in range(f...]
    convert_element_type x3 -> x0, local copies, waits for them, and re-layouts: 2.83 us -> none  [the longest x1 1.33 us: shards(): conv = conv_tok.reshape(width, local_len).astype(jnp.float32)]
    ppermute x2 -> x3, starting transfers between devices: 7.17 us -> 9.28 us  [shifted(): lax.ppermute(value, axis, [(source, source + steps) for source in range(f...]
  transfers between devices with their start and end apart: 5 -> 6, of which waited for: 4 -> 6; matrix products, arithmetic and copies ran while one was open for 3% -> 1% of each run, Pallas kernels for 9% -> 13%
where the time goes in v4:
time: 105 us; the launch traced here: 103 us
  waiting for transfers between devices  26 us (25%)
  blocking collectives  22.7 us (22%)
  Pallas kernels  21.1 us (20%)
  starting transfers between devices  17.4 us (17%)
  local copies, waits for them, and re-layouts  15.3 us (15%)
    all_to_all x1, blocking collectives, exchange(): lax.all_to_all(pieces, EVERYONE, split_axis=0, concat_axis=0, tiled=True)  22.7 us
    all_to_all x3, waiting for transfers between devices, exchange(): lax.all_to_all(pieces, EVERYONE, split_axis=0, concat_axis=0, tiled=True)  21.2 us
    unnamed x56, local copies, waits for them, and re-layouts  15.3 us
    ppermute x3, starting transfers between devices, shifted(): lax.ppermute(value, axis, [(source, source + steps) for source in range(f...  9.28 us
    all_to_all x3, starting transfers between devices, exchange(): lax.all_to_all(pieces, EVERYONE, split_axis=0, concat_axis=0, tiled=True)  8.11 us
    pallas_call x2, Pallas kernels, filtered(): pl.pallas_call(kernel, name='correlate' if backward else 'convolve', out_...  6.75 us
    pallas_call x2, Pallas kernels, gradient_call(): pl.pallas_call(kernel, name=name, grid=(parts * steps,), in_specs=[pl.Blo...  6.43 us
    pallas_call x3, Pallas kernels, whole_call(): pl.pallas_call(kernel, name=name, out_shape=out_shape, scratch_shapes=lis...  5.54 us
  transfers between devices with their start and end apart: 6, of which 6 were waited for; matrix products, arithmetic and copies ran while one was open for 1% of the time, Pallas kernels for 13%

profile of v4, /device:TPU:1, one launch (start us, length us, event | category | flops | bytes accessed | tf_op | source)
XLA Modules:
  0.0 103.4 jit_solution(11339093016447147308)
XLA Ops:
  0.6 0.0 copy-start.10
  0.7 1.8 %copy.16 = bf16[3072,256]{0,1:T(8,128)(2,1)S(1)} copy(bf16[3072,256]{1,0:T(8,128)(2,1)} %param.12) | data formatting | bytes 3145728 | tf_op args[0]
  2.4 4.6 %collective-permute-start = (bf16[8,3072]{1,0:T(8,128)(2,1)S(1)}, bf16[8,3072]{1,0:T(8,128)(2,1)S(1)}, u32[]{:S(2)}, u32[]{:S(2)}) collective-permute-start(bf16[8,3072]{1,0:T(8,128)(2,1)S(1)} %slice.4), channel_id=1, source_target_pairs={{0,1},{1,2},{2,3},{3,4},{4,5},{5,6},{6,7},{7,8},{8,9},{9,10},{10,1... | collective-permute-start | bytes 147464 | tf_op jit(solution)/shard_map/ppermute | solution.py:21
  7.1 1.0 copy.17
  8.1 0.1 collective-permute-done.rim_ref
  8.2 1.0 %copy-done = bf16[1024,256]{0,1:T(8,128)(2,1)S(1)} copy-done((bf16[1024,256]{0,1:T(8,128)(2,1)S(1)}, bf16[1024,256]{0,1:T(8,128)(2,1)}, u32[]{:S(2)}) %copy-start) | copy-done | bytes 524312
  9.2 2.9 %features.1 = (bf16[256,3072]{1,0:T(8,128)(2,1)S(1)}, bf16[1024,256]{1,0:T(8,128)(2,1)S(1)}, bf16[1024,256]{1,0:T(8,128)(2,1)S(1)}) custom-call(bf16[256,3072]{1,0:T(8,128)(2,1)S(1)} %bitcast.7, bf16[8,3072]{1,0:T(8,128)(2,1)S(1)} %collective-permute-done.rim_ref, bf16[7,3072]{1,0:T(8,128)(2,1)S(1)} %copy-done.10, bf16[256,1024]{1,0:T(8,128)(2,1)S(1)} %bitcast.8), custom_call_target="tpu_custom_call" | custom-call | flops 10000000 | bytes 4000000 | tf_op jit(solution)/shard_map/features/pallas_call | solution.py:266
  12.1 0.0 copy-start.11
  12.1 0.0 copy-start.12
  12.1 0.0 copy-start.13
  12.2 0.0 copy-start.15
  12.2 0.0 copy-start.16
  12.2 0.0 copy-start.14
  12.2 0.0 copy-start.18
  12.2 0.0 copy-start.20
  12.2 22.7 %all_to_all.20.refs_0_ = bf16[32,32,256]{2,1,0:T(8,128)(2,1)S(1)} all-to-all(bf16[32,32,256]{2,1,0:T(8,128)(2,1)S(1)} %bitcast.13), channel_id=1, replica_groups=mesh['dp'=4,'ctx'=8] {'dp','ctx'}, dimensions={0} | all-to-all | bytes 1048576 | tf_op jit(solution)/shard_map/all_to_all | solution.py:424
  34.9 2.7 %all-to-all-start.1 = ((bf16[32,32,256]{2,1,0:T(8,128)(2,1)}), bf16[32,32,256]{2,1,0:T(8,128)(2,1)S(1)}, u32[]{:S(2)}, u32[]{:S(2)}) async-start(bf16[32,32,256]{2,1,0:T(8,128)(2,1)} %bitcast.12), calls=%async_computation.1 | async-start | bytes 1048576 | tf_op jit(solution)/shard_map/all_to_all | solution.py:424
  37.6 1.1 %filter_dft.1.refs_1_ = f32[1024,256]{1,0:T(8,128)S(1)} custom-call(bf16[8,8192]{1,0:T(8,128)(2,1)S(1)} %copy-done.13, bf16[256,64]{1,0:T(8,128)(2,1)S(1)} %copy-done.16, bf16[256,256]{1,0:T(8,128)(2,1)S(1)} %copy-done.15, f32[128,128]{1,0:T(8,128)S(1)} %copy-done.12, f32[128,128]{1,0:T(8,128)S(1)} %copy-done.11), custom_call_target="tpu_custom_call" | custom-call | flops 200000000 | bytes 2000000 | tf_op jit(solution)/shard_map/filter_dft/pallas_call | solution.py:97
  38.7 3.6 %convolve.1 = (bf16[32,32,256]{2,1,0:T(8,128)(2,1)}, f32[2048,256]{1,0:T(8,128)S(1)}) custom-call(bf16[32,32,256]{2,1,0:T(8,128)(2,1)S(1)} %all_to_all.20.refs_0_, f32[1024,256]{1,0:T(8,128)S(1)} %filter_dft.1.refs_1_, bf16[256,128]{1,0:T(8,128)(2,1)S(1)} %copy-done.20, bf16[256,256]{1,0:T(8,128)(2,1)S(1)} %copy-done.15, bf16[256,256]{1,0:T(8,128)(2,1)S(1)} %copy-done.14, ...), custom_call_target="tpu_custom_call" | custom-call | flops 2000000000 | bytes 5000000 | tf_op jit(solution)/shard_map/convolve/pallas_call | solution.py:195
  42.4 1.0 copy-done.2
  43.3 1.4 %copy-done.22 = f32[2048,256]{1,0:T(8,128)} copy-done((f32[2048,256]{1,0:T(8,128)}, f32[2048,256]{1,0:T(8,128)S(1)}, u32[]{:S(2)}) %copy-start.22) | copy-done | bytes 2097176
  44.7 9.1 %all-to-all-done.1.refs_0_ = bf16[32,32,256]{2,1,0:T(8,128)(2,1)S(1)} async-done(((bf16[32,32,256]{2,1,0:T(8,128)(2,1)}), bf16[32,32,256]{2,1,0:T(8,128)(2,1)S(1)}, u32[]{:S(2)}, u32[]{:S(2)}) %all-to-all-start.1) | async-done | bytes 524320 | tf_op jit(solution)/shard_map/all_to_all | solution.py:424
  53.8 2.7 %all-to-all-start.2 = ((bf16[32,32,256]{2,1,0:T(8,128)(2,1)}), bf16[32,32,256]{2,1,0:T(8,128)(2,1)S(1)}, u32[]{:S(2)}, u32[]{:S(2)}) async-start(bf16[32,32,256]{2,1,0:T(8,128)(2,1)} %get-tuple-element.35), calls=%async_computation.2 | async-start | bytes 1048576 | tf_op jit(solution)/shard_map/all_to_all | solution.py:424
  56.6 1.2 %copy-done.3 = f32[1024,256]{1,0:T(8,128)S(1)} copy-done((f32[1024,256]{1,0:T(8,128)S(1)}, f32[1024,256]{1,0:T(8,128)}, u32[]{:S(2)}) %copy-start.3) | copy-done | bytes 1048600
  57.8 0.8 copy-done.19
  58.6 0.8 copy-done.21
  59.5 1.6 %copy-done.23 = f32[2048,256]{1,0:T(8,128)S(1)} copy-done((f32[2048,256]{1,0:T(8,128)S(1)}, f32[2048,256]{1,0:T(8,128)}, u32[]{:S(2)}) %copy-start.23) | copy-done | bytes 2097176
  61.1 3.1 %correlate.1 = (bf16[32,32,256]{2,1,0:T(8,128)(2,1)S(1)}, bf16[1024,256]{1,0:T(8,128)(2,1)S(1)}) custom-call(bf16[32,32,256]{2,1,0:T(8,128)(2,1)S(1)} %all-to-all-done.1.refs_0_, f32[1024,256]{1,0:T(8,128)S(1)} %copy-done.3, f32[2048,256]{1,0:T(8,128)S(1)} %copy-done.23, bf16[256,128]{1,0:T(8,128)(2,1)S(1)} %copy-done.21, bf16[256,256]{1,0:T(8,128)(2,1)S(1)} %copy-done.15, ...), custom_call_target="tpu_custom_call" | custom-call | flops 2000000000 | bytes 5000000 | tf_op jit(solution)/shard_map/correlate/pallas_call | solution.py:195
  64.2 0.8 copy-done.5
  65.0 0.8 copy-done.6
  65.8 7.0 %all-to-all-done.2 = bf16[32,32,256]{2,1,0:T(8,128)(2,1)S(1)} async-done(((bf16[32,32,256]{2,1,0:T(8,128)(2,1)}), bf16[32,32,256]{2,1,0:T(8,128)(2,1)S(1)}, u32[]{:S(2)}, u32[]{:S(2)}) %all-to-all-start.2) | async-done | bytes 524320 | tf_op jit(solution)/shard_map/all_to_all | solution.py:424
  72.8 2.7 %all-to-all-start.3 = ((bf16[32,32,256]{2,1,0:T(8,128)(2,1)}), bf16[32,32,256]{2,1,0:T(8,128)(2,1)S(1)}, u32[]{:S(2)}, u32[]{:S(2)}) async-start(bf16[32,32,256]{2,1,0:T(8,128)(2,1)} %copy-done.5), calls=%async_computation.3 | async-start | bytes 1048576 | tf_op jit(solution)/shard_map/all_to_all | solution.py:424
  75.5 0.0 copy-start.7
  75.5 0.0 copy-start.17
  75.6 1.9 %query_products.1 = (bf16[1024,256]{1,0:T(8,128)(2,1)}, bf16[256,1024]{1,0:T(8,128)(2,1)S(1)}, bf16[8,1024]{1,0:T(8,128)(2,1)S(1)}) custom-call(bf16[256,3072]{1,0:T(8,128)(2,1)S(1)} %get-tuple-element.33.f_ref, bf16[1024,256]{1,0:T(8,128)(2,1)S(1)} %bitcast.10, bf16[256,1024]{1,0:T(8,128)(2,1)S(1)} %bitcast.9), custom_call_target="tpu_custom_call" | custom-call | flops 10000000 | bytes 4000000 | tf_op jit(solution)/shard_map/query_products/pallas_call | solution.py:266
  77.5 0.8 copy-done.9
  78.3 2.3 %collective-permute-start.1 = (bf16[8,1024]{1,0:T(8,128)(2,1)S(1)}, bf16[8,1024]{1,0:T(8,128)(2,1)S(1)}, u32[]{:S(2)}, u32[]{:S(2)}) collective-permute-start(bf16[8,1024]{1,0:T(8,128)(2,1)S(1)} %get-tuple-element.39), channel_id=1, source_target_pairs={{1,0},{2,1},{3,2},{4,3},{5,4},{6,5},{7,6},{8,7},{9,8},{10,9},{11,1... | collective-permute-start | bytes 49160 | tf_op jit(solution)/shard_map/ppermute | solution.py:21
  80.6 1.3 %filter_gradient.1 = f32[8,8192]{1,0:T(8,128)} custom-call(bf16[1024,256]{1,0:T(8,128)(2,1)S(1)} %copy-done.7, bf16[256,256]{1,0:T(8,128)(2,1)S(1)} %copy-done.14, bf16[64,256]{1,0:T(8,128)(2,1)S(1)} %copy-done.17, f32[128,128]{1,0:T(8,128)S(1)} %copy-done.12, f32[128,128]{1,0:T(8,128)S(1)} %copy-done.11), custom_call_target="tpu_custom_call" | custom-call | flops 200000000 | bytes 2000000 | tf_op jit(solution)/shard_map/filter_gradient/pallas_call | solution.py:230
  81.9 1.9 %collective-permute-done.1.rim_ref = bf16[8,1024]{1,0:T(8,128)(2,1)S(1)} collective-permute-done((bf16[8,1024]{1,0:T(8,128)(2,1)S(1)}, bf16[8,1024]{1,0:T(8,128)(2,1)S(1)}, u32[]{:S(2)}, u32[]{:S(2)}) %collective-permute-start.1) | collective-permute-done | bytes 16416 | tf_op jit(solution)/shard_map/ppermute | solution.py:21
  83.8 0.6 copy-done.26
  84.4 2.4 %query_gradient.1._ = bf16[3072,256]{1,0:T(8,128)(2,1)} custom-call(bf16[256,1024]{1,0:T(8,128)(2,1)} %copy-done.9, bf16[8,1024]{1,0:T(8,128)(2,1)} %copy-done.26, bf16[7,3072]{1,0:T(8,128)(2,1)} %w_ref.5), custom_call_target="tpu_custom_call" | custom-call | flops 20000000 | bytes 4000000 | tf_op jit(solution)/shard_map/query_gradient/pallas_call | solution.py:392
  86.8 5.0 %all-to-all-done.3 = bf16[32,32,256]{2,1,0:T(8,128)(2,1)S(1)} async-done(((bf16[32,32,256]{2,1,0:T(8,128)(2,1)}), bf16[32,32,256]{2,1,0:T(8,128)(2,1)S(1)}, u32[]{:S(2)}, u32[]{:S(2)}) %all-to-all-start.3) | async-done | bytes 524320 | tf_op jit(solution)/shard_map/all_to_all | solution.py:424
  91.8 0.8 key_value_products.1
  92.6 1.0 copy-done.4
  93.6 2.4 %collective-permute-start.2 = (bf16[8,2048]{1,0:T(8,128)(2,1)S(1)}, bf16[8,2048]{1,0:T(8,128)(2,1)S(1)}, u32[]{:S(2)}, u32[]{:S(2)}) collective-permute-start(bf16[8,2048]{1,0:T(8,128)(2,1)S(1)} %get-tuple-element.45), channel_id=1, source_target_pairs={{1,0},{2,1},{3,2},{4,3},{5,4},{6,5},{7,6},{8,7},{9,8},{10,9},{11,1... | collective-permute-start | bytes 98312 | tf_op jit(solution)/shard_map/ppermute | solution.py:21
  96.0 2.8 %collective-permute-done.2.rim_ref = bf16[8,2048]{1,0:T(8,128)(2,1)S(1)} collective-permute-done((bf16[8,2048]{1,0:T(8,128)(2,1)S(1)}, bf16[8,2048]{1,0:T(8,128)(2,1)S(1)}, u32[]{:S(2)}, u32[]{:S(2)}) %collective-permute-start.2) | collective-permute-done | bytes 32800 | tf_op jit(solution)/shard_map/ppermute | solution.py:21
  98.8 0.6 copy-done.25
  99.4 4.0 %key_value_gradient.1 = bf16[3072,256]{1,0:T(8,128)(2,1)} custom-call(bf16[3072,256]{1,0:T(8,128)(2,1)} %query_gradient.1._, bf16[256,2048]{1,0:T(8,128)(2,1)} %copy-done.4, bf16[8,2048]{1,0:T(8,128)(2,1)} %copy-done.25, bf16[7,3072]{1,0:T(8,128)(2,1)} %w_ref.5), custom_call_target="tpu_custom_call", output_to_operand_aliasing={{}: (0, {})} | custom-call | flops 20000000 | bytes 4000000 | tf_op jit(solution)/shard_map/key_value_gradient/pallas_call | solution.py:392
  (31 shorter events, 0.1 us)
Async XLA Ops:
  0.6 6.4 %copy-start.24 = (bf16[1024,256]{1,0:T(8,128)(2,1)S(1)}, bf16[1024,256]{1,0:T(8,128)(2,1)}, u32[]{:S(2)}) copy-start(bf16[1024,256]{1,0:T(8,128)(2,1)} %param.15) | copy-start | bytes 1572868
  0.6 7.6 %copy-start.10 = (bf16[7,3072]{1,0:T(8,128)(2,1)S(1)}, bf16[7,3072]{1,0:T(8,128)(2,1)}, u32[]{:S(2)}) copy-start(bf16[7,3072]{1,0:T(8,128)(2,1)} %w_ref.5) | copy-start | bytes 129028
  2.4 5.8 %collective-permute-start = (bf16[8,3072]{1,0:T(8,128)(2,1)S(1)}, bf16[8,3072]{1,0:T(8,128)(2,1)S(1)}, u32[]{:S(2)}, u32[]{:S(2)}) collective-permute-start(bf16[8,3072]{1,0:T(8,128)(2,1)S(1)} %slice.4), channel_id=1, source_target_pairs={{0,1},{1,2},{2,3},{3,4},{4,5},{5,6},{6,7},{7,8},{8,9},{9,10},{10,1... | collective-permute-start | bytes 147464 | tf_op jit(solution)/shard_map/ppermute | solution.py:21
  8.2 1.0 %copy-start = (bf16[1024,256]{0,1:T(8,128)(2,1)S(1)}, bf16[1024,256]{0,1:T(8,128)(2,1)}, u32[]{:S(2)}) copy-start(bf16[1024,256]{0,1:T(8,128)(2,1)} %copy.17) | copy-start | bytes 1572868
  12.1 22.8 %copy-start.8 = (bf16[1024,256]{1,0:T(8,128)(2,1)}, bf16[1024,256]{1,0:T(8,128)(2,1)S(1)}, u32[]{:S(2)}) copy-start(bf16[1024,256]{1,0:T(8,128)(2,1)S(1)} %get-tuple-element.29) | copy-start | bytes 1572868
  12.1 25.5 %copy-start.11 = (f32[128,128]{1,0:T(8,128)S(1)}, f32[128,128]{1,0:T(8,128)}, u32[]{:S(2)}) copy-start(f32[128,128]{1,0:T(8,128)} %constant.17.clone.ti_ref.refs_7_.refs_8_) | copy-start | bytes 196612
  12.1 25.5 %copy-start.12 = (f32[128,128]{1,0:T(8,128)S(1)}, f32[128,128]{1,0:T(8,128)}, u32[]{:S(2)}) copy-start(f32[128,128]{1,0:T(8,128)} %constant.16.clone.tr_ref.refs_6_.refs_7_) | copy-start | bytes 196612
  12.1 25.5 %copy-start.13 = (bf16[8,8192]{1,0:T(8,128)(2,1)S(1)}, bf16[8,8192]{1,0:T(8,128)(2,1)}, u32[]{:S(2)}) copy-start(bf16[8,8192]{1,0:T(8,128)(2,1)} %x_ref.1) | copy-start | bytes 393220
  12.2 25.5 %copy-start.15 = (bf16[256,256]{1,0:T(8,128)(2,1)S(1)}, bf16[256,256]{1,0:T(8,128)(2,1)}, u32[]{:S(2)}) copy-start(bf16[256,256]{1,0:T(8,128)(2,1)} %constant.26.second_ref.refs_3_.refs_4_) | copy-start | bytes 393220
  12.2 25.5 %copy-start.16 = (bf16[256,64]{1,0:T(8,128)(2,1)S(1)}, bf16[256,64]{1,0:T(8,128)(2,1)}, u32[]{:S(2)}) copy-start(bf16[256,64]{1,0:T(8,128)(2,1)} %constant.25.first_ref) | copy-start | bytes 98308
  12.2 26.5 %copy-start.14 = (bf16[256,256]{1,0:T(8,128)(2,1)S(1)}, bf16[256,256]{1,0:T(8,128)(2,1)}, u32[]{:S(2)}) copy-start(bf16[256,256]{1,0:T(8,128)(2,1)} %constant.28.refs_4_.refs_5_.third_ref) | copy-start | bytes 393220
  12.2 26.5 %copy-start.18 = (bf16[128,256]{1,0:T(8,128)(2,1)S(1)}, bf16[128,256]{1,0:T(8,128)(2,1)}, u32[]{:S(2)}) copy-start(bf16[128,256]{1,0:T(8,128)(2,1)} %constant.29.refs_5_.refs_6_) | copy-start | bytes 196612
  12.2 26.5 %copy-start.20 = (bf16[256,128]{1,0:T(8,128)(2,1)S(1)}, bf16[256,128]{1,0:T(8,128)(2,1)}, u32[]{:S(2)}) copy-start(bf16[256,128]{1,0:T(8,128)(2,1)} %constant.27.refs_2_.refs_3_) | copy-start | bytes 196612
  34.9 19.0 %all-to-all-start.1 = ((bf16[32,32,256]{2,1,0:T(8,128)(2,1)}), bf16[32,32,256]{2,1,0:T(8,128)(2,1)S(1)}, u32[]{:S(2)}, u32[]{:S(2)}) async-start(bf16[32,32,256]{2,1,0:T(8,128)(2,1)} %bitcast.12), calls=%async_computation.1 | async-start | bytes 1048576 | tf_op jit(solution)/shard_map/all_to_all | solution.py:424
  42.4 1.0 copy-start.2
  43.3 1.4 %copy-start.22 = (f32[2048,256]{1,0:T(8,128)}, f32[2048,256]{1,0:T(8,128)S(1)}, u32[]{:S(2)}) copy-start(f32[2048,256]{1,0:T(8,128)S(1)} %get-tuple-element.31.refs_2_) | copy-start | bytes 6291460
  53.8 19.0 %all-to-all-start.2 = ((bf16[32,32,256]{2,1,0:T(8,128)(2,1)}), bf16[32,32,256]{2,1,0:T(8,128)(2,1)S(1)}, u32[]{:S(2)}, u32[]{:S(2)}) async-start(bf16[32,32,256]{2,1,0:T(8,128)(2,1)} %get-tuple-element.35), calls=%async_computation.2 | async-start | bytes 1048576 | tf_op jit(solution)/shard_map/all_to_all | solution.py:424
  56.6 1.2 %copy-start.3 = (f32[1024,256]{1,0:T(8,128)S(1)}, f32[1024,256]{1,0:T(8,128)}, u32[]{:S(2)}) copy-start(f32[1024,256]{1,0:T(8,128)} %copy-done.2) | copy-start | bytes 3145732
  57.8 0.8 copy-start.19
  58.6 0.8 copy-start.21
  59.5 1.6 %copy-start.23 = (f32[2048,256]{1,0:T(8,128)S(1)}, f32[2048,256]{1,0:T(8,128)}, u32[]{:S(2)}) copy-start(f32[2048,256]{1,0:T(8,128)} %copy-done.22) | copy-start | bytes 6291460
  61.1 14.5 %copy-start.1 = (bf16[1024,256]{0,1:T(8,128)(2,1)S(1)}, bf16[1024,256]{0,1:T(8,128)(2,1)}, u32[]{:S(2)}) copy-start(bf16[1024,256]{0,1:T(8,128)(2,1)} %copy.17) | copy-start | bytes 1572868
  64.2 0.8 copy-start.5
  65.0 0.8 copy-start.6
  72.8 19.0 %all-to-all-start.3 = ((bf16[32,32,256]{2,1,0:T(8,128)(2,1)}), bf16[32,32,256]{2,1,0:T(8,128)(2,1)S(1)}, u32[]{:S(2)}, u32[]{:S(2)}) async-start(bf16[32,32,256]{2,1,0:T(8,128)(2,1)} %copy-done.5), calls=%async_computation.3 | async-start | bytes 1048576 | tf_op jit(solution)/shard_map/all_to_all | solution.py:424
  75.5 5.1 %copy-start.7 = (bf16[1024,256]{1,0:T(8,128)(2,1)S(1)}, bf16[1024,256]{1,0:T(8,128)(2,1)}, u32[]{:S(2)}) copy-start(bf16[1024,256]{1,0:T(8,128)(2,1)} %copy-done.6) | copy-start | bytes 1572868
  75.5 5.0 %copy-start.17 = (bf16[64,256]{1,0:T(8,128)(2,1)S(1)}, bf16[64,256]{1,0:T(8,128)(2,1)}, u32[]{:S(2)}) copy-start(bf16[64,256]{1,0:T(8,128)(2,1)} %constant.30.fourth_ref) | copy-start | bytes 98308
  77.5 0.8 copy-start.9
  78.3 5.5 %collective-permute-start.1 = (bf16[8,1024]{1,0:T(8,128)(2,1)S(1)}, bf16[8,1024]{1,0:T(8,128)(2,1)S(1)}, u32[]{:S(2)}, u32[]{:S(2)}) collective-permute-start(bf16[8,1024]{1,0:T(8,128)(2,1)S(1)} %get-tuple-element.39), channel_id=1, source_target_pairs={{1,0},{2,1},{3,2},{4,3},{5,4},{6,5},{7,6},{8,7},{9,8},{10,9},{11,1... | collective-permute-start | bytes 49160 | tf_op jit(solution)/shard_map/ppermute | solution.py:21
  83.8 0.6 copy-start.26
  92.6 1.0 copy-start.4
  93.6 5.2 %collective-permute-start.2 = (bf16[8,2048]{1,0:T(8,128)(2,1)S(1)}, bf16[8,2048]{1,0:T(8,128)(2,1)S(1)}, u32[]{:S(2)}, u32[]{:S(2)}) collective-permute-start(bf16[8,2048]{1,0:T(8,128)(2,1)S(1)} %get-tuple-element.45), channel_id=1, source_target_pairs={{1,0},{2,1},{3,2},{4,3},{5,4},{6,5},{7,6},{8,7},{9,8},{10,9},{11,1... | collective-permute-start | bytes 98312 | tf_op jit(solution)/shard_map/ppermute | solution.py:21
  98.8 0.6 copy-start.25

commit v5 on v4

--- a/solution.py
+++ b/solution.py
@@ -12,7 +12,7 @@
 TAPS = 7
 PAIRS = CPG // 2
 EVERYONE = ("dp", "ctx")
-VMEM_LIMIT = 40 * 1024 * 1024
+VMEM_LIMIT = 20 * 1024 * 1024
 
 
 def shifted(value, axis, steps):
@@ -104,10 +104,10 @@
     )(long_filter, tables["first_real"], tables["second"], tables["twist_re"], tables["twist_im"])
 
 
-def filtered(arrived, filters, tables, seq_len, other=None):
+def filtered(arrived, channels, first_row, filters, tables, seq_len, other=None, edges=False):
     padded, inner, outer = sizes_of(seq_len)
     half = outer // 2
-    sources, channels, local = arrived.shape
+    sources, _, local = arrived.shape
     fold = local // inner
     groups = channels // CPG
     backward = other is not None
@@ -121,7 +121,7 @@
              y_ref, z_ref, tall, wide, stage, turn) = refs
         height = sources * channels
         for t in range(local // LANES):
-            block = x_ref[:, :, t * LANES : (t + 1) * LANES].astype(jnp.float32)
+            block = x_ref[:, first_row : first_row + channels, t * LANES : (t + 1) * LANES].astype(jnp.float32)
             tall[t * height : (t + 1) * height, :] = block.reshape(height, LANES)
         for c in range(channels):
             pair, part = divmod(c, 2)
@@ -182,10 +182,29 @@
                         rows = y[at : at + sources, p * inner : (p + 1) * inner]
                         put_spread(tall, rows, channels, c, height, (h * inner, (h + 1) * inner))
         for t in range(local // LANES):
-            block = tall[t * height : (t + 1) * height, :].reshape(sources, channels, LANES)
-            y_ref[:, :, t * LANES : (t + 1) * LANES] = block.astype(jnp.bfloat16)
+            block = tall[t * height : (t + 1) * height, :].reshape(sources, channels, LANES).astype(jnp.bfloat16)
+            if edges:
+                y_ref[:, t * channels : (t + 1) * channels, :] = block
+            else:
+                y_ref[:, :, t * LANES : (t + 1) * LANES] = block
+        if edges:
+            spot = lax.broadcasted_iota(jnp.int32, (RIM, LANES), 0)
+            lane = lax.broadcasted_iota(jnp.int32, (RIM, LANES), 1)
+            pick = jnp.where(spot == lane, 1.0, 0.0).astype(jnp.bfloat16)
+            first = tall[:height, :].astype(jnp.bfloat16)
+            rim = lax.dot_general(pick, first, (((1,), (1,)), ((), ())), preferred_element_type=jnp.float32)
+            at = local // LANES * channels
+            for d in range(sources):
+                tile, lanes = divmod((d + 1) % sources * channels, LANES)
+                piece = rim[:, tile * LANES : (tile + 1) * LANES]
+                if lanes:
+                    piece = pltpu.roll(piece, LANES - lanes, 1)
+                if d == sources - 1:
+                    piece = jnp.zeros_like(piece)
+                y_ref[d, at : at + RIM, :] = piece.astype(jnp.bfloat16)
 
     pairs = groups * PAIRS
+    sent = (local // LANES * channels + RIM, LANES) if edges else (channels, local)
     if backward:
         extra = jax.ShapeDtypeStruct((groups * outer, 2 * inner), jnp.bfloat16)
     else:
@@ -195,7 +214,7 @@
     return pl.pallas_call(
         kernel,
         name="correlate" if backward else "convolve",
-        out_shape=(jax.ShapeDtypeStruct(arrived.shape, jnp.bfloat16), extra),
+        out_shape=(narrow_shape(sources, *sent), extra),
         scratch_shapes=[
             pltpu.VMEM((sources * channels * local // LANES, LANES), jnp.float32),
             pltpu.VMEM((outer, pairs * inner), jnp.bfloat16),
@@ -241,6 +260,7 @@
 
 
 RIM = 8
+JOINED = True
 
 
 def seven_taps(tall, value, rim, weights, forward):
@@ -278,10 +298,13 @@
     return jax.ShapeDtypeStruct(shape, jnp.bfloat16)
 
 
-def features_of(turned, rim, short_filter, cotangent):
+def features_of(turned, rim, short_filter, cotangent, owned, joined):
     local, width = cotangent.shape
-
-    def kernel(x_ref, rim_ref, w_ref, og_ref, f_ref, kv_ref, dconv_ref, tall):
+    near = LANES // owned
+
+    def kernel(x_ref, rim_ref, w_ref, og_ref, f_ref, edge_ref, *rest):
+        tall = rest[-1]
+
         @pl.loop(0, width // LANES)
         def _(i):
             made = []
@@ -295,16 +318,28 @@
                     True,
                 ).astype(jnp.bfloat16)
                 f_ref[:, lanes] = total
+                edge_ref[:, lanes] = total[:RIM]
                 made.append(total.astype(jnp.float32))
             rows = lane_block(i)
-            kv_ref[rows, :] = (made[1] * made[2]).astype(jnp.bfloat16).T
+            kv = (made[1] * made[2]).astype(jnp.bfloat16).T
             og = og_ref[:, rows].astype(jnp.float32)
-            dconv_ref[rows, :] = (og * made[0]).astype(jnp.bfloat16).T
-
+            dconv = (og * made[0]).astype(jnp.bfloat16).T
+            if joined:
+                to = pl.ds(i * near, near)
+                rest[0][to, :owned, :] = kv.reshape(near, owned, local)
+                rest[0][to, owned:, :] = dconv.reshape(near, owned, local)
+            else:
+                rest[0][rows, :] = kv
+                rest[1][rows, :] = dconv
+
+    if joined:
+        products = (narrow_shape(width // owned, 2 * owned, local),)
+    else:
+        products = (narrow_shape(width, local), narrow_shape(width, local))
     return whole_call(
         kernel,
         "features",
-        (narrow_shape(local, 3 * width), narrow_shape(width, local), narrow_shape(width, local)),
+        (narrow_shape(local, 3 * width), narrow_shape(RIM, 3 * width)) + products,
         (turned, rim, short_filter, cotangent),
         [pltpu.VMEM((3, local + RIM, LANES), jnp.float32)],
     )
@@ -407,40 +442,110 @@
     )(*whole, grad, rim, short_filter)
 
 
+def key_value_side(whole, feats, edges, back, short_filter, owned):
+    local = feats.shape[0]
+    width = feats.shape[1] // 3
+    near = LANES // owned
+    blocks = width // LANES
+
+    def kernel(_, f_ref, edge_ref, back_ref, w_ref, out_ref, tall, made, sent):
+        lane = lax.broadcasted_iota(jnp.int32, (RIM, LANES), 1)
+
+        def copy(at):
+            rows = pl.ds(pl.multiple_of(width + at * LANES, LANES), LANES)
+            return pltpu.make_async_copy(made.at[at], out_ref.at[rows, :], sent.at[at])
+
+        @pl.loop(0, blocks)
+        def _(i):
+            held = pl.ds(i * near, near)
+            tiles = [
+                back_ref[held, t * owned : (t + 1) * owned, :].reshape(LANES, LANES).T for t in range(local // LANES)
+            ]
+            here = jnp.concatenate(tiles, axis=0).astype(jnp.float32)
+            at = local // LANES * owned
+            rim = back_ref[i * near, at : at + RIM, :].astype(jnp.float32)
+            for k in range(1, near):
+                piece = back_ref[i * near + k, at : at + RIM, :].astype(jnp.float32)
+                rim = jnp.where(lane >= k * owned, pltpu.roll(piece, k * owned, 1), rim)
+            for part in range(2):
+                lanes = lane_block(i, (2 - part) * width)
+                grad = (here * f_ref[:, lanes].astype(jnp.float32)).astype(jnp.bfloat16)
+                edge = (rim * edge_ref[:, lanes].astype(jnp.float32)).astype(jnp.bfloat16)
+                total = seven_taps(
+                    tall.at[part],
+                    grad.astype(jnp.float32),
+                    edge.astype(jnp.float32),
+                    w_ref[:, lane_block(i, (1 + part) * width)].astype(jnp.float32),
+                    False,
+                )
+                made[part * blocks + i] = total.astype(jnp.bfloat16).T
+                copy(part * blocks + i).start()
+
+        @pl.loop(0, 2 * blocks)
+        def _(at):
+            copy(at).wait()
+
+    vmem = pl.BlockSpec(memory_space=pltpu.VMEM)
+    return whole_call(
+        kernel,
+        "key_value_side",
+        narrow_shape(3 * width, local),
+        (whole, feats, edges, back, short_filter),
+        [
+            pltpu.VMEM((2, local + RIM, LANES), jnp.float32),
+            pltpu.VMEM((2 * blocks, LANES, local), jnp.bfloat16),
+            pltpu.SemaphoreType.DMA((2 * blocks,)),
+        ],
+        in_specs=[pl.BlockSpec(memory_space=pl.ANY), vmem, vmem, vmem, vmem],
+        out_specs=pl.BlockSpec(memory_space=pl.ANY),
+        input_output_aliases={0: 0},
+    )
+
+
 def shards(projections, short_filter, long_filter, out_grad):
     width, local_len = out_grad.shape
     devices = lax.axis_size(EVERYONE)
     seq_len = local_len * devices
     owned = width // devices
     tables = make_tables(seq_len, devices)
+    roomy = owned % 16 == 0 and LANES % owned == 0
 
     turned = projections.T
     cotangent = out_grad.T
     rim = shifted(turned[local_len - RIM :], EVERYONE, 1)
-    feats, product, conv_grad = features_of(turned, rim, short_filter, cotangent)
-
-    def exchange(block):
-        pieces = block.reshape(devices, owned, local_len)
+    feats, edges, *products = features_of(turned, rim, short_filter, cotangent, owned, JOINED and roomy)
+
+    def exchange(pieces):
         return lax.all_to_all(pieces, EVERYONE, split_axis=0, concat_axis=0, tiled=True)
 
     filters = transform_filters(long_filter, tables, seq_len)
-    prod_chan = exchange(product)
-    conv_grad, prod_chan = lax.optimization_barrier((conv_grad, prod_chan))
-    grad_chan = exchange(conv_grad)
-    conv_chan, prod_spec = filtered(prod_chan, filters, tables, seq_len)
+    if JOINED and roomy:
+        prod_chan = grad_chan = exchange(products[0])
+    else:
+        prod_chan = exchange(products[0].reshape(devices, owned, local_len))
+        conv_grad, prod_chan = lax.optimization_barrier((products[1], prod_chan))
+        grad_chan = exchange(conv_grad.reshape(devices, owned, local_len))
+    first_row = owned if JOINED and roomy else 0
+    conv_chan, prod_spec = filtered(prod_chan, owned, 0, filters, tables, seq_len)
     conv_chan, grad_chan = lax.optimization_barrier((conv_chan, grad_chan))
     conv_tok = exchange(conv_chan)
-    back_chan, cross = filtered(grad_chan, filters, tables, seq_len, prod_spec)
+    back_chan, cross = filtered(grad_chan, owned, first_row, filters, tables, seq_len, prod_spec, roomy)
     back_chan, conv_tok = lax.optimization_barrier((back_chan, conv_tok))
     back_tok = exchange(back_chan)
 
     filter_grad = filter_gradient(cross, tables, seq_len)
     mixed, grad_q, rim_q = query_products(feats, conv_tok.reshape(width, local_len), cotangent)
     grad = query_gradient(grad_q, shifted(rim_q, EVERYONE, -1), short_filter)
-    filter_grad, mixed, grad, back_tok = lax.optimization_barrier((filter_grad, mixed, grad, back_tok))
-
-    grad_kv, rim_kv = key_value_products(feats, back_tok.reshape(width, local_len))
-    grad = key_value_gradient(grad, grad_kv, shifted(rim_kv, EVERYONE, -1), short_filter)
+    if roomy:
+        edges = shifted(edges, EVERYONE, -1)
+        filter_grad, mixed, grad, edges, back_tok = lax.optimization_barrier(
+            (filter_grad, mixed, grad, edges, back_tok)
+        )
+        grad = key_value_side(grad, feats, edges, back_tok, short_filter, owned)
+    else:
+        filter_grad, mixed, grad, back_tok = lax.optimization_barrier((filter_grad, mixed, grad, back_tok))
+        grad_kv, rim_kv = key_value_products(feats, back_tok.reshape(width, local_len))
+        grad = key_value_gradient(grad, grad_kv, shifted(rim_kv, EVERYONE, -1), short_filter)
     return (mixed, grad, filter_grad)
 
 

time: 105 us -> 98.8 us (0.941)
  blocking collectives: 22.7 us -> 0 us
  waiting for transfers between devices: 26 us -> 36.5 us
  starting transfers between devices: 17.4 us -> 21.5 us
  local copies, waits for them, and re-layouts: 15.3 us -> 18.1 us
    all_to_all x1 -> x0, blocking collectives: 22.7 us -> none  [exchange(): lax.all_to_all(pieces, EVERYONE, split_axis=0, concat_axis=0, tiled=True)]
    all_to_all x3, waiting for transfers between devices: 21.2 us -> 34.1 us  [exchange(): lax.all_to_all(pieces, EVERYONE, split_axis=0, concat_axis=0, tiled=True)]
    all_to_all x3, starting transfers between devices: 8.11 us -> 12.6 us  [exchange(): lax.all_to_all(pieces, EVERYONE, split_axis=0, concat_axis=0, tiled=True)]
    pallas_call x2 -> x1, Pallas kernels: 6.43 us -> 2.38 us  [gradient_call(): pl.pallas_call(kernel, name=name, grid=(parts * steps,), in_specs=[pl.Blo...]
    unnamed x56 -> x62, local copies, waits for them, and re-layouts: 15.3 us -> 18.1 us
    ppermute x3, waiting for transfers between devices: 4.87 us -> 2.42 us  [shifted(): lax.ppermute(value, axis, [(source, source + steps) for source in range(f...]
    pallas_call x3, Pallas kernels: 5.54 us -> 7.94 us  [whole_call(): pl.pallas_call(kernel, name=name, out_shape=out_shape, scratch_shapes=lis...]
  transfers between devices with their start and end apart: 6 -> 6, of which waited for: 6 -> 5; matrix products, arithmetic and copies ran while one was open for 1% -> 1% of each run, Pallas kernels for 13% -> 11%
where the time goes in v5:
time: 98.8 us; the launch traced here: 97.4 us
  waiting for transfers between devices  36.5 us (37%)
  starting transfers between devices  21.5 us (22%)
  Pallas kernels  20.4 us (21%)
  local copies, waits for them, and re-layouts  18.1 us (18%)
    all_to_all x3, waiting for transfers between devices, exchange(): lax.all_to_all(pieces, EVERYONE, split_axis=0, concat_axis=0, tiled=True)  34.1 us
    unnamed x62, local copies, waits for them, and re-layouts  18.1 us
    all_to_all x3, starting transfers between devices, exchange(): lax.all_to_all(pieces, EVERYONE, split_axis=0, concat_axis=0, tiled=True)  12.6 us
    ppermute x3, starting transfers between devices, shifted(): lax.ppermute(value, axis, [(source, source + steps) for source in range(f...  8.81 us
    pallas_call x3, Pallas kernels, whole_call(): pl.pallas_call(kernel, name=name, out_shape=out_shape, scratch_shapes=lis...  7.94 us
    pallas_call x2, Pallas kernels, filtered(): pl.pallas_call(kernel, name='correlate' if backward else 'convolve', out_...  7.78 us
    ppermute x3, waiting for transfers between devices, shifted(): lax.ppermute(value, axis, [(source, source + steps) for source in range(f...  2.42 us
    pallas_call x1, Pallas kernels, gradient_call(): pl.pallas_call(kernel, name=name, grid=(parts * steps,), in_specs=[pl.Blo...  2.38 us
  transfers between devices with their start and end apart: 6, of which 5 were waited for; matrix products, arithmetic and copies ran while one was open for 1% of the time, Pallas kernels for 11%

profile of v5, /device:TPU:1, one launch (start us, length us, event | category | flops | bytes accessed | tf_op | source)
XLA Modules:
  0.0 97.4 jit_solution(14786421446448258108)
XLA Ops:
  0.6 0.0 copy-start.28
  0.6 0.0 copy-start.11
  0.7 1.8 %copy.16 = bf16[3072,256]{0,1:T(8,128)(2,1)S(1)} copy(bf16[3072,256]{1,0:T(8,128)(2,1)} %param.12) | data formatting | bytes 3145728 | tf_op args[0]
  2.4 4.6 %collective-permute-start = (bf16[8,3072]{1,0:T(8,128)(2,1)S(1)}, bf16[8,3072]{1,0:T(8,128)(2,1)S(1)}, u32[]{:S(2)}, u32[]{:S(2)}) collective-permute-start(bf16[8,3072]{1,0:T(8,128)(2,1)S(1)} %slice.4), channel_id=1, source_target_pairs={{0,1},{1,2},{2,3},{3,4},{4,5},{5,6},{6,7},{7,8},{8,9},{9,10},{10,1... | collective-permute-start | bytes 147464 | tf_op jit(solution)/shard_map/ppermute | solution.py:21
  7.1 1.0 %copy.17 = bf16[1024,256]{0,1:T(8,128)(2,1)} copy(bf16[1024,256]{1,0:T(8,128)(2,1)S(1)} %copy-done.28) | data formatting | bytes 1048576 | tf_op args[3]
  8.1 0.1 collective-permute-done.rim_ref
  8.2 1.0 %copy-done = bf16[1024,256]{0,1:T(8,128)(2,1)S(1)} copy-done((bf16[1024,256]{0,1:T(8,128)(2,1)S(1)}, bf16[1024,256]{0,1:T(8,128)(2,1)}, u32[]{:S(2)}) %copy-start) | copy-done | bytes 524312
  9.2 2.9 %features.1 = (bf16[256,3072]{1,0:T(8,128)(2,1)S(1)}, bf16[8,3072]{1,0:T(8,128)(2,1)S(1)}, bf16[32,64,256]{2,1,0:T(8,128)(2,1)S(1)}) custom-call(bf16[256,3072]{1,0:T(8,128)(2,1)S(1)} %bitcast.4, bf16[8,3072]{1,0:T(8,128)(2,1)S(1)} %collective-permute-done.rim_ref, bf16[7,3072]{1,0:T(8,128)(2,1)S(1)} %copy-done.11, bf16[256,1024]{1,0:T(8,128)(2,1)S(1)} %bitcast.5), custom_call_target="tpu_custom_call" | custom-call | flops 10000000 | bytes 4000000 | tf_op jit(solution)/shard_map/features/pallas_call | solution.py:286
  12.1 0.0 copy-start.9
  12.1 1.0 copy-done.9
  13.1 0.6 copy-done.21
  13.7 0.0 copy-start.19
  13.7 0.0 copy-start.16
  13.7 0.0 copy-start.22
  13.7 0.0 copy-start.24
  13.7 6.8 %all-to-all-start = ((bf16[32,64,256]{2,1,0:T(8,128)(2,1)}), bf16[32,64,256]{2,1,0:T(8,128)(2,1)S(1)}, u32[]{:S(2)}, u32[]{:S(2)}) async-start(bf16[32,64,256]{2,1,0:T(8,128)(2,1)} %copy-done.9), calls=%async_computation | async-start | bytes 2097152 | tf_op jit(solution)/shard_map/all_to_all | solution.py:519
  20.6 1.1 %filter_dft.1.refs_1_ = f32[1024,256]{1,0:T(8,128)S(1)} custom-call(bf16[8,8192]{1,0:T(8,128)(2,1)S(1)} %copy-done.15, bf16[256,64]{1,0:T(8,128)(2,1)S(1)} %copy-done.19, bf16[256,256]{1,0:T(8,128)(2,1)S(1)} %copy-done.17, f32[128,128]{1,0:T(8,128)S(1)} %copy-done.14, f32[128,128]{1,0:T(8,128)S(1)} %copy-done.13), custom_call_target="tpu_custom_call" | custom-call | flops 200000000 | bytes 2000000 | tf_op jit(solution)/shard_map/filter_dft/pallas_call | solution.py:97
  21.6 1.0 %copy-done.6 = f32[1024,256]{1,0:T(8,128)} copy-done((f32[1024,256]{1,0:T(8,128)}, f32[1024,256]{1,0:T(8,128)S(1)}, u32[]{:S(2)}) %copy-start.6) | copy-done | bytes 1048600
  22.6 24.9 %all-to-all-done.refs_0_ = bf16[32,64,256]{2,1,0:T(8,128)(2,1)S(1)} async-done(((bf16[32,64,256]{2,1,0:T(8,128)(2,1)}), bf16[32,64,256]{2,1,0:T(8,128)(2,1)S(1)}, u32[]{:S(2)}, u32[]{:S(2)}) %all-to-all-start) | async-done | bytes 1048608 | tf_op jit(solution)/shard_map/all_to_all | solution.py:519
  47.5 0.0 copy-done.16
  47.5 1.2 %copy-done.7 = f32[1024,256]{1,0:T(8,128)S(1)} copy-done((f32[1024,256]{1,0:T(8,128)S(1)}, f32[1024,256]{1,0:T(8,128)}, u32[]{:S(2)}) %copy-start.7) | copy-done | bytes 1048600
  48.7 3.6 %convolve.1 = (bf16[32,32,256]{2,1,0:T(8,128)(2,1)}, f32[2048,256]{1,0:T(8,128)S(1)}) custom-call(bf16[32,64,256]{2,1,0:T(8,128)(2,1)S(1)} %all-to-all-done.refs_0_, f32[1024,256]{1,0:T(8,128)S(1)} %copy-done.7, bf16[256,128]{1,0:T(8,128)(2,1)S(1)} %copy-done.24, bf16[256,256]{1,0:T(8,128)(2,1)S(1)} %copy-done.17, bf16[256,256]{1,0:T(8,128)(2,1)S(1)} %copy-done.16, ...), custom_call_target="tpu_custom_call" | custom-call | flops 2000000000 | bytes 5000000 | tf_op jit(solution)/shard_map/convolve/pallas_call | solution.py:214
  52.4 1.4 %copy-done.26 = f32[2048,256]{1,0:T(8,128)} copy-done((f32[2048,256]{1,0:T(8,128)}, f32[2048,256]{1,0:T(8,128)S(1)}, u32[]{:S(2)}) %copy-start.26) | copy-done | bytes 2097176
  53.7 3.1 %all-to-all-start.1 = ((bf16[32,32,256]{2,1,0:T(8,128)(2,1)}), bf16[32,32,256]{2,1,0:T(8,128)(2,1)S(1)}, u32[]{:S(2)}, u32[]{:S(2)}) async-start(bf16[32,32,256]{2,1,0:T(8,128)(2,1)} %get-tuple-element.29), calls=%async_computation.1 | async-start | bytes 1048576 | tf_op jit(solution)/shard_map/all_to_all | solution.py:519
  56.8 0.0 copy-start.5
  56.8 1.2 %copy-done.5 = bf16[32,64,256]{2,1,0:T(8,128)(2,1)S(1)} copy-done((bf16[32,64,256]{2,1,0:T(8,128)(2,1)S(1)}, bf16[32,64,256]{2,1,0:T(8,128)(2,1)}, u32[]{:S(2)}) %copy-start.5) | copy-done | bytes 1048600
  58.0 1.2 %copy-done.8 = f32[1024,256]{1,0:T(8,128)S(1)} copy-done((f32[1024,256]{1,0:T(8,128)S(1)}, f32[1024,256]{1,0:T(8,128)}, u32[]{:S(2)}) %copy-start.8) | copy-done | bytes 1048600
  59.3 0.9 copy-done.18
  60.2 0.8 copy-done.23
  61.0 0.8 copy-done.25
  61.8 1.6 %copy-done.27 = f32[2048,256]{1,0:T(8,128)S(1)} copy-done((f32[2048,256]{1,0:T(8,128)S(1)}, f32[2048,256]{1,0:T(8,128)}, u32[]{:S(2)}) %copy-start.27) | copy-done | bytes 2097176
  63.4 4.2 %correlate.1 = (bf16[32,72,128]{2,1,0:T(8,128)(2,1)}, bf16[1024,256]{1,0:T(8,128)(2,1)S(1)}) custom-call(bf16[32,64,256]{2,1,0:T(8,128)(2,1)S(1)} %copy-done.5, f32[1024,256]{1,0:T(8,128)S(1)} %copy-done.8, f32[2048,256]{1,0:T(8,128)S(1)} %copy-done.27, bf16[256,128]{1,0:T(8,128)(2,1)S(1)} %copy-done.25, bf16[256,256]{1,0:T(8,128)(2,1)S(1)} %copy-done.18, ...), custom_call_target="tpu_custom_call" | custom-call | flops 2000000000 | bytes 5000000 | tf_op jit(solution)/shard_map/correlate/pallas_call | solution.py:214
  67.6 5.5 %all-to-all-done.1 = bf16[32,32,256]{2,1,0:T(8,128)(2,1)S(1)} async-done(((bf16[32,32,256]{2,1,0:T(8,128)(2,1)}), bf16[32,32,256]{2,1,0:T(8,128)(2,1)S(1)}, u32[]{:S(2)}, u32[]{:S(2)}) %all-to-all-start.1) | async-done | bytes 524320 | tf_op jit(solution)/shard_map/all_to_all | solution.py:519
  73.1 0.8 copy-done.2
  73.8 2.8 %all-to-all-start.2 = ((bf16[32,72,128]{2,1,0:T(8,128)(2,1)}), bf16[32,72,128]{2,1,0:T(8,128)(2,1)S(1)}, u32[]{:S(2)}, u32[]{:S(2)}) async-start(bf16[32,72,128]{2,1,0:T(8,128)(2,1)} %get-tuple-element.35), calls=%async_computation.2 | async-start | bytes 1179648 | tf_op jit(solution)/shard_map/all_to_all | solution.py:519
  76.7 2.3 %collective-permute-start.2 = (bf16[8,3072]{1,0:T(8,128)(2,1)}, bf16[8,3072]{1,0:T(8,128)(2,1)S(1)}, u32[]{:S(2)}, u32[]{:S(2)}) collective-permute-start(bf16[8,3072]{1,0:T(8,128)(2,1)} %copy-done.21), channel_id=1, source_target_pairs={{1,0},{2,1},{3,2},{4,3},{5,4},{6,5},{7,6},{8,7},{9,8},{10,9},{11,1... | collective-permute-start | bytes 147464 | tf_op jit(solution)/shard_map/ppermute | solution.py:21
  79.0 0.0 copy-start.3
  79.0 1.0 %copy-done.3 = bf16[32,32,256]{2,1,0:T(8,128)(2,1)S(1)} copy-done((bf16[32,32,256]{2,1,0:T(8,128)(2,1)S(1)}, bf16[32,32,256]{2,1,0:T(8,128)(2,1)}, u32[]{:S(2)}) %copy-start.3) | copy-done | bytes 524312
  80.1 1.9 %query_products.1 = (bf16[1024,256]{1,0:T(8,128)(2,1)}, bf16[256,1024]{1,0:T(8,128)(2,1)S(1)}, bf16[8,1024]{1,0:T(8,128)(2,1)S(1)}) custom-call(bf16[256,3072]{1,0:T(8,128)(2,1)S(1)} %get-tuple-element.27.f_ref, bf16[1024,256]{1,0:T(8,128)(2,1)S(1)} %bitcast.7, bf16[256,1024]{1,0:T(8,128)(2,1)S(1)} %bitcast.6), custom_call_target="tpu_custom_call" | custom-call | flops 10000000 | bytes 4000000 | tf_op jit(solution)/shard_map/query_products/pallas_call | solution.py:286
  82.0 1.9 %collective-permute-start.1 = (bf16[8,1024]{1,0:T(8,128)(2,1)S(1)}, bf16[8,1024]{1,0:T(8,128)(2,1)S(1)}, u32[]{:S(2)}, u32[]{:S(2)}) collective-permute-start(bf16[8,1024]{1,0:T(8,128)(2,1)S(1)} %get-tuple-element.33), channel_id=1, source_target_pairs={{1,0},{2,1},{3,2},{4,3},{5,4},{6,5},{7,6},{8,7},{9,8},{10,9},{11,1... | collective-permute-start | bytes 49160 | tf_op jit(solution)/shard_map/ppermute | solution.py:21
  83.9 0.0 copy-start.12
  83.9 1.3 %filter_gradient.1 = f32[8,8192]{1,0:T(8,128)} custom-call(bf16[1024,256]{1,0:T(8,128)(2,1)S(1)} %get-tuple-element.26.s_ref, bf16[256,256]{1,0:T(8,128)(2,1)S(1)} %copy-done.16, bf16[64,256]{1,0:T(8,128)(2,1)S(1)} %copy-done.20, f32[128,128]{1,0:T(8,128)S(1)} %copy-done.14, f32[128,128]{1,0:T(8,128)S(1)} %copy-done.13), custom_call_target="tpu_custom_call" | custom-call | flops 200000000 | bytes 2000000 | tf_op jit(solution)/shard_map/filter_gradient/pallas_call | solution.py:249
  85.2 2.3 %collective-permute-done.1.rim_ref = bf16[8,1024]{1,0:T(8,128)(2,1)S(1)} collective-permute-done((bf16[8,1024]{1,0:T(8,128)(2,1)S(1)}, bf16[8,1024]{1,0:T(8,128)(2,1)S(1)}, u32[]{:S(2)}, u32[]{:S(2)}) %collective-permute-start.1) | collective-permute-done | bytes 16416 | tf_op jit(solution)/shard_map/ppermute | solution.py:21
  87.5 0.6 copy-done.29
  88.1 2.4 %query_gradient.1._ = bf16[3072,256]{1,0:T(8,128)(2,1)} custom-call(bf16[256,1024]{1,0:T(8,128)(2,1)} %copy-done.10, bf16[8,1024]{1,0:T(8,128)(2,1)} %copy-done.29, bf16[7,3072]{1,0:T(8,128)(2,1)} %w_ref.5), custom_call_target="tpu_custom_call" | custom-call | flops 20000000 | bytes 4000000 | tf_op jit(solution)/shard_map/query_gradient/pallas_call | solution.py:427
  90.5 0.0 collective-permute-done.2.edge_ref
  90.5 3.8 %all-to-all-done.2.back_ref = bf16[32,72,128]{2,1,0:T(8,128)(2,1)S(1)} async-done(((bf16[32,72,128]{2,1,0:T(8,128)(2,1)}), bf16[32,72,128]{2,1,0:T(8,128)(2,1)S(1)}, u32[]{:S(2)}, u32[]{:S(2)}) %all-to-all-start.2) | async-done | bytes 589856 | tf_op jit(solution)/shard_map/all_to_all | solution.py:519
  94.2 3.2 %key_value_side.1 = bf16[3072,256]{1,0:T(8,128)(2,1)} custom-call(bf16[3072,256]{1,0:T(8,128)(2,1)} %query_gradient.1._, bf16[256,3072]{1,0:T(8,128)(2,1)S(1)} %get-tuple-element.27.f_ref, bf16[8,3072]{1,0:T(8,128)(2,1)S(1)} %collective-permute-done.2.edge_ref, bf16[32,72,128]{2,1,0:T(8,128)(2,1)S(1)} %all-to-all-done.2.back_ref, ...), custom_call_target="tpu_custom_call", output_to_operand_aliasing={{}: (0, {})} | custom-call | flops 10000000 | bytes 4000000 | tf_op jit(solution)/shard_map/key_value_side/pallas_call | solution.py:286
  (35 shorter events, 0.1 us)
Async XLA Ops:
  0.6 6.4 %copy-start.28 = (bf16[1024,256]{1,0:T(8,128)(2,1)S(1)}, bf16[1024,256]{1,0:T(8,128)(2,1)}, u32[]{:S(2)}) copy-start(bf16[1024,256]{1,0:T(8,128)(2,1)} %param.15) | copy-start | bytes 1572868
  0.6 7.6 %copy-start.11 = (bf16[7,3072]{1,0:T(8,128)(2,1)S(1)}, bf16[7,3072]{1,0:T(8,128)(2,1)}, u32[]{:S(2)}) copy-start(bf16[7,3072]{1,0:T(8,128)(2,1)} %w_ref.5) | copy-start | bytes 129028
  2.4 5.8 %collective-permute-start = (bf16[8,3072]{1,0:T(8,128)(2,1)S(1)}, bf16[8,3072]{1,0:T(8,128)(2,1)S(1)}, u32[]{:S(2)}, u32[]{:S(2)}) collective-permute-start(bf16[8,3072]{1,0:T(8,128)(2,1)S(1)} %slice.4), channel_id=1, source_target_pairs={{0,1},{1,2},{2,3},{3,4},{4,5},{5,6},{6,7},{7,8},{8,9},{9,10},{10,1... | collective-permute-start | bytes 147464 | tf_op jit(solution)/shard_map/ppermute | solution.py:21
  8.2 1.0 %copy-start = (bf16[1024,256]{0,1:T(8,128)(2,1)S(1)}, bf16[1024,256]{0,1:T(8,128)(2,1)}, u32[]{:S(2)}) copy-start(bf16[1024,256]{0,1:T(8,128)(2,1)} %copy.17) | copy-start | bytes 1572868
  12.1 1.0 copy-start.9
  13.1 0.6 copy-start.21
  13.7 6.8 %copy-start.13 = (f32[128,128]{1,0:T(8,128)S(1)}, f32[128,128]{1,0:T(8,128)}, u32[]{:S(2)}) copy-start(f32[128,128]{1,0:T(8,128)} %constant.17.clone.ti_ref.refs_7_.refs_8_) | copy-start | bytes 196612
  13.7 6.8 %copy-start.14 = (f32[128,128]{1,0:T(8,128)S(1)}, f32[128,128]{1,0:T(8,128)}, u32[]{:S(2)}) copy-start(f32[128,128]{1,0:T(8,128)} %constant.16.clone.tr_ref.refs_6_.refs_7_) | copy-start | bytes 196612
  13.7 6.8 %copy-start.15 = (bf16[8,8192]{1,0:T(8,128)(2,1)S(1)}, bf16[8,8192]{1,0:T(8,128)(2,1)}, u32[]{:S(2)}) copy-start(bf16[8,8192]{1,0:T(8,128)(2,1)} %x_ref.1) | copy-start | bytes 393220
  13.7 6.8 %copy-start.17 = (bf16[256,256]{1,0:T(8,128)(2,1)S(1)}, bf16[256,256]{1,0:T(8,128)(2,1)}, u32[]{:S(2)}) copy-start(bf16[256,256]{1,0:T(8,128)(2,1)} %constant.26.second_ref.refs_3_.refs_4_) | copy-start | bytes 393220
  13.7 6.9 %copy-start.19 = (bf16[256,64]{1,0:T(8,128)(2,1)S(1)}, bf16[256,64]{1,0:T(8,128)(2,1)}, u32[]{:S(2)}) copy-start(bf16[256,64]{1,0:T(8,128)(2,1)} %constant.25.first_ref) | copy-start | bytes 98308
  13.7 33.8 %copy-start.16 = (bf16[256,256]{1,0:T(8,128)(2,1)S(1)}, bf16[256,256]{1,0:T(8,128)(2,1)}, u32[]{:S(2)}) copy-start(bf16[256,256]{1,0:T(8,128)(2,1)} %constant.28.refs_4_.refs_5_.third_ref) | copy-start | bytes 393220
  13.7 33.8 %copy-start.22 = (bf16[128,256]{1,0:T(8,128)(2,1)S(1)}, bf16[128,256]{1,0:T(8,128)(2,1)}, u32[]{:S(2)}) copy-start(bf16[128,256]{1,0:T(8,128)(2,1)} %constant.29.refs_5_.refs_6_) | copy-start | bytes 196612
  13.7 33.8 %copy-start.24 = (bf16[256,128]{1,0:T(8,128)(2,1)S(1)}, bf16[256,128]{1,0:T(8,128)(2,1)}, u32[]{:S(2)}) copy-start(bf16[256,128]{1,0:T(8,128)(2,1)} %constant.27.refs_2_.refs_3_) | copy-start | bytes 196612
  13.7 33.8 %all-to-all-start = ((bf16[32,64,256]{2,1,0:T(8,128)(2,1)}), bf16[32,64,256]{2,1,0:T(8,128)(2,1)S(1)}, u32[]{:S(2)}, u32[]{:S(2)}) async-start(bf16[32,64,256]{2,1,0:T(8,128)(2,1)} %copy-done.9), calls=%async_computation | async-start | bytes 2097152 | tf_op jit(solution)/shard_map/all_to_all | solution.py:519
  21.6 1.0 %copy-start.6 = (f32[1024,256]{1,0:T(8,128)}, f32[1024,256]{1,0:T(8,128)S(1)}, u32[]{:S(2)}) copy-start(f32[1024,256]{1,0:T(8,128)S(1)} %filter_dft.1.refs_1_) | copy-start | bytes 3145732
  47.5 1.2 %copy-start.7 = (f32[1024,256]{1,0:T(8,128)S(1)}, f32[1024,256]{1,0:T(8,128)}, u32[]{:S(2)}) copy-start(f32[1024,256]{1,0:T(8,128)} %copy-done.6) | copy-start | bytes 3145732
  48.7 3.6 %copy-start.4 = (bf16[32,64,256]{2,1,0:T(8,128)(2,1)}, bf16[32,64,256]{2,1,0:T(8,128)(2,1)S(1)}, u32[]{:S(2)}) copy-start(bf16[32,64,256]{2,1,0:T(8,128)(2,1)S(1)} %all-to-all-done.refs_0_) | copy-start | bytes 3145732
  52.4 1.4 %copy-start.26 = (f32[2048,256]{1,0:T(8,128)}, f32[2048,256]{1,0:T(8,128)S(1)}, u32[]{:S(2)}) copy-start(f32[2048,256]{1,0:T(8,128)S(1)} %get-tuple-element.25.refs_2_) | copy-start | bytes 6291460
  53.7 19.3 %all-to-all-start.1 = ((bf16[32,32,256]{2,1,0:T(8,128)(2,1)}), bf16[32,32,256]{2,1,0:T(8,128)(2,1)S(1)}, u32[]{:S(2)}, u32[]{:S(2)}) async-start(bf16[32,32,256]{2,1,0:T(8,128)(2,1)} %get-tuple-element.29), calls=%async_computation.1 | async-start | bytes 1048576 | tf_op jit(solution)/shard_map/all_to_all | solution.py:519
  56.8 1.2 %copy-start.5 = (bf16[32,64,256]{2,1,0:T(8,128)(2,1)S(1)}, bf16[32,64,256]{2,1,0:T(8,128)(2,1)}, u32[]{:S(2)}) copy-start(bf16[32,64,256]{2,1,0:T(8,128)(2,1)} %copy-done.4) | copy-start | bytes 3145732
  58.0 1.2 %copy-start.8 = (f32[1024,256]{1,0:T(8,128)S(1)}, f32[1024,256]{1,0:T(8,128)}, u32[]{:S(2)}) copy-start(f32[1024,256]{1,0:T(8,128)} %copy-done.6) | copy-start | bytes 3145732
  59.3 0.9 copy-start.18
  60.2 0.8 copy-start.23
  61.0 0.8 copy-start.25
  61.8 1.6 %copy-start.27 = (f32[2048,256]{1,0:T(8,128)S(1)}, f32[2048,256]{1,0:T(8,128)}, u32[]{:S(2)}) copy-start(f32[2048,256]{1,0:T(8,128)} %copy-done.26) | copy-start | bytes 6291460
  63.4 15.6 %copy-start.1 = (bf16[1024,256]{0,1:T(8,128)(2,1)S(1)}, bf16[1024,256]{0,1:T(8,128)(2,1)}, u32[]{:S(2)}) copy-start(bf16[1024,256]{0,1:T(8,128)(2,1)} %copy.17) | copy-start | bytes 1572868
  73.0 0.8 copy-start.2
  73.8 10.0 %copy-start.20 = (bf16[64,256]{1,0:T(8,128)(2,1)S(1)}, bf16[64,256]{1,0:T(8,128)(2,1)}, u32[]{:S(2)}) copy-start(bf16[64,256]{1,0:T(8,128)(2,1)} %constant.30.fourth_ref) | copy-start | bytes 98308
  73.8 20.4 %all-to-all-start.2 = ((bf16[32,72,128]{2,1,0:T(8,128)(2,1)}), bf16[32,72,128]{2,1,0:T(8,128)(2,1)S(1)}, u32[]{:S(2)}, u32[]{:S(2)}) async-start(bf16[32,72,128]{2,1,0:T(8,128)(2,1)} %get-tuple-element.35), calls=%async_computation.2 | async-start | bytes 1179648 | tf_op jit(solution)/shard_map/all_to_all | solution.py:519
  76.7 13.8 %collective-permute-start.2 = (bf16[8,3072]{1,0:T(8,128)(2,1)}, bf16[8,3072]{1,0:T(8,128)(2,1)S(1)}, u32[]{:S(2)}, u32[]{:S(2)}) collective-permute-start(bf16[8,3072]{1,0:T(8,128)(2,1)} %copy-done.21), channel_id=1, source_target_pairs={{1,0},{2,1},{3,2},{4,3},{5,4},{6,5},{7,6},{8,7},{9,8},{10,9},{11,1... | collective-permute-start | bytes 147464 | tf_op jit(solution)/shard_map/ppermute | solution.py:21
  79.0 1.0 %copy-start.3 = (bf16[32,32,256]{2,1,0:T(8,128)(2,1)S(1)}, bf16[32,32,256]{2,1,0:T(8,128)(2,1)}, u32[]{:S(2)}) copy-start(bf16[32,32,256]{2,1,0:T(8,128)(2,1)} %copy-done.2) | copy-start | bytes 1572868
  82.0 3.2 %copy-start.10 = (bf16[256,1024]{1,0:T(8,128)(2,1)}, bf16[256,1024]{1,0:T(8,128)(2,1)S(1)}, u32[]{:S(2)}) copy-start(bf16[256,1024]{1,0:T(8,128)(2,1)S(1)} %get-tuple-element.32.d_ref) | copy-start | bytes 1572868
  82.0 5.5 %collective-permute-start.1 = (bf16[8,1024]{1,0:T(8,128)(2,1)S(1)}, bf16[8,1024]{1,0:T(8,128)(2,1)S(1)}, u32[]{:S(2)}, u32[]{:S(2)}) collective-permute-start(bf16[8,1024]{1,0:T(8,128)(2,1)S(1)} %get-tuple-element.33), channel_id=1, source_target_pairs={{1,0},{2,1},{3,2},{4,3},{5,4},{6,5},{7,6},{8,7},{9,8},{10,9},{11,1... | collective-permute-start | bytes 49160 | tf_op jit(solution)/shard_map/ppermute | solution.py:21
  83.9 10.3 %copy-start.12 = (bf16[7,3072]{1,0:T(8,128)(2,1)S(1)}, bf16[7,3072]{1,0:T(8,128)(2,1)}, u32[]{:S(2)}) copy-start(bf16[7,3072]{1,0:T(8,128)(2,1)} %w_ref.5) | copy-start | bytes 129028
  87.5 0.6 copy-start.29

commit v6 on v4

--- a/solution.py
+++ b/solution.py
@@ -12,7 +12,7 @@
 TAPS = 7
 PAIRS = CPG // 2
 EVERYONE = ("dp", "ctx")
-VMEM_LIMIT = 40 * 1024 * 1024
+VMEM_LIMIT = 24 * 1024 * 1024
 
 
 def shifted(value, axis, steps):
@@ -352,6 +352,279 @@
     )
 
 
+def joined_features(turned, rim, short_filter, out_grad, owned):
+    width, local = out_grad.shape
+    near = LANES // owned
+    blocks = width // LANES
+
+    def kernel(x_ref, rim_ref, w_ref, og_ref, f_ref, msg_ref, edge_ref, tall, made, edge, sent):
+        def copy(i):
+            to = pl.ds(i * near, near)
+            return pltpu.make_async_copy(made.at[to], msg_ref.at[to], sent.at[i])
+
+        @pl.loop(0, blocks)
+        def _(i):
+            parts = []
+            for part in range(3):
+                lanes = lane_block(i, part * width)
+                total = seven_taps(
+                    tall.at[part],
+                    x_ref[:, lanes].astype(jnp.float32),
+                    rim_ref[:, lanes].astype(jnp.float32),
+                    w_ref[:, lanes].astype(jnp.float32),
+                    True,
+                ).astype(jnp.bfloat16)
+                f_ref[:, lanes] = total
+                if part:
+                    edge[:, lanes] = total[:RIM]
+                parts.append(total.astype(jnp.float32))
+            og = og_ref[lane_block(i), :].T
+            edge[:, lane_block(i)] = og[:RIM]
+            kv = (parts[1] * parts[2]).astype(jnp.bfloat16).T
+            dconv = (og.astype(jnp.float32) * parts[0]).astype(jnp.bfloat16).T
+            to = pl.ds(i * near, near)
+            made[to, :owned, :] = kv.reshape(near, owned, local)
+            made[to, owned:, :] = dconv.reshape(near, owned, local)
+            copy(i).start()
+
+        last = pltpu.make_async_copy(edge, edge_ref, sent.at[blocks])
+        last.start()
+
+        @pl.loop(0, blocks)
+        def _(i):
+            copy(i).wait()
+
+        last.wait()
+
+    vmem = pl.BlockSpec(memory_space=pltpu.VMEM)
+    hbm = pl.BlockSpec(memory_space=pltpu.HBM)
+    devices = width // owned
+    return whole_call(
+        kernel,
+        "joined_features",
+        (narrow_shape(local, 3 * width), narrow_shape(devices, 2 * owned, local), narrow_shape(RIM, 3 * width)),
+        (turned, rim, short_filter, out_grad),
+        [
+            pltpu.VMEM((3, local + RIM, LANES), jnp.float32),
+            pltpu.VMEM((devices, 2 * owned, local), jnp.bfloat16),
+            pltpu.VMEM((RIM, 3 * width), jnp.bfloat16),
+            pltpu.SemaphoreType.DMA((blocks + 1,)),
+        ],
+        in_specs=[vmem] * 4,
+        out_specs=(vmem, hbm, hbm),
+    )
+
+
+def joined_filtering(arrived, filters, tables, seq_len):
+    padded, inner, outer = sizes_of(seq_len)
+    half = outer // 2
+    sources, rows, local = arrived.shape
+    channels = rows // 2
+    tiles = local // LANES
+    fold = local // inner
+    groups = channels // CPG
+    pairs = groups * PAIRS
+    height = sources * channels
+    chunk = sources // 4
+
+    def kernel(x_ref, f_hbm, first_ref, second_ref, third_ref, fourth_ref, tr_ref, ti_ref,
+               y_hbm, cross_ref, f_ref, y_ref, talls, wides, stages, turns, sems):
+        fetch = pltpu.make_async_copy(f_hbm, f_ref, sems.at[0])
+        fetch.start()
+        tr, ti = tr_ref[...], ti_ref[...]
+        for s in range(2):
+            tall, wide, stage = talls.at[s], wides.at[s], stages.at[s]
+            for t in range(tiles):
+                block = x_ref[:, s * channels : (s + 1) * channels, t * LANES : (t + 1) * LANES]
+                tall[t * height : (t + 1) * height, :] = block.astype(jnp.float32).reshape(height, LANES)
+            for c in range(channels):
+                pair, part = divmod(c, 2)
+                for h in range(fold):
+                    line = spread(tall, sources, channels, c, height, (h * inner, (h + 1) * inner))
+                    at = part * half + h * sources
+                    wide[at : at + sources, pair * inner : (pair + 1) * inner] = line.astype(jnp.bfloat16)
+            for g in range(groups):
+                span = PAIRS * inner
+                f = dot(first_ref[...], wide[:, g * span : (g + 1) * span])
+                for p in range(PAIRS):
+                    f_re = f[:outer, p * inner : (p + 1) * inner]
+                    f_im = f[outer:, p * inner : (p + 1) * inner]
+                    at = (g * PAIRS + p) * outer
+                    stage[at : at + outer, :inner] = (f_re * tr + f_im * ti).astype(jnp.bfloat16)
+                    stage[at : at + outer, inner:] = (f_im * tr - f_re * ti).astype(jnp.bfloat16)
+        fetch.wait()
+        for g in range(groups):
+            s_re = f_ref[g * outer : (g + 1) * outer, :inner]
+            s_im = f_ref[g * outer : (g + 1) * outer, inner:]
+            cross_re = cross_im = 0.0
+            for p in range(PAIRS):
+                at = (g * PAIRS + p) * outer
+                k = dot(stages[0, at : at + outer, :], second_ref[...])
+                d = dot(stages[1, at : at + outer, :], second_ref[...])
+                k_re, k_im = k[:, :inner], k[:, inner:]
+                d_re, d_im = d[:, :inner], d[:, inner:]
+                cross_re = cross_re + (k_re * d_re + k_im * d_im)
+                cross_im = cross_im + (k_re * d_im - k_im * d_re)
+                stages[0, at : at + outer, :inner] = (s_re * k_re - s_im * k_im).astype(jnp.bfloat16)
+                stages[0, at : at + outer, inner:] = (s_re * k_im + s_im * k_re).astype(jnp.bfloat16)
+                stages[1, at : at + outer, :inner] = (s_re * d_re + s_im * d_im).astype(jnp.bfloat16)
+                stages[1, at : at + outer, inner:] = (s_re * d_im - s_im * d_re).astype(jnp.bfloat16)
+            cross_ref[g * outer : (g + 1) * outer, :inner] = cross_re.astype(jnp.bfloat16)
+            cross_ref[g * outer : (g + 1) * outer, inner:] = cross_im.astype(jnp.bfloat16)
+        spot = lax.broadcasted_iota(jnp.int32, (RIM, LANES), 0)
+        lane = lax.broadcasted_iota(jnp.int32, (RIM, LANES), 1)
+        pick = jnp.where(spot == lane, 1.0, 0.0).astype(jnp.bfloat16)
+        rims = []
+        for s in range(2):
+            tall, stage, turn = talls.at[s], stages.at[s], turns.at[s]
+            for pair in range(pairs):
+                at = pair * outer
+                h = dot(stage[at : at + outer, :], third_ref[...])
+                h_re, h_im = h[:, :inner], h[:, inner:]
+                lanes = slice(pair * inner, (pair + 1) * inner)
+                turn[:outer, lanes] = (h_re * tr - h_im * ti).astype(jnp.bfloat16)
+                turn[outer:, lanes] = (h_im * tr + h_re * ti).astype(jnp.bfloat16)
+            for g in range(groups):
+                span = PAIRS * inner
+                y = dot(fourth_ref[...], turn[:, g * span : (g + 1) * span]) * (1.0 / padded)
+                for p in range(PAIRS):
+                    for part in range(2):
+                        c = (g * PAIRS + p) * 2 + part
+                        for h in range(fold):
+                            at = part * half + h * sources
+                            line = y[at : at + sources, p * inner : (p + 1) * inner]
+                            put_spread(tall, line, channels, c, height, (h * inner, (h + 1) * inner))
+            first = tall[:height, :].astype(jnp.bfloat16)
+            rims.append(
+                lax.dot_general(pick, first, (((1,), (1,)), ((), ())), preferred_element_type=jnp.float32)
+            )
+        copies = []
+        for q in range(4):
+            to = slice(q * chunk, (q + 1) * chunk)
+            for s in range(2):
+                for t in range(tiles):
+                    at = t * height + q * chunk * channels
+                    block = talls[s, at : at + chunk * channels, :].reshape(chunk, channels, LANES)
+                    row = (s * tiles + t) * channels
+                    y_ref[to, row : row + channels, :] = block.astype(jnp.bfloat16)
+            for d in range(q * chunk, (q + 1) * chunk):
+                tile, lanes = divmod((d + 1) % sources * channels, LANES)
+                edge = jnp.zeros((RIM, LANES), jnp.float32)
+                if d < sources - 1:
+                    for s in range(2):
+                        piece = rims[s][:, tile * LANES : (tile + 1) * LANES]
+                        turn_by = (s * channels - lanes) % LANES
+                        if turn_by:
+                            piece = pltpu.roll(piece, turn_by, 1)
+                        edge = piece if s == 0 else jnp.where(lane < channels, edge, piece)
+                y_ref[d, 2 * tiles * channels :, :] = edge.astype(jnp.bfloat16)
+            copies.append(pltpu.make_async_copy(y_ref.at[to], y_hbm.at[to], sems.at[1 + q]))
+            copies[-1].start()
+        for copy in copies:
+            copy.wait()
+
+    sent = (sources, 2 * tiles * channels + RIM, LANES)
+    vmem = pl.BlockSpec(memory_space=pltpu.VMEM)
+    hbm = pl.BlockSpec(memory_space=pltpu.HBM)
+    names = ("first", "second", "third", "fourth", "twist_re", "twist_im")
+    return whole_call(
+        kernel,
+        "joined_filtering",
+        (narrow_shape(*sent), narrow_shape(groups * outer, 2 * inner)),
+        [arrived, filters] + [tables[n] for n in names],
+        [
+            pltpu.VMEM((groups * outer, 2 * inner), jnp.float32),
+            pltpu.VMEM(sent, jnp.bfloat16),
+            pltpu.VMEM((2, tiles * height, LANES), jnp.float32),
+            pltpu.VMEM((2, outer, pairs * inner), jnp.bfloat16),
+            pltpu.VMEM((2, pairs * outer, 2 * inner), jnp.bfloat16),
+            pltpu.VMEM((2, 2 * outer, pairs * inner), jnp.bfloat16),
+            pltpu.SemaphoreType.DMA((5,)),
+        ],
+        flops=4_000_000_000,
+        in_specs=[vmem, hbm] + [vmem] * 6,
+        out_specs=(hbm, vmem),
+    )
+
+
+def joined_gradients(feats, edges, returned, out_grad, short_filter, owned):
+    width, local = out_grad.shape
+    tiles = local // LANES
+    near = LANES // owned
+    blocks = width // LANES
+
+    def kernel(f_ref, edge_ref, back_ref, og_ref, w_ref, mixed_ref, out_ref, tall, made, sent):
+        lane = lax.broadcasted_iota(jnp.int32, (RIM, LANES), 1)
+
+        def copy(part, i):
+            at = part * blocks + i
+            if part < 3:
+                to = out_ref.at[pl.ds(pl.multiple_of(at * LANES, LANES), LANES), :]
+            else:
+                to = mixed_ref.at[lane_block(i), :]
+            return pltpu.make_async_copy(made.at[at], to, sent.at[at])
+
+        @pl.loop(0, blocks)
+        def _(i):
+            held = pl.ds(i * near, near)
+            sums = []
+            for s in range(2):
+                turned = [
+                    back_ref[held, (s * tiles + t) * owned : (s * tiles + t + 1) * owned, :].reshape(LANES, LANES).T
+                    for t in range(tiles)
+                ]
+                here = jnp.concatenate(turned, axis=0).astype(jnp.float32)
+                rim = jnp.zeros((RIM, LANES), jnp.float32)
+                for n in range(near):
+                    piece = back_ref[i * near + n, 2 * tiles * owned :, :].astype(jnp.float32)
+                    turn_by = (n - s) * owned % LANES
+                    if turn_by:
+                        piece = pltpu.roll(piece, turn_by, 1)
+                    rim = jnp.where(lane >= n * owned, piece, rim) if n else piece
+                sums.append((here, rim))
+            query = f_ref[:, lane_block(i)].astype(jnp.float32)
+            made[3 * blocks + i] = (query * sums[0][0]).astype(jnp.bfloat16).T
+            copy(3, i).start()
+            for part in range(3):
+                here, rim = sums[min(part, 1)]
+                if part == 0:
+                    other = og_ref[lane_block(i), :].T
+                else:
+                    other = f_ref[:, lane_block(i, (3 - part) * width)]
+                edge = edge_ref[:, lane_block(i, (3 - part) % 3 * width)].astype(jnp.float32)
+                grad = (here * other.astype(jnp.float32)).astype(jnp.bfloat16)
+                total = seven_taps(
+                    tall.at[part],
+                    grad.astype(jnp.float32),
+                    (rim * edge).astype(jnp.bfloat16).astype(jnp.float32),
+                    w_ref[:, lane_block(i, part * width)].astype(jnp.float32),
+                    False,
+                )
+                made[part * blocks + i] = total.astype(jnp.bfloat16).T
+                copy(part, i).start()
+
+        @pl.loop(0, blocks)
+        def _(i):
+            for part in range(4):
+                copy(part, i).wait()
+
+    vmem = pl.BlockSpec(memory_space=pltpu.VMEM)
+    hbm = pl.BlockSpec(memory_space=pltpu.HBM)
+    return whole_call(
+        kernel,
+        "joined_gradients",
+        (narrow_shape(width, local), narrow_shape(3 * width, local)),
+        (feats, edges, returned, out_grad, short_filter),
+        [
+            pltpu.VMEM((3, local + RIM, LANES), jnp.float32),
+            pltpu.VMEM((4 * blocks, LANES, local), jnp.bfloat16),
+            pltpu.SemaphoreType.DMA((4 * blocks,)),
+        ],
+        in_specs=[vmem] * 5,
+        out_specs=(hbm, hbm),
+    )
+
+
 def query_gradient(grad, rim, short_filter):
     local, width = grad.shape
     steps = width // GRAD_ROWS
@@ -415,8 +688,21 @@
     tables = make_tables(seq_len, devices)
 
     turned = projections.T
+    rim = shifted(turned[local_len - RIM :], EVERYONE, 1)
+
+    if owned % 16 == 0 and LANES % (2 * owned) == 0 and devices % 4 == 0:
+        feats, message, edges = joined_features(turned, rim, short_filter, out_grad, owned)
+        filters = transform_filters(long_filter, tables, seq_len)
+        arrived = lax.all_to_all(message, EVERYONE, split_axis=0, concat_axis=0, tiled=True)
+        edges, filters, arrived = lax.optimization_barrier((shifted(edges, EVERYONE, -1), filters, arrived))
+        answer, cross = joined_filtering(arrived, filters, tables, seq_len)
+        returned = lax.all_to_all(answer, EVERYONE, split_axis=0, concat_axis=0, tiled=True)
+        filter_grad = filter_gradient(cross, tables, seq_len)
+        filter_grad, returned = lax.optimization_barrier((filter_grad, returned))
+        mixed, grad = joined_gradients(feats, edges, returned, out_grad, short_filter, owned)
+        return (mixed, grad, filter_grad)
+
     cotangent = out_grad.T
-    rim = shifted(turned[local_len - RIM :], EVERYONE, 1)
     feats, product, conv_grad = features_of(turned, rim, short_filter, cotangent)
 
     def exchange(block):

time: 105 us -> 96 us (0.914)
  waiting for transfers between devices: 26 us -> 52 us
  blocking collectives: 22.7 us -> 0 us
  local copies, waits for them, and re-layouts: 15.3 us -> 7.73 us
  Pallas kernels: 21.1 us -> 17.4 us
    all_to_all x1 -> x0, blocking collectives: 22.7 us -> none  [exchange(): lax.all_to_all(pieces, EVERYONE, split_axis=0, concat_axis=0, tiled=True)]
    all_to_all x3 -> x2, waiting for transfers between devices: 21.2 us -> 41.4 us  [the longest x1 27.1 us: shards(): lax.all_to_all(answer, EVERYONE, split_axis=0, concat_axis=0, tiled=True)]
    pallas_call x4 -> x0, Pallas kernels: 13.2 us -> none  [the longest x2 6.75 us: filtered(): pl.pallas_call(kernel, name='correlate' if backward else 'convolve', out_...]
    pallas_call x3, Pallas kernels: 5.54 us -> 15 us  [whole_call(): pl.pallas_call(kernel, name=name, out_shape=out_shape, scratch_shapes=lis...]
    unnamed x56 -> x33, local copies, waits for them, and re-layouts: 15.3 us -> 7.73 us
    ppermute x3 -> x2, waiting for transfers between devices: 4.87 us -> 10.6 us  [shifted(): lax.ppermute(value, axis, [(source, source + steps) for source in range(f...]
    ppermute x3 -> x2, starting transfers between devices: 9.28 us -> 6.76 us  [shifted(): lax.ppermute(value, axis, [(source, source + steps) for source in range(f...]
    all_to_all x3 -> x2, starting transfers between devices: 8.11 us -> 10.1 us  [the longest x1 6.75 us: shards(): lax.all_to_all(message, EVERYONE, split_axis=0, concat_axis=0, tiled=True)]
  transfers between devices with their start and end apart: 6 -> 4, of which waited for: 6 -> 4; matrix products, arithmetic and copies ran while one was open for 1% -> 0% of each run, Pallas kernels for 13% -> 2%
where the time goes in v6:
time: 96 us; the launch traced here: 94.8 us
  waiting for transfers between devices  52 us (54%)
  Pallas kernels  17.4 us (18%)
  starting transfers between devices  16.8 us (18%)
  local copies, waits for them, and re-layouts  7.73 us (8%)
    all_to_all x1, waiting for transfers between devices, shards(): lax.all_to_all(answer, EVERYONE, split_axis=0, concat_axis=0, tiled=True)  27.1 us
    pallas_call x3, Pallas kernels, whole_call(): pl.pallas_call(kernel, name=name, out_shape=out_shape, scratch_shapes=lis...  15 us
    all_to_all x1, waiting for transfers between devices, shards(): lax.all_to_all(message, EVERYONE, split_axis=0, concat_axis=0, tiled=True)  14.3 us
    ppermute x2, waiting for transfers between devices, shifted(): lax.ppermute(value, axis, [(source, source + steps) for source in range(f...  10.6 us
    unnamed x33, local copies, waits for them, and re-layouts  7.73 us
    ppermute x2, starting transfers between devices, shifted(): lax.ppermute(value, axis, [(source, source + steps) for source in range(f...  6.76 us
    all_to_all x1, starting transfers between devices, shards(): lax.all_to_all(message, EVERYONE, split_axis=0, concat_axis=0, tiled=True)  6.75 us
    all_to_all x1, starting transfers between devices, shards(): lax.all_to_all(answer, EVERYONE, split_axis=0, concat_axis=0, tiled=True)  3.32 us
  transfers between devices with their start and end apart: 4, of which 4 were waited for; matrix products, arithmetic and copies ran while one was open for 0% of the time, Pallas kernels for 2%

profile of v6, /device:TPU:1, one launch (start us, length us, event | category | flops | bytes accessed | tf_op | source)
XLA Modules:
  0.0 94.8 jit_solution(10180399679830158781)
XLA Ops:
  0.6 0.0 copy-start
  0.6 0.0 copy-start.7
  0.7 1.8 %copy.15 = bf16[3072,256]{0,1:T(8,128)(2,1)S(1)} copy(bf16[3072,256]{1,0:T(8,128)(2,1)} %param.12) | data formatting | bytes 3145728 | tf_op args[0]
  2.4 4.6 %collective-permute-start = (bf16[8,3072]{1,0:T(8,128)(2,1)S(1)}, bf16[8,3072]{1,0:T(8,128)(2,1)S(1)}, u32[]{:S(2)}, u32[]{:S(2)}) collective-permute-start(bf16[8,3072]{1,0:T(8,128)(2,1)S(1)} %slice.4), channel_id=1, source_target_pairs={{0,1},{1,2},{2,3},{3,4},{4,5},{5,6},{6,7},{7,8},{8,9},{9,10},{10,1... | collective-permute-start | bytes 147464 | tf_op jit(solution)/shard_map/ppermute | solution.py:21
  7.0 1.2 %collective-permute-done.rim_ref = bf16[8,3072]{1,0:T(8,128)(2,1)S(1)} collective-permute-done((bf16[8,3072]{1,0:T(8,128)(2,1)S(1)}, bf16[8,3072]{1,0:T(8,128)(2,1)S(1)}, u32[]{:S(2)}, u32[]{:S(2)}) %collective-permute-start) | collective-permute-done | bytes 49184 | tf_op jit(solution)/shard_map/ppermute | solution.py:21
  8.2 0.0 copy-done
  8.2 0.0 copy-done.7
  8.2 3.5 %joined_features.1 = (bf16[256,3072]{1,0:T(8,128)(2,1)S(1)}, bf16[32,64,256]{2,1,0:T(8,128)(2,1)}, bf16[8,3072]{1,0:T(8,128)(2,1)S(1)}) custom-call(bf16[256,3072]{1,0:T(8,128)(2,1)S(1)} %bitcast.2, bf16[8,3072]{1,0:T(8,128)(2,1)S(1)} %collective-permute-done.rim_ref, bf16[7,3072]{1,0:T(8,128)(2,1)S(1)} %copy-done.7, bf16[1024,256]{1,0:T(8,128)(2,1)S(1)} %copy-done), custom_call_target="tpu_custom_call" | custom-call | flops 10000000 | bytes 4000000 | tf_op jit(solution)/shard_map/joined_features/pallas_call | solution.py:266
  11.8 0.0 copy-start.1
  11.8 1.1 %copy-done.1 = bf16[256,3072]{1,0:T(8,128)(2,1)} copy-done((bf16[256,3072]{1,0:T(8,128)(2,1)}, bf16[256,3072]{1,0:T(8,128)(2,1)S(1)}, u32[]{:S(2)}) %copy-start.1) | copy-done | bytes 1572888
  12.9 0.0 copy-start.5
  12.9 0.0 copy-start.6
  12.9 0.0 copy-start.8
  12.9 0.0 copy-start.10
  12.9 0.0 copy-start.12
  12.9 0.0 copy-start.9
  12.9 6.8 %all-to-all-start = ((bf16[32,64,256]{2,1,0:T(8,128)(2,1)}), bf16[32,64,256]{2,1,0:T(8,128)(2,1)S(1)}, u32[]{:S(2)}, u32[]{:S(2)}) async-start(bf16[32,64,256]{2,1,0:T(8,128)(2,1)} %get-tuple-element.17), calls=%async_computation | async-start | bytes 2097152 | tf_op jit(solution)/shard_map/all_to_all | solution.py:696
  19.7 2.2 %collective-permute-start.1 = (bf16[8,3072]{1,0:T(8,128)(2,1)S(1)}, bf16[8,3072]{1,0:T(8,128)(2,1)S(1)}, u32[]{:S(2)}, u32[]{:S(2)}) collective-permute-start(bf16[8,3072]{1,0:T(8,128)(2,1)S(1)} %get-tuple-element.16), channel_id=1, source_target_pairs={{1,0},{2,1},{3,2},{4,3},{5,4},{6,5},{7,6},{8,7},{9,8},{10,9},{11,1... | collective-permute-start | bytes 147464 | tf_op jit(solution)/shard_map/ppermute | solution.py:21
  21.9 0.0 copy-done.5
  21.9 0.0 copy-done.6
  21.9 0.0 copy-done.8
  21.9 0.0 copy-done.10
  21.9 0.0 copy-done.12
  21.9 1.1 %filter_dft.1.f_hbm = f32[1024,256]{1,0:T(8,128)S(1)} custom-call(bf16[8,8192]{1,0:T(8,128)(2,1)S(1)} %copy-done.8, bf16[256,64]{1,0:T(8,128)(2,1)S(1)} %copy-done.12, bf16[256,256]{1,0:T(8,128)(2,1)S(1)} %copy-done.10, f32[128,128]{1,0:T(8,128)S(1)} %copy-done.6, f32[128,128]{1,0:T(8,128)S(1)} %copy-done.5), custom_call_target="tpu_custom_call" | custom-call | flops 200000000 | bytes 2000000 | tf_op jit(solution)/shard_map/filter_dft/pallas_call | solution.py:97
  23.0 9.4 %collective-permute-done.1.edge_ref = bf16[8,3072]{1,0:T(8,128)(2,1)S(1)} collective-permute-done((bf16[8,3072]{1,0:T(8,128)(2,1)S(1)}, bf16[8,3072]{1,0:T(8,128)(2,1)S(1)}, u32[]{:S(2)}, u32[]{:S(2)}) %collective-permute-start.1) | collective-permute-done | bytes 49184 | tf_op jit(solution)/shard_map/ppermute | solution.py:21
  32.4 14.3 %all-to-all-done.x_ref = bf16[32,64,256]{2,1,0:T(8,128)(2,1)S(1)} async-done(((bf16[32,64,256]{2,1,0:T(8,128)(2,1)}), bf16[32,64,256]{2,1,0:T(8,128)(2,1)S(1)}, u32[]{:S(2)}, u32[]{:S(2)}) %all-to-all-start) | async-done | bytes 1048608 | tf_op jit(solution)/shard_map/all_to_all | solution.py:696
  46.7 0.0 copy-done.9
  46.7 0.0 copy-start.11
  46.7 0.9 copy-done.11
  47.6 0.0 copy-start.14
  47.6 0.8 copy-done.14
  48.4 0.0 copy-start.15
  48.4 0.8 copy-done.15
  49.3 7.3 %joined_filtering.1 = (bf16[32,136,128]{2,1,0:T(8,128)(2,1)}, bf16[1024,256]{1,0:T(8,128)(2,1)S(1)}) custom-call(bf16[32,64,256]{2,1,0:T(8,128)(2,1)S(1)} %all-to-all-done.x_ref, f32[1024,256]{1,0:T(8,128)S(1)} %filter_dft.1.f_hbm, bf16[256,128]{1,0:T(8,128)(2,1)S(1)} %copy-done.15, bf16[256,256]{1,0:T(8,128)(2,1)S(1)} %copy-done.11, ...), custom_call_target="tpu_custom_call" | custom-call | flops 4000000000 | bytes 4000000 | tf_op jit(solution)/shard_map/joined_filtering/pallas_call | solution.py:266
  56.5 0.0 copy-start.3
  56.6 0.8 copy-done.3
  57.3 0.0 copy-start.13
  57.3 0.0 copy-start.4
  57.3 3.3 %all-to-all-start.1 = ((bf16[32,136,128]{2,1,0:T(8,128)(2,1)}), bf16[32,136,128]{2,1,0:T(8,128)(2,1)S(1)}, u32[]{:S(2)}, u32[]{:S(2)}) async-start(bf16[32,136,128]{2,1,0:T(8,128)(2,1)} %get-tuple-element.22), calls=%async_computation.1 | async-start | bytes 2228224 | tf_op jit(solution)/shard_map/all_to_all | solution.py:699
  60.7 0.0 copy-done.13
  60.7 0.0 copy-done.4
  60.7 1.3 %filter_gradient.1 = f32[8,8192]{1,0:T(8,128)} custom-call(bf16[1024,256]{1,0:T(8,128)(2,1)S(1)} %copy-done.4, bf16[256,256]{1,0:T(8,128)(2,1)S(1)} %copy-done.9, bf16[64,256]{1,0:T(8,128)(2,1)S(1)} %copy-done.13, f32[128,128]{1,0:T(8,128)S(1)} %copy-done.6, f32[128,128]{1,0:T(8,128)S(1)} %copy-done.5), custom_call_target="tpu_custom_call" | custom-call | flops 200000000 | bytes 2000000 | tf_op jit(solution)/shard_map/filter_gradient/pallas_call | solution.py:230
  62.0 27.1 %all-to-all-done.1.back_ref = bf16[32,136,128]{2,1,0:T(8,128)(2,1)S(1)} async-done(((bf16[32,136,128]{2,1,0:T(8,128)(2,1)}), bf16[32,136,128]{2,1,0:T(8,128)(2,1)S(1)}, u32[]{:S(2)}, u32[]{:S(2)}) %all-to-all-start.1) | async-done | bytes 1114144 | tf_op jit(solution)/shard_map/all_to_all | solution.py:699
  89.1 0.0 copy-start.2
  89.1 1.4 %copy-done.2 = bf16[256,3072]{1,0:T(8,128)(2,1)S(1)} copy-done((bf16[256,3072]{1,0:T(8,128)(2,1)S(1)}, bf16[256,3072]{1,0:T(8,128)(2,1)}, u32[]{:S(2)}) %copy-start.2) | copy-done | bytes 1572888
  90.5 4.2 %joined_gradients.1 = (bf16[1024,256]{1,0:T(8,128)(2,1)}, bf16[3072,256]{1,0:T(8,128)(2,1)}) custom-call(bf16[256,3072]{1,0:T(8,128)(2,1)S(1)} %copy-done.2, bf16[8,3072]{1,0:T(8,128)(2,1)S(1)} %collective-permute-done.1.edge_ref, bf16[32,136,128]{2,1,0:T(8,128)(2,1)S(1)} %all-to-all-done.1.back_ref, bf16[1024,256]{1,0:T(8,128)(2,1)S(1)} %copy-done, ...), custom_call_target="tpu_custom_call" | custom-call | flops 10000000 | bytes 4000000 | tf_op jit(solution)/shard_map/joined_gradients/pallas_call | solution.py:266
  (1 shorter events, 0.0 us)
Async XLA Ops:
  0.6 7.6 %copy-start = (bf16[1024,256]{1,0:T(8,128)(2,1)S(1)}, bf16[1024,256]{1,0:T(8,128)(2,1)}, u32[]{:S(2)}) copy-start(bf16[1024,256]{1,0:T(8,128)(2,1)} %og_ref.3) | copy-start | bytes 1572868
  0.6 7.6 %copy-start.7 = (bf16[7,3072]{1,0:T(8,128)(2,1)S(1)}, bf16[7,3072]{1,0:T(8,128)(2,1)}, u32[]{:S(2)}) copy-start(bf16[7,3072]{1,0:T(8,128)(2,1)} %w_ref.3) | copy-start | bytes 129028
  2.4 5.8 %collective-permute-start = (bf16[8,3072]{1,0:T(8,128)(2,1)S(1)}, bf16[8,3072]{1,0:T(8,128)(2,1)S(1)}, u32[]{:S(2)}, u32[]{:S(2)}) collective-permute-start(bf16[8,3072]{1,0:T(8,128)(2,1)S(1)} %slice.4), channel_id=1, source_target_pairs={{0,1},{1,2},{2,3},{3,4},{4,5},{5,6},{6,7},{7,8},{8,9},{9,10},{10,1... | collective-permute-start | bytes 147464 | tf_op jit(solution)/shard_map/ppermute | solution.py:21
  11.8 1.1 %copy-start.1 = (bf16[256,3072]{1,0:T(8,128)(2,1)}, bf16[256,3072]{1,0:T(8,128)(2,1)S(1)}, u32[]{:S(2)}) copy-start(bf16[256,3072]{1,0:T(8,128)(2,1)S(1)} %get-tuple-element.15.f_ref) | copy-start | bytes 4718596
  12.9 9.0 %copy-start.5 = (f32[128,128]{1,0:T(8,128)S(1)}, f32[128,128]{1,0:T(8,128)}, u32[]{:S(2)}) copy-start(f32[128,128]{1,0:T(8,128)} %constant.17.clone.ti_ref) | copy-start | bytes 196612
  12.9 9.0 %copy-start.6 = (f32[128,128]{1,0:T(8,128)S(1)}, f32[128,128]{1,0:T(8,128)}, u32[]{:S(2)}) copy-start(f32[128,128]{1,0:T(8,128)} %constant.16.clone.tr_ref) | copy-start | bytes 196612
  12.9 9.0 %copy-start.8 = (bf16[8,8192]{1,0:T(8,128)(2,1)S(1)}, bf16[8,8192]{1,0:T(8,128)(2,1)}, u32[]{:S(2)}) copy-start(bf16[8,8192]{1,0:T(8,128)(2,1)} %x_ref.1) | copy-start | bytes 393220
  12.9 9.0 %copy-start.10 = (bf16[256,256]{1,0:T(8,128)(2,1)S(1)}, bf16[256,256]{1,0:T(8,128)(2,1)}, u32[]{:S(2)}) copy-start(bf16[256,256]{1,0:T(8,128)(2,1)} %constant.26.second_ref) | copy-start | bytes 393220
  12.9 9.0 %copy-start.12 = (bf16[256,64]{1,0:T(8,128)(2,1)S(1)}, bf16[256,64]{1,0:T(8,128)(2,1)}, u32[]{:S(2)}) copy-start(bf16[256,64]{1,0:T(8,128)(2,1)} %constant.25.first_ref) | copy-start | bytes 98308
  12.9 33.8 %copy-start.9 = (bf16[256,256]{1,0:T(8,128)(2,1)S(1)}, bf16[256,256]{1,0:T(8,128)(2,1)}, u32[]{:S(2)}) copy-start(bf16[256,256]{1,0:T(8,128)(2,1)} %constant.28.third_ref) | copy-start | bytes 393220
  12.9 33.8 %all-to-all-start = ((bf16[32,64,256]{2,1,0:T(8,128)(2,1)}), bf16[32,64,256]{2,1,0:T(8,128)(2,1)S(1)}, u32[]{:S(2)}, u32[]{:S(2)}) async-start(bf16[32,64,256]{2,1,0:T(8,128)(2,1)} %get-tuple-element.17), calls=%async_computation | async-start | bytes 2097152 | tf_op jit(solution)/shard_map/all_to_all | solution.py:696
  19.7 12.7 %collective-permute-start.1 = (bf16[8,3072]{1,0:T(8,128)(2,1)S(1)}, bf16[8,3072]{1,0:T(8,128)(2,1)S(1)}, u32[]{:S(2)}, u32[]{:S(2)}) collective-permute-start(bf16[8,3072]{1,0:T(8,128)(2,1)S(1)} %get-tuple-element.16), channel_id=1, source_target_pairs={{1,0},{2,1},{3,2},{4,3},{5,4},{6,5},{7,6},{8,7},{9,8},{10,9},{11,1... | collective-permute-start | bytes 147464 | tf_op jit(solution)/shard_map/ppermute | solution.py:21
  46.7 0.9 copy-start.11
  47.6 0.8 copy-start.14
  48.4 0.8 copy-start.15
  56.5 0.8 copy-start.3
  57.3 3.3 %copy-start.13 = (bf16[64,256]{1,0:T(8,128)(2,1)S(1)}, bf16[64,256]{1,0:T(8,128)(2,1)}, u32[]{:S(2)}) copy-start(bf16[64,256]{1,0:T(8,128)(2,1)} %constant.30.fourth_ref) | copy-start | bytes 98308
  57.3 3.3 %copy-start.4 = (bf16[1024,256]{1,0:T(8,128)(2,1)S(1)}, bf16[1024,256]{1,0:T(8,128)(2,1)}, u32[]{:S(2)}) copy-start(bf16[1024,256]{1,0:T(8,128)(2,1)} %copy-done.3) | copy-start | bytes 1572868
  57.3 31.8 %all-to-all-start.1 = ((bf16[32,136,128]{2,1,0:T(8,128)(2,1)}), bf16[32,136,128]{2,1,0:T(8,128)(2,1)S(1)}, u32[]{:S(2)}, u32[]{:S(2)}) async-start(bf16[32,136,128]{2,1,0:T(8,128)(2,1)} %get-tuple-element.22), calls=%async_computation.1 | async-start | bytes 2228224 | tf_op jit(solution)/shard_map/all_to_all | solution.py:699
  89.1 1.4 %copy-start.2 = (bf16[256,3072]{1,0:T(8,128)(2,1)S(1)}, bf16[256,3072]{1,0:T(8,128)(2,1)}, u32[]{:S(2)}) copy-start(bf16[256,3072]{1,0:T(8,128)(2,1)} %copy-done.1) | copy-start | bytes 4718596

commit v7 on v6

--- a/solution.py
+++ b/solution.py
@@ -48,6 +48,7 @@
         "second": narrow([[cos_i, -sin_i], [sin_i, cos_i]]),
         "third": narrow([[cos_i, sin_i], [-sin_i, cos_i]]),
         "fourth": narrow([[cos_p.T, -sin_p.T], [sin_p.T, cos_p.T]]),
+        "fourth_scaled": narrow([[cos_p.T / padded, -sin_p.T / padded], [sin_p.T / padded, cos_p.T / padded]]),
         "first_real": narrow([[cos_o], [-sin_o]]),
         "fourth_real": narrow([[cos_o.T, -sin_o.T]]),
         "twist_re": twist[0],
@@ -357,10 +358,14 @@
     near = LANES // owned
     blocks = width // LANES
 
-    def kernel(x_ref, rim_ref, w_ref, og_ref, f_ref, msg_ref, edge_ref, tall, made, edge, sent):
+    def kernel(x_ref, rim_ref, w_ref, og_ref, f_hbm, msg_ref, edge_ref, tall, made, f_ref, edge, sent):
         def copy(i):
             to = pl.ds(i * near, near)
             return pltpu.make_async_copy(made.at[to], msg_ref.at[to], sent.at[i])
+
+        def keep(i):
+            to = pl.ds(3 * i, 3)
+            return pltpu.make_async_copy(f_ref.at[to], f_hbm.at[to], sent.at[blocks + i])
 
         @pl.loop(0, blocks)
         def _(i):
@@ -374,7 +379,7 @@
                     w_ref[:, lanes].astype(jnp.float32),
                     True,
                 ).astype(jnp.bfloat16)
-                f_ref[:, lanes] = total
+                f_ref[3 * i + part] = total
                 if part:
                     edge[:, lanes] = total[:RIM]
                 parts.append(total.astype(jnp.float32))
@@ -386,13 +391,15 @@
             made[to, :owned, :] = kv.reshape(near, owned, local)
             made[to, owned:, :] = dconv.reshape(near, owned, local)
             copy(i).start()
-
-        last = pltpu.make_async_copy(edge, edge_ref, sent.at[blocks])
+            keep(i).start()
+
+        last = pltpu.make_async_copy(edge, edge_ref, sent.at[2 * blocks])
         last.start()
 
         @pl.loop(0, blocks)
         def _(i):
             copy(i).wait()
+            keep(i).wait()
 
         last.wait()
 
@@ -402,16 +409,21 @@
     return whole_call(
         kernel,
         "joined_features",
-        (narrow_shape(local, 3 * width), narrow_shape(devices, 2 * owned, local), narrow_shape(RIM, 3 * width)),
+        (
+            narrow_shape(3 * blocks, local, LANES),
+            narrow_shape(devices, 2 * owned, local),
+            narrow_shape(RIM, 3 * width),
+        ),
         (turned, rim, short_filter, out_grad),
         [
             pltpu.VMEM((3, local + RIM, LANES), jnp.float32),
             pltpu.VMEM((devices, 2 * owned, local), jnp.bfloat16),
+            pltpu.VMEM((3 * blocks, local, LANES), jnp.bfloat16),
             pltpu.VMEM((RIM, 3 * width), jnp.bfloat16),
-            pltpu.SemaphoreType.DMA((blocks + 1,)),
+            pltpu.SemaphoreType.DMA((2 * blocks + 1,)),
         ],
         in_specs=[vmem] * 4,
-        out_specs=(vmem, hbm, hbm),
+        out_specs=(hbm, hbm, hbm),
     )
 
 
@@ -427,11 +439,13 @@
     height = sources * channels
     chunk = sources // 4
 
-    def kernel(x_ref, f_hbm, first_ref, second_ref, third_ref, fourth_ref, tr_ref, ti_ref,
-               y_hbm, cross_ref, f_ref, y_ref, talls, wides, stages, turns, sems):
-        fetch = pltpu.make_async_copy(f_hbm, f_ref, sems.at[0])
-        fetch.start()
-        tr, ti = tr_ref[...], ti_ref[...]
+    def kernel(x_ref, *refs):
+        sources_hbm, (y_hbm, cross_hbm), held = refs[:7], refs[7:9], refs[9:16]
+        y_ref, cross_ref, talls, wides, stages, turns, sems, fetched = refs[16:]
+        first_ref, tr_ref, ti_ref, second_ref, f_ref, third_ref, fourth_ref = held
+        fetches = [pltpu.make_async_copy(a, b, fetched.at[n]) for n, (a, b) in enumerate(zip(sources_hbm, held))]
+        for fetch in fetches:
+            fetch.start()
         for s in range(2):
             tall, wide, stage = talls.at[s], wides.at[s], stages.at[s]
             for t in range(tiles):
@@ -443,6 +457,10 @@
                     line = spread(tall, sources, channels, c, height, (h * inner, (h + 1) * inner))
                     at = part * half + h * sources
                     wide[at : at + sources, pair * inner : (pair + 1) * inner] = line.astype(jnp.bfloat16)
+            if s == 0:
+                for fetch in fetches[:3]:
+                    fetch.wait()
+                tr, ti = tr_ref[...], ti_ref[...]
             for g in range(groups):
                 span = PAIRS * inner
                 f = dot(first_ref[...], wide[:, g * span : (g + 1) * span])
@@ -452,7 +470,8 @@
                     at = (g * PAIRS + p) * outer
                     stage[at : at + outer, :inner] = (f_re * tr + f_im * ti).astype(jnp.bfloat16)
                     stage[at : at + outer, inner:] = (f_im * tr - f_re * ti).astype(jnp.bfloat16)
-        fetch.wait()
+        for fetch in fetches[3:]:
+            fetch.wait()
         for g in range(groups):
             s_re = f_ref[g * outer : (g + 1) * outer, :inner]
             s_im = f_ref[g * outer : (g + 1) * outer, inner:]
@@ -471,6 +490,8 @@
                 stages[1, at : at + outer, inner:] = (s_re * d_im - s_im * d_re).astype(jnp.bfloat16)
             cross_ref[g * outer : (g + 1) * outer, :inner] = cross_re.astype(jnp.bfloat16)
             cross_ref[g * outer : (g + 1) * outer, inner:] = cross_im.astype(jnp.bfloat16)
+        copies = [pltpu.make_async_copy(cross_ref, cross_hbm, sems.at[4])]
+        copies[0].start()
         spot = lax.broadcasted_iota(jnp.int32, (RIM, LANES), 0)
         lane = lax.broadcasted_iota(jnp.int32, (RIM, LANES), 1)
         pick = jnp.where(spot == lane, 1.0, 0.0).astype(jnp.bfloat16)
@@ -486,7 +507,7 @@
                 turn[outer:, lanes] = (h_im * tr + h_re * ti).astype(jnp.bfloat16)
             for g in range(groups):
                 span = PAIRS * inner
-                y = dot(fourth_ref[...], turn[:, g * span : (g + 1) * span]) * (1.0 / padded)
+                y = dot(fourth_ref[...], turn[:, g * span : (g + 1) * span])
                 for p in range(PAIRS):
                     for part in range(2):
                         c = (g * PAIRS + p) * 2 + part
@@ -498,7 +519,6 @@
             rims.append(
                 lax.dot_general(pick, first, (((1,), (1,)), ((), ())), preferred_element_type=jnp.float32)
             )
-        copies = []
         for q in range(4):
             to = slice(q * chunk, (q + 1) * chunk)
             for s in range(2):
@@ -518,7 +538,7 @@
                             piece = pltpu.roll(piece, turn_by, 1)
                         edge = piece if s == 0 else jnp.where(lane < channels, edge, piece)
                 y_ref[d, 2 * tiles * channels :, :] = edge.astype(jnp.bfloat16)
-            copies.append(pltpu.make_async_copy(y_ref.at[to], y_hbm.at[to], sems.at[1 + q]))
+            copies.append(pltpu.make_async_copy(y_ref.at[to], y_hbm.at[to], sems.at[q]))
             copies[-1].start()
         for copy in copies:
             copy.wait()
@@ -526,24 +546,27 @@
     sent = (sources, 2 * tiles * channels + RIM, LANES)
     vmem = pl.BlockSpec(memory_space=pltpu.VMEM)
     hbm = pl.BlockSpec(memory_space=pltpu.HBM)
-    names = ("first", "second", "third", "fourth", "twist_re", "twist_im")
+    fetched = [tables[n] for n in ("first", "twist_re", "twist_im", "second")] + [filters]
+    fetched += [tables[n] for n in ("third", "fourth_scaled")]
     return whole_call(
         kernel,
         "joined_filtering",
         (narrow_shape(*sent), narrow_shape(groups * outer, 2 * inner)),
-        [arrived, filters] + [tables[n] for n in names],
-        [
-            pltpu.VMEM((groups * outer, 2 * inner), jnp.float32),
+        [arrived] + fetched,
+        [pltpu.VMEM(array.shape, array.dtype) for array in fetched]
+        + [
             pltpu.VMEM(sent, jnp.bfloat16),
+            pltpu.VMEM((groups * outer, 2 * inner), jnp.bfloat16),
             pltpu.VMEM((2, tiles * height, LANES), jnp.float32),
             pltpu.VMEM((2, outer, pairs * inner), jnp.bfloat16),
             pltpu.VMEM((2, pairs * outer, 2 * inner), jnp.bfloat16),
             pltpu.VMEM((2, 2 * outer, pairs * inner), jnp.bfloat16),
             pltpu.SemaphoreType.DMA((5,)),
+            pltpu.SemaphoreType.DMA((7,)),
         ],
         flops=4_000_000_000,
-        in_specs=[vmem, hbm] + [vmem] * 6,
-        out_specs=(hbm, vmem),
+        in_specs=[vmem] + [hbm] * 7,
+        out_specs=(hbm, hbm),
     )
 
 
@@ -553,7 +576,20 @@
     near = LANES // owned
     blocks = width // LANES
 
-    def kernel(f_ref, edge_ref, back_ref, og_ref, w_ref, mixed_ref, out_ref, tall, made, sent):
+    def kernel(f_hbm, edge_ref, back_ref, og_hbm, w_ref, mixed_ref, out_ref, tall, made, f_ref, og_ref, sent, fetched):
+        def fetch(i):
+            to = pl.ds(3 * i, 3)
+            rows = lane_block(i)
+            return (
+                pltpu.make_async_copy(f_hbm.at[to], f_ref.at[to], fetched.at[i]),
+                pltpu.make_async_copy(og_hbm.at[rows, :], og_ref.at[rows, :], fetched.at[blocks + i]),
+            )
+
+        @pl.loop(0, blocks)
+        def _(i):
+            for one in fetch(i):
+                one.start()
+
         lane = lax.broadcasted_iota(jnp.int32, (RIM, LANES), 1)
 
         def copy(part, i):
@@ -582,7 +618,9 @@
                         piece = pltpu.roll(piece, turn_by, 1)
                     rim = jnp.where(lane >= n * owned, piece, rim) if n else piece
                 sums.append((here, rim))
-            query = f_ref[:, lane_block(i)].astype(jnp.float32)
+            for one in fetch(i):
+                one.wait()
+            query = f_ref[3 * i].astype(jnp.float32)
             made[3 * blocks + i] = (query * sums[0][0]).astype(jnp.bfloat16).T
             copy(3, i).start()
             for part in range(3):
@@ -590,7 +628,7 @@
                 if part == 0:
                     other = og_ref[lane_block(i), :].T
                 else:
-                    other = f_ref[:, lane_block(i, (3 - part) * width)]
+                    other = f_ref[3 * i + 3 - part]
                 edge = edge_ref[:, lane_block(i, (3 - part) % 3 * width)].astype(jnp.float32)
                 grad = (here * other.astype(jnp.float32)).astype(jnp.bfloat16)
                 total = seven_taps(
@@ -618,9 +656,12 @@
         [
             pltpu.VMEM((3, local + RIM, LANES), jnp.float32),
             pltpu.VMEM((4 * blocks, LANES, local), jnp.bfloat16),
+            pltpu.VMEM((3 * blocks, local, LANES), jnp.bfloat16),
+            pltpu.VMEM((width, local), jnp.bfloat16),
             pltpu.SemaphoreType.DMA((4 * blocks,)),
+            pltpu.SemaphoreType.DMA((2 * blocks,)),
         ],
-        in_specs=[vmem] * 5,
+        in_specs=[hbm, vmem, vmem, hbm, vmem],
         out_specs=(hbm, hbm),
     )
 

time: 96 us -> 102 us (1.062)
  Pallas kernels: 17.4 us -> 23.1 us
    pallas_call x3, Pallas kernels: 15 us -> 20.8 us  [whole_call(): pl.pallas_call(kernel, name=name, out_shape=out_shape, scratch_shapes=lis...]
where the time goes in v7:
time: 102 us; the launch traced here: 101 us
  waiting for transfers between devices  52 us (51%)
  Pallas kernels  23.1 us (23%)
  starting transfers between devices  16.8 us (16%)
  local copies, waits for them, and re-layouts  7.73 us (8%)
    all_to_all x1, waiting for transfers between devices, shards(): lax.all_to_all(answer, EVERYONE, split_axis=0, concat_axis=0, tiled=True)  27.1 us
    pallas_call x3, Pallas kernels, whole_call(): pl.pallas_call(kernel, name=name, out_shape=out_shape, scratch_shapes=lis...  20.8 us
    all_to_all x1, waiting for transfers between devices, shards(): lax.all_to_all(message, EVERYONE, split_axis=0, concat_axis=0, tiled=True)  14.3 us
    ppermute x2, waiting for transfers between devices, shifted(): lax.ppermute(value, axis, [(source, source + steps) for source in range(f...  10.6 us
    unnamed x33, local copies, waits for them, and re-layouts  7.73 us
    ppermute x2, starting transfers between devices, shifted(): lax.ppermute(value, axis, [(source, source + steps) for source in range(f...  6.76 us
    all_to_all x1, starting transfers between devices, shards(): lax.all_to_all(message, EVERYONE, split_axis=0, concat_axis=0, tiled=True)  6.75 us
    all_to_all x1, starting transfers between devices, shards(): lax.all_to_all(answer, EVERYONE, split_axis=0, concat_axis=0, tiled=True)  3.33 us
  transfers between devices with their start and end apart: 4, of which 4 were waited for; matrix products, arithmetic and copies ran while one was open for 0% of the time, Pallas kernels for 2%

profile of v7, /device:TPU:1, one launch (start us, length us, event | category | flops | bytes accessed | tf_op | source)
XLA Modules:
  0.0 100.5 jit_solution(11193550625404082436)
XLA Ops:
  0.6 0.0 copy-start
  0.6 0.0 copy-start.7
  0.7 1.8 %copy.15 = bf16[3072,256]{0,1:T(8,128)(2,1)S(1)} copy(bf16[3072,256]{1,0:T(8,128)(2,1)} %param.12) | data formatting | bytes 3145728 | tf_op args[0]
  2.4 4.6 %collective-permute-start = (bf16[8,3072]{1,0:T(8,128)(2,1)S(1)}, bf16[8,3072]{1,0:T(8,128)(2,1)S(1)}, u32[]{:S(2)}, u32[]{:S(2)}) collective-permute-start(bf16[8,3072]{1,0:T(8,128)(2,1)S(1)} %slice.4), channel_id=1, source_target_pairs={{0,1},{1,2},{2,3},{3,4},{4,5},{5,6},{6,7},{7,8},{8,9},{9,10},{10,1... | collective-permute-start | bytes 147464 | tf_op jit(solution)/shard_map/ppermute | solution.py:21
  7.0 1.2 %collective-permute-done.rim_ref = bf16[8,3072]{1,0:T(8,128)(2,1)S(1)} collective-permute-done((bf16[8,3072]{1,0:T(8,128)(2,1)S(1)}, bf16[8,3072]{1,0:T(8,128)(2,1)S(1)}, u32[]{:S(2)}, u32[]{:S(2)}) %collective-permute-start) | collective-permute-done | bytes 49184 | tf_op jit(solution)/shard_map/ppermute | solution.py:21
  8.2 0.0 copy-done
  8.2 0.0 copy-done.7
  8.2 5.1 %joined_features.1 = (bf16[24,256,128]{2,1,0:T(8,128)(2,1)S(1)}, bf16[32,64,256]{2,1,0:T(8,128)(2,1)}, bf16[8,3072]{1,0:T(8,128)(2,1)S(1)}) custom-call(bf16[256,3072]{1,0:T(8,128)(2,1)S(1)} %bitcast.2, bf16[8,3072]{1,0:T(8,128)(2,1)S(1)} %collective-permute-done.rim_ref, bf16[7,3072]{1,0:T(8,128)(2,1)S(1)} %copy-done.7, bf16[1024,256]{1,0:T(8,128)(2,1)S(1)} %copy-done), custom_call_target="tpu_custom_call" | custom-call | flops 10000000 | bytes 4000000 | tf_op jit(solution)/shard_map/joined_features/pallas_call | solution.py:267
  13.3 0.0 copy-start.1
  13.3 1.1 %copy-done.1 = bf16[24,256,128]{2,1,0:T(8,128)(2,1)} copy-done((bf16[24,256,128]{2,1,0:T(8,128)(2,1)}, bf16[24,256,128]{2,1,0:T(8,128)(2,1)S(1)}, u32[]{:S(2)}) %copy-start.1) | copy-done | bytes 1572888
  14.5 0.0 copy-start.5
  14.5 0.0 copy-start.6
  14.5 0.0 copy-start.8
  14.5 0.0 copy-start.10
  14.5 0.0 copy-start.12
  14.5 0.0 copy-start.9
  14.5 6.8 %all-to-all-start = ((bf16[32,64,256]{2,1,0:T(8,128)(2,1)}), bf16[32,64,256]{2,1,0:T(8,128)(2,1)S(1)}, u32[]{:S(2)}, u32[]{:S(2)}) async-start(bf16[32,64,256]{2,1,0:T(8,128)(2,1)} %get-tuple-element.17), calls=%async_computation | async-start | bytes 2097152 | tf_op jit(solution)/shard_map/all_to_all | solution.py:737
  21.3 2.2 %collective-permute-start.1 = (bf16[8,3072]{1,0:T(8,128)(2,1)S(1)}, bf16[8,3072]{1,0:T(8,128)(2,1)S(1)}, u32[]{:S(2)}, u32[]{:S(2)}) collective-permute-start(bf16[8,3072]{1,0:T(8,128)(2,1)S(1)} %get-tuple-element.16), channel_id=1, source_target_pairs={{1,0},{2,1},{3,2},{4,3},{5,4},{6,5},{7,6},{8,7},{9,8},{10,9},{11,1... | collective-permute-start | bytes 147464 | tf_op jit(solution)/shard_map/ppermute | solution.py:21
  23.4 0.0 copy-done.5
  23.4 0.0 copy-done.6
  23.5 0.0 copy-done.8
  23.5 0.0 copy-done.10
  23.5 0.0 copy-done.12
  23.5 1.1 %filter_dft.1.refs_4_ = f32[1024,256]{1,0:T(8,128)S(1)} custom-call(bf16[8,8192]{1,0:T(8,128)(2,1)S(1)} %copy-done.8, bf16[256,64]{1,0:T(8,128)(2,1)S(1)} %copy-done.12, bf16[256,256]{1,0:T(8,128)(2,1)S(1)} %copy-done.10, f32[128,128]{1,0:T(8,128)S(1)} %copy-done.6, f32[128,128]{1,0:T(8,128)S(1)} %copy-done.5), custom_call_target="tpu_custom_call" | custom-call | flops 200000000 | bytes 2000000 | tf_op jit(solution)/shard_map/filter_dft/pallas_call | solution.py:98
  24.6 9.4 %collective-permute-done.1.edge_ref = bf16[8,3072]{1,0:T(8,128)(2,1)S(1)} collective-permute-done((bf16[8,3072]{1,0:T(8,128)(2,1)S(1)}, bf16[8,3072]{1,0:T(8,128)(2,1)S(1)}, u32[]{:S(2)}, u32[]{:S(2)}) %collective-permute-start.1) | collective-permute-done | bytes 49184 | tf_op jit(solution)/shard_map/ppermute | solution.py:21
  34.0 14.3 %all-to-all-done.x_ref = bf16[32,64,256]{2,1,0:T(8,128)(2,1)S(1)} async-done(((bf16[32,64,256]{2,1,0:T(8,128)(2,1)}), bf16[32,64,256]{2,1,0:T(8,128)(2,1)S(1)}, u32[]{:S(2)}, u32[]{:S(2)}) %all-to-all-start) | async-done | bytes 1048608 | tf_op jit(solution)/shard_map/all_to_all | solution.py:737
  48.3 0.0 copy-done.9
  48.3 0.0 copy-start.11
  48.3 0.9 copy-done.11
  49.2 0.0 copy-start.14
  49.2 0.8 copy-done.14
  50.0 0.0 copy-start.15
  50.0 0.8 copy-done.15
  50.9 8.0 %joined_filtering.1 = (bf16[32,136,128]{2,1,0:T(8,128)(2,1)}, bf16[1024,256]{1,0:T(8,128)(2,1)S(1)}) custom-call(bf16[32,64,256]{2,1,0:T(8,128)(2,1)S(1)} %all-to-all-done.x_ref, bf16[256,128]{1,0:T(8,128)(2,1)S(1)} %copy-done.15, f32[128,128]{1,0:T(8,128)S(1)} %copy-done.6, f32[128,128]{1,0:T(8,128)S(1)} %copy-done.5, bf16[256,256]{1,0:T(8,128)(2,1)S(1)} %copy-done.11, ...), custom_call_target="tpu_custom_call" | custom-call | flops 4000000000 | bytes 4000000 | tf_op jit(solution)/shard_map/joined_filtering/pallas_call | solution.py:267
  58.8 0.0 copy-start.3
  58.8 0.8 copy-done.3
  59.6 0.0 copy-start.13
  59.6 0.0 copy-start.4
  59.6 3.3 %all-to-all-start.1 = ((bf16[32,136,128]{2,1,0:T(8,128)(2,1)}), bf16[32,136,128]{2,1,0:T(8,128)(2,1)S(1)}, u32[]{:S(2)}, u32[]{:S(2)}) async-start(bf16[32,136,128]{2,1,0:T(8,128)(2,1)} %get-tuple-element.22), calls=%async_computation.1 | async-start | bytes 2228224 | tf_op jit(solution)/shard_map/all_to_all | solution.py:740
  63.0 0.0 copy-done.13
  63.0 0.0 copy-done.4
  63.0 1.3 %filter_gradient.1 = f32[8,8192]{1,0:T(8,128)} custom-call(bf16[1024,256]{1,0:T(8,128)(2,1)S(1)} %copy-done.4, bf16[256,256]{1,0:T(8,128)(2,1)S(1)} %copy-done.9, bf16[64,256]{1,0:T(8,128)(2,1)S(1)} %copy-done.13, f32[128,128]{1,0:T(8,128)S(1)} %copy-done.6, f32[128,128]{1,0:T(8,128)S(1)} %copy-done.5), custom_call_target="tpu_custom_call" | custom-call | flops 200000000 | bytes 2000000 | tf_op jit(solution)/shard_map/filter_gradient/pallas_call | solution.py:231
  64.3 27.1 %all-to-all-done.1.back_ref = bf16[32,136,128]{2,1,0:T(8,128)(2,1)S(1)} async-done(((bf16[32,136,128]{2,1,0:T(8,128)(2,1)}), bf16[32,136,128]{2,1,0:T(8,128)(2,1)S(1)}, u32[]{:S(2)}, u32[]{:S(2)}) %all-to-all-start.1) | async-done | bytes 1114144 | tf_op jit(solution)/shard_map/all_to_all | solution.py:740
  91.4 0.0 copy-start.2
  91.4 1.4 %copy-done.2 = bf16[24,256,128]{2,1,0:T(8,128)(2,1)S(1)} copy-done((bf16[24,256,128]{2,1,0:T(8,128)(2,1)S(1)}, bf16[24,256,128]{2,1,0:T(8,128)(2,1)}, u32[]{:S(2)}) %copy-start.2) | copy-done | bytes 1572888
  92.8 7.7 %joined_gradients.1 = (bf16[1024,256]{1,0:T(8,128)(2,1)}, bf16[3072,256]{1,0:T(8,128)(2,1)}) custom-call(bf16[24,256,128]{2,1,0:T(8,128)(2,1)S(1)} %copy-done.2, bf16[8,3072]{1,0:T(8,128)(2,1)S(1)} %collective-permute-done.1.edge_ref, bf16[32,136,128]{2,1,0:T(8,128)(2,1)S(1)} %all-to-all-done.1.back_ref, bf16[1024,256]{1,0:T(8,128)(2,1)S(1)} %copy-done, ...), custom_call_target="tpu_custom_call" | custom-call | flops 10000000 | bytes 4000000 | tf_op jit(solution)/shard_map/joined_gradients/pallas_call | solution.py:267
  (1 shorter events, 0.0 us)
Async XLA Ops:
  0.6 7.6 %copy-start = (bf16[1024,256]{1,0:T(8,128)(2,1)S(1)}, bf16[1024,256]{1,0:T(8,128)(2,1)}, u32[]{:S(2)}) copy-start(bf16[1024,256]{1,0:T(8,128)(2,1)} %og_hbm.1) | copy-start | bytes 1572868
  0.6 7.6 %copy-start.7 = (bf16[7,3072]{1,0:T(8,128)(2,1)S(1)}, bf16[7,3072]{1,0:T(8,128)(2,1)}, u32[]{:S(2)}) copy-start(bf16[7,3072]{1,0:T(8,128)(2,1)} %w_ref.3) | copy-start | bytes 129028
  2.4 5.8 %collective-permute-start = (bf16[8,3072]{1,0:T(8,128)(2,1)S(1)}, bf16[8,3072]{1,0:T(8,128)(2,1)S(1)}, u32[]{:S(2)}, u32[]{:S(2)}) collective-permute-start(bf16[8,3072]{1,0:T(8,128)(2,1)S(1)} %slice.4), channel_id=1, source_target_pairs={{0,1},{1,2},{2,3},{3,4},{4,5},{5,6},{6,7},{7,8},{8,9},{9,10},{10,1... | collective-permute-start | bytes 147464 | tf_op jit(solution)/shard_map/ppermute | solution.py:21
  13.3 1.1 %copy-start.1 = (bf16[24,256,128]{2,1,0:T(8,128)(2,1)}, bf16[24,256,128]{2,1,0:T(8,128)(2,1)S(1)}, u32[]{:S(2)}) copy-start(bf16[24,256,128]{2,1,0:T(8,128)(2,1)S(1)} %get-tuple-element.15.f_hbm) | copy-start | bytes 4718596
  14.5 9.0 %copy-start.5 = (f32[128,128]{1,0:T(8,128)S(1)}, f32[128,128]{1,0:T(8,128)}, u32[]{:S(2)}) copy-start(f32[128,128]{1,0:T(8,128)} %constant.17.clone.ti_ref.refs_2_) | copy-start | bytes 196612
  14.5 9.0 %copy-start.6 = (f32[128,128]{1,0:T(8,128)S(1)}, f32[128,128]{1,0:T(8,128)}, u32[]{:S(2)}) copy-start(f32[128,128]{1,0:T(8,128)} %constant.16.clone.tr_ref.refs_1_) | copy-start | bytes 196612
  14.5 9.0 %copy-start.8 = (bf16[8,8192]{1,0:T(8,128)(2,1)S(1)}, bf16[8,8192]{1,0:T(8,128)(2,1)}, u32[]{:S(2)}) copy-start(bf16[8,8192]{1,0:T(8,128)(2,1)} %x_ref.1) | copy-start | bytes 393220
  14.5 9.0 %copy-start.10 = (bf16[256,256]{1,0:T(8,128)(2,1)S(1)}, bf16[256,256]{1,0:T(8,128)(2,1)}, u32[]{:S(2)}) copy-start(bf16[256,256]{1,0:T(8,128)(2,1)} %constant.26.second_ref.refs_3_) | copy-start | bytes 393220
  14.5 9.0 %copy-start.12 = (bf16[256,64]{1,0:T(8,128)(2,1)S(1)}, bf16[256,64]{1,0:T(8,128)(2,1)}, u32[]{:S(2)}) copy-start(bf16[256,64]{1,0:T(8,128)(2,1)} %constant.25.first_ref) | copy-start | bytes 98308
  14.5 33.8 %copy-start.9 = (bf16[256,256]{1,0:T(8,128)(2,1)S(1)}, bf16[256,256]{1,0:T(8,128)(2,1)}, u32[]{:S(2)}) copy-start(bf16[256,256]{1,0:T(8,128)(2,1)} %constant.28.refs_5_.third_ref) | copy-start | bytes 393220
  14.5 33.8 %all-to-all-start = ((bf16[32,64,256]{2,1,0:T(8,128)(2,1)}), bf16[32,64,256]{2,1,0:T(8,128)(2,1)S(1)}, u32[]{:S(2)}, u32[]{:S(2)}) async-start(bf16[32,64,256]{2,1,0:T(8,128)(2,1)} %get-tuple-element.17), calls=%async_computation | async-start | bytes 2097152 | tf_op jit(solution)/shard_map/all_to_all | solution.py:737
  21.3 12.7 %collective-permute-start.1 = (bf16[8,3072]{1,0:T(8,128)(2,1)S(1)}, bf16[8,3072]{1,0:T(8,128)(2,1)S(1)}, u32[]{:S(2)}, u32[]{:S(2)}) collective-permute-start(bf16[8,3072]{1,0:T(8,128)(2,1)S(1)} %get-tuple-element.16), channel_id=1, source_target_pairs={{1,0},{2,1},{3,2},{4,3},{5,4},{6,5},{7,6},{8,7},{9,8},{10,9},{11,1... | collective-permute-start | bytes 147464 | tf_op jit(solution)/shard_map/ppermute | solution.py:21
  48.3 0.9 copy-start.11
  49.2 0.8 copy-start.14
  50.0 0.8 copy-start.15
  58.8 0.8 copy-start.3
  59.6 3.3 %copy-start.13 = (bf16[64,256]{1,0:T(8,128)(2,1)S(1)}, bf16[64,256]{1,0:T(8,128)(2,1)}, u32[]{:S(2)}) copy-start(bf16[64,256]{1,0:T(8,128)(2,1)} %constant.30.fourth_ref) | copy-start | bytes 98308
  59.6 3.4 %copy-start.4 = (bf16[1024,256]{1,0:T(8,128)(2,1)S(1)}, bf16[1024,256]{1,0:T(8,128)(2,1)}, u32[]{:S(2)}) copy-start(bf16[1024,256]{1,0:T(8,128)(2,1)} %copy-done.3) | copy-start | bytes 1572868
  59.6 31.8 %all-to-all-start.1 = ((bf16[32,136,128]{2,1,0:T(8,128)(2,1)}), bf16[32,136,128]{2,1,0:T(8,128)(2,1)S(1)}, u32[]{:S(2)}, u32[]{:S(2)}) async-start(bf16[32,136,128]{2,1,0:T(8,128)(2,1)} %get-tuple-element.22), calls=%async_computation.1 | async-start | bytes 2228224 | tf_op jit(solution)/shard_map/all_to_all | solution.py:740
  91.4 1.4 %copy-start.2 = (bf16[24,256,128]{2,1,0:T(8,128)(2,1)S(1)}, bf16[24,256,128]{2,1,0:T(8,128)(2,1)}, u32[]{:S(2)}) copy-start(bf16[24,256,128]{2,1,0:T(8,128)(2,1)} %copy-done.1) | copy-start | bytes 4718596

commit v8 on v7

--- a/solution.py
+++ b/solution.py
@@ -13,6 +13,7 @@
 PAIRS = CPG // 2
 EVERYONE = ("dp", "ctx")
 VMEM_LIMIT = 24 * 1024 * 1024
+VMEM_MOST = 62 * 1024 * 1024
 
 
 def shifted(value, axis, steps):
@@ -263,13 +264,13 @@
     return pl.ds(pl.multiple_of(i * LANES + offset, LANES), LANES)
 
 
-def whole_call(kernel, name, out_shape, operands, scratch=(), flops=10_000_000, **kwargs):
+def whole_call(kernel, name, out_shape, operands, scratch=(), flops=10_000_000, limit=VMEM_LIMIT, **kwargs):
     return pl.pallas_call(
         kernel,
         name=name,
         out_shape=out_shape,
         scratch_shapes=list(scratch),
-        compiler_params=pltpu.CompilerParams(vmem_limit_bytes=VMEM_LIMIT),
+        compiler_params=pltpu.CompilerParams(vmem_limit_bytes=limit),
         cost_estimate=pl.CostEstimate(flops=flops, bytes_accessed=4_000_000, transcendentals=0),
         **kwargs,
     )(*operands)
@@ -358,14 +359,10 @@
     near = LANES // owned
     blocks = width // LANES
 
-    def kernel(x_ref, rim_ref, w_ref, og_ref, f_hbm, msg_ref, edge_ref, tall, made, f_ref, edge, sent):
+    def kernel(x_ref, rim_ref, w_ref, og_ref, f_ref, msg_ref, edge_ref, tall, made, edge, sent):
         def copy(i):
             to = pl.ds(i * near, near)
             return pltpu.make_async_copy(made.at[to], msg_ref.at[to], sent.at[i])
-
-        def keep(i):
-            to = pl.ds(3 * i, 3)
-            return pltpu.make_async_copy(f_ref.at[to], f_hbm.at[to], sent.at[blocks + i])
 
         @pl.loop(0, blocks)
         def _(i):
@@ -391,15 +388,13 @@
             made[to, :owned, :] = kv.reshape(near, owned, local)
             made[to, owned:, :] = dconv.reshape(near, owned, local)
             copy(i).start()
-            keep(i).start()
-
-        last = pltpu.make_async_copy(edge, edge_ref, sent.at[2 * blocks])
+
+        last = pltpu.make_async_copy(edge, edge_ref, sent.at[blocks])
         last.start()
 
         @pl.loop(0, blocks)
         def _(i):
             copy(i).wait()
-            keep(i).wait()
 
         last.wait()
 
@@ -418,12 +413,11 @@
         [
             pltpu.VMEM((3, local + RIM, LANES), jnp.float32),
             pltpu.VMEM((devices, 2 * owned, local), jnp.bfloat16),
-            pltpu.VMEM((3 * blocks, local, LANES), jnp.bfloat16),
             pltpu.VMEM((RIM, 3 * width), jnp.bfloat16),
-            pltpu.SemaphoreType.DMA((2 * blocks + 1,)),
+            pltpu.SemaphoreType.DMA((blocks + 1,)),
         ],
         in_specs=[vmem] * 4,
-        out_specs=(hbm, hbm, hbm),
+        out_specs=(vmem, hbm, hbm),
     )
 
 
@@ -439,15 +433,27 @@
     height = sources * channels
     chunk = sources // 4
 
-    def kernel(x_ref, *refs):
+    def kernel(x_hbm, *refs):
         sources_hbm, (y_hbm, cross_hbm), held = refs[:7], refs[7:9], refs[9:16]
-        y_ref, cross_ref, talls, wides, stages, turns, sems, fetched = refs[16:]
+        y_ref, cross_ref, x_ref, talls, wides, stages, turns, sems, fetched = refs[16:]
+        arrivals = []
+        for s in range(2):
+            rows = slice(s * channels, (s + 1) * channels)
+            for half_sources in range(2):
+                to = slice(half_sources * sources // 2, (half_sources + 1) * sources // 2)
+                arrivals.append(
+                    pltpu.make_async_copy(x_hbm.at[to, rows, :], x_ref.at[to, rows, :], fetched.at[7 + len(arrivals)])
+                )
+        for arrival in arrivals[:2]:
+            arrival.start()
         first_ref, tr_ref, ti_ref, second_ref, f_ref, third_ref, fourth_ref = held
         fetches = [pltpu.make_async_copy(a, b, fetched.at[n]) for n, (a, b) in enumerate(zip(sources_hbm, held))]
-        for fetch in fetches:
+        for fetch in fetches[:3] + arrivals[2:] + fetches[3:]:
             fetch.start()
         for s in range(2):
             tall, wide, stage = talls.at[s], wides.at[s], stages.at[s]
+            arrivals[2 * s].wait()
+            arrivals[2 * s + 1].wait()
             for t in range(tiles):
                 block = x_ref[:, s * channels : (s + 1) * channels, t * LANES : (t + 1) * LANES]
                 tall[t * height : (t + 1) * height, :] = block.astype(jnp.float32).reshape(height, LANES)
@@ -544,7 +550,6 @@
             copy.wait()
 
     sent = (sources, 2 * tiles * channels + RIM, LANES)
-    vmem = pl.BlockSpec(memory_space=pltpu.VMEM)
     hbm = pl.BlockSpec(memory_space=pltpu.HBM)
     fetched = [tables[n] for n in ("first", "twist_re", "twist_im", "second")] + [filters]
     fetched += [tables[n] for n in ("third", "fourth_scaled")]
@@ -557,15 +562,17 @@
         + [
             pltpu.VMEM(sent, jnp.bfloat16),
             pltpu.VMEM((groups * outer, 2 * inner), jnp.bfloat16),
+            pltpu.VMEM(arrived.shape, jnp.bfloat16),
             pltpu.VMEM((2, tiles * height, LANES), jnp.float32),
             pltpu.VMEM((2, outer, pairs * inner), jnp.bfloat16),
             pltpu.VMEM((2, pairs * outer, 2 * inner), jnp.bfloat16),
             pltpu.VMEM((2, 2 * outer, pairs * inner), jnp.bfloat16),
             pltpu.SemaphoreType.DMA((5,)),
-            pltpu.SemaphoreType.DMA((7,)),
+            pltpu.SemaphoreType.DMA((11,)),
         ],
         flops=4_000_000_000,
-        in_specs=[vmem] + [hbm] * 7,
+        limit=VMEM_MOST,
+        in_specs=[hbm] * 8,
         out_specs=(hbm, hbm),
     )
 
@@ -576,14 +583,24 @@
     near = LANES // owned
     blocks = width // LANES
 
-    def kernel(f_hbm, edge_ref, back_ref, og_hbm, w_ref, mixed_ref, out_ref, tall, made, f_ref, og_ref, sent, fetched):
+    def kernel(f_hbm, edge_hbm, back_hbm, og_hbm, w_hbm, mixed_ref, out_ref,
+               tall, made, f_ref, edge_ref, back_ref, og_ref, w_ref, sent, fetched):
         def fetch(i):
             to = pl.ds(3 * i, 3)
             rows = lane_block(i)
+            held = pl.ds(i * near, near)
             return (
+                pltpu.make_async_copy(back_hbm.at[held], back_ref.at[held], fetched.at[2 * blocks + i]),
                 pltpu.make_async_copy(f_hbm.at[to], f_ref.at[to], fetched.at[i]),
                 pltpu.make_async_copy(og_hbm.at[rows, :], og_ref.at[rows, :], fetched.at[blocks + i]),
             )
+
+        small = [
+            pltpu.make_async_copy(edge_hbm, edge_ref, fetched.at[3 * blocks]),
+            pltpu.make_async_copy(w_hbm, w_ref, fetched.at[3 * blocks + 1]),
+        ]
+        for one in small:
+            one.start()
 
         @pl.loop(0, blocks)
         def _(i):
@@ -591,6 +608,8 @@
                 one.start()
 
         lane = lax.broadcasted_iota(jnp.int32, (RIM, LANES), 1)
+        for one in small:
+            one.wait()
 
         def copy(part, i):
             at = part * blocks + i
@@ -602,6 +621,8 @@
 
         @pl.loop(0, blocks)
         def _(i):
+            for one in fetch(i):
+                one.wait()
             held = pl.ds(i * near, near)
             sums = []
             for s in range(2):
@@ -618,8 +639,6 @@
                         piece = pltpu.roll(piece, turn_by, 1)
                     rim = jnp.where(lane >= n * owned, piece, rim) if n else piece
                 sums.append((here, rim))
-            for one in fetch(i):
-                one.wait()
             query = f_ref[3 * i].astype(jnp.float32)
             made[3 * blocks + i] = (query * sums[0][0]).astype(jnp.bfloat16).T
             copy(3, i).start()
@@ -646,7 +665,6 @@
             for part in range(4):
                 copy(part, i).wait()
 
-    vmem = pl.BlockSpec(memory_space=pltpu.VMEM)
     hbm = pl.BlockSpec(memory_space=pltpu.HBM)
     return whole_call(
         kernel,
@@ -657,11 +675,15 @@
             pltpu.VMEM((3, local + RIM, LANES), jnp.float32),
             pltpu.VMEM((4 * blocks, LANES, local), jnp.bfloat16),
             pltpu.VMEM((3 * blocks, local, LANES), jnp.bfloat16),
+            pltpu.VMEM(edges.shape, jnp.bfloat16),
+            pltpu.VMEM(returned.shape, jnp.bfloat16),
             pltpu.VMEM((width, local), jnp.bfloat16),
+            pltpu.VMEM(short_filter.shape, jnp.bfloat16),
             pltpu.SemaphoreType.DMA((4 * blocks,)),
-            pltpu.SemaphoreType.DMA((2 * blocks,)),
+            pltpu.SemaphoreType.DMA((3 * blocks + 2,)),
         ],
-        in_specs=[hbm, vmem, vmem, hbm, vmem],
+        limit=VMEM_MOST,
+        in_specs=[hbm] * 5,
         out_specs=(hbm, hbm),
     )
 

time: 102 us -> 95.3 us (0.934)
  Pallas kernels: 23.1 us -> 19.4 us
  local copies, waits for them, and re-layouts: 7.73 us -> 5.97 us
    pallas_call x3, Pallas kernels: 20.8 us -> 17.1 us  [whole_call(): pl.pallas_call(kernel, name=name, out_shape=out_shape, scratch_shapes=lis...]
    unnamed x33 -> x35, local copies, waits for them, and re-layouts: 7.73 us -> 5.97 us
where the time goes in v8:
time: 95.3 us; the launch traced here: 94.2 us
  waiting for transfers between devices  51 us (54%)
  Pallas kernels  19.4 us (20%)
  starting transfers between devices  16.9 us (18%)
  local copies, waits for them, and re-layouts  5.97 us (6%)
    all_to_all x1, waiting for transfers between devices, shards(): lax.all_to_all(answer, EVERYONE, split_axis=0, concat_axis=0, tiled=True)  27.1 us
    pallas_call x3, Pallas kernels, whole_call(): pl.pallas_call(kernel, name=name, out_shape=out_shape, scratch_shapes=lis...  17.1 us
    all_to_all x1, waiting for transfers between devices, shards(): lax.all_to_all(message, EVERYONE, split_axis=0, concat_axis=0, tiled=True)  14.3 us
    ppermute x2, waiting for transfers between devices, shifted(): lax.ppermute(value, axis, [(source, source + steps) for source in range(f...  9.62 us
    ppermute x2, starting transfers between devices, shifted(): lax.ppermute(value, axis, [(source, source + steps) for source in range(f...  6.76 us
    all_to_all x1, starting transfers between devices, shards(): lax.all_to_all(message, EVERYONE, split_axis=0, concat_axis=0, tiled=True)  6.75 us
    unnamed x35, local copies, waits for them, and re-layouts  5.97 us
    all_to_all x1, starting transfers between devices, shards(): lax.all_to_all(answer, EVERYONE, split_axis=0, concat_axis=0, tiled=True)  3.34 us
  transfers between devices with their start and end apart: 4, of which 4 were waited for; matrix products, arithmetic and copies ran while one was open for 0% of the time, Pallas kernels for 2%

profile of v8, /device:TPU:1, one launch (start us, length us, event | category | flops | bytes accessed | tf_op | source)
XLA Modules:
  0.0 94.2 jit_solution(13833835932169648754)
XLA Ops:
  0.6 0.0 copy-start
  0.6 0.0 copy-start.8
  0.7 1.8 %copy.15 = bf16[3072,256]{0,1:T(8,128)(2,1)S(1)} copy(bf16[3072,256]{1,0:T(8,128)(2,1)} %param.12) | data formatting | bytes 3145728 | tf_op args[0]
  2.4 4.6 %collective-permute-start = (bf16[8,3072]{1,0:T(8,128)(2,1)S(1)}, bf16[8,3072]{1,0:T(8,128)(2,1)S(1)}, u32[]{:S(2)}, u32[]{:S(2)}) collective-permute-start(bf16[8,3072]{1,0:T(8,128)(2,1)S(1)} %slice.4), channel_id=1, source_target_pairs={{0,1},{1,2},{2,3},{3,4},{4,5},{5,6},{6,7},{7,8},{8,9},{9,10},{10,1... | collective-permute-start | bytes 147464 | tf_op jit(solution)/shard_map/ppermute | solution.py:22
  7.0 1.2 %collective-permute-done.rim_ref = bf16[8,3072]{1,0:T(8,128)(2,1)S(1)} collective-permute-done((bf16[8,3072]{1,0:T(8,128)(2,1)S(1)}, bf16[8,3072]{1,0:T(8,128)(2,1)S(1)}, u32[]{:S(2)}, u32[]{:S(2)}) %collective-permute-start) | collective-permute-done | bytes 49184 | tf_op jit(solution)/shard_map/ppermute | solution.py:22
  8.2 0.0 copy-done
  8.2 0.0 copy-done.8
  8.2 3.3 %joined_features.1 = (bf16[24,256,128]{2,1,0:T(8,128)(2,1)S(1)}, bf16[32,64,256]{2,1,0:T(8,128)(2,1)}, bf16[8,3072]{1,0:T(8,128)(2,1)S(1)}) custom-call(bf16[256,3072]{1,0:T(8,128)(2,1)S(1)} %bitcast.2, bf16[8,3072]{1,0:T(8,128)(2,1)S(1)} %collective-permute-done.rim_ref, bf16[7,3072]{1,0:T(8,128)(2,1)S(1)} %copy-done.8, bf16[1024,256]{1,0:T(8,128)(2,1)S(1)} %copy-done), custom_call_target="tpu_custom_call" | custom-call | flops 10000000 | bytes 4000000 | tf_op jit(solution)/shard_map/joined_features/pallas_call | solution.py:268
  11.5 0.0 copy-start.1
  11.5 1.2 %copy-done.1 = bf16[24,256,128]{2,1,0:T(8,128)(2,1)} copy-done((bf16[24,256,128]{2,1,0:T(8,128)(2,1)}, bf16[24,256,128]{2,1,0:T(8,128)(2,1)S(1)}, u32[]{:S(2)}) %copy-start.1) | copy-done | bytes 1572888
  12.7 0.0 copy-start.4
  12.7 0.0 copy-start.6
  12.7 0.0 copy-start.9
  12.7 0.0 copy-start.11
  12.7 0.0 copy-start.12
  12.7 6.8 %all-to-all-start = ((bf16[32,64,256]{2,1,0:T(8,128)(2,1)}), bf16[32,64,256]{2,1,0:T(8,128)(2,1)S(1)}, u32[]{:S(2)}, u32[]{:S(2)}) async-start(bf16[32,64,256]{2,1,0:T(8,128)(2,1)} %get-tuple-element.17), calls=%async_computation | async-start | bytes 2097152 | tf_op jit(solution)/shard_map/all_to_all | solution.py:759
  19.5 2.2 %collective-permute-start.1 = (bf16[8,3072]{1,0:T(8,128)(2,1)S(1)}, bf16[8,3072]{1,0:T(8,128)(2,1)S(1)}, u32[]{:S(2)}, u32[]{:S(2)}) collective-permute-start(bf16[8,3072]{1,0:T(8,128)(2,1)S(1)} %get-tuple-element.16), channel_id=1, source_target_pairs={{1,0},{2,1},{3,2},{4,3},{5,4},{6,5},{7,6},{8,7},{9,8},{10,9},{11,1... | collective-permute-start | bytes 147464 | tf_op jit(solution)/shard_map/ppermute | solution.py:22
  21.6 0.0 copy-done.4
  21.7 0.0 copy-done.6
  21.7 0.0 copy-done.9
  21.7 0.0 copy-done.11
  21.7 0.0 copy-done.12
  21.7 1.1 %filter_dft.1.refs_4_ = f32[1024,256]{1,0:T(8,128)S(1)} custom-call(bf16[8,8192]{1,0:T(8,128)(2,1)S(1)} %copy-done.9, bf16[256,64]{1,0:T(8,128)(2,1)S(1)} %copy-done.12, bf16[256,256]{1,0:T(8,128)(2,1)S(1)} %copy-done.11, f32[128,128]{1,0:T(8,128)S(1)} %copy-done.6, f32[128,128]{1,0:T(8,128)S(1)} %copy-done.4), custom_call_target="tpu_custom_call" | custom-call | flops 200000000 | bytes 2000000 | tf_op jit(solution)/shard_map/filter_dft/pallas_call | solution.py:99
  22.8 0.0 copy-start.2
  22.8 1.0 %copy-done.2 = f32[1024,256]{1,0:T(8,128)} copy-done((f32[1024,256]{1,0:T(8,128)}, f32[1024,256]{1,0:T(8,128)S(1)}, u32[]{:S(2)}) %copy-start.2) | copy-done | bytes 1048600
  23.7 8.5 %collective-permute-done.1.edge_hbm = bf16[8,3072]{1,0:T(8,128)(2,1)S(1)} collective-permute-done((bf16[8,3072]{1,0:T(8,128)(2,1)S(1)}, bf16[8,3072]{1,0:T(8,128)(2,1)S(1)}, u32[]{:S(2)}, u32[]{:S(2)}) %collective-permute-start.1) | collective-permute-done | bytes 49184 | tf_op jit(solution)/shard_map/ppermute | solution.py:22
  32.2 0.0 copy-start.16
  32.2 14.3 %all-to-all-done.x_hbm = bf16[32,64,256]{2,1,0:T(8,128)(2,1)S(1)} async-done(((bf16[32,64,256]{2,1,0:T(8,128)(2,1)}), bf16[32,64,256]{2,1,0:T(8,128)(2,1)S(1)}, u32[]{:S(2)}, u32[]{:S(2)}) %all-to-all-start) | async-done | bytes 1048608 | tf_op jit(solution)/shard_map/all_to_all | solution.py:759
  46.5 0.0 copy-start.15
  46.5 1.0 %copy-done.15 = bf16[32,64,256]{2,1,0:T(8,128)(2,1)} copy-done((bf16[32,64,256]{2,1,0:T(8,128)(2,1)}, bf16[32,64,256]{2,1,0:T(8,128)(2,1)S(1)}, u32[]{:S(2)}) %copy-start.15) | copy-done | bytes 1048600
  47.5 8.3 %joined_filtering.1 = (bf16[32,136,128]{2,1,0:T(8,128)(2,1)}, bf16[1024,256]{1,0:T(8,128)(2,1)}) custom-call(bf16[32,64,256]{2,1,0:T(8,128)(2,1)} %copy-done.15, bf16[256,128]{1,0:T(8,128)(2,1)} %constant.27.refs_0_, f32[128,128]{1,0:T(8,128)} %constant.16.clone.tr_ref.refs_1_, f32[128,128]{1,0:T(8,128)} %constant.17.clone.ti_ref.refs_2_, ...), custom_call_target="tpu_custom_call" | custom-call | flops 4000000000 | bytes 4000000 | tf_op jit(solution)/shard_map/joined_filtering/pallas_call | solution.py:268
  55.8 0.0 copy-done.16
  55.8 0.0 copy-start.3
  55.8 0.0 copy-start.5
  55.8 0.0 copy-start.7
  55.8 0.0 copy-start.10
  55.8 0.0 copy-start.13
  55.8 3.3 %all-to-all-start.1 = ((bf16[32,136,128]{2,1,0:T(8,128)(2,1)}), bf16[32,136,128]{2,1,0:T(8,128)(2,1)S(1)}, u32[]{:S(2)}, u32[]{:S(2)}) async-start(bf16[32,136,128]{2,1,0:T(8,128)(2,1)} %get-tuple-element.22), calls=%async_computation.1 | async-start | bytes 2228224 | tf_op jit(solution)/shard_map/all_to_all | solution.py:762
  59.2 0.0 copy-done.3
  59.2 0.0 copy-done.5
  59.2 0.0 copy-done.7
  59.2 0.0 copy-done.10
  59.2 0.0 copy-done.13
  59.2 1.3 %filter_gradient.1 = f32[8,8192]{1,0:T(8,128)} custom-call(bf16[1024,256]{1,0:T(8,128)(2,1)S(1)} %copy-done.3, bf16[256,256]{1,0:T(8,128)(2,1)S(1)} %copy-done.10, bf16[64,256]{1,0:T(8,128)(2,1)S(1)} %copy-done.13, f32[128,128]{1,0:T(8,128)S(1)} %copy-done.7, f32[128,128]{1,0:T(8,128)S(1)} %copy-done.5), custom_call_target="tpu_custom_call" | custom-call | flops 200000000 | bytes 2000000 | tf_op jit(solution)/shard_map/filter_gradient/pallas_call | solution.py:232
  60.5 27.1 %all-to-all-done.1.back_hbm = bf16[32,136,128]{2,1,0:T(8,128)(2,1)S(1)} async-done(((bf16[32,136,128]{2,1,0:T(8,128)(2,1)}), bf16[32,136,128]{2,1,0:T(8,128)(2,1)S(1)}, u32[]{:S(2)}, u32[]{:S(2)}) %all-to-all-start.1) | async-done | bytes 1114144 | tf_op jit(solution)/shard_map/all_to_all | solution.py:762
  87.6 0.0 copy-start.14
  87.6 1.0 %copy-done.14 = bf16[32,136,128]{2,1,0:T(8,128)(2,1)} copy-done((bf16[32,136,128]{2,1,0:T(8,128)(2,1)}, bf16[32,136,128]{2,1,0:T(8,128)(2,1)S(1)}, u32[]{:S(2)}) %copy-start.14) | copy-done | bytes 1114136
  88.7 5.5 %joined_gradients.1 = (bf16[1024,256]{1,0:T(8,128)(2,1)}, bf16[3072,256]{1,0:T(8,128)(2,1)}) custom-call(bf16[24,256,128]{2,1,0:T(8,128)(2,1)} %copy-done.1, bf16[8,3072]{1,0:T(8,128)(2,1)} %copy-done.16, bf16[32,136,128]{2,1,0:T(8,128)(2,1)} %copy-done.14, bf16[1024,256]{1,0:T(8,128)(2,1)} %og_hbm.1, bf16[7,3072]{1,0:T(8,128)(2,1)} %w_hbm.1), custom_call_target="tpu_custom_call" | custom-call | flops 10000000 | bytes 4000000 | tf_op jit(solution)/shard_map/joined_gradients/pallas_call | solution.py:268
  (1 shorter events, 0.0 us)
Async XLA Ops:
  0.6 7.6 %copy-start = (bf16[1024,256]{1,0:T(8,128)(2,1)S(1)}, bf16[1024,256]{1,0:T(8,128)(2,1)}, u32[]{:S(2)}) copy-start(bf16[1024,256]{1,0:T(8,128)(2,1)} %og_hbm.1) | copy-start | bytes 1572868
  0.6 7.6 %copy-start.8 = (bf16[7,3072]{1,0:T(8,128)(2,1)S(1)}, bf16[7,3072]{1,0:T(8,128)(2,1)}, u32[]{:S(2)}) copy-start(bf16[7,3072]{1,0:T(8,128)(2,1)} %w_hbm.1) | copy-start | bytes 129028
  2.4 5.8 %collective-permute-start = (bf16[8,3072]{1,0:T(8,128)(2,1)S(1)}, bf16[8,3072]{1,0:T(8,128)(2,1)S(1)}, u32[]{:S(2)}, u32[]{:S(2)}) collective-permute-start(bf16[8,3072]{1,0:T(8,128)(2,1)S(1)} %slice.4), channel_id=1, source_target_pairs={{0,1},{1,2},{2,3},{3,4},{4,5},{5,6},{6,7},{7,8},{8,9},{9,10},{10,1... | collective-permute-start | bytes 147464 | tf_op jit(solution)/shard_map/ppermute | solution.py:22
  11.5 1.2 %copy-start.1 = (bf16[24,256,128]{2,1,0:T(8,128)(2,1)}, bf16[24,256,128]{2,1,0:T(8,128)(2,1)S(1)}, u32[]{:S(2)}) copy-start(bf16[24,256,128]{2,1,0:T(8,128)(2,1)S(1)} %get-tuple-element.15.f_hbm) | copy-start | bytes 4718596
  12.7 9.0 %copy-start.4 = (f32[128,128]{1,0:T(8,128)S(1)}, f32[128,128]{1,0:T(8,128)}, u32[]{:S(2)}) copy-start(f32[128,128]{1,0:T(8,128)} %constant.17.clone.ti_ref.refs_2_) | copy-start | bytes 196612
  12.7 9.0 %copy-start.6 = (f32[128,128]{1,0:T(8,128)S(1)}, f32[128,128]{1,0:T(8,128)}, u32[]{:S(2)}) copy-start(f32[128,128]{1,0:T(8,128)} %constant.16.clone.tr_ref.refs_1_) | copy-start | bytes 196612
  12.7 9.0 %copy-start.9 = (bf16[8,8192]{1,0:T(8,128)(2,1)S(1)}, bf16[8,8192]{1,0:T(8,128)(2,1)}, u32[]{:S(2)}) copy-start(bf16[8,8192]{1,0:T(8,128)(2,1)} %x_ref.1) | copy-start | bytes 393220
  12.7 9.0 %copy-start.11 = (bf16[256,256]{1,0:T(8,128)(2,1)S(1)}, bf16[256,256]{1,0:T(8,128)(2,1)}, u32[]{:S(2)}) copy-start(bf16[256,256]{1,0:T(8,128)(2,1)} %constant.26.second_ref.refs_3_) | copy-start | bytes 393220
  12.7 9.0 %copy-start.12 = (bf16[256,64]{1,0:T(8,128)(2,1)S(1)}, bf16[256,64]{1,0:T(8,128)(2,1)}, u32[]{:S(2)}) copy-start(bf16[256,64]{1,0:T(8,128)(2,1)} %constant.25.first_ref) | copy-start | bytes 98308
  12.7 33.8 %all-to-all-start = ((bf16[32,64,256]{2,1,0:T(8,128)(2,1)}), bf16[32,64,256]{2,1,0:T(8,128)(2,1)S(1)}, u32[]{:S(2)}, u32[]{:S(2)}) async-start(bf16[32,64,256]{2,1,0:T(8,128)(2,1)} %get-tuple-element.17), calls=%async_computation | async-start | bytes 2097152 | tf_op jit(solution)/shard_map/all_to_all | solution.py:759
  19.5 12.7 %collective-permute-start.1 = (bf16[8,3072]{1,0:T(8,128)(2,1)S(1)}, bf16[8,3072]{1,0:T(8,128)(2,1)S(1)}, u32[]{:S(2)}, u32[]{:S(2)}) collective-permute-start(bf16[8,3072]{1,0:T(8,128)(2,1)S(1)} %get-tuple-element.16), channel_id=1, source_target_pairs={{1,0},{2,1},{3,2},{4,3},{5,4},{6,5},{7,6},{8,7},{9,8},{10,9},{11,1... | collective-permute-start | bytes 147464 | tf_op jit(solution)/shard_map/ppermute | solution.py:22
  22.8 1.0 %copy-start.2 = (f32[1024,256]{1,0:T(8,128)}, f32[1024,256]{1,0:T(8,128)S(1)}, u32[]{:S(2)}) copy-start(f32[1024,256]{1,0:T(8,128)S(1)} %filter_dft.1.refs_4_) | copy-start | bytes 3145732
  32.2 23.6 %copy-start.16 = (bf16[8,3072]{1,0:T(8,128)(2,1)}, bf16[8,3072]{1,0:T(8,128)(2,1)S(1)}, u32[]{:S(2)}) copy-start(bf16[8,3072]{1,0:T(8,128)(2,1)S(1)} %collective-permute-done.1.edge_hbm) | copy-start | bytes 147460
  46.5 1.0 %copy-start.15 = (bf16[32,64,256]{2,1,0:T(8,128)(2,1)}, bf16[32,64,256]{2,1,0:T(8,128)(2,1)S(1)}, u32[]{:S(2)}) copy-start(bf16[32,64,256]{2,1,0:T(8,128)(2,1)S(1)} %all-to-all-done.x_hbm) | copy-start | bytes 3145732
  55.8 3.4 %copy-start.3 = (bf16[1024,256]{1,0:T(8,128)(2,1)S(1)}, bf16[1024,256]{1,0:T(8,128)(2,1)}, u32[]{:S(2)}) copy-start(bf16[1024,256]{1,0:T(8,128)(2,1)} %get-tuple-element.21.s_ref) | copy-start | bytes 1572868
  55.8 3.4 %copy-start.5 = (f32[128,128]{1,0:T(8,128)S(1)}, f32[128,128]{1,0:T(8,128)}, u32[]{:S(2)}) copy-start(f32[128,128]{1,0:T(8,128)} %constant.17.clone.ti_ref.refs_2_) | copy-start | bytes 196612
  55.8 3.4 %copy-start.7 = (f32[128,128]{1,0:T(8,128)S(1)}, f32[128,128]{1,0:T(8,128)}, u32[]{:S(2)}) copy-start(f32[128,128]{1,0:T(8,128)} %constant.16.clone.tr_ref.refs_1_) | copy-start | bytes 196612
  55.8 3.4 %copy-start.10 = (bf16[256,256]{1,0:T(8,128)(2,1)S(1)}, bf16[256,256]{1,0:T(8,128)(2,1)}, u32[]{:S(2)}) copy-start(bf16[256,256]{1,0:T(8,128)(2,1)} %constant.28.refs_5_.third_ref) | copy-start | bytes 393220
  55.8 3.4 %copy-start.13 = (bf16[64,256]{1,0:T(8,128)(2,1)S(1)}, bf16[64,256]{1,0:T(8,128)(2,1)}, u32[]{:S(2)}) copy-start(bf16[64,256]{1,0:T(8,128)(2,1)} %constant.30.fourth_ref) | copy-start | bytes 98308
  55.8 31.8 %all-to-all-start.1 = ((bf16[32,136,128]{2,1,0:T(8,128)(2,1)}), bf16[32,136,128]{2,1,0:T(8,128)(2,1)S(1)}, u32[]{:S(2)}, u32[]{:S(2)}) async-start(bf16[32,136,128]{2,1,0:T(8,128)(2,1)} %get-tuple-element.22), calls=%async_computation.1 | async-start | bytes 2228224 | tf_op jit(solution)/shard_map/all_to_all | solution.py:762
  87.6 1.0 %copy-start.14 = (bf16[32,136,128]{2,1,0:T(8,128)(2,1)}, bf16[32,136,128]{2,1,0:T(8,128)(2,1)S(1)}, u32[]{:S(2)}) copy-start(bf16[32,136,128]{2,1,0:T(8,128)(2,1)S(1)} %all-to-all-done.1.back_hbm) | copy-start | bytes 3342340

commit v9 on v6

--- a/solution.py
+++ b/solution.py
@@ -48,6 +48,19 @@
         "second": narrow([[cos_i, -sin_i], [sin_i, cos_i]]),
         "third": narrow([[cos_i, sin_i], [-sin_i, cos_i]]),
         "fourth": narrow([[cos_p.T, -sin_p.T], [sin_p.T, cos_p.T]]),
+        "joined": narrow(
+            [
+                [cos_i, -sin_i],
+                [sin_i, cos_i],
+                [cos_i, sin_i],
+                [-sin_i, cos_i],
+                [cos_p.T / padded, -sin_p.T / padded],
+                [sin_p.T / padded, cos_p.T / padded],
+                [np.hstack([cos_p, sin_p]), np.hstack([-sin_p, cos_p])],
+            ]
+        )
+        if inner == outer
+        else None,
         "first_real": narrow([[cos_o], [-sin_o]]),
         "fourth_real": narrow([[cos_o.T, -sin_o.T]]),
         "twist_re": twist[0],
@@ -357,10 +370,15 @@
     near = LANES // owned
     blocks = width // LANES
 
-    def kernel(x_ref, rim_ref, w_ref, og_ref, f_ref, msg_ref, edge_ref, tall, made, edge, sent):
+    def kernel(x_ref, rim_ref, w_ref, og_ref, f_hbm, msg_ref, edge_ref, tall, made, f_ref, edge, sent):
         def copy(i):
             to = pl.ds(i * near, near)
             return pltpu.make_async_copy(made.at[to], msg_ref.at[to], sent.at[i])
+
+        def keep(part, i):
+            at = part * blocks + i
+            to = pl.ds(pl.multiple_of(at * LANES, LANES), LANES)
+            return pltpu.make_async_copy(f_ref.at[at], f_hbm.at[to, :], sent.at[blocks + at])
 
         @pl.loop(0, blocks)
         def _(i):
@@ -374,7 +392,9 @@
                     w_ref[:, lanes].astype(jnp.float32),
                     True,
                 ).astype(jnp.bfloat16)
-                f_ref[:, lanes] = total
+                for t in range(local // LANES):
+                    f_ref[part * blocks + i, :, t * LANES : (t + 1) * LANES] = total[t * LANES : (t + 1) * LANES]
+                keep(part, i).start()
                 if part:
                     edge[:, lanes] = total[:RIM]
                 parts.append(total.astype(jnp.float32))
@@ -387,12 +407,14 @@
             made[to, owned:, :] = dconv.reshape(near, owned, local)
             copy(i).start()
 
-        last = pltpu.make_async_copy(edge, edge_ref, sent.at[blocks])
+        last = pltpu.make_async_copy(edge, edge_ref, sent.at[4 * blocks])
         last.start()
 
         @pl.loop(0, blocks)
         def _(i):
             copy(i).wait()
+            for part in range(3):
+                keep(part, i).wait()
 
         last.wait()
 
@@ -402,16 +424,17 @@
     return whole_call(
         kernel,
         "joined_features",
-        (narrow_shape(local, 3 * width), narrow_shape(devices, 2 * owned, local), narrow_shape(RIM, 3 * width)),
+        (narrow_shape(3 * width, local), narrow_shape(devices, 2 * owned, local), narrow_shape(RIM, 3 * width)),
         (turned, rim, short_filter, out_grad),
         [
             pltpu.VMEM((3, local + RIM, LANES), jnp.float32),
             pltpu.VMEM((devices, 2 * owned, local), jnp.bfloat16),
+            pltpu.VMEM((3 * blocks, LANES, local), jnp.bfloat16),
             pltpu.VMEM((RIM, 3 * width), jnp.bfloat16),
-            pltpu.SemaphoreType.DMA((blocks + 1,)),
+            pltpu.SemaphoreType.DMA((4 * blocks + 1,)),
         ],
         in_specs=[vmem] * 4,
-        out_specs=(vmem, hbm, hbm),
+        out_specs=(hbm, hbm, hbm),
     )
 
 
@@ -427,10 +450,11 @@
     height = sources * channels
     chunk = sources // 4
 
-    def kernel(x_ref, f_hbm, first_ref, second_ref, third_ref, fourth_ref, tr_ref, ti_ref,
-               y_hbm, cross_ref, f_ref, y_ref, talls, wides, stages, turns, sems):
-        fetch = pltpu.make_async_copy(f_hbm, f_ref, sems.at[0])
-        fetch.start()
+    def kernel(x_ref, f_ref, table_ref, tr_ref, ti_ref, y_hbm, cross_hbm, y_ref, cross_ref, talls, wides, stages, turns, sems):
+        second_ref, third_ref = table_ref.at[: 2 * inner], table_ref.at[2 * inner : 4 * inner]
+        fourth_ref = table_ref.at[4 * inner : 4 * inner + 2 * half]
+        firsts = table_ref[4 * inner + 2 * half :, :]
+        first = jnp.concatenate([firsts[:, : 2 * half], firsts[:, 2 * half :]], axis=0)
         tr, ti = tr_ref[...], ti_ref[...]
         for s in range(2):
             tall, wide, stage = talls.at[s], wides.at[s], stages.at[s]
@@ -445,14 +469,13 @@
                     wide[at : at + sources, pair * inner : (pair + 1) * inner] = line.astype(jnp.bfloat16)
             for g in range(groups):
                 span = PAIRS * inner
-                f = dot(first_ref[...], wide[:, g * span : (g + 1) * span])
+                f = dot(first, wide[:, g * span : (g + 1) * span])
                 for p in range(PAIRS):
                     f_re = f[:outer, p * inner : (p + 1) * inner]
                     f_im = f[outer:, p * inner : (p + 1) * inner]
                     at = (g * PAIRS + p) * outer
                     stage[at : at + outer, :inner] = (f_re * tr + f_im * ti).astype(jnp.bfloat16)
                     stage[at : at + outer, inner:] = (f_im * tr - f_re * ti).astype(jnp.bfloat16)
-        fetch.wait()
         for g in range(groups):
             s_re = f_ref[g * outer : (g + 1) * outer, :inner]
             s_im = f_ref[g * outer : (g + 1) * outer, inner:]
@@ -471,6 +494,8 @@
                 stages[1, at : at + outer, inner:] = (s_re * d_im - s_im * d_re).astype(jnp.bfloat16)
             cross_ref[g * outer : (g + 1) * outer, :inner] = cross_re.astype(jnp.bfloat16)
             cross_ref[g * outer : (g + 1) * outer, inner:] = cross_im.astype(jnp.bfloat16)
+        copies = [pltpu.make_async_copy(cross_ref, cross_hbm, sems.at[4])]
+        copies[0].start()
         spot = lax.broadcasted_iota(jnp.int32, (RIM, LANES), 0)
         lane = lax.broadcasted_iota(jnp.int32, (RIM, LANES), 1)
         pick = jnp.where(spot == lane, 1.0, 0.0).astype(jnp.bfloat16)
@@ -486,7 +511,7 @@
                 turn[outer:, lanes] = (h_im * tr + h_re * ti).astype(jnp.bfloat16)
             for g in range(groups):
                 span = PAIRS * inner
-                y = dot(fourth_ref[...], turn[:, g * span : (g + 1) * span]) * (1.0 / padded)
+                y = dot(fourth_ref[...], turn[:, g * span : (g + 1) * span])
                 for p in range(PAIRS):
                     for part in range(2):
                         c = (g * PAIRS + p) * 2 + part
@@ -494,11 +519,10 @@
                             at = part * half + h * sources
                             line = y[at : at + sources, p * inner : (p + 1) * inner]
                             put_spread(tall, line, channels, c, height, (h * inner, (h + 1) * inner))
-            first = tall[:height, :].astype(jnp.bfloat16)
+            front = tall[:height, :].astype(jnp.bfloat16)
             rims.append(
-                lax.dot_general(pick, first, (((1,), (1,)), ((), ())), preferred_element_type=jnp.float32)
+                lax.dot_general(pick, front, (((1,), (1,)), ((), ())), preferred_element_type=jnp.float32)
             )
-        copies = []
         for q in range(4):
             to = slice(q * chunk, (q + 1) * chunk)
             for s in range(2):
@@ -518,7 +542,7 @@
                             piece = pltpu.roll(piece, turn_by, 1)
                         edge = piece if s == 0 else jnp.where(lane < channels, edge, piece)
                 y_ref[d, 2 * tiles * channels :, :] = edge.astype(jnp.bfloat16)
-            copies.append(pltpu.make_async_copy(y_ref.at[to], y_hbm.at[to], sems.at[1 + q]))
+            copies.append(pltpu.make_async_copy(y_ref.at[to], y_hbm.at[to], sems.at[q]))
             copies[-1].start()
         for copy in copies:
             copy.wait()
@@ -526,15 +550,14 @@
     sent = (sources, 2 * tiles * channels + RIM, LANES)
     vmem = pl.BlockSpec(memory_space=pltpu.VMEM)
     hbm = pl.BlockSpec(memory_space=pltpu.HBM)
-    names = ("first", "second", "third", "fourth", "twist_re", "twist_im")
     return whole_call(
         kernel,
         "joined_filtering",
         (narrow_shape(*sent), narrow_shape(groups * outer, 2 * inner)),
-        [arrived, filters] + [tables[n] for n in names],
+        [arrived, filters] + [tables[n] for n in ("joined", "twist_re", "twist_im")],
         [
-            pltpu.VMEM((groups * outer, 2 * inner), jnp.float32),
             pltpu.VMEM(sent, jnp.bfloat16),
+            pltpu.VMEM((groups * outer, 2 * inner), jnp.bfloat16),
             pltpu.VMEM((2, tiles * height, LANES), jnp.float32),
             pltpu.VMEM((2, outer, pairs * inner), jnp.bfloat16),
             pltpu.VMEM((2, pairs * outer, 2 * inner), jnp.bfloat16),
@@ -542,18 +565,33 @@
             pltpu.SemaphoreType.DMA((5,)),
         ],
         flops=4_000_000_000,
-        in_specs=[vmem, hbm] + [vmem] * 6,
-        out_specs=(hbm, vmem),
+        in_specs=[vmem] * 5,
+        out_specs=(hbm, hbm),
     )
 
 
-def joined_gradients(feats, edges, returned, out_grad, short_filter, owned):
+def joined_gradients(cross, feats, edges, returned, out_grad, short_filter, owned):
     width, local = out_grad.shape
     tiles = local // LANES
     near = LANES // owned
     blocks = width // LANES
 
-    def kernel(f_ref, edge_ref, back_ref, og_ref, w_ref, mixed_ref, out_ref, tall, made, sent):
+    def kernel(_, f_hbm, edge_ref, back_ref, og_ref, w_ref, mixed_ref, out_ref, tall, made, f_ref, sent, fetched):
+        def fetch(part, i):
+            at = part * blocks + i
+            rows = pl.ds(pl.multiple_of(at * LANES, LANES), LANES)
+            return pltpu.make_async_copy(f_hbm.at[rows, :], f_ref.at[at], fetched.at[at])
+
+        @pl.loop(0, blocks)
+        def _(i):
+            for part in range(3):
+                fetch(part, i).start()
+
+        def features(part, i):
+            fetch(part, i).wait()
+            held = [f_ref[part * blocks + i, :, t * LANES : (t + 1) * LANES] for t in range(tiles)]
+            return jnp.concatenate(held, axis=0).astype(jnp.float32)
+
         lane = lax.broadcasted_iota(jnp.int32, (RIM, LANES), 1)
 
         def copy(part, i):
@@ -582,17 +620,14 @@
                         piece = pltpu.roll(piece, turn_by, 1)
                     rim = jnp.where(lane >= n * owned, piece, rim) if n else piece
                 sums.append((here, rim))
-            query = f_ref[:, lane_block(i)].astype(jnp.float32)
+            query, key, value = [features(part, i) for part in range(3)]
             made[3 * blocks + i] = (query * sums[0][0]).astype(jnp.bfloat16).T
             copy(3, i).start()
             for part in range(3):
                 here, rim = sums[min(part, 1)]
-                if part == 0:
-                    other = og_ref[lane_block(i), :].T
-                else:
-                    other = f_ref[:, lane_block(i, (3 - part) * width)]
+                other = (og_ref[lane_block(i), :].T.astype(jnp.float32), value, key)[part]
                 edge = edge_ref[:, lane_block(i, (3 - part) % 3 * width)].astype(jnp.float32)
-                grad = (here * other.astype(jnp.float32)).astype(jnp.bfloat16)
+                grad = (here * other).astype(jnp.bfloat16)
                 total = seven_taps(
                     tall.at[part],
                     grad.astype(jnp.float32),
@@ -614,14 +649,17 @@
         kernel,
         "joined_gradients",
         (narrow_shape(width, local), narrow_shape(3 * width, local)),
-        (feats, edges, returned, out_grad, short_filter),
+        (cross, feats, edges, returned, out_grad, short_filter),
         [
             pltpu.VMEM((3, local + RIM, LANES), jnp.float32),
             pltpu.VMEM((4 * blocks, LANES, local), jnp.bfloat16),
+            pltpu.VMEM((3 * blocks, LANES, local), jnp.bfloat16),
             pltpu.SemaphoreType.DMA((4 * blocks,)),
+            pltpu.SemaphoreType.DMA((3 * blocks,)),
         ],
-        in_specs=[vmem] * 5,
+        in_specs=[hbm, hbm] + [vmem] * 4,
         out_specs=(hbm, hbm),
+        input_output_aliases={0: 0, 1: 1},
     )
 
 
@@ -690,7 +728,9 @@
     turned = projections.T
     rim = shifted(turned[local_len - RIM :], EVERYONE, 1)
 
-    if owned % 16 == 0 and LANES % (2 * owned) == 0 and devices % 4 == 0:
+    _, inner, outer = sizes_of(seq_len)
+    twin = owned // CPG * outer == width and 2 * inner == local_len and inner == outer
+    if owned % 16 == 0 and LANES % (2 * owned) == 0 and devices % 4 == 0 and twin:
         feats, message, edges = joined_features(turned, rim, short_filter, out_grad, owned)
         filters = transform_filters(long_filter, tables, seq_len)
         arrived = lax.all_to_all(message, EVERYONE, split_axis=0, concat_axis=0, tiled=True)
@@ -698,8 +738,8 @@
         answer, cross = joined_filtering(arrived, filters, tables, seq_len)
         returned = lax.all_to_all(answer, EVERYONE, split_axis=0, concat_axis=0, tiled=True)
         filter_grad = filter_gradient(cross, tables, seq_len)
-        filter_grad, returned = lax.optimization_barrier((filter_grad, returned))
-        mixed, grad = joined_gradients(feats, edges, returned, out_grad, short_filter, owned)
+        filter_grad, returned, cross = lax.optimization_barrier((filter_grad, returned, cross))
+        mixed, grad = joined_gradients(cross, feats, edges, returned, out_grad, short_filter, owned)
         return (mixed, grad, filter_grad)
 
     cotangent = out_grad.T

time: 96 us -> 92.3 us (0.961)
  local copies, waits for them, and re-layouts: 7.73 us -> 2.83 us
  Pallas kernels: 17.4 us -> 18.6 us
    unnamed x33 -> x23, local copies, waits for them, and re-layouts: 7.73 us -> 2.83 us
    pallas_call x3, Pallas kernels: 15 us -> 16.2 us  [whole_call(): pl.pallas_call(kernel, name=name, out_shape=out_shape, scratch_shapes=lis...]
  transfers between devices with their start and end apart: 4 -> 4, of which waited for: 4 -> 4; matrix products, arithmetic and copies ran while one was open for 0% -> 0% of each run, Pallas kernels for 2% -> 3%
where the time goes in v9:
time: 92.3 us; the launch traced here: 91.1 us
  waiting for transfers between devices  52 us (56%)
  Pallas kernels  18.6 us (20%)
  starting transfers between devices  16.9 us (18%)
  local copies, waits for them, and re-layouts  2.83 us (3%)
    all_to_all x1, waiting for transfers between devices, shards(): lax.all_to_all(answer, EVERYONE, split_axis=0, concat_axis=0, tiled=True)  27.1 us
    pallas_call x3, Pallas kernels, whole_call(): pl.pallas_call(kernel, name=name, out_shape=out_shape, scratch_shapes=lis...  16.2 us
    all_to_all x1, waiting for transfers between devices, shards(): lax.all_to_all(message, EVERYONE, split_axis=0, concat_axis=0, tiled=True)  14.3 us
    ppermute x2, waiting for transfers between devices, shifted(): lax.ppermute(value, axis, [(source, source + steps) for source in range(f...  10.6 us
    ppermute x2, starting transfers between devices, shifted(): lax.ppermute(value, axis, [(source, source + steps) for source in range(f...  6.76 us
    all_to_all x1, starting transfers between devices, shards(): lax.all_to_all(message, EVERYONE, split_axis=0, concat_axis=0, tiled=True)  6.75 us
    all_to_all x1, starting transfers between devices, shards(): lax.all_to_all(answer, EVERYONE, split_axis=0, concat_axis=0, tiled=True)  3.34 us
    unnamed x23, local copies, waits for them, and re-layouts  2.83 us
  transfers between devices with their start and end apart: 4, of which 4 were waited for; matrix products, arithmetic and copies ran while one was open for 0% of the time, Pallas kernels for 3%

profile of v9, /device:TPU:1, one launch (start us, length us, event | category | flops | bytes accessed | tf_op | source)
XLA Modules:
  0.0 91.1 jit_solution(1718853542572764329)
XLA Ops:
  0.6 0.0 copy-start.1
  0.6 0.0 copy-start.4
  0.7 1.8 %copy.16 = bf16[3072,256]{0,1:T(8,128)(2,1)S(1)} copy(bf16[3072,256]{1,0:T(8,128)(2,1)} %param.11) | data formatting | bytes 3145728 | tf_op args[0]
  2.4 4.6 %collective-permute-start = (bf16[8,3072]{1,0:T(8,128)(2,1)S(1)}, bf16[8,3072]{1,0:T(8,128)(2,1)S(1)}, u32[]{:S(2)}, u32[]{:S(2)}) collective-permute-start(bf16[8,3072]{1,0:T(8,128)(2,1)S(1)} %slice.4), channel_id=1, source_target_pairs={{0,1},{1,2},{2,3},{3,4},{4,5},{5,6},{6,7},{7,8},{8,9},{9,10},{10,1... | collective-permute-start | bytes 147464 | tf_op jit(solution)/shard_map/ppermute | solution.py:21
  7.0 1.2 %collective-permute-done.rim_ref = bf16[8,3072]{1,0:T(8,128)(2,1)S(1)} collective-permute-done((bf16[8,3072]{1,0:T(8,128)(2,1)S(1)}, bf16[8,3072]{1,0:T(8,128)(2,1)S(1)}, u32[]{:S(2)}, u32[]{:S(2)}) %collective-permute-start) | collective-permute-done | bytes 49184 | tf_op jit(solution)/shard_map/ppermute | solution.py:21
  8.2 0.0 copy-done.1
  8.2 0.0 copy-done.4
  8.2 3.6 %joined_features.1 = (bf16[3072,256]{1,0:T(8,128)(2,1)}, bf16[32,64,256]{2,1,0:T(8,128)(2,1)}, bf16[8,3072]{1,0:T(8,128)(2,1)S(1)}) custom-call(bf16[256,3072]{1,0:T(8,128)(2,1)S(1)} %bitcast.2, bf16[8,3072]{1,0:T(8,128)(2,1)S(1)} %collective-permute-done.rim_ref, bf16[7,3072]{1,0:T(8,128)(2,1)S(1)} %copy-done.4, bf16[1024,256]{1,0:T(8,128)(2,1)S(1)} %copy-done.1), custom_call_target="tpu_custom_call" | custom-call | flops 10000000 | bytes 4000000 | tf_op jit(solution)/shard_map/joined_features/pallas_call | solution.py:279
  11.9 0.0 copy-start.2
  11.9 0.0 copy-start.3
  11.9 0.0 copy-start.5
  11.9 0.0 copy-start.7
  11.9 0.0 copy-start.8
  11.9 6.8 %all-to-all-start = ((bf16[32,64,256]{2,1,0:T(8,128)(2,1)}), bf16[32,64,256]{2,1,0:T(8,128)(2,1)S(1)}, u32[]{:S(2)}, u32[]{:S(2)}) async-start(bf16[32,64,256]{2,1,0:T(8,128)(2,1)} %get-tuple-element.17), calls=%async_computation | async-start | bytes 2097152 | tf_op jit(solution)/shard_map/all_to_all | solution.py:736
  18.7 2.2 %collective-permute-start.1 = (bf16[8,3072]{1,0:T(8,128)(2,1)S(1)}, bf16[8,3072]{1,0:T(8,128)(2,1)S(1)}, u32[]{:S(2)}, u32[]{:S(2)}) collective-permute-start(bf16[8,3072]{1,0:T(8,128)(2,1)S(1)} %get-tuple-element.16), channel_id=1, source_target_pairs={{1,0},{2,1},{3,2},{4,3},{5,4},{6,5},{7,6},{8,7},{9,8},{10,9},{11,1... | collective-permute-start | bytes 147464 | tf_op jit(solution)/shard_map/ppermute | solution.py:21
  20.9 0.0 copy-done.2
  20.9 0.0 copy-done.3
  20.9 0.0 copy-done.5
  20.9 0.0 copy-done.7
  20.9 0.0 copy-done.8
  20.9 1.1 %filter_dft.1.f_ref = f32[1024,256]{1,0:T(8,128)S(1)} custom-call(bf16[8,8192]{1,0:T(8,128)(2,1)S(1)} %copy-done.5, bf16[256,64]{1,0:T(8,128)(2,1)S(1)} %copy-done.8, bf16[256,256]{1,0:T(8,128)(2,1)S(1)} %copy-done.7, f32[128,128]{1,0:T(8,128)S(1)} %copy-done.3, f32[128,128]{1,0:T(8,128)S(1)} %copy-done.2), custom_call_target="tpu_custom_call" | custom-call | flops 200000000 | bytes 2000000 | tf_op jit(solution)/shard_map/filter_dft/pallas_call | solution.py:110
  22.0 9.4 %collective-permute-done.1.edge_ref = bf16[8,3072]{1,0:T(8,128)(2,1)S(1)} collective-permute-done((bf16[8,3072]{1,0:T(8,128)(2,1)S(1)}, bf16[8,3072]{1,0:T(8,128)(2,1)S(1)}, u32[]{:S(2)}, u32[]{:S(2)}) %collective-permute-start.1) | collective-permute-done | bytes 49184 | tf_op jit(solution)/shard_map/ppermute | solution.py:21
  31.4 14.3 %all-to-all-done.x_ref = bf16[32,64,256]{2,1,0:T(8,128)(2,1)S(1)} async-done(((bf16[32,64,256]{2,1,0:T(8,128)(2,1)}), bf16[32,64,256]{2,1,0:T(8,128)(2,1)S(1)}, u32[]{:S(2)}, u32[]{:S(2)}) %all-to-all-start) | async-done | bytes 1048608 | tf_op jit(solution)/shard_map/all_to_all | solution.py:736
  45.7 0.0 copy-start.10
  45.7 1.0 %copy-done.10 = bf16[768,256]{1,0:T(8,128)(2,1)S(1)} copy-done((bf16[768,256]{1,0:T(8,128)(2,1)S(1)}, bf16[768,256]{1,0:T(8,128)(2,1)}, u32[]{:S(2)}) %copy-start.10) | copy-done | bytes 393240
  46.7 6.8 %joined_filtering.1 = (bf16[32,136,128]{2,1,0:T(8,128)(2,1)}, bf16[1024,256]{1,0:T(8,128)(2,1)}) custom-call(bf16[32,64,256]{2,1,0:T(8,128)(2,1)S(1)} %all-to-all-done.x_ref, f32[1024,256]{1,0:T(8,128)S(1)} %filter_dft.1.f_ref, bf16[768,256]{1,0:T(8,128)(2,1)S(1)} %copy-done.10, f32[128,128]{1,0:T(8,128)S(1)} %copy-done.3, f32[128,128]{1,0:T(8,128)S(1)} %copy-done.2), custom_call_target="tpu_custom_call" | custom-call | flops 4000000000 | bytes 4000000 | tf_op jit(solution)/shard_map/joined_filtering/pallas_call | solution.py:279
  53.5 0.0 copy-start
  53.5 0.0 copy-start.6
  53.5 0.0 copy-start.9
  53.6 3.3 %all-to-all-start.1 = ((bf16[32,136,128]{2,1,0:T(8,128)(2,1)}), bf16[32,136,128]{2,1,0:T(8,128)(2,1)S(1)}, u32[]{:S(2)}, u32[]{:S(2)}) async-start(bf16[32,136,128]{2,1,0:T(8,128)(2,1)} %get-tuple-element.21), calls=%async_computation.1 | async-start | bytes 2228224 | tf_op jit(solution)/shard_map/all_to_all | solution.py:739
  56.9 0.0 copy-done
  56.9 0.0 copy-done.6
  56.9 0.0 copy-done.9
  56.9 1.3 %filter_gradient.1 = f32[8,8192]{1,0:T(8,128)} custom-call(bf16[1024,256]{1,0:T(8,128)(2,1)S(1)} %copy-done, bf16[256,256]{1,0:T(8,128)(2,1)S(1)} %copy-done.6, bf16[64,256]{1,0:T(8,128)(2,1)S(1)} %copy-done.9, f32[128,128]{1,0:T(8,128)S(1)} %copy-done.3, f32[128,128]{1,0:T(8,128)S(1)} %copy-done.2), custom_call_target="tpu_custom_call" | custom-call | flops 200000000 | bytes 2000000 | tf_op jit(solution)/shard_map/filter_gradient/pallas_call | solution.py:243
  58.2 27.1 %all-to-all-done.1.back_ref = bf16[32,136,128]{2,1,0:T(8,128)(2,1)S(1)} async-done(((bf16[32,136,128]{2,1,0:T(8,128)(2,1)}), bf16[32,136,128]{2,1,0:T(8,128)(2,1)S(1)}, u32[]{:S(2)}, u32[]{:S(2)}) %all-to-all-start.1) | async-done | bytes 1114144 | tf_op jit(solution)/shard_map/all_to_all | solution.py:739
  85.4 5.8 %joined_gradients.1 = (bf16[1024,256]{1,0:T(8,128)(2,1)}, bf16[3072,256]{1,0:T(8,128)(2,1)}) custom-call(bf16[1024,256]{1,0:T(8,128)(2,1)} %get-tuple-element.22.s_ref._, bf16[3072,256]{1,0:T(8,128)(2,1)} %get-tuple-element.23.f_hbm, bf16[8,3072]{1,0:T(8,128)(2,1)S(1)} %collective-permute-done.1.edge_ref, ...), custom_call_target="tpu_custom_call", output_to_operand_aliasing={{0}: (0, {}), {1}: (1, {})} | custom-call | flops 10000000 | bytes 4000000 | tf_op jit(solution)/shard_map/joined_gradients/pallas_call | solution.py:279
  (1 shorter events, 0.0 us)
Async XLA Ops:
  0.6 7.6 %copy-start.1 = (bf16[1024,256]{1,0:T(8,128)(2,1)S(1)}, bf16[1024,256]{1,0:T(8,128)(2,1)}, u32[]{:S(2)}) copy-start(bf16[1024,256]{1,0:T(8,128)(2,1)} %og_ref.3) | copy-start | bytes 1572868
  0.6 7.6 %copy-start.4 = (bf16[7,3072]{1,0:T(8,128)(2,1)S(1)}, bf16[7,3072]{1,0:T(8,128)(2,1)}, u32[]{:S(2)}) copy-start(bf16[7,3072]{1,0:T(8,128)(2,1)} %w_ref.3) | copy-start | bytes 129028
  2.4 5.8 %collective-permute-start = (bf16[8,3072]{1,0:T(8,128)(2,1)S(1)}, bf16[8,3072]{1,0:T(8,128)(2,1)S(1)}, u32[]{:S(2)}, u32[]{:S(2)}) collective-permute-start(bf16[8,3072]{1,0:T(8,128)(2,1)S(1)} %slice.4), channel_id=1, source_target_pairs={{0,1},{1,2},{2,3},{3,4},{4,5},{5,6},{6,7},{7,8},{8,9},{9,10},{10,1... | collective-permute-start | bytes 147464 | tf_op jit(solution)/shard_map/ppermute | solution.py:21
  11.9 9.0 %copy-start.2 = (f32[128,128]{1,0:T(8,128)S(1)}, f32[128,128]{1,0:T(8,128)}, u32[]{:S(2)}) copy-start(f32[128,128]{1,0:T(8,128)} %constant.15.clone.ti_ref) | copy-start | bytes 196612
  11.9 9.0 %copy-start.3 = (f32[128,128]{1,0:T(8,128)S(1)}, f32[128,128]{1,0:T(8,128)}, u32[]{:S(2)}) copy-start(f32[128,128]{1,0:T(8,128)} %constant.14.clone.tr_ref) | copy-start | bytes 196612
  11.9 9.0 %copy-start.5 = (bf16[8,8192]{1,0:T(8,128)(2,1)S(1)}, bf16[8,8192]{1,0:T(8,128)(2,1)}, u32[]{:S(2)}) copy-start(bf16[8,8192]{1,0:T(8,128)(2,1)} %x_ref.1) | copy-start | bytes 393220
  11.9 9.0 %copy-start.7 = (bf16[256,256]{1,0:T(8,128)(2,1)S(1)}, bf16[256,256]{1,0:T(8,128)(2,1)}, u32[]{:S(2)}) copy-start(bf16[256,256]{1,0:T(8,128)(2,1)} %constant.23.second_ref) | copy-start | bytes 393220
  11.9 9.0 %copy-start.8 = (bf16[256,64]{1,0:T(8,128)(2,1)S(1)}, bf16[256,64]{1,0:T(8,128)(2,1)}, u32[]{:S(2)}) copy-start(bf16[256,64]{1,0:T(8,128)(2,1)} %constant.22.first_ref) | copy-start | bytes 98308
  11.9 33.8 %all-to-all-start = ((bf16[32,64,256]{2,1,0:T(8,128)(2,1)}), bf16[32,64,256]{2,1,0:T(8,128)(2,1)S(1)}, u32[]{:S(2)}, u32[]{:S(2)}) async-start(bf16[32,64,256]{2,1,0:T(8,128)(2,1)} %get-tuple-element.17), calls=%async_computation | async-start | bytes 2097152 | tf_op jit(solution)/shard_map/all_to_all | solution.py:736
  18.7 12.7 %collective-permute-start.1 = (bf16[8,3072]{1,0:T(8,128)(2,1)S(1)}, bf16[8,3072]{1,0:T(8,128)(2,1)S(1)}, u32[]{:S(2)}, u32[]{:S(2)}) collective-permute-start(bf16[8,3072]{1,0:T(8,128)(2,1)S(1)} %get-tuple-element.16), channel_id=1, source_target_pairs={{1,0},{2,1},{3,2},{4,3},{5,4},{6,5},{7,6},{8,7},{9,8},{10,9},{11,1... | collective-permute-start | bytes 147464 | tf_op jit(solution)/shard_map/ppermute | solution.py:21
  45.7 1.0 %copy-start.10 = (bf16[768,256]{1,0:T(8,128)(2,1)S(1)}, bf16[768,256]{1,0:T(8,128)(2,1)}, u32[]{:S(2)}) copy-start(bf16[768,256]{1,0:T(8,128)(2,1)} %constant.24.table_ref) | copy-start | bytes 1179652
  53.5 3.4 %copy-start = (bf16[1024,256]{1,0:T(8,128)(2,1)S(1)}, bf16[1024,256]{1,0:T(8,128)(2,1)}, u32[]{:S(2)}) copy-start(bf16[1024,256]{1,0:T(8,128)(2,1)} %get-tuple-element.22.s_ref._) | copy-start | bytes 1572868
  53.5 3.4 %copy-start.6 = (bf16[256,256]{1,0:T(8,128)(2,1)S(1)}, bf16[256,256]{1,0:T(8,128)(2,1)}, u32[]{:S(2)}) copy-start(bf16[256,256]{1,0:T(8,128)(2,1)} %constant.25.third_ref) | copy-start | bytes 393220
  53.5 3.4 %copy-start.9 = (bf16[64,256]{1,0:T(8,128)(2,1)S(1)}, bf16[64,256]{1,0:T(8,128)(2,1)}, u32[]{:S(2)}) copy-start(bf16[64,256]{1,0:T(8,128)(2,1)} %constant.26.fourth_ref) | copy-start | bytes 98308
  53.6 31.8 %all-to-all-start.1 = ((bf16[32,136,128]{2,1,0:T(8,128)(2,1)}), bf16[32,136,128]{2,1,0:T(8,128)(2,1)S(1)}, u32[]{:S(2)}, u32[]{:S(2)}) async-start(bf16[32,136,128]{2,1,0:T(8,128)(2,1)} %get-tuple-element.21), calls=%async_computation.1 | async-start | bytes 2228224 | tf_op jit(solution)/shard_map/all_to_all | solution.py:739

commit v10 on v9

--- a/solution.py
+++ b/solution.py
@@ -85,13 +85,17 @@
     return jnp.dot(left, right, preferred_element_type=jnp.float32)
 
 
-def transform_filters(long_filter, tables, seq_len):
+def transform_filters(long_filter, tables, seq_len, handed=()):
     padded, inner, outer = sizes_of(seq_len)
     half = outer // 2
     groups = long_filter.shape[0]
     scale = seq_len ** -0.5
 
-    def kernel(x_ref, first_ref, second_ref, tr_ref, ti_ref, out_ref, tall):
+    def kernel(x_ref, first_ref, second_ref, tr_ref, ti_ref, *refs):
+        count = len(handed)
+        out_ref, tall = refs[count], refs[-1]
+        for n in range(count):
+            refs[count + 1 + n][...] = refs[n][...]
         height = half * groups
         for b in range(half):
             for t in range(inner // LANES):
@@ -110,11 +114,12 @@
     return pl.pallas_call(
         kernel,
         name="filter_dft",
-        out_shape=jax.ShapeDtypeStruct((groups * outer, 2 * inner), jnp.float32),
+        out_shape=[jax.ShapeDtypeStruct((groups * outer, 2 * inner), jnp.float32)]
+        + [jax.ShapeDtypeStruct(array.shape, array.dtype) for array in handed],
         scratch_shapes=[pltpu.VMEM((half * groups * inner // LANES, LANES), jnp.float32)],
         compiler_params=pltpu.CompilerParams(vmem_limit_bytes=VMEM_LIMIT),
         cost_estimate=pl.CostEstimate(flops=200_000_000, bytes_accessed=2_000_000, transcendentals=0),
-    )(long_filter, tables["first_real"], tables["second"], tables["twist_re"], tables["twist_im"])
+    )(long_filter, tables["first_real"], tables["second"], tables["twist_re"], tables["twist_im"], *handed)
 
 
 def filtered(arrived, filters, tables, seq_len, other=None):
@@ -438,7 +443,7 @@
     )
 
 
-def joined_filtering(arrived, filters, tables, seq_len):
+def joined_filtering(arrived, filters, joined, tables, seq_len):
     padded, inner, outer = sizes_of(seq_len)
     half = outer // 2
     sources, rows, local = arrived.shape
@@ -554,7 +559,7 @@
         kernel,
         "joined_filtering",
         (narrow_shape(*sent), narrow_shape(groups * outer, 2 * inner)),
-        [arrived, filters] + [tables[n] for n in ("joined", "twist_re", "twist_im")],
+        [arrived, filters, joined, tables["twist_re"], tables["twist_im"]],
         [
             pltpu.VMEM(sent, jnp.bfloat16),
             pltpu.VMEM((groups * outer, 2 * inner), jnp.bfloat16),
@@ -588,7 +593,6 @@
                 fetch(part, i).start()
 
         def features(part, i):
-            fetch(part, i).wait()
             held = [f_ref[part * blocks + i, :, t * LANES : (t + 1) * LANES] for t in range(tiles)]
             return jnp.concatenate(held, axis=0).astype(jnp.float32)
 
@@ -602,41 +606,52 @@
                 to = mixed_ref.at[lane_block(i), :]
             return pltpu.make_async_copy(made.at[at], to, sent.at[at])
 
+        def turned(s, i):
+            held = pl.ds(i * near, near)
+            pieces = [
+                back_ref[held, (s * tiles + t) * owned : (s * tiles + t + 1) * owned, :].reshape(LANES, LANES).T
+                for t in range(tiles)
+            ]
+            return jnp.concatenate(pieces, axis=0).astype(jnp.float32)
+
+        def rim_of(s, i):
+            rim = None
+            for n in range(near):
+                piece = back_ref[i * near + n, 2 * tiles * owned :, :].astype(jnp.float32)
+                turn_by = (n - s) * owned % LANES
+                if turn_by:
+                    piece = pltpu.roll(piece, turn_by, 1)
+                rim = jnp.where(lane >= n * owned, piece, rim) if n else piece
+            return rim
+
+        def third(part, i, here, rim, other):
+            edge = edge_ref[:, lane_block(i, (3 - part) % 3 * width)].astype(jnp.float32)
+            total = seven_taps(
+                tall.at[part],
+                (here * other).astype(jnp.bfloat16).astype(jnp.float32),
+                (rim * edge).astype(jnp.bfloat16).astype(jnp.float32),
+                w_ref[:, lane_block(i, part * width)].astype(jnp.float32),
+                False,
+            )
+            made[part * blocks + i] = total.astype(jnp.bfloat16).T
+            if part == 0:
+                fetch(0, i).wait()
+            copy(part, i).start()
+
         @pl.loop(0, blocks)
         def _(i):
-            held = pl.ds(i * near, near)
-            sums = []
-            for s in range(2):
-                turned = [
-                    back_ref[held, (s * tiles + t) * owned : (s * tiles + t + 1) * owned, :].reshape(LANES, LANES).T
-                    for t in range(tiles)
-                ]
-                here = jnp.concatenate(turned, axis=0).astype(jnp.float32)
-                rim = jnp.zeros((RIM, LANES), jnp.float32)
-                for n in range(near):
-                    piece = back_ref[i * near + n, 2 * tiles * owned :, :].astype(jnp.float32)
-                    turn_by = (n - s) * owned % LANES
-                    if turn_by:
-                        piece = pltpu.roll(piece, turn_by, 1)
-                    rim = jnp.where(lane >= n * owned, piece, rim) if n else piece
-                sums.append((here, rim))
+            third(0, i, turned(0, i), rim_of(0, i), og_ref[lane_block(i), :].T.astype(jnp.float32))
+
+        @pl.loop(0, blocks)
+        def _(i):
+            fetch(1, i).wait()
+            fetch(2, i).wait()
             query, key, value = [features(part, i) for part in range(3)]
-            made[3 * blocks + i] = (query * sums[0][0]).astype(jnp.bfloat16).T
+            made[3 * blocks + i] = (query * turned(0, i)).astype(jnp.bfloat16).T
             copy(3, i).start()
-            for part in range(3):
-                here, rim = sums[min(part, 1)]
-                other = (og_ref[lane_block(i), :].T.astype(jnp.float32), value, key)[part]
-                edge = edge_ref[:, lane_block(i, (3 - part) % 3 * width)].astype(jnp.float32)
-                grad = (here * other).astype(jnp.bfloat16)
-                total = seven_taps(
-                    tall.at[part],
-                    grad.astype(jnp.float32),
-                    (rim * edge).astype(jnp.bfloat16).astype(jnp.float32),
-                    w_ref[:, lane_block(i, part * width)].astype(jnp.float32),
-                    False,
-                )
-                made[part * blocks + i] = total.astype(jnp.bfloat16).T
-                copy(part, i).start()
+            here, rim = turned(1, i), rim_of(1, i)
+            third(1, i, here, rim, value)
+            third(2, i, here, rim, key)
 
         @pl.loop(0, blocks)
         def _(i):
@@ -732,10 +747,12 @@
     twin = owned // CPG * outer == width and 2 * inner == local_len and inner == outer
     if owned % 16 == 0 and LANES % (2 * owned) == 0 and devices % 4 == 0 and twin:
         feats, message, edges = joined_features(turned, rim, short_filter, out_grad, owned)
-        filters = transform_filters(long_filter, tables, seq_len)
+        filters, joined = transform_filters(long_filter, tables, seq_len, [tables["joined"]])
         arrived = lax.all_to_all(message, EVERYONE, split_axis=0, concat_axis=0, tiled=True)
-        edges, filters, arrived = lax.optimization_barrier((shifted(edges, EVERYONE, -1), filters, arrived))
-        answer, cross = joined_filtering(arrived, filters, tables, seq_len)
+        edges, filters, joined, arrived = lax.optimization_barrier(
+            (shifted(edges, EVERYONE, -1), filters, joined, arrived)
+        )
+        answer, cross = joined_filtering(arrived, filters, joined, tables, seq_len)
         returned = lax.all_to_all(answer, EVERYONE, split_axis=0, concat_axis=0, tiled=True)
         filter_grad = filter_gradient(cross, tables, seq_len)
         filter_grad, returned, cross = lax.optimization_barrier((filter_grad, returned, cross))
@@ -749,7 +766,7 @@
         pieces = block.reshape(devices, owned, local_len)
         return lax.all_to_all(pieces, EVERYONE, split_axis=0, concat_axis=0, tiled=True)
 
-    filters = transform_filters(long_filter, tables, seq_len)
+    (filters,) = transform_filters(long_filter, tables, seq_len)
     prod_chan = exchange(product)
     conv_grad, prod_chan = lax.optimization_barrier((conv_grad, prod_chan))
     grad_chan = exchange(conv_grad)

time: 92.3 us -> 93 us (level)
  local copies, waits for them, and re-layouts: 2.83 us -> 4.03 us
  waiting for transfers between devices: 52 us -> 51 us
    unnamed x23 -> x27, local copies, waits for them, and re-layouts: 2.83 us -> 4.03 us
    ppermute x2, waiting for transfers between devices: 10.6 us -> 9.59 us  [shifted(): lax.ppermute(value, axis, [(source, source + steps) for source in range(f...]
where the time goes in v10:
time: 93 us; the launch traced here: 91.8 us
  waiting for transfers between devices  51 us (55%)
  Pallas kernels  19 us (20%)
  starting transfers between devices  16.9 us (18%)
  local copies, waits for them, and re-layouts  4.03 us (4%)
    all_to_all x1, waiting for transfers between devices, shards(): lax.all_to_all(answer, EVERYONE, split_axis=0, concat_axis=0, tiled=True)  27.1 us
    pallas_call x3, Pallas kernels, whole_call(): pl.pallas_call(kernel, name=name, out_shape=out_shape, scratch_shapes=lis...  16.7 us
    all_to_all x1, waiting for transfers between devices, shards(): lax.all_to_all(message, EVERYONE, split_axis=0, concat_axis=0, tiled=True)  14.3 us
    ppermute x2, waiting for transfers between devices, shifted(): lax.ppermute(value, axis, [(source, source + steps) for source in range(f...  9.59 us
    ppermute x2, starting transfers between devices, shifted(): lax.ppermute(value, axis, [(source, source + steps) for source in range(f...  6.76 us
    all_to_all x1, starting transfers between devices, shards(): lax.all_to_all(message, EVERYONE, split_axis=0, concat_axis=0, tiled=True)  6.75 us
    unnamed x27, local copies, waits for them, and re-layouts  4.03 us
    all_to_all x1, starting transfers between devices, shards(): lax.all_to_all(answer, EVERYONE, split_axis=0, concat_axis=0, tiled=True)  3.34 us
  transfers between devices with their start and end apart: 4, of which 4 were waited for; matrix products, arithmetic and copies ran while one was open for 0% of the time, Pallas kernels for 3%

profile of v10, /device:TPU:1, one launch (start us, length us, event | category | flops | bytes accessed | tf_op | source)
XLA Modules:
  0.0 91.8 jit_solution(17625218907485820631)
XLA Ops:
  0.6 0.0 copy-start.1
  0.6 0.0 copy-start.5
  0.7 1.8 %copy.16 = bf16[3072,256]{0,1:T(8,128)(2,1)S(1)} copy(bf16[3072,256]{1,0:T(8,128)(2,1)} %param.11) | data formatting | bytes 3145728 | tf_op args[0]
  2.4 4.6 %collective-permute-start = (bf16[8,3072]{1,0:T(8,128)(2,1)S(1)}, bf16[8,3072]{1,0:T(8,128)(2,1)S(1)}, u32[]{:S(2)}, u32[]{:S(2)}) collective-permute-start(bf16[8,3072]{1,0:T(8,128)(2,1)S(1)} %slice.4), channel_id=1, source_target_pairs={{0,1},{1,2},{2,3},{3,4},{4,5},{5,6},{6,7},{7,8},{8,9},{9,10},{10,1... | collective-permute-start | bytes 147464 | tf_op jit(solution)/shard_map/ppermute | solution.py:21
  7.0 1.2 %collective-permute-done.rim_ref = bf16[8,3072]{1,0:T(8,128)(2,1)S(1)} collective-permute-done((bf16[8,3072]{1,0:T(8,128)(2,1)S(1)}, bf16[8,3072]{1,0:T(8,128)(2,1)S(1)}, u32[]{:S(2)}, u32[]{:S(2)}) %collective-permute-start) | collective-permute-done | bytes 49184 | tf_op jit(solution)/shard_map/ppermute | solution.py:21
  8.2 0.0 copy-done.1
  8.2 0.0 copy-done.5
  8.2 3.7 %joined_features.1 = (bf16[3072,256]{1,0:T(8,128)(2,1)}, bf16[32,64,256]{2,1,0:T(8,128)(2,1)}, bf16[8,3072]{1,0:T(8,128)(2,1)S(1)}) custom-call(bf16[256,3072]{1,0:T(8,128)(2,1)S(1)} %bitcast.2, bf16[8,3072]{1,0:T(8,128)(2,1)S(1)} %collective-permute-done.rim_ref, bf16[7,3072]{1,0:T(8,128)(2,1)S(1)} %copy-done.5, bf16[1024,256]{1,0:T(8,128)(2,1)S(1)} %copy-done.1), custom_call_target="tpu_custom_call" | custom-call | flops 10000000 | bytes 4000000 | tf_op jit(solution)/shard_map/joined_features/pallas_call | solution.py:284
  11.9 0.0 copy-start.2
  11.9 0.0 copy-start.3
  11.9 0.0 copy-start.4
  11.9 0.0 copy-start.7
  11.9 0.0 copy-start.8
  11.9 0.0 copy-start.9
  11.9 6.8 %all-to-all-start = ((bf16[32,64,256]{2,1,0:T(8,128)(2,1)}), bf16[32,64,256]{2,1,0:T(8,128)(2,1)S(1)}, u32[]{:S(2)}, u32[]{:S(2)}) async-start(bf16[32,64,256]{2,1,0:T(8,128)(2,1)} %get-tuple-element.22), calls=%async_computation | async-start | bytes 2097152 | tf_op jit(solution)/shard_map/all_to_all | solution.py:751
  18.7 2.2 %collective-permute-start.1 = (bf16[8,3072]{1,0:T(8,128)(2,1)S(1)}, bf16[8,3072]{1,0:T(8,128)(2,1)S(1)}, u32[]{:S(2)}, u32[]{:S(2)}) collective-permute-start(bf16[8,3072]{1,0:T(8,128)(2,1)S(1)} %get-tuple-element.19), channel_id=1, source_target_pairs={{1,0},{2,1},{3,2},{4,3},{5,4},{6,5},{7,6},{8,7},{9,8},{10,9},{11,1... | collective-permute-start | bytes 147464 | tf_op jit(solution)/shard_map/ppermute | solution.py:21
  20.9 0.0 copy-done.2
  20.9 0.0 copy-done.3
  20.9 0.0 copy-done.4
  20.9 0.0 copy-done.7
  20.9 0.0 copy-done.8
  20.9 0.0 copy-done.9
  20.9 1.1 %filter_dft.1 = (f32[1024,256]{1,0:T(8,128)S(1)}, bf16[768,256]{1,0:T(8,128)(2,1)S(1)}) custom-call(bf16[8,8192]{1,0:T(8,128)(2,1)S(1)} %copy-done.7, bf16[256,64]{1,0:T(8,128)(2,1)S(1)} %copy-done.9, bf16[256,256]{1,0:T(8,128)(2,1)S(1)} %copy-done.8, f32[128,128]{1,0:T(8,128)S(1)} %copy-done.4, f32[128,128]{1,0:T(8,128)S(1)} %copy-done.3, ...), custom_call_target="tpu_custom_call" | custom-call | flops 200000000 | bytes 2000000 | tf_op jit(solution)/shard_map/filter_dft/pallas_call | solution.py:114
  22.0 0.0 copy-start.11
  22.0 1.0 %copy-done.11 = f32[1024,256]{1,0:T(8,128)} copy-done((f32[1024,256]{1,0:T(8,128)}, f32[1024,256]{1,0:T(8,128)S(1)}, u32[]{:S(2)}) %copy-start.11) | copy-done | bytes 1048600
  23.0 8.4 %collective-permute-done.1.edge_ref = bf16[8,3072]{1,0:T(8,128)(2,1)S(1)} collective-permute-done((bf16[8,3072]{1,0:T(8,128)(2,1)S(1)}, bf16[8,3072]{1,0:T(8,128)(2,1)S(1)}, u32[]{:S(2)}, u32[]{:S(2)}) %collective-permute-start.1) | collective-permute-done | bytes 49184 | tf_op jit(solution)/shard_map/ppermute | solution.py:21
  31.4 14.3 %all-to-all-done.x_ref = bf16[32,64,256]{2,1,0:T(8,128)(2,1)S(1)} async-done(((bf16[32,64,256]{2,1,0:T(8,128)(2,1)}), bf16[32,64,256]{2,1,0:T(8,128)(2,1)S(1)}, u32[]{:S(2)}, u32[]{:S(2)}) %all-to-all-start) | async-done | bytes 1048608 | tf_op jit(solution)/shard_map/all_to_all | solution.py:751
  45.7 0.0 copy-start.12
  45.7 1.2 %copy-done.12 = f32[1024,256]{1,0:T(8,128)S(1)} copy-done((f32[1024,256]{1,0:T(8,128)S(1)}, f32[1024,256]{1,0:T(8,128)}, u32[]{:S(2)}) %copy-start.12) | copy-done | bytes 1048600
  46.9 6.9 %joined_filtering.1 = (bf16[32,136,128]{2,1,0:T(8,128)(2,1)}, bf16[1024,256]{1,0:T(8,128)(2,1)}) custom-call(bf16[32,64,256]{2,1,0:T(8,128)(2,1)S(1)} %all-to-all-done.x_ref, f32[1024,256]{1,0:T(8,128)S(1)} %copy-done.12, bf16[768,256]{1,0:T(8,128)(2,1)S(1)} %get-tuple-element.25.table_ref, f32[128,128]{1,0:T(8,128)S(1)} %copy-done.4, f32[128,128]{1,0:T(8,128)S(1)} %copy-done.3), custom_call_target="tpu_custom_call" | custom-call | flops 4000000000 | bytes 4000000 | tf_op jit(solution)/shard_map/joined_filtering/pallas_call | solution.py:284
  53.8 0.0 copy-start
  53.8 0.0 copy-start.6
  53.8 0.0 copy-start.10
  53.8 3.3 %all-to-all-start.1 = ((bf16[32,136,128]{2,1,0:T(8,128)(2,1)}), bf16[32,136,128]{2,1,0:T(8,128)(2,1)S(1)}, u32[]{:S(2)}, u32[]{:S(2)}) async-start(bf16[32,136,128]{2,1,0:T(8,128)(2,1)} %get-tuple-element.27), calls=%async_computation.1 | async-start | bytes 2228224 | tf_op jit(solution)/shard_map/all_to_all | solution.py:756
  57.2 0.0 copy-done
  57.2 0.0 copy-done.6
  57.2 0.0 copy-done.10
  57.2 1.3 %filter_gradient.1 = f32[8,8192]{1,0:T(8,128)} custom-call(bf16[1024,256]{1,0:T(8,128)(2,1)S(1)} %copy-done, bf16[256,256]{1,0:T(8,128)(2,1)S(1)} %copy-done.6, bf16[64,256]{1,0:T(8,128)(2,1)S(1)} %copy-done.10, f32[128,128]{1,0:T(8,128)S(1)} %copy-done.4, f32[128,128]{1,0:T(8,128)S(1)} %copy-done.3), custom_call_target="tpu_custom_call" | custom-call | flops 200000000 | bytes 2000000 | tf_op jit(solution)/shard_map/filter_gradient/pallas_call | solution.py:248
  58.5 27.1 %all-to-all-done.1.back_ref = bf16[32,136,128]{2,1,0:T(8,128)(2,1)S(1)} async-done(((bf16[32,136,128]{2,1,0:T(8,128)(2,1)}), bf16[32,136,128]{2,1,0:T(8,128)(2,1)S(1)}, u32[]{:S(2)}, u32[]{:S(2)}) %all-to-all-start.1) | async-done | bytes 1114144 | tf_op jit(solution)/shard_map/all_to_all | solution.py:756
  85.6 6.1 %joined_gradients.1 = (bf16[1024,256]{1,0:T(8,128)(2,1)}, bf16[3072,256]{1,0:T(8,128)(2,1)}) custom-call(bf16[1024,256]{1,0:T(8,128)(2,1)} %get-tuple-element.28.s_ref._, bf16[3072,256]{1,0:T(8,128)(2,1)} %get-tuple-element.29.f_hbm, bf16[8,3072]{1,0:T(8,128)(2,1)S(1)} %collective-permute-done.1.edge_ref, ...), custom_call_target="tpu_custom_call", output_to_operand_aliasing={{0}: (0, {}), {1}: (1, {})} | custom-call | flops 10000000 | bytes 4000000 | tf_op jit(solution)/shard_map/joined_gradients/pallas_call | solution.py:284
  (1 shorter events, 0.0 us)
Async XLA Ops:
  0.6 7.6 %copy-start.1 = (bf16[1024,256]{1,0:T(8,128)(2,1)S(1)}, bf16[1024,256]{1,0:T(8,128)(2,1)}, u32[]{:S(2)}) copy-start(bf16[1024,256]{1,0:T(8,128)(2,1)} %og_ref.3) | copy-start | bytes 1572868
  0.6 7.6 %copy-start.5 = (bf16[7,3072]{1,0:T(8,128)(2,1)S(1)}, bf16[7,3072]{1,0:T(8,128)(2,1)}, u32[]{:S(2)}) copy-start(bf16[7,3072]{1,0:T(8,128)(2,1)} %w_ref.3) | copy-start | bytes 129028
  2.4 5.8 %collective-permute-start = (bf16[8,3072]{1,0:T(8,128)(2,1)S(1)}, bf16[8,3072]{1,0:T(8,128)(2,1)S(1)}, u32[]{:S(2)}, u32[]{:S(2)}) collective-permute-start(bf16[8,3072]{1,0:T(8,128)(2,1)S(1)} %slice.4), channel_id=1, source_target_pairs={{0,1},{1,2},{2,3},{3,4},{4,5},{5,6},{6,7},{7,8},{8,9},{9,10},{10,1... | collective-permute-start | bytes 147464 | tf_op jit(solution)/shard_map/ppermute | solution.py:21
  11.9 9.0 %copy-start.2 = (bf16[768,256]{1,0:T(8,128)(2,1)S(1)}, bf16[768,256]{1,0:T(8,128)(2,1)}, u32[]{:S(2)}) copy-start(bf16[768,256]{1,0:T(8,128)(2,1)} %constant.24.refs_0_) | copy-start | bytes 1179652
  11.9 9.0 %copy-start.3 = (f32[128,128]{1,0:T(8,128)S(1)}, f32[128,128]{1,0:T(8,128)}, u32[]{:S(2)}) copy-start(f32[128,128]{1,0:T(8,128)} %constant.15.clone.ti_ref) | copy-start | bytes 196612
  11.9 9.0 %copy-start.4 = (f32[128,128]{1,0:T(8,128)S(1)}, f32[128,128]{1,0:T(8,128)}, u32[]{:S(2)}) copy-start(f32[128,128]{1,0:T(8,128)} %constant.14.clone.tr_ref) | copy-start | bytes 196612
  11.9 9.0 %copy-start.7 = (bf16[8,8192]{1,0:T(8,128)(2,1)S(1)}, bf16[8,8192]{1,0:T(8,128)(2,1)}, u32[]{:S(2)}) copy-start(bf16[8,8192]{1,0:T(8,128)(2,1)} %x_ref.1) | copy-start | bytes 393220
  11.9 9.0 %copy-start.8 = (bf16[256,256]{1,0:T(8,128)(2,1)S(1)}, bf16[256,256]{1,0:T(8,128)(2,1)}, u32[]{:S(2)}) copy-start(bf16[256,256]{1,0:T(8,128)(2,1)} %constant.23.second_ref) | copy-start | bytes 393220
  11.9 9.0 %copy-start.9 = (bf16[256,64]{1,0:T(8,128)(2,1)S(1)}, bf16[256,64]{1,0:T(8,128)(2,1)}, u32[]{:S(2)}) copy-start(bf16[256,64]{1,0:T(8,128)(2,1)} %constant.22.first_ref) | copy-start | bytes 98308
  11.9 33.8 %all-to-all-start = ((bf16[32,64,256]{2,1,0:T(8,128)(2,1)}), bf16[32,64,256]{2,1,0:T(8,128)(2,1)S(1)}, u32[]{:S(2)}, u32[]{:S(2)}) async-start(bf16[32,64,256]{2,1,0:T(8,128)(2,1)} %get-tuple-element.22), calls=%async_computation | async-start | bytes 2097152 | tf_op jit(solution)/shard_map/all_to_all | solution.py:751
  18.7 12.7 %collective-permute-start.1 = (bf16[8,3072]{1,0:T(8,128)(2,1)S(1)}, bf16[8,3072]{1,0:T(8,128)(2,1)S(1)}, u32[]{:S(2)}, u32[]{:S(2)}) collective-permute-start(bf16[8,3072]{1,0:T(8,128)(2,1)S(1)} %get-tuple-element.19), channel_id=1, source_target_pairs={{1,0},{2,1},{3,2},{4,3},{5,4},{6,5},{7,6},{8,7},{9,8},{10,9},{11,1... | collective-permute-start | bytes 147464 | tf_op jit(solution)/shard_map/ppermute | solution.py:21
  22.0 1.0 %copy-start.11 = (f32[1024,256]{1,0:T(8,128)}, f32[1024,256]{1,0:T(8,128)S(1)}, u32[]{:S(2)}) copy-start(f32[1024,256]{1,0:T(8,128)S(1)} %get-tuple-element.24.f_ref) | copy-start | bytes 3145732
  45.7 1.2 %copy-start.12 = (f32[1024,256]{1,0:T(8,128)S(1)}, f32[1024,256]{1,0:T(8,128)}, u32[]{:S(2)}) copy-start(f32[1024,256]{1,0:T(8,128)} %copy-done.11) | copy-start | bytes 3145732
  53.8 3.4 %copy-start = (bf16[1024,256]{1,0:T(8,128)(2,1)S(1)}, bf16[1024,256]{1,0:T(8,128)(2,1)}, u32[]{:S(2)}) copy-start(bf16[1024,256]{1,0:T(8,128)(2,1)} %get-tuple-element.28.s_ref._) | copy-start | bytes 1572868
  53.8 3.4 %copy-start.6 = (bf16[256,256]{1,0:T(8,128)(2,1)S(1)}, bf16[256,256]{1,0:T(8,128)(2,1)}, u32[]{:S(2)}) copy-start(bf16[256,256]{1,0:T(8,128)(2,1)} %constant.25.third_ref) | copy-start | bytes 393220
  53.8 3.4 %copy-start.10 = (bf16[64,256]{1,0:T(8,128)(2,1)S(1)}, bf16[64,256]{1,0:T(8,128)(2,1)}, u32[]{:S(2)}) copy-start(bf16[64,256]{1,0:T(8,128)(2,1)} %constant.26.fourth_ref) | copy-start | bytes 98308
  53.8 31.8 %all-to-all-start.1 = ((bf16[32,136,128]{2,1,0:T(8,128)(2,1)}), bf16[32,136,128]{2,1,0:T(8,128)(2,1)S(1)}, u32[]{:S(2)}, u32[]{:S(2)}) async-start(bf16[32,136,128]{2,1,0:T(8,128)(2,1)} %get-tuple-element.27), calls=%async_computation.1 | async-start | bytes 2228224 | tf_op jit(solution)/shard_map/all_to_all | solution.py:756

commit v11 on v10

--- a/solution.py
+++ b/solution.py
@@ -85,7 +85,7 @@
     return jnp.dot(left, right, preferred_element_type=jnp.float32)
 
 
-def transform_filters(long_filter, tables, seq_len, handed=()):
+def transform_filters(long_filter, tables, seq_len, kind=jnp.float32, handed=()):
     padded, inner, outer = sizes_of(seq_len)
     half = outer // 2
     groups = long_filter.shape[0]
@@ -109,12 +109,12 @@
             g_re = (f_re * tr_ref[...] + f_im * ti_ref[...]).astype(jnp.bfloat16)
             g_im = (f_im * tr_ref[...] - f_re * ti_ref[...]).astype(jnp.bfloat16)
             spec = dot(g_re, second_ref[:inner]) + dot(g_im, second_ref[inner:])
-            out_ref[g * outer : (g + 1) * outer, :] = spec * scale
+            out_ref[g * outer : (g + 1) * outer, :] = (spec * scale).astype(kind)
 
     return pl.pallas_call(
         kernel,
         name="filter_dft",
-        out_shape=[jax.ShapeDtypeStruct((groups * outer, 2 * inner), jnp.float32)]
+        out_shape=[jax.ShapeDtypeStruct((groups * outer, 2 * inner), kind)]
         + [jax.ShapeDtypeStruct(array.shape, array.dtype) for array in handed],
         scratch_shapes=[pltpu.VMEM((half * groups * inner // LANES, LANES), jnp.float32)],
         compiler_params=pltpu.CompilerParams(vmem_limit_bytes=VMEM_LIMIT),
@@ -259,6 +259,7 @@
 
 
 RIM = 8
+STEP = 2
 
 
 def seven_taps(tall, value, rim, weights, forward):
@@ -385,32 +386,36 @@
             to = pl.ds(pl.multiple_of(at * LANES, LANES), LANES)
             return pltpu.make_async_copy(f_ref.at[at], f_hbm.at[to, :], sent.at[blocks + at])
 
-        @pl.loop(0, blocks)
-        def _(i):
-            parts = []
-            for part in range(3):
-                lanes = lane_block(i, part * width)
-                total = seven_taps(
-                    tall.at[part],
-                    x_ref[:, lanes].astype(jnp.float32),
-                    rim_ref[:, lanes].astype(jnp.float32),
-                    w_ref[:, lanes].astype(jnp.float32),
-                    True,
-                ).astype(jnp.bfloat16)
-                for t in range(local // LANES):
-                    f_ref[part * blocks + i, :, t * LANES : (t + 1) * LANES] = total[t * LANES : (t + 1) * LANES]
-                keep(part, i).start()
-                if part:
-                    edge[:, lanes] = total[:RIM]
-                parts.append(total.astype(jnp.float32))
-            og = og_ref[lane_block(i), :].T
-            edge[:, lane_block(i)] = og[:RIM]
-            kv = (parts[1] * parts[2]).astype(jnp.bfloat16).T
-            dconv = (og.astype(jnp.float32) * parts[0]).astype(jnp.bfloat16).T
-            to = pl.ds(i * near, near)
-            made[to, :owned, :] = kv.reshape(near, owned, local)
-            made[to, owned:, :] = dconv.reshape(near, owned, local)
-            copy(i).start()
+        @pl.loop(0, blocks // STEP)
+        def _(step):
+            for slot in range(STEP):
+                i = step * STEP + slot
+                parts = []
+                for part in range(3):
+                    lanes = lane_block(i, part * width)
+                    total = seven_taps(
+                        tall.at[3 * slot + part],
+                        x_ref[:, lanes].astype(jnp.float32),
+                        rim_ref[:, lanes].astype(jnp.float32),
+                        w_ref[:, lanes].astype(jnp.float32),
+                        True,
+                    ).astype(jnp.bfloat16)
+                    for t in range(local // LANES):
+                        f_ref[part * blocks + i, :, t * LANES : (t + 1) * LANES] = total[t * LANES : (t + 1) * LANES]
+                    if part:
+                        edge[:, lanes] = total[:RIM]
+                    parts.append(total.astype(jnp.float32))
+                og = og_ref[lane_block(i), :].T
+                edge[:, lane_block(i)] = og[:RIM]
+                kv = (parts[1] * parts[2]).astype(jnp.bfloat16).T
+                dconv = (og.astype(jnp.float32) * parts[0]).astype(jnp.bfloat16).T
+                to = pl.ds(i * near, near)
+                made[to, :owned, :] = kv.reshape(near, owned, local)
+                made[to, owned:, :] = dconv.reshape(near, owned, local)
+            for slot in range(STEP):
+                copy(step * STEP + slot).start()
+                for part in range(3):
+                    keep(part, step * STEP + slot).start()
 
         last = pltpu.make_async_copy(edge, edge_ref, sent.at[4 * blocks])
         last.start()
@@ -432,7 +437,7 @@
         (narrow_shape(3 * width, local), narrow_shape(devices, 2 * owned, local), narrow_shape(RIM, 3 * width)),
         (turned, rim, short_filter, out_grad),
         [
-            pltpu.VMEM((3, local + RIM, LANES), jnp.float32),
+            pltpu.VMEM((3 * STEP, local + RIM, LANES), jnp.float32),
             pltpu.VMEM((devices, 2 * owned, local), jnp.bfloat16),
             pltpu.VMEM((3 * blocks, LANES, local), jnp.bfloat16),
             pltpu.VMEM((RIM, 3 * width), jnp.bfloat16),
@@ -482,8 +487,8 @@
                     stage[at : at + outer, :inner] = (f_re * tr + f_im * ti).astype(jnp.bfloat16)
                     stage[at : at + outer, inner:] = (f_im * tr - f_re * ti).astype(jnp.bfloat16)
         for g in range(groups):
-            s_re = f_ref[g * outer : (g + 1) * outer, :inner]
-            s_im = f_ref[g * outer : (g + 1) * outer, inner:]
+            s_re = f_ref[g * outer : (g + 1) * outer, :inner].astype(jnp.float32)
+            s_im = f_ref[g * outer : (g + 1) * outer, inner:].astype(jnp.float32)
             cross_re = cross_im = 0.0
             for p in range(PAIRS):
                 at = (g * PAIRS + p) * outer
@@ -624,34 +629,34 @@
                 rim = jnp.where(lane >= n * owned, piece, rim) if n else piece
             return rim
 
-        def third(part, i, here, rim, other):
+        def third(part, slot, i, here, rim, other):
             edge = edge_ref[:, lane_block(i, (3 - part) % 3 * width)].astype(jnp.float32)
             total = seven_taps(
-                tall.at[part],
+                tall.at[3 * slot + part],
                 (here * other).astype(jnp.bfloat16).astype(jnp.float32),
                 (rim * edge).astype(jnp.bfloat16).astype(jnp.float32),
                 w_ref[:, lane_block(i, part * width)].astype(jnp.float32),
                 False,
             )
             made[part * blocks + i] = total.astype(jnp.bfloat16).T
-            if part == 0:
-                fetch(0, i).wait()
-            copy(part, i).start()
-
-        @pl.loop(0, blocks)
-        def _(i):
-            third(0, i, turned(0, i), rim_of(0, i), og_ref[lane_block(i), :].T.astype(jnp.float32))
-
-        @pl.loop(0, blocks)
-        def _(i):
-            fetch(1, i).wait()
-            fetch(2, i).wait()
-            query, key, value = [features(part, i) for part in range(3)]
-            made[3 * blocks + i] = (query * turned(0, i)).astype(jnp.bfloat16).T
-            copy(3, i).start()
-            here, rim = turned(1, i), rim_of(1, i)
-            third(1, i, here, rim, value)
-            third(2, i, here, rim, key)
+
+        @pl.loop(0, blocks // STEP)
+        def _(step):
+            for slot in range(STEP):
+                for part in range(3):
+                    fetch(part, step * STEP + slot).wait()
+            for slot in range(STEP):
+                i = step * STEP + slot
+                query, key, value = [features(part, i) for part in range(3)]
+                conv = turned(0, i)
+                made[3 * blocks + i] = (query * conv).astype(jnp.bfloat16).T
+                third(0, slot, i, conv, rim_of(0, i), og_ref[lane_block(i), :].T.astype(jnp.float32))
+                back, rim = turned(1, i), rim_of(1, i)
+                third(1, slot, i, back, rim, value)
+                third(2, slot, i, back, rim, key)
+            for slot in range(STEP):
+                for part in range(4):
+                    copy(part, step * STEP + slot).start()
 
         @pl.loop(0, blocks)
         def _(i):
@@ -666,7 +671,7 @@
         (narrow_shape(width, local), narrow_shape(3 * width, local)),
         (cross, feats, edges, returned, out_grad, short_filter),
         [
-            pltpu.VMEM((3, local + RIM, LANES), jnp.float32),
+            pltpu.VMEM((3 * STEP, local + RIM, LANES), jnp.float32),
             pltpu.VMEM((4 * blocks, LANES, local), jnp.bfloat16),
             pltpu.VMEM((3 * blocks, LANES, local), jnp.bfloat16),
             pltpu.SemaphoreType.DMA((4 * blocks,)),
@@ -745,9 +750,9 @@
 
     _, inner, outer = sizes_of(seq_len)
     twin = owned // CPG * outer == width and 2 * inner == local_len and inner == outer
-    if owned % 16 == 0 and LANES % (2 * owned) == 0 and devices % 4 == 0 and twin:
+    if owned % 16 == 0 and LANES % (2 * owned) == 0 and devices % 4 == 0 and twin and width % (STEP * LANES) == 0:
         feats, message, edges = joined_features(turned, rim, short_filter, out_grad, owned)
-        filters, joined = transform_filters(long_filter, tables, seq_len, [tables["joined"]])
+        filters, joined = transform_filters(long_filter, tables, seq_len, jnp.bfloat16, [tables["joined"]])
         arrived = lax.all_to_all(message, EVERYONE, split_axis=0, concat_axis=0, tiled=True)
         edges, filters, joined, arrived = lax.optimization_barrier(
             (shifted(edges, EVERYONE, -1), filters, joined, arrived)

time: 93 us -> 91.2 us (0.981)
  local copies, waits for them, and re-layouts: 4.03 us -> 1.84 us
  waiting for transfers between devices: 51 us -> 52 us
    unnamed x27 -> x23, local copies, waits for them, and re-layouts: 4.03 us -> 1.84 us
    ppermute x2, waiting for transfers between devices: 9.59 us -> 10.6 us  [shifted(): lax.ppermute(value, axis, [(source, source + steps) for source in range(f...]
where the time goes in v11:
time: 91.2 us; the launch traced here: 90.1 us
  waiting for transfers between devices  52 us (57%)
  Pallas kernels  18.6 us (20%)
  starting transfers between devices  16.8 us (18%)
  local copies, waits for them, and re-layouts  1.84 us (2%)
    all_to_all x1, waiting for transfers between devices, shards(): lax.all_to_all(answer, EVERYONE, split_axis=0, concat_axis=0, tiled=True)  27.1 us
    pallas_call x3, Pallas kernels, whole_call(): pl.pallas_call(kernel, name=name, out_shape=out_shape, scratch_shapes=lis...  16.2 us
    all_to_all x1, waiting for transfers between devices, shards(): lax.all_to_all(message, EVERYONE, split_axis=0, concat_axis=0, tiled=True)  14.3 us
    ppermute x2, waiting for transfers between devices, shifted(): lax.ppermute(value, axis, [(source, source + steps) for source in range(f...  10.6 us
    ppermute x2, starting transfers between devices, shifted(): lax.ppermute(value, axis, [(source, source + steps) for source in range(f...  6.76 us
    all_to_all x1, starting transfers between devices, shards(): lax.all_to_all(message, EVERYONE, split_axis=0, concat_axis=0, tiled=True)  6.75 us
    all_to_all x1, starting transfers between devices, shards(): lax.all_to_all(answer, EVERYONE, split_axis=0, concat_axis=0, tiled=True)  3.33 us
    unnamed x23, local copies, waits for them, and re-layouts  1.84 us
  transfers between devices with their start and end apart: 4, of which 4 were waited for; matrix products, arithmetic and copies ran while one was open for 0% of the time, Pallas kernels for 3%

profile of v11, /device:TPU:1, one launch (start us, length us, event | category | flops | bytes accessed | tf_op | source)
XLA Modules:
  0.0 90.1 jit_solution(1686240902688778074)
XLA Ops:
  0.6 0.0 copy-start.1
  0.6 0.0 copy-start.5
  0.7 1.8 %copy.16 = bf16[3072,256]{0,1:T(8,128)(2,1)S(1)} copy(bf16[3072,256]{1,0:T(8,128)(2,1)} %param.11) | data formatting | bytes 3145728 | tf_op args[0]
  2.4 4.6 %collective-permute-start = (bf16[8,3072]{1,0:T(8,128)(2,1)S(1)}, bf16[8,3072]{1,0:T(8,128)(2,1)S(1)}, u32[]{:S(2)}, u32[]{:S(2)}) collective-permute-start(bf16[8,3072]{1,0:T(8,128)(2,1)S(1)} %slice.4), channel_id=1, source_target_pairs={{0,1},{1,2},{2,3},{3,4},{4,5},{5,6},{6,7},{7,8},{8,9},{9,10},{10,1... | collective-permute-start | bytes 147464 | tf_op jit(solution)/shard_map/ppermute | solution.py:21
  7.0 1.2 %collective-permute-done.rim_ref = bf16[8,3072]{1,0:T(8,128)(2,1)S(1)} collective-permute-done((bf16[8,3072]{1,0:T(8,128)(2,1)S(1)}, bf16[8,3072]{1,0:T(8,128)(2,1)S(1)}, u32[]{:S(2)}, u32[]{:S(2)}) %collective-permute-start) | collective-permute-done | bytes 49184 | tf_op jit(solution)/shard_map/ppermute | solution.py:21
  8.2 0.0 copy-done.1
  8.2 0.0 copy-done.5
  8.2 3.6 %joined_features.1 = (bf16[3072,256]{1,0:T(8,128)(2,1)}, bf16[32,64,256]{2,1,0:T(8,128)(2,1)}, bf16[8,3072]{1,0:T(8,128)(2,1)S(1)}) custom-call(bf16[256,3072]{1,0:T(8,128)(2,1)S(1)} %bitcast.2, bf16[8,3072]{1,0:T(8,128)(2,1)S(1)} %collective-permute-done.rim_ref, bf16[7,3072]{1,0:T(8,128)(2,1)S(1)} %copy-done.5, bf16[1024,256]{1,0:T(8,128)(2,1)S(1)} %copy-done.1), custom_call_target="tpu_custom_call" | custom-call | flops 10000000 | bytes 4000000 | tf_op jit(solution)/shard_map/joined_features/pallas_call | solution.py:285
  11.8 0.0 copy-start.2
  11.8 0.0 copy-start.3
  11.8 0.0 copy-start.4
  11.8 0.0 copy-start.7
  11.8 0.0 copy-start.8
  11.8 0.0 copy-start.9
  11.9 6.8 %all-to-all-start = ((bf16[32,64,256]{2,1,0:T(8,128)(2,1)}), bf16[32,64,256]{2,1,0:T(8,128)(2,1)S(1)}, u32[]{:S(2)}, u32[]{:S(2)}) async-start(bf16[32,64,256]{2,1,0:T(8,128)(2,1)} %get-tuple-element.22), calls=%async_computation | async-start | bytes 2097152 | tf_op jit(solution)/shard_map/all_to_all | solution.py:756
  18.6 2.2 %collective-permute-start.1 = (bf16[8,3072]{1,0:T(8,128)(2,1)S(1)}, bf16[8,3072]{1,0:T(8,128)(2,1)S(1)}, u32[]{:S(2)}, u32[]{:S(2)}) collective-permute-start(bf16[8,3072]{1,0:T(8,128)(2,1)S(1)} %get-tuple-element.19), channel_id=1, source_target_pairs={{1,0},{2,1},{3,2},{4,3},{5,4},{6,5},{7,6},{8,7},{9,8},{10,9},{11,1... | collective-permute-start | bytes 147464 | tf_op jit(solution)/shard_map/ppermute | solution.py:21
  20.8 0.0 copy-done.2
  20.8 0.0 copy-done.3
  20.8 0.0 copy-done.4
  20.8 0.0 copy-done.7
  20.8 0.0 copy-done.8
  20.8 0.0 copy-done.9
  20.9 1.1 %filter_dft.1 = (bf16[1024,256]{1,0:T(8,128)(2,1)S(1)}, bf16[768,256]{1,0:T(8,128)(2,1)S(1)}) custom-call(bf16[8,8192]{1,0:T(8,128)(2,1)S(1)} %copy-done.7, bf16[256,64]{1,0:T(8,128)(2,1)S(1)} %copy-done.9, bf16[256,256]{1,0:T(8,128)(2,1)S(1)} %copy-done.8, f32[128,128]{1,0:T(8,128)S(1)} %copy-done.4, f32[128,128]{1,0:T(8,128)S(1)} %copy-done.3, ...), custom_call_target="tpu_custom_call" | custom-call | flops 200000000 | bytes 2000000 | tf_op jit(solution)/shard_map/filter_dft/pallas_call | solution.py:114
  21.9 9.4 %collective-permute-done.1.edge_ref = bf16[8,3072]{1,0:T(8,128)(2,1)S(1)} collective-permute-done((bf16[8,3072]{1,0:T(8,128)(2,1)S(1)}, bf16[8,3072]{1,0:T(8,128)(2,1)S(1)}, u32[]{:S(2)}, u32[]{:S(2)}) %collective-permute-start.1) | collective-permute-done | bytes 49184 | tf_op jit(solution)/shard_map/ppermute | solution.py:21
  31.4 14.3 %all-to-all-done.x_ref = bf16[32,64,256]{2,1,0:T(8,128)(2,1)S(1)} async-done(((bf16[32,64,256]{2,1,0:T(8,128)(2,1)}), bf16[32,64,256]{2,1,0:T(8,128)(2,1)S(1)}, u32[]{:S(2)}, u32[]{:S(2)}) %all-to-all-start) | async-done | bytes 1048608 | tf_op jit(solution)/shard_map/all_to_all | solution.py:756
  45.6 6.9 %joined_filtering.1 = (bf16[32,136,128]{2,1,0:T(8,128)(2,1)}, bf16[1024,256]{1,0:T(8,128)(2,1)}) custom-call(bf16[32,64,256]{2,1,0:T(8,128)(2,1)S(1)} %all-to-all-done.x_ref, bf16[1024,256]{1,0:T(8,128)(2,1)S(1)} %get-tuple-element.24.f_ref, bf16[768,256]{1,0:T(8,128)(2,1)S(1)} %get-tuple-element.25.table_ref, f32[128,128]{1,0:T(8,128)S(1)} %copy-done.4, ...), custom_call_target="tpu_custom_call" | custom-call | flops 4000000000 | bytes 4000000 | tf_op jit(solution)/shard_map/joined_filtering/pallas_call | solution.py:285
  52.5 0.0 copy-start
  52.5 0.0 copy-start.6
  52.5 0.0 copy-start.10
  52.5 3.3 %all-to-all-start.1 = ((bf16[32,136,128]{2,1,0:T(8,128)(2,1)}), bf16[32,136,128]{2,1,0:T(8,128)(2,1)S(1)}, u32[]{:S(2)}, u32[]{:S(2)}) async-start(bf16[32,136,128]{2,1,0:T(8,128)(2,1)} %get-tuple-element.27), calls=%async_computation.1 | async-start | bytes 2228224 | tf_op jit(solution)/shard_map/all_to_all | solution.py:761
  55.9 0.0 copy-done
  55.9 0.0 copy-done.6
  55.9 0.0 copy-done.10
  55.9 1.3 %filter_gradient.1 = f32[8,8192]{1,0:T(8,128)} custom-call(bf16[1024,256]{1,0:T(8,128)(2,1)S(1)} %copy-done, bf16[256,256]{1,0:T(8,128)(2,1)S(1)} %copy-done.6, bf16[64,256]{1,0:T(8,128)(2,1)S(1)} %copy-done.10, f32[128,128]{1,0:T(8,128)S(1)} %copy-done.4, f32[128,128]{1,0:T(8,128)S(1)} %copy-done.3), custom_call_target="tpu_custom_call" | custom-call | flops 200000000 | bytes 2000000 | tf_op jit(solution)/shard_map/filter_gradient/pallas_call | solution.py:248
  57.2 27.1 %all-to-all-done.1.back_ref = bf16[32,136,128]{2,1,0:T(8,128)(2,1)S(1)} async-done(((bf16[32,136,128]{2,1,0:T(8,128)(2,1)}), bf16[32,136,128]{2,1,0:T(8,128)(2,1)S(1)}, u32[]{:S(2)}, u32[]{:S(2)}) %all-to-all-start.1) | async-done | bytes 1114144 | tf_op jit(solution)/shard_map/all_to_all | solution.py:761
  84.3 5.8 %joined_gradients.1 = (bf16[1024,256]{1,0:T(8,128)(2,1)}, bf16[3072,256]{1,0:T(8,128)(2,1)}) custom-call(bf16[1024,256]{1,0:T(8,128)(2,1)} %get-tuple-element.28.s_ref._, bf16[3072,256]{1,0:T(8,128)(2,1)} %get-tuple-element.29.f_hbm, bf16[8,3072]{1,0:T(8,128)(2,1)S(1)} %collective-permute-done.1.edge_ref, ...), custom_call_target="tpu_custom_call", output_to_operand_aliasing={{0}: (0, {}), {1}: (1, {})} | custom-call | flops 10000000 | bytes 4000000 | tf_op jit(solution)/shard_map/joined_gradients/pallas_call | solution.py:285
  (1 shorter events, 0.0 us)
Async XLA Ops:
  0.6 7.6 %copy-start.1 = (bf16[1024,256]{1,0:T(8,128)(2,1)S(1)}, bf16[1024,256]{1,0:T(8,128)(2,1)}, u32[]{:S(2)}) copy-start(bf16[1024,256]{1,0:T(8,128)(2,1)} %og_ref.3) | copy-start | bytes 1572868
  0.6 7.6 %copy-start.5 = (bf16[7,3072]{1,0:T(8,128)(2,1)S(1)}, bf16[7,3072]{1,0:T(8,128)(2,1)}, u32[]{:S(2)}) copy-start(bf16[7,3072]{1,0:T(8,128)(2,1)} %w_ref.3) | copy-start | bytes 129028
  2.4 5.8 %collective-permute-start = (bf16[8,3072]{1,0:T(8,128)(2,1)S(1)}, bf16[8,3072]{1,0:T(8,128)(2,1)S(1)}, u32[]{:S(2)}, u32[]{:S(2)}) collective-permute-start(bf16[8,3072]{1,0:T(8,128)(2,1)S(1)} %slice.4), channel_id=1, source_target_pairs={{0,1},{1,2},{2,3},{3,4},{4,5},{5,6},{6,7},{7,8},{8,9},{9,10},{10,1... | collective-permute-start | bytes 147464 | tf_op jit(solution)/shard_map/ppermute | solution.py:21
  11.8 9.0 %copy-start.2 = (bf16[768,256]{1,0:T(8,128)(2,1)S(1)}, bf16[768,256]{1,0:T(8,128)(2,1)}, u32[]{:S(2)}) copy-start(bf16[768,256]{1,0:T(8,128)(2,1)} %constant.24.refs_0_) | copy-start | bytes 1179652
  11.8 9.0 %copy-start.3 = (f32[128,128]{1,0:T(8,128)S(1)}, f32[128,128]{1,0:T(8,128)}, u32[]{:S(2)}) copy-start(f32[128,128]{1,0:T(8,128)} %constant.15.clone.ti_ref) | copy-start | bytes 196612
  11.8 9.0 %copy-start.4 = (f32[128,128]{1,0:T(8,128)S(1)}, f32[128,128]{1,0:T(8,128)}, u32[]{:S(2)}) copy-start(f32[128,128]{1,0:T(8,128)} %constant.14.clone.tr_ref) | copy-start | bytes 196612
  11.8 9.0 %copy-start.7 = (bf16[8,8192]{1,0:T(8,128)(2,1)S(1)}, bf16[8,8192]{1,0:T(8,128)(2,1)}, u32[]{:S(2)}) copy-start(bf16[8,8192]{1,0:T(8,128)(2,1)} %x_ref.1) | copy-start | bytes 393220
  11.8 9.0 %copy-start.8 = (bf16[256,256]{1,0:T(8,128)(2,1)S(1)}, bf16[256,256]{1,0:T(8,128)(2,1)}, u32[]{:S(2)}) copy-start(bf16[256,256]{1,0:T(8,128)(2,1)} %constant.23.second_ref) | copy-start | bytes 393220
  11.8 9.0 %copy-start.9 = (bf16[256,64]{1,0:T(8,128)(2,1)S(1)}, bf16[256,64]{1,0:T(8,128)(2,1)}, u32[]{:S(2)}) copy-start(bf16[256,64]{1,0:T(8,128)(2,1)} %constant.22.first_ref) | copy-start | bytes 98308
  11.9 33.8 %all-to-all-start = ((bf16[32,64,256]{2,1,0:T(8,128)(2,1)}), bf16[32,64,256]{2,1,0:T(8,128)(2,1)S(1)}, u32[]{:S(2)}, u32[]{:S(2)}) async-start(bf16[32,64,256]{2,1,0:T(8,128)(2,1)} %get-tuple-element.22), calls=%async_computation | async-start | bytes 2097152 | tf_op jit(solution)/shard_map/all_to_all | solution.py:756
  18.6 12.7 %collective-permute-start.1 = (bf16[8,3072]{1,0:T(8,128)(2,1)S(1)}, bf16[8,3072]{1,0:T(8,128)(2,1)S(1)}, u32[]{:S(2)}, u32[]{:S(2)}) collective-permute-start(bf16[8,3072]{1,0:T(8,128)(2,1)S(1)} %get-tuple-element.19), channel_id=1, source_target_pairs={{1,0},{2,1},{3,2},{4,3},{5,4},{6,5},{7,6},{8,7},{9,8},{10,9},{11,1... | collective-permute-start | bytes 147464 | tf_op jit(solution)/shard_map/ppermute | solution.py:21
  52.5 3.4 %copy-start = (bf16[1024,256]{1,0:T(8,128)(2,1)S(1)}, bf16[1024,256]{1,0:T(8,128)(2,1)}, u32[]{:S(2)}) copy-start(bf16[1024,256]{1,0:T(8,128)(2,1)} %get-tuple-element.28.s_ref._) | copy-start | bytes 1572868
  52.5 3.4 %copy-start.6 = (bf16[256,256]{1,0:T(8,128)(2,1)S(1)}, bf16[256,256]{1,0:T(8,128)(2,1)}, u32[]{:S(2)}) copy-start(bf16[256,256]{1,0:T(8,128)(2,1)} %constant.25.third_ref) | copy-start | bytes 393220
  52.5 3.4 %copy-start.10 = (bf16[64,256]{1,0:T(8,128)(2,1)S(1)}, bf16[64,256]{1,0:T(8,128)(2,1)}, u32[]{:S(2)}) copy-start(bf16[64,256]{1,0:T(8,128)(2,1)} %constant.26.fourth_ref) | copy-start | bytes 98308
  52.5 31.8 %all-to-all-start.1 = ((bf16[32,136,128]{2,1,0:T(8,128)(2,1)}), bf16[32,136,128]{2,1,0:T(8,128)(2,1)S(1)}, u32[]{:S(2)}, u32[]{:S(2)}) async-start(bf16[32,136,128]{2,1,0:T(8,128)(2,1)} %get-tuple-element.27), calls=%async_computation.1 | async-start | bytes 2228224 | tf_op jit(solution)/shard_map/all_to_all | solution.py:761

commit v12 on v11

--- a/solution.py
+++ b/solution.py
@@ -260,6 +260,7 @@
 
 RIM = 8
 STEP = 2
+BATCH = 2
 
 
 def seven_taps(tall, value, rim, weights, forward):
@@ -486,14 +487,19 @@
                     at = (g * PAIRS + p) * outer
                     stage[at : at + outer, :inner] = (f_re * tr + f_im * ti).astype(jnp.bfloat16)
                     stage[at : at + outer, inner:] = (f_im * tr - f_re * ti).astype(jnp.bfloat16)
+        batch = PAIRS * outer
         for g in range(groups):
+            if g % BATCH == 0:
+                rows = slice(g * batch, min(g + BATCH, groups) * batch)
+                k_many = dot(stages[0, rows, :], second_ref[...])
+                d_many = dot(stages[1, rows, :], second_ref[...])
             s_re = f_ref[g * outer : (g + 1) * outer, :inner].astype(jnp.float32)
             s_im = f_ref[g * outer : (g + 1) * outer, inner:].astype(jnp.float32)
             cross_re = cross_im = 0.0
             for p in range(PAIRS):
                 at = (g * PAIRS + p) * outer
-                k = dot(stages[0, at : at + outer, :], second_ref[...])
-                d = dot(stages[1, at : at + outer, :], second_ref[...])
+                here = slice((g % BATCH * PAIRS + p) * outer, (g % BATCH * PAIRS + p + 1) * outer)
+                k, d = k_many[here], d_many[here]
                 k_re, k_im = k[:, :inner], k[:, inner:]
                 d_re, d_im = d[:, :inner], d[:, inner:]
                 cross_re = cross_re + (k_re * d_re + k_im * d_im)
@@ -513,8 +519,9 @@
         for s in range(2):
             tall, stage, turn = talls.at[s], stages.at[s], turns.at[s]
             for pair in range(pairs):
-                at = pair * outer
-                h = dot(stage[at : at + outer, :], third_ref[...])
+                if pair % (BATCH * PAIRS) == 0:
+                    h_many = dot(stage[pair * outer : min(pair + BATCH * PAIRS, pairs) * outer, :], third_ref[...])
+                h = h_many[pair % (BATCH * PAIRS) * outer : (pair % (BATCH * PAIRS) + 1) * outer]
                 h_re, h_im = h[:, :inner], h[:, inner:]
                 lanes = slice(pair * inner, (pair + 1) * inner)
                 turn[:outer, lanes] = (h_re * tr - h_im * ti).astype(jnp.bfloat16)

time: 91.2 us -> 91.4 us (level)
  no operation moved by 1% of the time
where the time goes in v12:
time: 91.4 us; the launch traced here: 90.2 us
  waiting for transfers between devices  52 us (57%)
  Pallas kernels  18.7 us (20%)
  starting transfers between devices  16.9 us (18%)
  local copies, waits for them, and re-layouts  1.84 us (2%)
    all_to_all x1, waiting for transfers between devices, shards(): lax.all_to_all(answer, EVERYONE, split_axis=0, concat_axis=0, tiled=True)  27.1 us
    pallas_call x3, Pallas kernels, whole_call(): pl.pallas_call(kernel, name=name, out_shape=out_shape, scratch_shapes=lis...  16.3 us
    all_to_all x1, waiting for transfers between devices, shards(): lax.all_to_all(message, EVERYONE, split_axis=0, concat_axis=0, tiled=True)  14.3 us
    ppermute x2, waiting for transfers between devices, shifted(): lax.ppermute(value, axis, [(source, source + steps) for source in range(f...  10.6 us
    ppermute x2, starting transfers between devices, shifted(): lax.ppermute(value, axis, [(source, source + steps) for source in range(f...  6.76 us
    all_to_all x1, starting transfers between devices, shards(): lax.all_to_all(message, EVERYONE, split_axis=0, concat_axis=0, tiled=True)  6.75 us
    all_to_all x1, starting transfers between devices, shards(): lax.all_to_all(answer, EVERYONE, split_axis=0, concat_axis=0, tiled=True)  3.34 us
    unnamed x23, local copies, waits for them, and re-layouts  1.84 us
  transfers between devices with their start and end apart: 4, of which 4 were waited for; matrix products, arithmetic and copies ran while one was open for 0% of the time, Pallas kernels for 3%

profile of v12, /device:TPU:1, one launch (start us, length us, event | category | flops | bytes accessed | tf_op | source)
XLA Modules:
  0.0 90.2 jit_solution(5177701788177121008)
XLA Ops:
  0.6 0.0 copy-start.1
  0.6 0.0 copy-start.5
  0.7 1.8 %copy.16 = bf16[3072,256]{0,1:T(8,128)(2,1)S(1)} copy(bf16[3072,256]{1,0:T(8,128)(2,1)} %param.11) | data formatting | bytes 3145728 | tf_op args[0]
  2.4 4.6 %collective-permute-start = (bf16[8,3072]{1,0:T(8,128)(2,1)S(1)}, bf16[8,3072]{1,0:T(8,128)(2,1)S(1)}, u32[]{:S(2)}, u32[]{:S(2)}) collective-permute-start(bf16[8,3072]{1,0:T(8,128)(2,1)S(1)} %slice.4), channel_id=1, source_target_pairs={{0,1},{1,2},{2,3},{3,4},{4,5},{5,6},{6,7},{7,8},{8,9},{9,10},{10,1... | collective-permute-start | bytes 147464 | tf_op jit(solution)/shard_map/ppermute | solution.py:21
  7.0 1.2 %collective-permute-done.rim_ref = bf16[8,3072]{1,0:T(8,128)(2,1)S(1)} collective-permute-done((bf16[8,3072]{1,0:T(8,128)(2,1)S(1)}, bf16[8,3072]{1,0:T(8,128)(2,1)S(1)}, u32[]{:S(2)}, u32[]{:S(2)}) %collective-permute-start) | collective-permute-done | bytes 49184 | tf_op jit(solution)/shard_map/ppermute | solution.py:21
  8.2 0.0 copy-done.1
  8.2 0.0 copy-done.5
  8.2 3.6 %joined_features.1 = (bf16[3072,256]{1,0:T(8,128)(2,1)}, bf16[32,64,256]{2,1,0:T(8,128)(2,1)}, bf16[8,3072]{1,0:T(8,128)(2,1)S(1)}) custom-call(bf16[256,3072]{1,0:T(8,128)(2,1)S(1)} %bitcast.2, bf16[8,3072]{1,0:T(8,128)(2,1)S(1)} %collective-permute-done.rim_ref, bf16[7,3072]{1,0:T(8,128)(2,1)S(1)} %copy-done.5, bf16[1024,256]{1,0:T(8,128)(2,1)S(1)} %copy-done.1), custom_call_target="tpu_custom_call" | custom-call | flops 10000000 | bytes 4000000 | tf_op jit(solution)/shard_map/joined_features/pallas_call | solution.py:286
  11.8 0.0 copy-start.2
  11.8 0.0 copy-start.3
  11.8 0.0 copy-start.4
  11.8 0.0 copy-start.7
  11.8 0.0 copy-start.8
  11.8 0.0 copy-start.9
  11.9 6.8 %all-to-all-start = ((bf16[32,64,256]{2,1,0:T(8,128)(2,1)}), bf16[32,64,256]{2,1,0:T(8,128)(2,1)S(1)}, u32[]{:S(2)}, u32[]{:S(2)}) async-start(bf16[32,64,256]{2,1,0:T(8,128)(2,1)} %get-tuple-element.22), calls=%async_computation | async-start | bytes 2097152 | tf_op jit(solution)/shard_map/all_to_all | solution.py:763
  18.6 2.2 %collective-permute-start.1 = (bf16[8,3072]{1,0:T(8,128)(2,1)S(1)}, bf16[8,3072]{1,0:T(8,128)(2,1)S(1)}, u32[]{:S(2)}, u32[]{:S(2)}) collective-permute-start(bf16[8,3072]{1,0:T(8,128)(2,1)S(1)} %get-tuple-element.19), channel_id=1, source_target_pairs={{1,0},{2,1},{3,2},{4,3},{5,4},{6,5},{7,6},{8,7},{9,8},{10,9},{11,1... | collective-permute-start | bytes 147464 | tf_op jit(solution)/shard_map/ppermute | solution.py:21
  20.8 0.0 copy-done.2
  20.8 0.0 copy-done.3
  20.8 0.0 copy-done.4
  20.8 0.0 copy-done.7
  20.8 0.0 copy-done.8
  20.8 0.0 copy-done.9
  20.9 1.1 %filter_dft.1 = (bf16[1024,256]{1,0:T(8,128)(2,1)S(1)}, bf16[768,256]{1,0:T(8,128)(2,1)S(1)}) custom-call(bf16[8,8192]{1,0:T(8,128)(2,1)S(1)} %copy-done.7, bf16[256,64]{1,0:T(8,128)(2,1)S(1)} %copy-done.9, bf16[256,256]{1,0:T(8,128)(2,1)S(1)} %copy-done.8, f32[128,128]{1,0:T(8,128)S(1)} %copy-done.4, f32[128,128]{1,0:T(8,128)S(1)} %copy-done.3, ...), custom_call_target="tpu_custom_call" | custom-call | flops 200000000 | bytes 2000000 | tf_op jit(solution)/shard_map/filter_dft/pallas_call | solution.py:114
  21.9 9.4 %collective-permute-done.1.edge_ref = bf16[8,3072]{1,0:T(8,128)(2,1)S(1)} collective-permute-done((bf16[8,3072]{1,0:T(8,128)(2,1)S(1)}, bf16[8,3072]{1,0:T(8,128)(2,1)S(1)}, u32[]{:S(2)}, u32[]{:S(2)}) %collective-permute-start.1) | collective-permute-done | bytes 49184 | tf_op jit(solution)/shard_map/ppermute | solution.py:21
  31.4 14.3 %all-to-all-done.x_ref = bf16[32,64,256]{2,1,0:T(8,128)(2,1)S(1)} async-done(((bf16[32,64,256]{2,1,0:T(8,128)(2,1)}), bf16[32,64,256]{2,1,0:T(8,128)(2,1)S(1)}, u32[]{:S(2)}, u32[]{:S(2)}) %all-to-all-start) | async-done | bytes 1048608 | tf_op jit(solution)/shard_map/all_to_all | solution.py:763
  45.6 7.0 %joined_filtering.1 = (bf16[32,136,128]{2,1,0:T(8,128)(2,1)}, bf16[1024,256]{1,0:T(8,128)(2,1)}) custom-call(bf16[32,64,256]{2,1,0:T(8,128)(2,1)S(1)} %all-to-all-done.x_ref, bf16[1024,256]{1,0:T(8,128)(2,1)S(1)} %get-tuple-element.24.f_ref, bf16[768,256]{1,0:T(8,128)(2,1)S(1)} %get-tuple-element.25.table_ref, f32[128,128]{1,0:T(8,128)S(1)} %copy-done.4, ...), custom_call_target="tpu_custom_call" | custom-call | flops 4000000000 | bytes 4000000 | tf_op jit(solution)/shard_map/joined_filtering/pallas_call | solution.py:286
  52.6 0.0 copy-start
  52.6 0.0 copy-start.6
  52.6 0.0 copy-start.10
  52.6 3.3 %all-to-all-start.1 = ((bf16[32,136,128]{2,1,0:T(8,128)(2,1)}), bf16[32,136,128]{2,1,0:T(8,128)(2,1)S(1)}, u32[]{:S(2)}, u32[]{:S(2)}) async-start(bf16[32,136,128]{2,1,0:T(8,128)(2,1)} %get-tuple-element.27), calls=%async_computation.1 | async-start | bytes 2228224 | tf_op jit(solution)/shard_map/all_to_all | solution.py:768
  56.0 0.0 copy-done
  56.0 0.0 copy-done.6
  56.0 0.0 copy-done.10
  56.0 1.3 %filter_gradient.1 = f32[8,8192]{1,0:T(8,128)} custom-call(bf16[1024,256]{1,0:T(8,128)(2,1)S(1)} %copy-done, bf16[256,256]{1,0:T(8,128)(2,1)S(1)} %copy-done.6, bf16[64,256]{1,0:T(8,128)(2,1)S(1)} %copy-done.10, f32[128,128]{1,0:T(8,128)S(1)} %copy-done.4, f32[128,128]{1,0:T(8,128)S(1)} %copy-done.3), custom_call_target="tpu_custom_call" | custom-call | flops 200000000 | bytes 2000000 | tf_op jit(solution)/shard_map/filter_gradient/pallas_call | solution.py:248
  57.3 27.1 %all-to-all-done.1.back_ref = bf16[32,136,128]{2,1,0:T(8,128)(2,1)S(1)} async-done(((bf16[32,136,128]{2,1,0:T(8,128)(2,1)}), bf16[32,136,128]{2,1,0:T(8,128)(2,1)S(1)}, u32[]{:S(2)}, u32[]{:S(2)}) %all-to-all-start.1) | async-done | bytes 1114144 | tf_op jit(solution)/shard_map/all_to_all | solution.py:768
  84.4 5.8 %joined_gradients.1 = (bf16[1024,256]{1,0:T(8,128)(2,1)}, bf16[3072,256]{1,0:T(8,128)(2,1)}) custom-call(bf16[1024,256]{1,0:T(8,128)(2,1)} %get-tuple-element.28.s_ref._, bf16[3072,256]{1,0:T(8,128)(2,1)} %get-tuple-element.29.f_hbm, bf16[8,3072]{1,0:T(8,128)(2,1)S(1)} %collective-permute-done.1.edge_ref, ...), custom_call_target="tpu_custom_call", output_to_operand_aliasing={{0}: (0, {}), {1}: (1, {})} | custom-call | flops 10000000 | bytes 4000000 | tf_op jit(solution)/shard_map/joined_gradients/pallas_call | solution.py:286
  (1 shorter events, 0.0 us)
Async XLA Ops:
  0.6 7.6 %copy-start.1 = (bf16[1024,256]{1,0:T(8,128)(2,1)S(1)}, bf16[1024,256]{1,0:T(8,128)(2,1)}, u32[]{:S(2)}) copy-start(bf16[1024,256]{1,0:T(8,128)(2,1)} %og_ref.3) | copy-start | bytes 1572868
  0.6 7.6 %copy-start.5 = (bf16[7,3072]{1,0:T(8,128)(2,1)S(1)}, bf16[7,3072]{1,0:T(8,128)(2,1)}, u32[]{:S(2)}) copy-start(bf16[7,3072]{1,0:T(8,128)(2,1)} %w_ref.3) | copy-start | bytes 129028
  2.4 5.8 %collective-permute-start = (bf16[8,3072]{1,0:T(8,128)(2,1)S(1)}, bf16[8,3072]{1,0:T(8,128)(2,1)S(1)}, u32[]{:S(2)}, u32[]{:S(2)}) collective-permute-start(bf16[8,3072]{1,0:T(8,128)(2,1)S(1)} %slice.4), channel_id=1, source_target_pairs={{0,1},{1,2},{2,3},{3,4},{4,5},{5,6},{6,7},{7,8},{8,9},{9,10},{10,1... | collective-permute-start | bytes 147464 | tf_op jit(solution)/shard_map/ppermute | solution.py:21
  11.8 9.0 %copy-start.2 = (bf16[768,256]{1,0:T(8,128)(2,1)S(1)}, bf16[768,256]{1,0:T(8,128)(2,1)}, u32[]{:S(2)}) copy-start(bf16[768,256]{1,0:T(8,128)(2,1)} %constant.24.refs_0_) | copy-start | bytes 1179652
  11.8 9.0 %copy-start.3 = (f32[128,128]{1,0:T(8,128)S(1)}, f32[128,128]{1,0:T(8,128)}, u32[]{:S(2)}) copy-start(f32[128,128]{1,0:T(8,128)} %constant.15.clone.ti_ref) | copy-start | bytes 196612
  11.8 9.0 %copy-start.4 = (f32[128,128]{1,0:T(8,128)S(1)}, f32[128,128]{1,0:T(8,128)}, u32[]{:S(2)}) copy-start(f32[128,128]{1,0:T(8,128)} %constant.14.clone.tr_ref) | copy-start | bytes 196612
  11.8 9.0 %copy-start.7 = (bf16[8,8192]{1,0:T(8,128)(2,1)S(1)}, bf16[8,8192]{1,0:T(8,128)(2,1)}, u32[]{:S(2)}) copy-start(bf16[8,8192]{1,0:T(8,128)(2,1)} %x_ref.1) | copy-start | bytes 393220
  11.8 9.0 %copy-start.8 = (bf16[256,256]{1,0:T(8,128)(2,1)S(1)}, bf16[256,256]{1,0:T(8,128)(2,1)}, u32[]{:S(2)}) copy-start(bf16[256,256]{1,0:T(8,128)(2,1)} %constant.23.second_ref) | copy-start | bytes 393220
  11.8 9.0 %copy-start.9 = (bf16[256,64]{1,0:T(8,128)(2,1)S(1)}, bf16[256,64]{1,0:T(8,128)(2,1)}, u32[]{:S(2)}) copy-start(bf16[256,64]{1,0:T(8,128)(2,1)} %constant.22.first_ref) | copy-start | bytes 98308
  11.9 33.8 %all-to-all-start = ((bf16[32,64,256]{2,1,0:T(8,128)(2,1)}), bf16[32,64,256]{2,1,0:T(8,128)(2,1)S(1)}, u32[]{:S(2)}, u32[]{:S(2)}) async-start(bf16[32,64,256]{2,1,0:T(8,128)(2,1)} %get-tuple-element.22), calls=%async_computation | async-start | bytes 2097152 | tf_op jit(solution)/shard_map/all_to_all | solution.py:763
  18.6 12.7 %collective-permute-start.1 = (bf16[8,3072]{1,0:T(8,128)(2,1)S(1)}, bf16[8,3072]{1,0:T(8,128)(2,1)S(1)}, u32[]{:S(2)}, u32[]{:S(2)}) collective-permute-start(bf16[8,3072]{1,0:T(8,128)(2,1)S(1)} %get-tuple-element.19), channel_id=1, source_target_pairs={{1,0},{2,1},{3,2},{4,3},{5,4},{6,5},{7,6},{8,7},{9,8},{10,9},{11,1... | collective-permute-start | bytes 147464 | tf_op jit(solution)/shard_map/ppermute | solution.py:21
  52.6 3.4 %copy-start = (bf16[1024,256]{1,0:T(8,128)(2,1)S(1)}, bf16[1024,256]{1,0:T(8,128)(2,1)}, u32[]{:S(2)}) copy-start(bf16[1024,256]{1,0:T(8,128)(2,1)} %get-tuple-element.28.s_ref._) | copy-start | bytes 1572868
  52.6 3.4 %copy-start.6 = (bf16[256,256]{1,0:T(8,128)(2,1)S(1)}, bf16[256,256]{1,0:T(8,128)(2,1)}, u32[]{:S(2)}) copy-start(bf16[256,256]{1,0:T(8,128)(2,1)} %constant.25.third_ref) | copy-start | bytes 393220
  52.6 3.4 %copy-start.10 = (bf16[64,256]{1,0:T(8,128)(2,1)S(1)}, bf16[64,256]{1,0:T(8,128)(2,1)}, u32[]{:S(2)}) copy-start(bf16[64,256]{1,0:T(8,128)(2,1)} %constant.26.fourth_ref) | copy-start | bytes 98308
  52.6 31.8 %all-to-all-start.1 = ((bf16[32,136,128]{2,1,0:T(8,128)(2,1)}), bf16[32,136,128]{2,1,0:T(8,128)(2,1)S(1)}, u32[]{:S(2)}, u32[]{:S(2)}) async-start(bf16[32,136,128]{2,1,0:T(8,128)(2,1)} %get-tuple-element.27), calls=%async_computation.1 | async-start | bytes 2228224 | tf_op jit(solution)/shard_map/all_to_all | solution.py:768

commit v13 on v11

--- a/solution.py
+++ b/solution.py
@@ -374,19 +374,18 @@
 def joined_features(turned, rim, short_filter, out_grad, owned):
     width, local = out_grad.shape
     near = LANES // owned
-    blocks = width // LANES
+    steps = width // LANES // STEP
 
     def kernel(x_ref, rim_ref, w_ref, og_ref, f_hbm, msg_ref, edge_ref, tall, made, f_ref, edge, sent):
-        def copy(i):
-            to = pl.ds(i * near, near)
-            return pltpu.make_async_copy(made.at[to], msg_ref.at[to], sent.at[i])
-
-        def keep(part, i):
-            at = part * blocks + i
-            to = pl.ds(pl.multiple_of(at * LANES, LANES), LANES)
-            return pltpu.make_async_copy(f_ref.at[at], f_hbm.at[to, :], sent.at[blocks + at])
-
-        @pl.loop(0, blocks // STEP)
+        def copy(step):
+            to = pl.ds(step * STEP * near, STEP * near)
+            return pltpu.make_async_copy(made.at[to], msg_ref.at[to], sent.at[step])
+
+        def keep(part, step):
+            to = pl.ds(pl.multiple_of(part * width + step * STEP * LANES, STEP * LANES), STEP * LANES)
+            return pltpu.make_async_copy(f_ref.at[to, :], f_hbm.at[to, :], sent.at[(1 + part) * steps + step])
+
+        @pl.loop(0, steps)
         def _(step):
             for slot in range(STEP):
                 i = step * STEP + slot
@@ -401,7 +400,7 @@
                         True,
                     ).astype(jnp.bfloat16)
                     for t in range(local // LANES):
-                        f_ref[part * blocks + i, :, t * LANES : (t + 1) * LANES] = total[t * LANES : (t + 1) * LANES]
+                        f_ref[lanes, t * LANES : (t + 1) * LANES] = total[t * LANES : (t + 1) * LANES]
                     if part:
                         edge[:, lanes] = total[:RIM]
                     parts.append(total.astype(jnp.float32))
@@ -412,19 +411,18 @@
                 to = pl.ds(i * near, near)
                 made[to, :owned, :] = kv.reshape(near, owned, local)
                 made[to, owned:, :] = dconv.reshape(near, owned, local)
-            for slot in range(STEP):
-                copy(step * STEP + slot).start()
-                for part in range(3):
-                    keep(part, step * STEP + slot).start()
-
-        last = pltpu.make_async_copy(edge, edge_ref, sent.at[4 * blocks])
+            copy(step).start()
+            for part in range(3):
+                keep(part, step).start()
+
+        last = pltpu.make_async_copy(edge, edge_ref, sent.at[4 * steps])
         last.start()
 
-        @pl.loop(0, blocks)
-        def _(i):
-            copy(i).wait()
+        @pl.loop(0, steps)
+        def _(step):
+            copy(step).wait()
             for part in range(3):
-                keep(part, i).wait()
+                keep(part, step).wait()
 
         last.wait()
 
@@ -439,9 +437,9 @@
         [
             pltpu.VMEM((3 * STEP, local + RIM, LANES), jnp.float32),
             pltpu.VMEM((devices, 2 * owned, local), jnp.bfloat16),
-            pltpu.VMEM((3 * blocks, LANES, local), jnp.bfloat16),
+            pltpu.VMEM((3 * width, local), jnp.bfloat16),
             pltpu.VMEM((RIM, 3 * width), jnp.bfloat16),
-            pltpu.SemaphoreType.DMA((4 * blocks + 1,)),
+            pltpu.SemaphoreType.DMA((4 * steps + 1,)),
         ],
         in_specs=[vmem] * 4,
         out_specs=(hbm, hbm, hbm),
@@ -584,32 +582,32 @@
     width, local = out_grad.shape
     tiles = local // LANES
     near = LANES // owned
-    blocks = width // LANES
+    steps = width // LANES // STEP
 
     def kernel(_, f_hbm, edge_ref, back_ref, og_ref, w_ref, mixed_ref, out_ref, tall, made, f_ref, sent, fetched):
-        def fetch(part, i):
-            at = part * blocks + i
-            rows = pl.ds(pl.multiple_of(at * LANES, LANES), LANES)
-            return pltpu.make_async_copy(f_hbm.at[rows, :], f_ref.at[at], fetched.at[at])
-
-        @pl.loop(0, blocks)
-        def _(i):
+        def step_rows(part, step):
+            return pl.ds(pl.multiple_of(part * width + step * STEP * LANES, STEP * LANES), STEP * LANES)
+
+        def fetch(part, step):
+            rows = step_rows(part, step)
+            return pltpu.make_async_copy(f_hbm.at[rows, :], f_ref.at[rows, :], fetched.at[part * steps + step])
+
+        @pl.loop(0, steps)
+        def _(step):
             for part in range(3):
-                fetch(part, i).start()
+                fetch(part, step).start()
 
         def features(part, i):
-            held = [f_ref[part * blocks + i, :, t * LANES : (t + 1) * LANES] for t in range(tiles)]
+            rows = lane_block(i, part * width)
+            held = [f_ref[rows, t * LANES : (t + 1) * LANES] for t in range(tiles)]
             return jnp.concatenate(held, axis=0).astype(jnp.float32)
 
         lane = lax.broadcasted_iota(jnp.int32, (RIM, LANES), 1)
 
-        def copy(part, i):
-            at = part * blocks + i
-            if part < 3:
-                to = out_ref.at[pl.ds(pl.multiple_of(at * LANES, LANES), LANES), :]
-            else:
-                to = mixed_ref.at[lane_block(i), :]
-            return pltpu.make_async_copy(made.at[at], to, sent.at[at])
+        def copy(part, step):
+            rows = step_rows(part, step)
+            to = out_ref.at[rows, :] if part < 3 else mixed_ref.at[step_rows(0, step), :]
+            return pltpu.make_async_copy(made.at[rows, :], to, sent.at[part * steps + step])
 
         def turned(s, i):
             held = pl.ds(i * near, near)
@@ -638,30 +636,28 @@
                 w_ref[:, lane_block(i, part * width)].astype(jnp.float32),
                 False,
             )
-            made[part * blocks + i] = total.astype(jnp.bfloat16).T
-
-        @pl.loop(0, blocks // STEP)
+            made[lane_block(i, part * width), :] = total.astype(jnp.bfloat16).T
+
+        @pl.loop(0, steps)
         def _(step):
-            for slot in range(STEP):
-                for part in range(3):
-                    fetch(part, step * STEP + slot).wait()
+            for part in range(3):
+                fetch(part, step).wait()
             for slot in range(STEP):
                 i = step * STEP + slot
                 query, key, value = [features(part, i) for part in range(3)]
                 conv = turned(0, i)
-                made[3 * blocks + i] = (query * conv).astype(jnp.bfloat16).T
+                made[lane_block(i, 3 * width), :] = (query * conv).astype(jnp.bfloat16).T
                 third(0, slot, i, conv, rim_of(0, i), og_ref[lane_block(i), :].T.astype(jnp.float32))
                 back, rim = turned(1, i), rim_of(1, i)
                 third(1, slot, i, back, rim, value)
                 third(2, slot, i, back, rim, key)
-            for slot in range(STEP):
-                for part in range(4):
-                    copy(part, step * STEP + slot).start()
-
-        @pl.loop(0, blocks)
-        def _(i):
             for part in range(4):
-                copy(part, i).wait()
+                copy(part, step).start()
+
+        @pl.loop(0, steps)
+        def _(step):
+            for part in range(4):
+                copy(part, step).wait()
 
     vmem = pl.BlockSpec(memory_space=pltpu.VMEM)
     hbm = pl.BlockSpec(memory_space=pltpu.HBM)
@@ -672,10 +668,10 @@
         (cross, feats, edges, returned, out_grad, short_filter),
         [
             pltpu.VMEM((3 * STEP, local + RIM, LANES), jnp.float32),
-            pltpu.VMEM((4 * blocks, LANES, local), jnp.bfloat16),
-            pltpu.VMEM((3 * blocks, LANES, local), jnp.bfloat16),
-            pltpu.SemaphoreType.DMA((4 * blocks,)),
-            pltpu.SemaphoreType.DMA((3 * blocks,)),
+            pltpu.VMEM((4 * width, local), jnp.bfloat16),
+            pltpu.VMEM((3 * width, local), jnp.bfloat16),
+            pltpu.SemaphoreType.DMA((4 * steps,)),
+            pltpu.SemaphoreType.DMA((3 * steps,)),
         ],
         in_specs=[hbm, hbm] + [vmem] * 4,
         out_specs=(hbm, hbm),

time: 91.2 us -> 91.1 us (level)
  no operation moved by 1% of the time
where the time goes in v13:
time: 91.1 us; the launch traced here: 90 us
  waiting for transfers between devices  52 us (57%)
  Pallas kernels  18.5 us (20%)
  starting transfers between devices  16.9 us (19%)
  local copies, waits for them, and re-layouts  1.84 us (2%)
    all_to_all x1, waiting for transfers between devices, shards(): lax.all_to_all(answer, EVERYONE, split_axis=0, concat_axis=0, tiled=True)  27.1 us
    pallas_call x3, Pallas kernels, whole_call(): pl.pallas_call(kernel, name=name, out_shape=out_shape, scratch_shapes=lis...  16.1 us
    all_to_all x1, waiting for transfers between devices, shards(): lax.all_to_all(message, EVERYONE, split_axis=0, concat_axis=0, tiled=True)  14.3 us
    ppermute x2, waiting for transfers between devices, shifted(): lax.ppermute(value, axis, [(source, source + steps) for source in range(f...  10.6 us
    ppermute x2, starting transfers between devices, shifted(): lax.ppermute(value, axis, [(source, source + steps) for source in range(f...  6.76 us
    all_to_all x1, starting transfers between devices, shards(): lax.all_to_all(message, EVERYONE, split_axis=0, concat_axis=0, tiled=True)  6.75 us
    all_to_all x1, starting transfers between devices, shards(): lax.all_to_all(answer, EVERYONE, split_axis=0, concat_axis=0, tiled=True)  3.34 us
    unnamed x23, local copies, waits for them, and re-layouts  1.84 us
  transfers between devices with their start and end apart: 4, of which 4 were waited for; matrix products, arithmetic and copies ran while one was open for 0% of the time, Pallas kernels for 3%

profile of v13, /device:TPU:1, one launch (start us, length us, event | category | flops | bytes accessed | tf_op | source)
XLA Modules:
  0.0 90.0 jit_solution(3608831039042380702)
XLA Ops:
  0.6 0.0 copy-start.1
  0.6 0.0 copy-start.5
  0.7 1.8 %copy.16 = bf16[3072,256]{0,1:T(8,128)(2,1)S(1)} copy(bf16[3072,256]{1,0:T(8,128)(2,1)} %param.11) | data formatting | bytes 3145728 | tf_op args[0]
  2.4 4.6 %collective-permute-start = (bf16[8,3072]{1,0:T(8,128)(2,1)S(1)}, bf16[8,3072]{1,0:T(8,128)(2,1)S(1)}, u32[]{:S(2)}, u32[]{:S(2)}) collective-permute-start(bf16[8,3072]{1,0:T(8,128)(2,1)S(1)} %slice.4), channel_id=1, source_target_pairs={{0,1},{1,2},{2,3},{3,4},{4,5},{5,6},{6,7},{7,8},{8,9},{9,10},{10,1... | collective-permute-start | bytes 147464 | tf_op jit(solution)/shard_map/ppermute | solution.py:21
  7.0 1.2 %collective-permute-done.rim_ref = bf16[8,3072]{1,0:T(8,128)(2,1)S(1)} collective-permute-done((bf16[8,3072]{1,0:T(8,128)(2,1)S(1)}, bf16[8,3072]{1,0:T(8,128)(2,1)S(1)}, u32[]{:S(2)}, u32[]{:S(2)}) %collective-permute-start) | collective-permute-done | bytes 49184 | tf_op jit(solution)/shard_map/ppermute | solution.py:21
  8.2 0.0 copy-done.1
  8.2 0.0 copy-done.5
  8.2 3.7 %joined_features.1 = (bf16[3072,256]{1,0:T(8,128)(2,1)}, bf16[32,64,256]{2,1,0:T(8,128)(2,1)}, bf16[8,3072]{1,0:T(8,128)(2,1)S(1)}) custom-call(bf16[256,3072]{1,0:T(8,128)(2,1)S(1)} %bitcast.2, bf16[8,3072]{1,0:T(8,128)(2,1)S(1)} %collective-permute-done.rim_ref, bf16[7,3072]{1,0:T(8,128)(2,1)S(1)} %copy-done.5, bf16[1024,256]{1,0:T(8,128)(2,1)S(1)} %copy-done.1), custom_call_target="tpu_custom_call" | custom-call | flops 10000000 | bytes 4000000 | tf_op jit(solution)/shard_map/joined_features/pallas_call | solution.py:285
  11.9 0.0 copy-start.2
  11.9 0.0 copy-start.3
  11.9 0.0 copy-start.4
  12.0 0.0 copy-start.7
  12.0 0.0 copy-start.8
  12.0 0.0 copy-start.9
  12.0 6.8 %all-to-all-start = ((bf16[32,64,256]{2,1,0:T(8,128)(2,1)}), bf16[32,64,256]{2,1,0:T(8,128)(2,1)S(1)}, u32[]{:S(2)}, u32[]{:S(2)}) async-start(bf16[32,64,256]{2,1,0:T(8,128)(2,1)} %get-tuple-element.22), calls=%async_computation | async-start | bytes 2097152 | tf_op jit(solution)/shard_map/all_to_all | solution.py:752
  18.8 2.2 %collective-permute-start.1 = (bf16[8,3072]{1,0:T(8,128)(2,1)S(1)}, bf16[8,3072]{1,0:T(8,128)(2,1)S(1)}, u32[]{:S(2)}, u32[]{:S(2)}) collective-permute-start(bf16[8,3072]{1,0:T(8,128)(2,1)S(1)} %get-tuple-element.19), channel_id=1, source_target_pairs={{1,0},{2,1},{3,2},{4,3},{5,4},{6,5},{7,6},{8,7},{9,8},{10,9},{11,1... | collective-permute-start | bytes 147464 | tf_op jit(solution)/shard_map/ppermute | solution.py:21
  20.9 0.0 copy-done.2
  20.9 0.0 copy-done.3
  21.0 0.0 copy-done.4
  21.0 0.0 copy-done.7
  21.0 0.0 copy-done.8
  21.0 0.0 copy-done.9
  21.0 1.1 %filter_dft.1 = (bf16[1024,256]{1,0:T(8,128)(2,1)S(1)}, bf16[768,256]{1,0:T(8,128)(2,1)S(1)}) custom-call(bf16[8,8192]{1,0:T(8,128)(2,1)S(1)} %copy-done.7, bf16[256,64]{1,0:T(8,128)(2,1)S(1)} %copy-done.9, bf16[256,256]{1,0:T(8,128)(2,1)S(1)} %copy-done.8, f32[128,128]{1,0:T(8,128)S(1)} %copy-done.4, f32[128,128]{1,0:T(8,128)S(1)} %copy-done.3, ...), custom_call_target="tpu_custom_call" | custom-call | flops 200000000 | bytes 2000000 | tf_op jit(solution)/shard_map/filter_dft/pallas_call | solution.py:114
  22.1 9.4 %collective-permute-done.1.edge_ref = bf16[8,3072]{1,0:T(8,128)(2,1)S(1)} collective-permute-done((bf16[8,3072]{1,0:T(8,128)(2,1)S(1)}, bf16[8,3072]{1,0:T(8,128)(2,1)S(1)}, u32[]{:S(2)}, u32[]{:S(2)}) %collective-permute-start.1) | collective-permute-done | bytes 49184 | tf_op jit(solution)/shard_map/ppermute | solution.py:21
  31.5 14.3 %all-to-all-done.x_ref = bf16[32,64,256]{2,1,0:T(8,128)(2,1)S(1)} async-done(((bf16[32,64,256]{2,1,0:T(8,128)(2,1)}), bf16[32,64,256]{2,1,0:T(8,128)(2,1)S(1)}, u32[]{:S(2)}, u32[]{:S(2)}) %all-to-all-start) | async-done | bytes 1048608 | tf_op jit(solution)/shard_map/all_to_all | solution.py:752
  45.8 6.9 %joined_filtering.1 = (bf16[32,136,128]{2,1,0:T(8,128)(2,1)}, bf16[1024,256]{1,0:T(8,128)(2,1)}) custom-call(bf16[32,64,256]{2,1,0:T(8,128)(2,1)S(1)} %all-to-all-done.x_ref, bf16[1024,256]{1,0:T(8,128)(2,1)S(1)} %get-tuple-element.24.f_ref, bf16[768,256]{1,0:T(8,128)(2,1)S(1)} %get-tuple-element.25.table_ref, f32[128,128]{1,0:T(8,128)S(1)} %copy-done.4, ...), custom_call_target="tpu_custom_call" | custom-call | flops 4000000000 | bytes 4000000 | tf_op jit(solution)/shard_map/joined_filtering/pallas_call | solution.py:285
  52.6 0.0 copy-start
  52.6 0.0 copy-start.6
  52.6 0.0 copy-start.10
  52.7 3.3 %all-to-all-start.1 = ((bf16[32,136,128]{2,1,0:T(8,128)(2,1)}), bf16[32,136,128]{2,1,0:T(8,128)(2,1)S(1)}, u32[]{:S(2)}, u32[]{:S(2)}) async-start(bf16[32,136,128]{2,1,0:T(8,128)(2,1)} %get-tuple-element.27), calls=%async_computation.1 | async-start | bytes 2228224 | tf_op jit(solution)/shard_map/all_to_all | solution.py:757
  56.0 0.0 copy-done
  56.0 0.0 copy-done.6
  56.0 0.0 copy-done.10
  56.0 1.3 %filter_gradient.1 = f32[8,8192]{1,0:T(8,128)} custom-call(bf16[1024,256]{1,0:T(8,128)(2,1)S(1)} %copy-done, bf16[256,256]{1,0:T(8,128)(2,1)S(1)} %copy-done.6, bf16[64,256]{1,0:T(8,128)(2,1)S(1)} %copy-done.10, f32[128,128]{1,0:T(8,128)S(1)} %copy-done.4, f32[128,128]{1,0:T(8,128)S(1)} %copy-done.3), custom_call_target="tpu_custom_call" | custom-call | flops 200000000 | bytes 2000000 | tf_op jit(solution)/shard_map/filter_gradient/pallas_call | solution.py:248
  57.3 27.1 %all-to-all-done.1.back_ref = bf16[32,136,128]{2,1,0:T(8,128)(2,1)S(1)} async-done(((bf16[32,136,128]{2,1,0:T(8,128)(2,1)}), bf16[32,136,128]{2,1,0:T(8,128)(2,1)S(1)}, u32[]{:S(2)}, u32[]{:S(2)}) %all-to-all-start.1) | async-done | bytes 1114144 | tf_op jit(solution)/shard_map/all_to_all | solution.py:757
  84.5 5.5 %joined_gradients.1 = (bf16[1024,256]{1,0:T(8,128)(2,1)}, bf16[3072,256]{1,0:T(8,128)(2,1)}) custom-call(bf16[1024,256]{1,0:T(8,128)(2,1)} %get-tuple-element.28.s_ref._, bf16[3072,256]{1,0:T(8,128)(2,1)} %get-tuple-element.29.f_hbm, bf16[8,3072]{1,0:T(8,128)(2,1)S(1)} %collective-permute-done.1.edge_ref, ...), custom_call_target="tpu_custom_call", output_to_operand_aliasing={{0}: (0, {}), {1}: (1, {})} | custom-call | flops 10000000 | bytes 4000000 | tf_op jit(solution)/shard_map/joined_gradients/pallas_call | solution.py:285
  (1 shorter events, 0.0 us)
Async XLA Ops:
  0.6 7.6 %copy-start.1 = (bf16[1024,256]{1,0:T(8,128)(2,1)S(1)}, bf16[1024,256]{1,0:T(8,128)(2,1)}, u32[]{:S(2)}) copy-start(bf16[1024,256]{1,0:T(8,128)(2,1)} %og_ref.3) | copy-start | bytes 1572868
  0.6 7.6 %copy-start.5 = (bf16[7,3072]{1,0:T(8,128)(2,1)S(1)}, bf16[7,3072]{1,0:T(8,128)(2,1)}, u32[]{:S(2)}) copy-start(bf16[7,3072]{1,0:T(8,128)(2,1)} %w_ref.3) | copy-start | bytes 129028
  2.4 5.8 %collective-permute-start = (bf16[8,3072]{1,0:T(8,128)(2,1)S(1)}, bf16[8,3072]{1,0:T(8,128)(2,1)S(1)}, u32[]{:S(2)}, u32[]{:S(2)}) collective-permute-start(bf16[8,3072]{1,0:T(8,128)(2,1)S(1)} %slice.4), channel_id=1, source_target_pairs={{0,1},{1,2},{2,3},{3,4},{4,5},{5,6},{6,7},{7,8},{8,9},{9,10},{10,1... | collective-permute-start | bytes 147464 | tf_op jit(solution)/shard_map/ppermute | solution.py:21
  11.9 9.0 %copy-start.2 = (bf16[768,256]{1,0:T(8,128)(2,1)S(1)}, bf16[768,256]{1,0:T(8,128)(2,1)}, u32[]{:S(2)}) copy-start(bf16[768,256]{1,0:T(8,128)(2,1)} %constant.24.refs_0_) | copy-start | bytes 1179652
  11.9 9.0 %copy-start.3 = (f32[128,128]{1,0:T(8,128)S(1)}, f32[128,128]{1,0:T(8,128)}, u32[]{:S(2)}) copy-start(f32[128,128]{1,0:T(8,128)} %constant.15.clone.ti_ref) | copy-start | bytes 196612
  11.9 9.0 %copy-start.4 = (f32[128,128]{1,0:T(8,128)S(1)}, f32[128,128]{1,0:T(8,128)}, u32[]{:S(2)}) copy-start(f32[128,128]{1,0:T(8,128)} %constant.14.clone.tr_ref) | copy-start | bytes 196612
  12.0 9.0 %copy-start.7 = (bf16[8,8192]{1,0:T(8,128)(2,1)S(1)}, bf16[8,8192]{1,0:T(8,128)(2,1)}, u32[]{:S(2)}) copy-start(bf16[8,8192]{1,0:T(8,128)(2,1)} %x_ref.1) | copy-start | bytes 393220
  12.0 9.0 %copy-start.8 = (bf16[256,256]{1,0:T(8,128)(2,1)S(1)}, bf16[256,256]{1,0:T(8,128)(2,1)}, u32[]{:S(2)}) copy-start(bf16[256,256]{1,0:T(8,128)(2,1)} %constant.23.second_ref) | copy-start | bytes 393220
  12.0 9.0 %copy-start.9 = (bf16[256,64]{1,0:T(8,128)(2,1)S(1)}, bf16[256,64]{1,0:T(8,128)(2,1)}, u32[]{:S(2)}) copy-start(bf16[256,64]{1,0:T(8,128)(2,1)} %constant.22.first_ref) | copy-start | bytes 98308
  12.0 33.8 %all-to-all-start = ((bf16[32,64,256]{2,1,0:T(8,128)(2,1)}), bf16[32,64,256]{2,1,0:T(8,128)(2,1)S(1)}, u32[]{:S(2)}, u32[]{:S(2)}) async-start(bf16[32,64,256]{2,1,0:T(8,128)(2,1)} %get-tuple-element.22), calls=%async_computation | async-start | bytes 2097152 | tf_op jit(solution)/shard_map/all_to_all | solution.py:752
  18.8 12.7 %collective-permute-start.1 = (bf16[8,3072]{1,0:T(8,128)(2,1)S(1)}, bf16[8,3072]{1,0:T(8,128)(2,1)S(1)}, u32[]{:S(2)}, u32[]{:S(2)}) collective-permute-start(bf16[8,3072]{1,0:T(8,128)(2,1)S(1)} %get-tuple-element.19), channel_id=1, source_target_pairs={{1,0},{2,1},{3,2},{4,3},{5,4},{6,5},{7,6},{8,7},{9,8},{10,9},{11,1... | collective-permute-start | bytes 147464 | tf_op jit(solution)/shard_map/ppermute | solution.py:21
  52.6 3.4 %copy-start = (bf16[1024,256]{1,0:T(8,128)(2,1)S(1)}, bf16[1024,256]{1,0:T(8,128)(2,1)}, u32[]{:S(2)}) copy-start(bf16[1024,256]{1,0:T(8,128)(2,1)} %get-tuple-element.28.s_ref._) | copy-start | bytes 1572868
  52.6 3.4 %copy-start.6 = (bf16[256,256]{1,0:T(8,128)(2,1)S(1)}, bf16[256,256]{1,0:T(8,128)(2,1)}, u32[]{:S(2)}) copy-start(bf16[256,256]{1,0:T(8,128)(2,1)} %constant.25.third_ref) | copy-start | bytes 393220
  52.6 3.4 %copy-start.10 = (bf16[64,256]{1,0:T(8,128)(2,1)S(1)}, bf16[64,256]{1,0:T(8,128)(2,1)}, u32[]{:S(2)}) copy-start(bf16[64,256]{1,0:T(8,128)(2,1)} %constant.26.fourth_ref) | copy-start | bytes 98308
  52.7 31.8 %all-to-all-start.1 = ((bf16[32,136,128]{2,1,0:T(8,128)(2,1)}), bf16[32,136,128]{2,1,0:T(8,128)(2,1)S(1)}, u32[]{:S(2)}, u32[]{:S(2)}) async-start(bf16[32,136,128]{2,1,0:T(8,128)(2,1)} %get-tuple-element.27), calls=%async_computation.1 | async-start | bytes 2228224 | tf_op jit(solution)/shard_map/all_to_all | solution.py:757

commit v14 on v13

--- a/solution.py
+++ b/solution.py
@@ -454,54 +454,85 @@
     tiles = local // LANES
     fold = local // inner
     groups = channels // CPG
-    pairs = groups * PAIRS
     height = sources * channels
     chunk = sources // 4
 
-    def kernel(x_ref, f_ref, table_ref, tr_ref, ti_ref, y_hbm, cross_hbm, y_ref, cross_ref, talls, wides, stages, turns, sems):
+    def kernel(x_ref, f_ref, table_ref, tr_ref, ti_ref, y_hbm, cross_hbm, y_ref, cross_ref, talls, sems):
         second_ref, third_ref = table_ref.at[: 2 * inner], table_ref.at[2 * inner : 4 * inner]
         fourth_ref = table_ref.at[4 * inner : 4 * inner + 2 * half]
         firsts = table_ref[4 * inner + 2 * half :, :]
         first = jnp.concatenate([firsts[:, : 2 * half], firsts[:, 2 * half :]], axis=0)
         tr, ti = tr_ref[...], ti_ref[...]
         for s in range(2):
-            tall, wide, stage = talls.at[s], wides.at[s], stages.at[s]
             for t in range(tiles):
                 block = x_ref[:, s * channels : (s + 1) * channels, t * LANES : (t + 1) * LANES]
-                tall[t * height : (t + 1) * height, :] = block.astype(jnp.float32).reshape(height, LANES)
-            for c in range(channels):
-                pair, part = divmod(c, 2)
-                for h in range(fold):
-                    line = spread(tall, sources, channels, c, height, (h * inner, (h + 1) * inner))
-                    at = part * half + h * sources
-                    wide[at : at + sources, pair * inner : (pair + 1) * inner] = line.astype(jnp.bfloat16)
-            for g in range(groups):
-                span = PAIRS * inner
-                f = dot(first, wide[:, g * span : (g + 1) * span])
+                talls[s, t * height : (t + 1) * height, :] = block.astype(jnp.float32).reshape(height, LANES)
+
+        def gathered(s, g):
+            pieces = []
+            for p in range(PAIRS):
+                lines = [
+                    spread(talls.at[s], sources, channels, g * CPG + 2 * p + part, height, (h * inner, (h + 1) * inner))
+                    for part in range(2)
+                    for h in range(fold)
+                ]
+                pieces.append(jnp.concatenate(lines, axis=0).astype(jnp.bfloat16))
+            return jnp.concatenate(pieces, axis=1)
+
+        def spectrum(s, g):
+            f = dot(first, gathered(s, g))
+            turned = []
+            for p in range(PAIRS):
+                f_re = f[:outer, p * inner : (p + 1) * inner]
+                f_im = f[outer:, p * inner : (p + 1) * inner]
+                parts = [f_re * tr + f_im * ti, f_im * tr - f_re * ti]
+                turned.append(jnp.concatenate([part.astype(jnp.bfloat16) for part in parts], axis=1))
+            return dot(jnp.concatenate(turned, axis=0), second_ref[...])
+
+        def back(s, g, products):
+            joined = [jnp.concatenate([part.astype(jnp.bfloat16) for part in pair], axis=1) for pair in products]
+            h = dot(jnp.concatenate(joined, axis=0), third_ref[...])
+            turned = []
+            for p in range(PAIRS):
+                h_re = h[p * outer : (p + 1) * outer, :inner]
+                h_im = h[p * outer : (p + 1) * outer, inner:]
+                parts = [h_re * tr - h_im * ti, h_im * tr + h_re * ti]
+                turned.append(jnp.concatenate([part.astype(jnp.bfloat16) for part in parts], axis=0))
+            y = dot(fourth_ref[...], jnp.concatenate(turned, axis=1))
+            for p in range(PAIRS):
+                for part in range(2):
+                    for h in range(fold):
+                        at = part * half + h * sources
+                        line = y[at : at + sources, p * inner : (p + 1) * inner]
+                        c = g * CPG + 2 * p + part
+                        put_spread(talls.at[s], line, channels, c, height, (h * inner, (h + 1) * inner))
+
+        @pl.loop(0, groups // STEP)
+        def _(step):
+            slots = [step * STEP + slot for slot in range(STEP)]
+            spectra = [[spectrum(s, g) for s in range(2)] for g in slots]
+            answers = []
+            for g, (k, d) in zip(slots, spectra):
+                lines = pl.ds(pl.multiple_of(g * outer, outer), outer)
+                s_re = f_ref[lines, :inner].astype(jnp.float32)
+                s_im = f_ref[lines, inner:].astype(jnp.float32)
+                cross_re = cross_im = 0.0
+                conv, dkv = [], []
                 for p in range(PAIRS):
-                    f_re = f[:outer, p * inner : (p + 1) * inner]
-                    f_im = f[outer:, p * inner : (p + 1) * inner]
-                    at = (g * PAIRS + p) * outer
-                    stage[at : at + outer, :inner] = (f_re * tr + f_im * ti).astype(jnp.bfloat16)
-                    stage[at : at + outer, inner:] = (f_im * tr - f_re * ti).astype(jnp.bfloat16)
-        for g in range(groups):
-            s_re = f_ref[g * outer : (g + 1) * outer, :inner].astype(jnp.float32)
-            s_im = f_ref[g * outer : (g + 1) * outer, inner:].astype(jnp.float32)
-            cross_re = cross_im = 0.0
-            for p in range(PAIRS):
-                at = (g * PAIRS + p) * outer
-                k = dot(stages[0, at : at + outer, :], second_ref[...])
-                d = dot(stages[1, at : at + outer, :], second_ref[...])
-                k_re, k_im = k[:, :inner], k[:, inner:]
-                d_re, d_im = d[:, :inner], d[:, inner:]
-                cross_re = cross_re + (k_re * d_re + k_im * d_im)
-                cross_im = cross_im + (k_re * d_im - k_im * d_re)
-                stages[0, at : at + outer, :inner] = (s_re * k_re - s_im * k_im).astype(jnp.bfloat16)
-                stages[0, at : at + outer, inner:] = (s_re * k_im + s_im * k_re).astype(jnp.bfloat16)
-                stages[1, at : at + outer, :inner] = (s_re * d_re + s_im * d_im).astype(jnp.bfloat16)
-                stages[1, at : at + outer, inner:] = (s_re * d_im - s_im * d_re).astype(jnp.bfloat16)
-            cross_ref[g * outer : (g + 1) * outer, :inner] = cross_re.astype(jnp.bfloat16)
-            cross_ref[g * outer : (g + 1) * outer, inner:] = cross_im.astype(jnp.bfloat16)
+                    here = slice(p * outer, (p + 1) * outer)
+                    k_re, k_im = k[here, :inner], k[here, inner:]
+                    d_re, d_im = d[here, :inner], d[here, inner:]
+                    cross_re = cross_re + (k_re * d_re + k_im * d_im)
+                    cross_im = cross_im + (k_re * d_im - k_im * d_re)
+                    conv.append((s_re * k_re - s_im * k_im, s_re * k_im + s_im * k_re))
+                    dkv.append((s_re * d_re + s_im * d_im, s_re * d_im - s_im * d_re))
+                cross_ref[lines, :inner] = cross_re.astype(jnp.bfloat16)
+                cross_ref[lines, inner:] = cross_im.astype(jnp.bfloat16)
+                answers.append((conv, dkv))
+            for g, answer in zip(slots, answers):
+                for s in range(2):
+                    back(s, g, answer[s])
+
         copies = [pltpu.make_async_copy(cross_ref, cross_hbm, sems.at[4])]
         copies[0].start()
         spot = lax.broadcasted_iota(jnp.int32, (RIM, LANES), 0)
@@ -509,25 +540,7 @@
         pick = jnp.where(spot == lane, 1.0, 0.0).astype(jnp.bfloat16)
         rims = []
         for s in range(2):
-            tall, stage, turn = talls.at[s], stages.at[s], turns.at[s]
-            for pair in range(pairs):
-                at = pair * outer
-                h = dot(stage[at : at + outer, :], third_ref[...])
-                h_re, h_im = h[:, :inner], h[:, inner:]
-                lanes = slice(pair * inner, (pair + 1) * inner)
-                turn[:outer, lanes] = (h_re * tr - h_im * ti).astype(jnp.bfloat16)
-                turn[outer:, lanes] = (h_im * tr + h_re * ti).astype(jnp.bfloat16)
-            for g in range(groups):
-                span = PAIRS * inner
-                y = dot(fourth_ref[...], turn[:, g * span : (g + 1) * span])
-                for p in range(PAIRS):
-                    for part in range(2):
-                        c = (g * PAIRS + p) * 2 + part
-                        for h in range(fold):
-                            at = part * half + h * sources
-                            line = y[at : at + sources, p * inner : (p + 1) * inner]
-                            put_spread(tall, line, channels, c, height, (h * inner, (h + 1) * inner))
-            front = tall[:height, :].astype(jnp.bfloat16)
+            front = talls[s, :height, :].astype(jnp.bfloat16)
             rims.append(
                 lax.dot_general(pick, front, (((1,), (1,)), ((), ())), preferred_element_type=jnp.float32)
             )
@@ -567,9 +580,6 @@
             pltpu.VMEM(sent, jnp.bfloat16),
             pltpu.VMEM((groups * outer, 2 * inner), jnp.bfloat16),
             pltpu.VMEM((2, tiles * height, LANES), jnp.float32),
-            pltpu.VMEM((2, outer, pairs * inner), jnp.bfloat16),
-            pltpu.VMEM((2, pairs * outer, 2 * inner), jnp.bfloat16),
-            pltpu.VMEM((2, 2 * outer, pairs * inner), jnp.bfloat16),
             pltpu.SemaphoreType.DMA((5,)),
         ],
         flops=4_000_000_000,
@@ -746,7 +756,7 @@
 
     _, inner, outer = sizes_of(seq_len)
     twin = owned // CPG * outer == width and 2 * inner == local_len and inner == outer
-    if owned % 16 == 0 and LANES % (2 * owned) == 0 and devices % 4 == 0 and twin and width % (STEP * LANES) == 0:
+    if owned % 16 == 0 and LANES % (2 * owned) == 0 and devices % 4 == 0 and twin and width % (STEP * LANES) == owned // CPG % STEP == 0:
         feats, message, edges = joined_features(turned, rim, short_filter, out_grad, owned)
         filters, joined = transform_filters(long_filter, tables, seq_len, jnp.bfloat16, [tables["joined"]])
         arrived = lax.all_to_all(message, EVERYONE, split_axis=0, concat_axis=0, tiled=True)

time: 91.1 us -> 92.5 us (1.015)
  Pallas kernels: 18.5 us -> 19.9 us
    pallas_call x3, Pallas kernels: 16.1 us -> 17.5 us  [whole_call(): pl.pallas_call(kernel, name=name, out_shape=out_shape, scratch_shapes=lis...]
where the time goes in v14:
time: 92.5 us; the launch traced here: 91.4 us
  waiting for transfers between devices  51.9 us (56%)
  Pallas kernels  19.9 us (22%)
  starting transfers between devices  16.8 us (18%)
  local copies, waits for them, and re-layouts  1.84 us (2%)
    all_to_all x1, waiting for transfers between devices, shards(): lax.all_to_all(answer, EVERYONE, split_axis=0, concat_axis=0, tiled=True)  27.1 us
    pallas_call x3, Pallas kernels, whole_call(): pl.pallas_call(kernel, name=name, out_shape=out_shape, scratch_shapes=lis...  17.5 us
    all_to_all x1, waiting for transfers between devices, shards(): lax.all_to_all(message, EVERYONE, split_axis=0, concat_axis=0, tiled=True)  14.3 us
    ppermute x2, waiting for transfers between devices, shifted(): lax.ppermute(value, axis, [(source, source + steps) for source in range(f...  10.6 us
    ppermute x2, starting transfers between devices, shifted(): lax.ppermute(value, axis, [(source, source + steps) for source in range(f...  6.76 us
    all_to_all x1, starting transfers between devices, shards(): lax.all_to_all(message, EVERYONE, split_axis=0, concat_axis=0, tiled=True)  6.75 us
    all_to_all x1, starting transfers between devices, shards(): lax.all_to_all(answer, EVERYONE, split_axis=0, concat_axis=0, tiled=True)  3.33 us
  transfers between devices with their start and end apart: 4, of which 4 were waited for; matrix products, arithmetic and copies ran while one was open for 0% of the time, Pallas kernels for 3%

profile of v14, /device:TPU:1, one launch (start us, length us, event | category | flops | bytes accessed | tf_op | source)
XLA Modules:
  0.0 91.4 jit_solution(18430940260447396674)
XLA Ops:
  0.6 0.0 copy-start.1
  0.6 0.0 copy-start.5
  0.7 1.8 %copy.16 = bf16[3072,256]{0,1:T(8,128)(2,1)S(1)} copy(bf16[3072,256]{1,0:T(8,128)(2,1)} %param.11) | data formatting | bytes 3145728 | tf_op args[0]
  2.4 4.6 %collective-permute-start = (bf16[8,3072]{1,0:T(8,128)(2,1)S(1)}, bf16[8,3072]{1,0:T(8,128)(2,1)S(1)}, u32[]{:S(2)}, u32[]{:S(2)}) collective-permute-start(bf16[8,3072]{1,0:T(8,128)(2,1)S(1)} %slice.4), channel_id=1, source_target_pairs={{0,1},{1,2},{2,3},{3,4},{4,5},{5,6},{6,7},{7,8},{8,9},{9,10},{10,1... | collective-permute-start | bytes 147464 | tf_op jit(solution)/shard_map/ppermute | solution.py:21
  7.0 1.2 %collective-permute-done.rim_ref = bf16[8,3072]{1,0:T(8,128)(2,1)S(1)} collective-permute-done((bf16[8,3072]{1,0:T(8,128)(2,1)S(1)}, bf16[8,3072]{1,0:T(8,128)(2,1)S(1)}, u32[]{:S(2)}, u32[]{:S(2)}) %collective-permute-start) | collective-permute-done | bytes 49184 | tf_op jit(solution)/shard_map/ppermute | solution.py:21
  8.2 0.0 copy-done.1
  8.2 0.0 copy-done.5
  8.2 3.7 %joined_features.1 = (bf16[3072,256]{1,0:T(8,128)(2,1)}, bf16[32,64,256]{2,1,0:T(8,128)(2,1)}, bf16[8,3072]{1,0:T(8,128)(2,1)S(1)}) custom-call(bf16[256,3072]{1,0:T(8,128)(2,1)S(1)} %bitcast.2, bf16[8,3072]{1,0:T(8,128)(2,1)S(1)} %collective-permute-done.rim_ref, bf16[7,3072]{1,0:T(8,128)(2,1)S(1)} %copy-done.5, bf16[1024,256]{1,0:T(8,128)(2,1)S(1)} %copy-done.1), custom_call_target="tpu_custom_call" | custom-call | flops 10000000 | bytes 4000000 | tf_op jit(solution)/shard_map/joined_features/pallas_call | solution.py:285
  11.9 0.0 copy-start.2
  11.9 0.0 copy-start.3
  11.9 0.0 copy-start.4
  12.0 0.0 copy-start.7
  12.0 0.0 copy-start.8
  12.0 0.0 copy-start.9
  12.0 6.8 %all-to-all-start = ((bf16[32,64,256]{2,1,0:T(8,128)(2,1)}), bf16[32,64,256]{2,1,0:T(8,128)(2,1)S(1)}, u32[]{:S(2)}, u32[]{:S(2)}) async-start(bf16[32,64,256]{2,1,0:T(8,128)(2,1)} %get-tuple-element.22), calls=%async_computation | async-start | bytes 2097152 | tf_op jit(solution)/shard_map/all_to_all | solution.py:762
  18.8 2.2 %collective-permute-start.1 = (bf16[8,3072]{1,0:T(8,128)(2,1)S(1)}, bf16[8,3072]{1,0:T(8,128)(2,1)S(1)}, u32[]{:S(2)}, u32[]{:S(2)}) collective-permute-start(bf16[8,3072]{1,0:T(8,128)(2,1)S(1)} %get-tuple-element.19), channel_id=1, source_target_pairs={{1,0},{2,1},{3,2},{4,3},{5,4},{6,5},{7,6},{8,7},{9,8},{10,9},{11,1... | collective-permute-start | bytes 147464 | tf_op jit(solution)/shard_map/ppermute | solution.py:21
  20.9 0.0 copy-done.2
  20.9 0.0 copy-done.3
  21.0 0.0 copy-done.4
  21.0 0.0 copy-done.7
  21.0 0.0 copy-done.8
  21.0 0.0 copy-done.9
  21.0 1.1 %filter_dft.1 = (bf16[1024,256]{1,0:T(8,128)(2,1)S(1)}, bf16[768,256]{1,0:T(8,128)(2,1)S(1)}) custom-call(bf16[8,8192]{1,0:T(8,128)(2,1)S(1)} %copy-done.7, bf16[256,64]{1,0:T(8,128)(2,1)S(1)} %copy-done.9, bf16[256,256]{1,0:T(8,128)(2,1)S(1)} %copy-done.8, f32[128,128]{1,0:T(8,128)S(1)} %copy-done.4, f32[128,128]{1,0:T(8,128)S(1)} %copy-done.3, ...), custom_call_target="tpu_custom_call" | custom-call | flops 200000000 | bytes 2000000 | tf_op jit(solution)/shard_map/filter_dft/pallas_call | solution.py:114
  22.1 9.4 %collective-permute-done.1.edge_ref = bf16[8,3072]{1,0:T(8,128)(2,1)S(1)} collective-permute-done((bf16[8,3072]{1,0:T(8,128)(2,1)S(1)}, bf16[8,3072]{1,0:T(8,128)(2,1)S(1)}, u32[]{:S(2)}, u32[]{:S(2)}) %collective-permute-start.1) | collective-permute-done | bytes 49184 | tf_op jit(solution)/shard_map/ppermute | solution.py:21
  31.5 14.3 %all-to-all-done.x_ref = bf16[32,64,256]{2,1,0:T(8,128)(2,1)S(1)} async-done(((bf16[32,64,256]{2,1,0:T(8,128)(2,1)}), bf16[32,64,256]{2,1,0:T(8,128)(2,1)S(1)}, u32[]{:S(2)}, u32[]{:S(2)}) %all-to-all-start) | async-done | bytes 1048608 | tf_op jit(solution)/shard_map/all_to_all | solution.py:762
  45.8 8.3 %joined_filtering.1 = (bf16[32,136,128]{2,1,0:T(8,128)(2,1)}, bf16[1024,256]{1,0:T(8,128)(2,1)}) custom-call(bf16[32,64,256]{2,1,0:T(8,128)(2,1)S(1)} %all-to-all-done.x_ref, bf16[1024,256]{1,0:T(8,128)(2,1)S(1)} %get-tuple-element.24.f_ref, bf16[768,256]{1,0:T(8,128)(2,1)S(1)} %get-tuple-element.25.table_ref, f32[128,128]{1,0:T(8,128)S(1)} %copy-done.4, ...), custom_call_target="tpu_custom_call" | custom-call | flops 4000000000 | bytes 4000000 | tf_op jit(solution)/shard_map/joined_filtering/pallas_call | solution.py:285
  54.0 0.0 copy-start
  54.0 0.0 copy-start.6
  54.1 0.0 copy-start.10
  54.1 3.3 %all-to-all-start.1 = ((bf16[32,136,128]{2,1,0:T(8,128)(2,1)}), bf16[32,136,128]{2,1,0:T(8,128)(2,1)S(1)}, u32[]{:S(2)}, u32[]{:S(2)}) async-start(bf16[32,136,128]{2,1,0:T(8,128)(2,1)} %get-tuple-element.27), calls=%async_computation.1 | async-start | bytes 2228224 | tf_op jit(solution)/shard_map/all_to_all | solution.py:767
  57.4 0.0 copy-done
  57.4 0.0 copy-done.6
  57.4 0.0 copy-done.10
  57.4 1.3 %filter_gradient.1 = f32[8,8192]{1,0:T(8,128)} custom-call(bf16[1024,256]{1,0:T(8,128)(2,1)S(1)} %copy-done, bf16[256,256]{1,0:T(8,128)(2,1)S(1)} %copy-done.6, bf16[64,256]{1,0:T(8,128)(2,1)S(1)} %copy-done.10, f32[128,128]{1,0:T(8,128)S(1)} %copy-done.4, f32[128,128]{1,0:T(8,128)S(1)} %copy-done.3), custom_call_target="tpu_custom_call" | custom-call | flops 200000000 | bytes 2000000 | tf_op jit(solution)/shard_map/filter_gradient/pallas_call | solution.py:248
  58.7 27.1 %all-to-all-done.1.back_ref = bf16[32,136,128]{2,1,0:T(8,128)(2,1)S(1)} async-done(((bf16[32,136,128]{2,1,0:T(8,128)(2,1)}), bf16[32,136,128]{2,1,0:T(8,128)(2,1)S(1)}, u32[]{:S(2)}, u32[]{:S(2)}) %all-to-all-start.1) | async-done | bytes 1114144 | tf_op jit(solution)/shard_map/all_to_all | solution.py:767
  85.8 5.5 %joined_gradients.1 = (bf16[1024,256]{1,0:T(8,128)(2,1)}, bf16[3072,256]{1,0:T(8,128)(2,1)}) custom-call(bf16[1024,256]{1,0:T(8,128)(2,1)} %get-tuple-element.28.s_ref._, bf16[3072,256]{1,0:T(8,128)(2,1)} %get-tuple-element.29.f_hbm, bf16[8,3072]{1,0:T(8,128)(2,1)S(1)} %collective-permute-done.1.edge_ref, ...), custom_call_target="tpu_custom_call", output_to_operand_aliasing={{0}: (0, {}), {1}: (1, {})} | custom-call | flops 10000000 | bytes 4000000 | tf_op jit(solution)/shard_map/joined_gradients/pallas_call | solution.py:285
  (1 shorter events, 0.0 us)
Async XLA Ops:
  0.6 7.6 %copy-start.1 = (bf16[1024,256]{1,0:T(8,128)(2,1)S(1)}, bf16[1024,256]{1,0:T(8,128)(2,1)}, u32[]{:S(2)}) copy-start(bf16[1024,256]{1,0:T(8,128)(2,1)} %og_ref.3) | copy-start | bytes 1572868
  0.6 7.6 %copy-start.5 = (bf16[7,3072]{1,0:T(8,128)(2,1)S(1)}, bf16[7,3072]{1,0:T(8,128)(2,1)}, u32[]{:S(2)}) copy-start(bf16[7,3072]{1,0:T(8,128)(2,1)} %w_ref.3) | copy-start | bytes 129028
  2.4 5.8 %collective-permute-start = (bf16[8,3072]{1,0:T(8,128)(2,1)S(1)}, bf16[8,3072]{1,0:T(8,128)(2,1)S(1)}, u32[]{:S(2)}, u32[]{:S(2)}) collective-permute-start(bf16[8,3072]{1,0:T(8,128)(2,1)S(1)} %slice.4), channel_id=1, source_target_pairs={{0,1},{1,2},{2,3},{3,4},{4,5},{5,6},{6,7},{7,8},{8,9},{9,10},{10,1... | collective-permute-start | bytes 147464 | tf_op jit(solution)/shard_map/ppermute | solution.py:21
  11.9 9.0 %copy-start.2 = (bf16[768,256]{1,0:T(8,128)(2,1)S(1)}, bf16[768,256]{1,0:T(8,128)(2,1)}, u32[]{:S(2)}) copy-start(bf16[768,256]{1,0:T(8,128)(2,1)} %constant.24.refs_0_) | copy-start | bytes 1179652
  11.9 9.0 %copy-start.3 = (f32[128,128]{1,0:T(8,128)S(1)}, f32[128,128]{1,0:T(8,128)}, u32[]{:S(2)}) copy-start(f32[128,128]{1,0:T(8,128)} %constant.15.clone.ti_ref) | copy-start | bytes 196612
  11.9 9.0 %copy-start.4 = (f32[128,128]{1,0:T(8,128)S(1)}, f32[128,128]{1,0:T(8,128)}, u32[]{:S(2)}) copy-start(f32[128,128]{1,0:T(8,128)} %constant.14.clone.tr_ref) | copy-start | bytes 196612
  12.0 9.0 %copy-start.7 = (bf16[8,8192]{1,0:T(8,128)(2,1)S(1)}, bf16[8,8192]{1,0:T(8,128)(2,1)}, u32[]{:S(2)}) copy-start(bf16[8,8192]{1,0:T(8,128)(2,1)} %x_ref.1) | copy-start | bytes 393220
  12.0 9.0 %copy-start.8 = (bf16[256,256]{1,0:T(8,128)(2,1)S(1)}, bf16[256,256]{1,0:T(8,128)(2,1)}, u32[]{:S(2)}) copy-start(bf16[256,256]{1,0:T(8,128)(2,1)} %constant.23.second_ref) | copy-start | bytes 393220
  12.0 9.0 %copy-start.9 = (bf16[256,64]{1,0:T(8,128)(2,1)S(1)}, bf16[256,64]{1,0:T(8,128)(2,1)}, u32[]{:S(2)}) copy-start(bf16[256,64]{1,0:T(8,128)(2,1)} %constant.22.first_ref) | copy-start | bytes 98308
  12.0 33.8 %all-to-all-start = ((bf16[32,64,256]{2,1,0:T(8,128)(2,1)}), bf16[32,64,256]{2,1,0:T(8,128)(2,1)S(1)}, u32[]{:S(2)}, u32[]{:S(2)}) async-start(bf16[32,64,256]{2,1,0:T(8,128)(2,1)} %get-tuple-element.22), calls=%async_computation | async-start | bytes 2097152 | tf_op jit(solution)/shard_map/all_to_all | solution.py:762
  18.8 12.7 %collective-permute-start.1 = (bf16[8,3072]{1,0:T(8,128)(2,1)S(1)}, bf16[8,3072]{1,0:T(8,128)(2,1)S(1)}, u32[]{:S(2)}, u32[]{:S(2)}) collective-permute-start(bf16[8,3072]{1,0:T(8,128)(2,1)S(1)} %get-tuple-element.19), channel_id=1, source_target_pairs={{1,0},{2,1},{3,2},{4,3},{5,4},{6,5},{7,6},{8,7},{9,8},{10,9},{11,1... | collective-permute-start | bytes 147464 | tf_op jit(solution)/shard_map/ppermute | solution.py:21
  54.0 3.4 %copy-start = (bf16[1024,256]{1,0:T(8,128)(2,1)S(1)}, bf16[1024,256]{1,0:T(8,128)(2,1)}, u32[]{:S(2)}) copy-start(bf16[1024,256]{1,0:T(8,128)(2,1)} %get-tuple-element.28.s_ref._) | copy-start | bytes 1572868
  54.0 3.4 %copy-start.6 = (bf16[256,256]{1,0:T(8,128)(2,1)S(1)}, bf16[256,256]{1,0:T(8,128)(2,1)}, u32[]{:S(2)}) copy-start(bf16[256,256]{1,0:T(8,128)(2,1)} %constant.25.third_ref) | copy-start | bytes 393220
  54.1 3.4 %copy-start.10 = (bf16[64,256]{1,0:T(8,128)(2,1)S(1)}, bf16[64,256]{1,0:T(8,128)(2,1)}, u32[]{:S(2)}) copy-start(bf16[64,256]{1,0:T(8,128)(2,1)} %constant.26.fourth_ref) | copy-start | bytes 98308
  54.1 31.8 %all-to-all-start.1 = ((bf16[32,136,128]{2,1,0:T(8,128)(2,1)}), bf16[32,136,128]{2,1,0:T(8,128)(2,1)S(1)}, u32[]{:S(2)}, u32[]{:S(2)}) async-start(bf16[32,136,128]{2,1,0:T(8,128)(2,1)} %get-tuple-element.27), calls=%async_computation.1 | async-start | bytes 2228224 | tf_op jit(solution)/shard_map/all_to_all | solution.py:767

commit v15 on v14

--- a/solution.py
+++ b/solution.py
@@ -374,18 +374,19 @@
 def joined_features(turned, rim, short_filter, out_grad, owned):
     width, local = out_grad.shape
     near = LANES // owned
-    steps = width // LANES // STEP
+    blocks = width // LANES
 
     def kernel(x_ref, rim_ref, w_ref, og_ref, f_hbm, msg_ref, edge_ref, tall, made, f_ref, edge, sent):
-        def copy(step):
-            to = pl.ds(step * STEP * near, STEP * near)
-            return pltpu.make_async_copy(made.at[to], msg_ref.at[to], sent.at[step])
-
-        def keep(part, step):
-            to = pl.ds(pl.multiple_of(part * width + step * STEP * LANES, STEP * LANES), STEP * LANES)
-            return pltpu.make_async_copy(f_ref.at[to, :], f_hbm.at[to, :], sent.at[(1 + part) * steps + step])
-
-        @pl.loop(0, steps)
+        def copy(i):
+            to = pl.ds(i * near, near)
+            return pltpu.make_async_copy(made.at[to], msg_ref.at[to], sent.at[i])
+
+        def keep(part, i):
+            at = part * blocks + i
+            to = pl.ds(pl.multiple_of(at * LANES, LANES), LANES)
+            return pltpu.make_async_copy(f_ref.at[at], f_hbm.at[to, :], sent.at[blocks + at])
+
+        @pl.loop(0, blocks // STEP)
         def _(step):
             for slot in range(STEP):
                 i = step * STEP + slot
@@ -400,7 +401,7 @@
                         True,
                     ).astype(jnp.bfloat16)
                     for t in range(local // LANES):
-                        f_ref[lanes, t * LANES : (t + 1) * LANES] = total[t * LANES : (t + 1) * LANES]
+                        f_ref[part * blocks + i, :, t * LANES : (t + 1) * LANES] = total[t * LANES : (t + 1) * LANES]
                     if part:
                         edge[:, lanes] = total[:RIM]
                     parts.append(total.astype(jnp.float32))
@@ -411,18 +412,19 @@
                 to = pl.ds(i * near, near)
                 made[to, :owned, :] = kv.reshape(near, owned, local)
                 made[to, owned:, :] = dconv.reshape(near, owned, local)
-            copy(step).start()
+            for slot in range(STEP):
+                copy(step * STEP + slot).start()
+                for part in range(3):
+                    keep(part, step * STEP + slot).start()
+
+        last = pltpu.make_async_copy(edge, edge_ref, sent.at[4 * blocks])
+        last.start()
+
+        @pl.loop(0, blocks)
+        def _(i):
+            copy(i).wait()
             for part in range(3):
-                keep(part, step).start()
-
-        last = pltpu.make_async_copy(edge, edge_ref, sent.at[4 * steps])
-        last.start()
-
-        @pl.loop(0, steps)
-        def _(step):
-            copy(step).wait()
-            for part in range(3):
-                keep(part, step).wait()
+                keep(part, i).wait()
 
         last.wait()
 
@@ -437,9 +439,9 @@
         [
             pltpu.VMEM((3 * STEP, local + RIM, LANES), jnp.float32),
             pltpu.VMEM((devices, 2 * owned, local), jnp.bfloat16),
-            pltpu.VMEM((3 * width, local), jnp.bfloat16),
+            pltpu.VMEM((3 * blocks, LANES, local), jnp.bfloat16),
             pltpu.VMEM((RIM, 3 * width), jnp.bfloat16),
-            pltpu.SemaphoreType.DMA((4 * steps + 1,)),
+            pltpu.SemaphoreType.DMA((4 * blocks + 1,)),
         ],
         in_specs=[vmem] * 4,
         out_specs=(hbm, hbm, hbm),
@@ -457,7 +459,7 @@
     height = sources * channels
     chunk = sources // 4
 
-    def kernel(x_ref, f_ref, table_ref, tr_ref, ti_ref, y_hbm, cross_hbm, y_ref, cross_ref, talls, sems):
+    def kernel(x_ref, f_ref, table_ref, tr_ref, ti_ref, y_hbm, cross_hbm, y_ref, cross_ref, talls, results, sems):
         second_ref, third_ref = table_ref.at[: 2 * inner], table_ref.at[2 * inner : 4 * inner]
         fourth_ref = table_ref.at[4 * inner : 4 * inner + 2 * half]
         firsts = table_ref[4 * inner + 2 * half :, :]
@@ -505,15 +507,14 @@
                         at = part * half + h * sources
                         line = y[at : at + sources, p * inner : (p + 1) * inner]
                         c = g * CPG + 2 * p + part
-                        put_spread(talls.at[s], line, channels, c, height, (h * inner, (h + 1) * inner))
-
-        @pl.loop(0, groups // STEP)
-        def _(step):
+                        put_spread(results.at[s], line, channels, c, height, (h * inner, (h + 1) * inner))
+
+        for step in range(groups // STEP):
             slots = [step * STEP + slot for slot in range(STEP)]
             spectra = [[spectrum(s, g) for s in range(2)] for g in slots]
             answers = []
             for g, (k, d) in zip(slots, spectra):
-                lines = pl.ds(pl.multiple_of(g * outer, outer), outer)
+                lines = slice(g * outer, (g + 1) * outer)
                 s_re = f_ref[lines, :inner].astype(jnp.float32)
                 s_im = f_ref[lines, inner:].astype(jnp.float32)
                 cross_re = cross_im = 0.0
@@ -540,7 +541,7 @@
         pick = jnp.where(spot == lane, 1.0, 0.0).astype(jnp.bfloat16)
         rims = []
         for s in range(2):
-            front = talls[s, :height, :].astype(jnp.bfloat16)
+            front = results[s, :height, :].astype(jnp.bfloat16)
             rims.append(
                 lax.dot_general(pick, front, (((1,), (1,)), ((), ())), preferred_element_type=jnp.float32)
             )
@@ -549,7 +550,7 @@
             for s in range(2):
                 for t in range(tiles):
                     at = t * height + q * chunk * channels
-                    block = talls[s, at : at + chunk * channels, :].reshape(chunk, channels, LANES)
+                    block = results[s, at : at + chunk * channels, :].reshape(chunk, channels, LANES)
                     row = (s * tiles + t) * channels
                     y_ref[to, row : row + channels, :] = block.astype(jnp.bfloat16)
             for d in range(q * chunk, (q + 1) * chunk):
@@ -580,6 +581,7 @@
             pltpu.VMEM(sent, jnp.bfloat16),
             pltpu.VMEM((groups * outer, 2 * inner), jnp.bfloat16),
             pltpu.VMEM((2, tiles * height, LANES), jnp.float32),
+            pltpu.VMEM((2, tiles * height, LANES), jnp.float32),
             pltpu.SemaphoreType.DMA((5,)),
         ],
         flops=4_000_000_000,

time: 92.5 us -> 92.1 us (level)
  no operation moved by 1% of the time
where the time goes in v15:
time: 92.1 us; the launch traced here: 90.9 us
  waiting for transfers between devices  52 us (56%)
  Pallas kernels  19.4 us (21%)
  starting transfers between devices  16.8 us (18%)
  local copies, waits for them, and re-layouts  1.84 us (2%)
    all_to_all x1, waiting for transfers between devices, shards(): lax.all_to_all(answer, EVERYONE, split_axis=0, concat_axis=0, tiled=True)  27.1 us
    pallas_call x3, Pallas kernels, whole_call(): pl.pallas_call(kernel, name=name, out_shape=out_shape, scratch_shapes=lis...  17 us
    all_to_all x1, waiting for transfers between devices, shards(): lax.all_to_all(message, EVERYONE, split_axis=0, concat_axis=0, tiled=True)  14.3 us
    ppermute x2, waiting for transfers between devices, shifted(): lax.ppermute(value, axis, [(source, source + steps) for source in range(f...  10.6 us
    ppermute x2, starting transfers between devices, shifted(): lax.ppermute(value, axis, [(source, source + steps) for source in range(f...  6.76 us
    all_to_all x1, starting transfers between devices, shards(): lax.all_to_all(message, EVERYONE, split_axis=0, concat_axis=0, tiled=True)  6.75 us
    all_to_all x1, starting transfers between devices, shards(): lax.all_to_all(answer, EVERYONE, split_axis=0, concat_axis=0, tiled=True)  3.33 us
  transfers between devices with their start and end apart: 4, of which 4 were waited for; matrix products, arithmetic and copies ran while one was open for 0% of the time, Pallas kernels for 3%

profile of v15, /device:TPU:1, one launch (start us, length us, event | category | flops | bytes accessed | tf_op | source)
XLA Modules:
  0.0 90.9 jit_solution(1276151470421116723)
XLA Ops:
  0.6 0.0 copy-start.1
  0.6 0.0 copy-start.5
  0.7 1.8 %copy.16 = bf16[3072,256]{0,1:T(8,128)(2,1)S(1)} copy(bf16[3072,256]{1,0:T(8,128)(2,1)} %param.11) | data formatting | bytes 3145728 | tf_op args[0]
  2.4 4.6 %collective-permute-start = (bf16[8,3072]{1,0:T(8,128)(2,1)S(1)}, bf16[8,3072]{1,0:T(8,128)(2,1)S(1)}, u32[]{:S(2)}, u32[]{:S(2)}) collective-permute-start(bf16[8,3072]{1,0:T(8,128)(2,1)S(1)} %slice.4), channel_id=1, source_target_pairs={{0,1},{1,2},{2,3},{3,4},{4,5},{5,6},{6,7},{7,8},{8,9},{9,10},{10,1... | collective-permute-start | bytes 147464 | tf_op jit(solution)/shard_map/ppermute | solution.py:21
  7.0 1.2 %collective-permute-done.rim_ref = bf16[8,3072]{1,0:T(8,128)(2,1)S(1)} collective-permute-done((bf16[8,3072]{1,0:T(8,128)(2,1)S(1)}, bf16[8,3072]{1,0:T(8,128)(2,1)S(1)}, u32[]{:S(2)}, u32[]{:S(2)}) %collective-permute-start) | collective-permute-done | bytes 49184 | tf_op jit(solution)/shard_map/ppermute | solution.py:21
  8.2 0.0 copy-done.1
  8.2 0.0 copy-done.5
  8.2 3.6 %joined_features.1 = (bf16[3072,256]{1,0:T(8,128)(2,1)}, bf16[32,64,256]{2,1,0:T(8,128)(2,1)}, bf16[8,3072]{1,0:T(8,128)(2,1)S(1)}) custom-call(bf16[256,3072]{1,0:T(8,128)(2,1)S(1)} %bitcast.2, bf16[8,3072]{1,0:T(8,128)(2,1)S(1)} %collective-permute-done.rim_ref, bf16[7,3072]{1,0:T(8,128)(2,1)S(1)} %copy-done.5, bf16[1024,256]{1,0:T(8,128)(2,1)S(1)} %copy-done.1), custom_call_target="tpu_custom_call" | custom-call | flops 10000000 | bytes 4000000 | tf_op jit(solution)/shard_map/joined_features/pallas_call | solution.py:285
  11.8 0.0 copy-start.2
  11.8 0.0 copy-start.3
  11.8 0.0 copy-start.4
  11.8 0.0 copy-start.7
  11.8 0.0 copy-start.8
  11.8 0.0 copy-start.9
  11.9 6.8 %all-to-all-start = ((bf16[32,64,256]{2,1,0:T(8,128)(2,1)}), bf16[32,64,256]{2,1,0:T(8,128)(2,1)S(1)}, u32[]{:S(2)}, u32[]{:S(2)}) async-start(bf16[32,64,256]{2,1,0:T(8,128)(2,1)} %get-tuple-element.22), calls=%async_computation | async-start | bytes 2097152 | tf_op jit(solution)/shard_map/all_to_all | solution.py:764
  18.6 2.2 %collective-permute-start.1 = (bf16[8,3072]{1,0:T(8,128)(2,1)S(1)}, bf16[8,3072]{1,0:T(8,128)(2,1)S(1)}, u32[]{:S(2)}, u32[]{:S(2)}) collective-permute-start(bf16[8,3072]{1,0:T(8,128)(2,1)S(1)} %get-tuple-element.19), channel_id=1, source_target_pairs={{1,0},{2,1},{3,2},{4,3},{5,4},{6,5},{7,6},{8,7},{9,8},{10,9},{11,1... | collective-permute-start | bytes 147464 | tf_op jit(solution)/shard_map/ppermute | solution.py:21
  20.8 0.0 copy-done.2
  20.8 0.0 copy-done.3
  20.8 0.0 copy-done.4
  20.8 0.0 copy-done.7
  20.8 0.0 copy-done.8
  20.8 0.0 copy-done.9
  20.9 1.1 %filter_dft.1 = (bf16[1024,256]{1,0:T(8,128)(2,1)S(1)}, bf16[768,256]{1,0:T(8,128)(2,1)S(1)}) custom-call(bf16[8,8192]{1,0:T(8,128)(2,1)S(1)} %copy-done.7, bf16[256,64]{1,0:T(8,128)(2,1)S(1)} %copy-done.9, bf16[256,256]{1,0:T(8,128)(2,1)S(1)} %copy-done.8, f32[128,128]{1,0:T(8,128)S(1)} %copy-done.4, f32[128,128]{1,0:T(8,128)S(1)} %copy-done.3, ...), custom_call_target="tpu_custom_call" | custom-call | flops 200000000 | bytes 2000000 | tf_op jit(solution)/shard_map/filter_dft/pallas_call | solution.py:114
  21.9 9.4 %collective-permute-done.1.edge_ref = bf16[8,3072]{1,0:T(8,128)(2,1)S(1)} collective-permute-done((bf16[8,3072]{1,0:T(8,128)(2,1)S(1)}, bf16[8,3072]{1,0:T(8,128)(2,1)S(1)}, u32[]{:S(2)}, u32[]{:S(2)}) %collective-permute-start.1) | collective-permute-done | bytes 49184 | tf_op jit(solution)/shard_map/ppermute | solution.py:21
  31.4 14.3 %all-to-all-done.x_ref = bf16[32,64,256]{2,1,0:T(8,128)(2,1)S(1)} async-done(((bf16[32,64,256]{2,1,0:T(8,128)(2,1)}), bf16[32,64,256]{2,1,0:T(8,128)(2,1)S(1)}, u32[]{:S(2)}, u32[]{:S(2)}) %all-to-all-start) | async-done | bytes 1048608 | tf_op jit(solution)/shard_map/all_to_all | solution.py:764
  45.6 7.9 %joined_filtering.1 = (bf16[32,136,128]{2,1,0:T(8,128)(2,1)}, bf16[1024,256]{1,0:T(8,128)(2,1)}) custom-call(bf16[32,64,256]{2,1,0:T(8,128)(2,1)S(1)} %all-to-all-done.x_ref, bf16[1024,256]{1,0:T(8,128)(2,1)S(1)} %get-tuple-element.24.f_ref, bf16[768,256]{1,0:T(8,128)(2,1)S(1)} %get-tuple-element.25.table_ref, f32[128,128]{1,0:T(8,128)S(1)} %copy-done.4, ...), custom_call_target="tpu_custom_call" | custom-call | flops 4000000000 | bytes 4000000 | tf_op jit(solution)/shard_map/joined_filtering/pallas_call | solution.py:285
  53.6 0.0 copy-start
  53.6 0.0 copy-start.6
  53.6 0.0 copy-start.10
  53.6 3.3 %all-to-all-start.1 = ((bf16[32,136,128]{2,1,0:T(8,128)(2,1)}), bf16[32,136,128]{2,1,0:T(8,128)(2,1)S(1)}, u32[]{:S(2)}, u32[]{:S(2)}) async-start(bf16[32,136,128]{2,1,0:T(8,128)(2,1)} %get-tuple-element.27), calls=%async_computation.1 | async-start | bytes 2228224 | tf_op jit(solution)/shard_map/all_to_all | solution.py:769
  56.9 0.0 copy-done
  57.0 0.0 copy-done.6
  57.0 0.0 copy-done.10
  57.0 1.3 %filter_gradient.1 = f32[8,8192]{1,0:T(8,128)} custom-call(bf16[1024,256]{1,0:T(8,128)(2,1)S(1)} %copy-done, bf16[256,256]{1,0:T(8,128)(2,1)S(1)} %copy-done.6, bf16[64,256]{1,0:T(8,128)(2,1)S(1)} %copy-done.10, f32[128,128]{1,0:T(8,128)S(1)} %copy-done.4, f32[128,128]{1,0:T(8,128)S(1)} %copy-done.3), custom_call_target="tpu_custom_call" | custom-call | flops 200000000 | bytes 2000000 | tf_op jit(solution)/shard_map/filter_gradient/pallas_call | solution.py:248
  58.3 27.1 %all-to-all-done.1.back_ref = bf16[32,136,128]{2,1,0:T(8,128)(2,1)S(1)} async-done(((bf16[32,136,128]{2,1,0:T(8,128)(2,1)}), bf16[32,136,128]{2,1,0:T(8,128)(2,1)S(1)}, u32[]{:S(2)}, u32[]{:S(2)}) %all-to-all-start.1) | async-done | bytes 1114144 | tf_op jit(solution)/shard_map/all_to_all | solution.py:769
  85.4 5.5 %joined_gradients.1 = (bf16[1024,256]{1,0:T(8,128)(2,1)}, bf16[3072,256]{1,0:T(8,128)(2,1)}) custom-call(bf16[1024,256]{1,0:T(8,128)(2,1)} %get-tuple-element.28.s_ref._, bf16[3072,256]{1,0:T(8,128)(2,1)} %get-tuple-element.29.f_hbm, bf16[8,3072]{1,0:T(8,128)(2,1)S(1)} %collective-permute-done.1.edge_ref, ...), custom_call_target="tpu_custom_call", output_to_operand_aliasing={{0}: (0, {}), {1}: (1, {})} | custom-call | flops 10000000 | bytes 4000000 | tf_op jit(solution)/shard_map/joined_gradients/pallas_call | solution.py:285
  (1 shorter events, 0.0 us)
Async XLA Ops:
  0.6 7.6 %copy-start.1 = (bf16[1024,256]{1,0:T(8,128)(2,1)S(1)}, bf16[1024,256]{1,0:T(8,128)(2,1)}, u32[]{:S(2)}) copy-start(bf16[1024,256]{1,0:T(8,128)(2,1)} %og_ref.3) | copy-start | bytes 1572868
  0.6 7.6 %copy-start.5 = (bf16[7,3072]{1,0:T(8,128)(2,1)S(1)}, bf16[7,3072]{1,0:T(8,128)(2,1)}, u32[]{:S(2)}) copy-start(bf16[7,3072]{1,0:T(8,128)(2,1)} %w_ref.3) | copy-start | bytes 129028
  2.4 5.8 %collective-permute-start = (bf16[8,3072]{1,0:T(8,128)(2,1)S(1)}, bf16[8,3072]{1,0:T(8,128)(2,1)S(1)}, u32[]{:S(2)}, u32[]{:S(2)}) collective-permute-start(bf16[8,3072]{1,0:T(8,128)(2,1)S(1)} %slice.4), channel_id=1, source_target_pairs={{0,1},{1,2},{2,3},{3,4},{4,5},{5,6},{6,7},{7,8},{8,9},{9,10},{10,1... | collective-permute-start | bytes 147464 | tf_op jit(solution)/shard_map/ppermute | solution.py:21
  11.8 9.0 %copy-start.2 = (bf16[768,256]{1,0:T(8,128)(2,1)S(1)}, bf16[768,256]{1,0:T(8,128)(2,1)}, u32[]{:S(2)}) copy-start(bf16[768,256]{1,0:T(8,128)(2,1)} %constant.24.refs_0_) | copy-start | bytes 1179652
  11.8 9.0 %copy-start.3 = (f32[128,128]{1,0:T(8,128)S(1)}, f32[128,128]{1,0:T(8,128)}, u32[]{:S(2)}) copy-start(f32[128,128]{1,0:T(8,128)} %constant.15.clone.ti_ref) | copy-start | bytes 196612
  11.8 9.0 %copy-start.4 = (f32[128,128]{1,0:T(8,128)S(1)}, f32[128,128]{1,0:T(8,128)}, u32[]{:S(2)}) copy-start(f32[128,128]{1,0:T(8,128)} %constant.14.clone.tr_ref) | copy-start | bytes 196612
  11.8 9.0 %copy-start.7 = (bf16[8,8192]{1,0:T(8,128)(2,1)S(1)}, bf16[8,8192]{1,0:T(8,128)(2,1)}, u32[]{:S(2)}) copy-start(bf16[8,8192]{1,0:T(8,128)(2,1)} %x_ref.1) | copy-start | bytes 393220
  11.8 9.0 %copy-start.8 = (bf16[256,256]{1,0:T(8,128)(2,1)S(1)}, bf16[256,256]{1,0:T(8,128)(2,1)}, u32[]{:S(2)}) copy-start(bf16[256,256]{1,0:T(8,128)(2,1)} %constant.23.second_ref) | copy-start | bytes 393220
  11.8 9.0 %copy-start.9 = (bf16[256,64]{1,0:T(8,128)(2,1)S(1)}, bf16[256,64]{1,0:T(8,128)(2,1)}, u32[]{:S(2)}) copy-start(bf16[256,64]{1,0:T(8,128)(2,1)} %constant.22.first_ref) | copy-start | bytes 98308
  11.9 33.8 %all-to-all-start = ((bf16[32,64,256]{2,1,0:T(8,128)(2,1)}), bf16[32,64,256]{2,1,0:T(8,128)(2,1)S(1)}, u32[]{:S(2)}, u32[]{:S(2)}) async-start(bf16[32,64,256]{2,1,0:T(8,128)(2,1)} %get-tuple-element.22), calls=%async_computation | async-start | bytes 2097152 | tf_op jit(solution)/shard_map/all_to_all | solution.py:764
  18.6 12.7 %collective-permute-start.1 = (bf16[8,3072]{1,0:T(8,128)(2,1)S(1)}, bf16[8,3072]{1,0:T(8,128)(2,1)S(1)}, u32[]{:S(2)}, u32[]{:S(2)}) collective-permute-start(bf16[8,3072]{1,0:T(8,128)(2,1)S(1)} %get-tuple-element.19), channel_id=1, source_target_pairs={{1,0},{2,1},{3,2},{4,3},{5,4},{6,5},{7,6},{8,7},{9,8},{10,9},{11,1... | collective-permute-start | bytes 147464 | tf_op jit(solution)/shard_map/ppermute | solution.py:21
  53.6 3.4 %copy-start = (bf16[1024,256]{1,0:T(8,128)(2,1)S(1)}, bf16[1024,256]{1,0:T(8,128)(2,1)}, u32[]{:S(2)}) copy-start(bf16[1024,256]{1,0:T(8,128)(2,1)} %get-tuple-element.28.s_ref._) | copy-start | bytes 1572868
  53.6 3.4 %copy-start.6 = (bf16[256,256]{1,0:T(8,128)(2,1)S(1)}, bf16[256,256]{1,0:T(8,128)(2,1)}, u32[]{:S(2)}) copy-start(bf16[256,256]{1,0:T(8,128)(2,1)} %constant.25.third_ref) | copy-start | bytes 393220
  53.6 3.4 %copy-start.10 = (bf16[64,256]{1,0:T(8,128)(2,1)S(1)}, bf16[64,256]{1,0:T(8,128)(2,1)}, u32[]{:S(2)}) copy-start(bf16[64,256]{1,0:T(8,128)(2,1)} %constant.26.fourth_ref) | copy-start | bytes 98308
  53.6 31.8 %all-to-all-start.1 = ((bf16[32,136,128]{2,1,0:T(8,128)(2,1)}), bf16[32,136,128]{2,1,0:T(8,128)(2,1)S(1)}, u32[]{:S(2)}, u32[]{:S(2)}) async-start(bf16[32,136,128]{2,1,0:T(8,128)(2,1)} %get-tuple-element.27), calls=%async_computation.1 | async-start | bytes 2228224 | tf_op jit(solution)/shard_map/all_to_all | solution.py:769

commit v16 on v13

--- a/solution.py
+++ b/solution.py
@@ -374,18 +374,19 @@
 def joined_features(turned, rim, short_filter, out_grad, owned):
     width, local = out_grad.shape
     near = LANES // owned
-    steps = width // LANES // STEP
+    blocks = width // LANES
 
     def kernel(x_ref, rim_ref, w_ref, og_ref, f_hbm, msg_ref, edge_ref, tall, made, f_ref, edge, sent):
-        def copy(step):
-            to = pl.ds(step * STEP * near, STEP * near)
-            return pltpu.make_async_copy(made.at[to], msg_ref.at[to], sent.at[step])
-
-        def keep(part, step):
-            to = pl.ds(pl.multiple_of(part * width + step * STEP * LANES, STEP * LANES), STEP * LANES)
-            return pltpu.make_async_copy(f_ref.at[to, :], f_hbm.at[to, :], sent.at[(1 + part) * steps + step])
-
-        @pl.loop(0, steps)
+        def copy(i):
+            to = pl.ds(i * near, near)
+            return pltpu.make_async_copy(made.at[to], msg_ref.at[to], sent.at[i])
+
+        def keep(part, i):
+            at = part * blocks + i
+            to = pl.ds(pl.multiple_of(at * LANES, LANES), LANES)
+            return pltpu.make_async_copy(f_ref.at[at], f_hbm.at[to, :], sent.at[blocks + at])
+
+        @pl.loop(0, blocks // STEP)
         def _(step):
             for slot in range(STEP):
                 i = step * STEP + slot
@@ -400,7 +401,7 @@
                         True,
                     ).astype(jnp.bfloat16)
                     for t in range(local // LANES):
-                        f_ref[lanes, t * LANES : (t + 1) * LANES] = total[t * LANES : (t + 1) * LANES]
+                        f_ref[part * blocks + i, :, t * LANES : (t + 1) * LANES] = total[t * LANES : (t + 1) * LANES]
                     if part:
                         edge[:, lanes] = total[:RIM]
                     parts.append(total.astype(jnp.float32))
@@ -411,18 +412,19 @@
                 to = pl.ds(i * near, near)
                 made[to, :owned, :] = kv.reshape(near, owned, local)
                 made[to, owned:, :] = dconv.reshape(near, owned, local)
-            copy(step).start()
+            for slot in range(STEP):
+                copy(step * STEP + slot).start()
+                for part in range(3):
+                    keep(part, step * STEP + slot).start()
+
+        last = pltpu.make_async_copy(edge, edge_ref, sent.at[4 * blocks])
+        last.start()
+
+        @pl.loop(0, blocks)
+        def _(i):
+            copy(i).wait()
             for part in range(3):
-                keep(part, step).start()
-
-        last = pltpu.make_async_copy(edge, edge_ref, sent.at[4 * steps])
-        last.start()
-
-        @pl.loop(0, steps)
-        def _(step):
-            copy(step).wait()
-            for part in range(3):
-                keep(part, step).wait()
+                keep(part, i).wait()
 
         last.wait()
 
@@ -437,9 +439,9 @@
         [
             pltpu.VMEM((3 * STEP, local + RIM, LANES), jnp.float32),
             pltpu.VMEM((devices, 2 * owned, local), jnp.bfloat16),
-            pltpu.VMEM((3 * width, local), jnp.bfloat16),
+            pltpu.VMEM((3 * blocks, LANES, local), jnp.bfloat16),
             pltpu.VMEM((RIM, 3 * width), jnp.bfloat16),
-            pltpu.SemaphoreType.DMA((4 * steps + 1,)),
+            pltpu.SemaphoreType.DMA((4 * blocks + 1,)),
         ],
         in_specs=[vmem] * 4,
         out_specs=(hbm, hbm, hbm),

time: 91.1 us -> 91 us (level)
  no operation moved by 1% of the time
where the time goes in v16:
time: 91 us; the launch traced here: 89.8 us
  waiting for transfers between devices  52 us (57%)
  Pallas kernels  18.3 us (20%)
  starting transfers between devices  16.8 us (18%)
  local copies, waits for them, and re-layouts  1.84 us (2%)
    all_to_all x1, waiting for transfers between devices, shards(): lax.all_to_all(answer, EVERYONE, split_axis=0, concat_axis=0, tiled=True)  27.1 us
    pallas_call x3, Pallas kernels, whole_call(): pl.pallas_call(kernel, name=name, out_shape=out_shape, scratch_shapes=lis...  16 us
    all_to_all x1, waiting for transfers between devices, shards(): lax.all_to_all(message, EVERYONE, split_axis=0, concat_axis=0, tiled=True)  14.3 us
    ppermute x2, waiting for transfers between devices, shifted(): lax.ppermute(value, axis, [(source, source + steps) for source in range(f...  10.6 us
    ppermute x2, starting transfers between devices, shifted(): lax.ppermute(value, axis, [(source, source + steps) for source in range(f...  6.76 us
    all_to_all x1, starting transfers between devices, shards(): lax.all_to_all(message, EVERYONE, split_axis=0, concat_axis=0, tiled=True)  6.75 us
    all_to_all x1, starting transfers between devices, shards(): lax.all_to_all(answer, EVERYONE, split_axis=0, concat_axis=0, tiled=True)  3.33 us
    unnamed x23, local copies, waits for them, and re-layouts  1.84 us
  transfers between devices with their start and end apart: 4, of which 4 were waited for; matrix products, arithmetic and copies ran while one was open for 0% of the time, Pallas kernels for 3%

profile of v16, /device:TPU:1, one launch (start us, length us, event | category | flops | bytes accessed | tf_op | source)
XLA Modules:
  0.0 89.8 jit_solution(4696300608972712579)
XLA Ops:
  0.6 0.0 copy-start.1
  0.6 0.0 copy-start.5
  0.7 1.8 %copy.16 = bf16[3072,256]{0,1:T(8,128)(2,1)S(1)} copy(bf16[3072,256]{1,0:T(8,128)(2,1)} %param.11) | data formatting | bytes 3145728 | tf_op args[0]
  2.4 4.6 %collective-permute-start = (bf16[8,3072]{1,0:T(8,128)(2,1)S(1)}, bf16[8,3072]{1,0:T(8,128)(2,1)S(1)}, u32[]{:S(2)}, u32[]{:S(2)}) collective-permute-start(bf16[8,3072]{1,0:T(8,128)(2,1)S(1)} %slice.4), channel_id=1, source_target_pairs={{0,1},{1,2},{2,3},{3,4},{4,5},{5,6},{6,7},{7,8},{8,9},{9,10},{10,1... | collective-permute-start | bytes 147464 | tf_op jit(solution)/shard_map/ppermute | solution.py:21
  7.0 1.2 %collective-permute-done.rim_ref = bf16[8,3072]{1,0:T(8,128)(2,1)S(1)} collective-permute-done((bf16[8,3072]{1,0:T(8,128)(2,1)S(1)}, bf16[8,3072]{1,0:T(8,128)(2,1)S(1)}, u32[]{:S(2)}, u32[]{:S(2)}) %collective-permute-start) | collective-permute-done | bytes 49184 | tf_op jit(solution)/shard_map/ppermute | solution.py:21
  8.2 0.0 copy-done.1
  8.2 0.0 copy-done.5
  8.2 3.6 %joined_features.1 = (bf16[3072,256]{1,0:T(8,128)(2,1)}, bf16[32,64,256]{2,1,0:T(8,128)(2,1)}, bf16[8,3072]{1,0:T(8,128)(2,1)S(1)}) custom-call(bf16[256,3072]{1,0:T(8,128)(2,1)S(1)} %bitcast.2, bf16[8,3072]{1,0:T(8,128)(2,1)S(1)} %collective-permute-done.rim_ref, bf16[7,3072]{1,0:T(8,128)(2,1)S(1)} %copy-done.5, bf16[1024,256]{1,0:T(8,128)(2,1)S(1)} %copy-done.1), custom_call_target="tpu_custom_call" | custom-call | flops 10000000 | bytes 4000000 | tf_op jit(solution)/shard_map/joined_features/pallas_call | solution.py:285
  11.8 0.0 copy-start.2
  11.8 0.0 copy-start.3
  11.8 0.0 copy-start.4
  11.8 0.0 copy-start.7
  11.8 0.0 copy-start.8
  11.8 0.0 copy-start.9
  11.9 6.8 %all-to-all-start = ((bf16[32,64,256]{2,1,0:T(8,128)(2,1)}), bf16[32,64,256]{2,1,0:T(8,128)(2,1)S(1)}, u32[]{:S(2)}, u32[]{:S(2)}) async-start(bf16[32,64,256]{2,1,0:T(8,128)(2,1)} %get-tuple-element.22), calls=%async_computation | async-start | bytes 2097152 | tf_op jit(solution)/shard_map/all_to_all | solution.py:754
  18.6 2.2 %collective-permute-start.1 = (bf16[8,3072]{1,0:T(8,128)(2,1)S(1)}, bf16[8,3072]{1,0:T(8,128)(2,1)S(1)}, u32[]{:S(2)}, u32[]{:S(2)}) collective-permute-start(bf16[8,3072]{1,0:T(8,128)(2,1)S(1)} %get-tuple-element.19), channel_id=1, source_target_pairs={{1,0},{2,1},{3,2},{4,3},{5,4},{6,5},{7,6},{8,7},{9,8},{10,9},{11,1... | collective-permute-start | bytes 147464 | tf_op jit(solution)/shard_map/ppermute | solution.py:21
  20.8 0.0 copy-done.2
  20.8 0.0 copy-done.3
  20.8 0.0 copy-done.4
  20.8 0.0 copy-done.7
  20.8 0.0 copy-done.8
  20.8 0.0 copy-done.9
  20.9 1.1 %filter_dft.1 = (bf16[1024,256]{1,0:T(8,128)(2,1)S(1)}, bf16[768,256]{1,0:T(8,128)(2,1)S(1)}) custom-call(bf16[8,8192]{1,0:T(8,128)(2,1)S(1)} %copy-done.7, bf16[256,64]{1,0:T(8,128)(2,1)S(1)} %copy-done.9, bf16[256,256]{1,0:T(8,128)(2,1)S(1)} %copy-done.8, f32[128,128]{1,0:T(8,128)S(1)} %copy-done.4, f32[128,128]{1,0:T(8,128)S(1)} %copy-done.3, ...), custom_call_target="tpu_custom_call" | custom-call | flops 200000000 | bytes 2000000 | tf_op jit(solution)/shard_map/filter_dft/pallas_call | solution.py:114
  21.9 9.4 %collective-permute-done.1.edge_ref = bf16[8,3072]{1,0:T(8,128)(2,1)S(1)} collective-permute-done((bf16[8,3072]{1,0:T(8,128)(2,1)S(1)}, bf16[8,3072]{1,0:T(8,128)(2,1)S(1)}, u32[]{:S(2)}, u32[]{:S(2)}) %collective-permute-start.1) | collective-permute-done | bytes 49184 | tf_op jit(solution)/shard_map/ppermute | solution.py:21
  31.4 14.3 %all-to-all-done.x_ref = bf16[32,64,256]{2,1,0:T(8,128)(2,1)S(1)} async-done(((bf16[32,64,256]{2,1,0:T(8,128)(2,1)}), bf16[32,64,256]{2,1,0:T(8,128)(2,1)S(1)}, u32[]{:S(2)}, u32[]{:S(2)}) %all-to-all-start) | async-done | bytes 1048608 | tf_op jit(solution)/shard_map/all_to_all | solution.py:754
  45.6 6.9 %joined_filtering.1 = (bf16[32,136,128]{2,1,0:T(8,128)(2,1)}, bf16[1024,256]{1,0:T(8,128)(2,1)}) custom-call(bf16[32,64,256]{2,1,0:T(8,128)(2,1)S(1)} %all-to-all-done.x_ref, bf16[1024,256]{1,0:T(8,128)(2,1)S(1)} %get-tuple-element.24.f_ref, bf16[768,256]{1,0:T(8,128)(2,1)S(1)} %get-tuple-element.25.table_ref, f32[128,128]{1,0:T(8,128)S(1)} %copy-done.4, ...), custom_call_target="tpu_custom_call" | custom-call | flops 4000000000 | bytes 4000000 | tf_op jit(solution)/shard_map/joined_filtering/pallas_call | solution.py:285
  52.5 0.0 copy-start
  52.5 0.0 copy-start.6
  52.5 0.0 copy-start.10
  52.5 3.3 %all-to-all-start.1 = ((bf16[32,136,128]{2,1,0:T(8,128)(2,1)}), bf16[32,136,128]{2,1,0:T(8,128)(2,1)S(1)}, u32[]{:S(2)}, u32[]{:S(2)}) async-start(bf16[32,136,128]{2,1,0:T(8,128)(2,1)} %get-tuple-element.27), calls=%async_computation.1 | async-start | bytes 2228224 | tf_op jit(solution)/shard_map/all_to_all | solution.py:759
  55.9 0.0 copy-done
  55.9 0.0 copy-done.6
  55.9 0.0 copy-done.10
  55.9 1.3 %filter_gradient.1 = f32[8,8192]{1,0:T(8,128)} custom-call(bf16[1024,256]{1,0:T(8,128)(2,1)S(1)} %copy-done, bf16[256,256]{1,0:T(8,128)(2,1)S(1)} %copy-done.6, bf16[64,256]{1,0:T(8,128)(2,1)S(1)} %copy-done.10, f32[128,128]{1,0:T(8,128)S(1)} %copy-done.4, f32[128,128]{1,0:T(8,128)S(1)} %copy-done.3), custom_call_target="tpu_custom_call" | custom-call | flops 200000000 | bytes 2000000 | tf_op jit(solution)/shard_map/filter_gradient/pallas_call | solution.py:248
  57.2 27.1 %all-to-all-done.1.back_ref = bf16[32,136,128]{2,1,0:T(8,128)(2,1)S(1)} async-done(((bf16[32,136,128]{2,1,0:T(8,128)(2,1)}), bf16[32,136,128]{2,1,0:T(8,128)(2,1)S(1)}, u32[]{:S(2)}, u32[]{:S(2)}) %all-to-all-start.1) | async-done | bytes 1114144 | tf_op jit(solution)/shard_map/all_to_all | solution.py:759
  84.3 5.5 %joined_gradients.1 = (bf16[1024,256]{1,0:T(8,128)(2,1)}, bf16[3072,256]{1,0:T(8,128)(2,1)}) custom-call(bf16[1024,256]{1,0:T(8,128)(2,1)} %get-tuple-element.28.s_ref._, bf16[3072,256]{1,0:T(8,128)(2,1)} %get-tuple-element.29.f_hbm, bf16[8,3072]{1,0:T(8,128)(2,1)S(1)} %collective-permute-done.1.edge_ref, ...), custom_call_target="tpu_custom_call", output_to_operand_aliasing={{0}: (0, {}), {1}: (1, {})} | custom-call | flops 10000000 | bytes 4000000 | tf_op jit(solution)/shard_map/joined_gradients/pallas_call | solution.py:285
  (1 shorter events, 0.0 us)
Async XLA Ops:
  0.6 7.6 %copy-start.1 = (bf16[1024,256]{1,0:T(8,128)(2,1)S(1)}, bf16[1024,256]{1,0:T(8,128)(2,1)}, u32[]{:S(2)}) copy-start(bf16[1024,256]{1,0:T(8,128)(2,1)} %og_ref.3) | copy-start | bytes 1572868
  0.6 7.6 %copy-start.5 = (bf16[7,3072]{1,0:T(8,128)(2,1)S(1)}, bf16[7,3072]{1,0:T(8,128)(2,1)}, u32[]{:S(2)}) copy-start(bf16[7,3072]{1,0:T(8,128)(2,1)} %w_ref.3) | copy-start | bytes 129028
  2.4 5.8 %collective-permute-start = (bf16[8,3072]{1,0:T(8,128)(2,1)S(1)}, bf16[8,3072]{1,0:T(8,128)(2,1)S(1)}, u32[]{:S(2)}, u32[]{:S(2)}) collective-permute-start(bf16[8,3072]{1,0:T(8,128)(2,1)S(1)} %slice.4), channel_id=1, source_target_pairs={{0,1},{1,2},{2,3},{3,4},{4,5},{5,6},{6,7},{7,8},{8,9},{9,10},{10,1... | collective-permute-start | bytes 147464 | tf_op jit(solution)/shard_map/ppermute | solution.py:21
  11.8 9.0 %copy-start.2 = (bf16[768,256]{1,0:T(8,128)(2,1)S(1)}, bf16[768,256]{1,0:T(8,128)(2,1)}, u32[]{:S(2)}) copy-start(bf16[768,256]{1,0:T(8,128)(2,1)} %constant.24.refs_0_) | copy-start | bytes 1179652
  11.8 9.0 %copy-start.3 = (f32[128,128]{1,0:T(8,128)S(1)}, f32[128,128]{1,0:T(8,128)}, u32[]{:S(2)}) copy-start(f32[128,128]{1,0:T(8,128)} %constant.15.clone.ti_ref) | copy-start | bytes 196612
  11.8 9.0 %copy-start.4 = (f32[128,128]{1,0:T(8,128)S(1)}, f32[128,128]{1,0:T(8,128)}, u32[]{:S(2)}) copy-start(f32[128,128]{1,0:T(8,128)} %constant.14.clone.tr_ref) | copy-start | bytes 196612
  11.8 9.0 %copy-start.7 = (bf16[8,8192]{1,0:T(8,128)(2,1)S(1)}, bf16[8,8192]{1,0:T(8,128)(2,1)}, u32[]{:S(2)}) copy-start(bf16[8,8192]{1,0:T(8,128)(2,1)} %x_ref.1) | copy-start | bytes 393220
  11.8 9.0 %copy-start.8 = (bf16[256,256]{1,0:T(8,128)(2,1)S(1)}, bf16[256,256]{1,0:T(8,128)(2,1)}, u32[]{:S(2)}) copy-start(bf16[256,256]{1,0:T(8,128)(2,1)} %constant.23.second_ref) | copy-start | bytes 393220
  11.8 9.0 %copy-start.9 = (bf16[256,64]{1,0:T(8,128)(2,1)S(1)}, bf16[256,64]{1,0:T(8,128)(2,1)}, u32[]{:S(2)}) copy-start(bf16[256,64]{1,0:T(8,128)(2,1)} %constant.22.first_ref) | copy-start | bytes 98308
  11.9 33.8 %all-to-all-start = ((bf16[32,64,256]{2,1,0:T(8,128)(2,1)}), bf16[32,64,256]{2,1,0:T(8,128)(2,1)S(1)}, u32[]{:S(2)}, u32[]{:S(2)}) async-start(bf16[32,64,256]{2,1,0:T(8,128)(2,1)} %get-tuple-element.22), calls=%async_computation | async-start | bytes 2097152 | tf_op jit(solution)/shard_map/all_to_all | solution.py:754
  18.6 12.7 %collective-permute-start.1 = (bf16[8,3072]{1,0:T(8,128)(2,1)S(1)}, bf16[8,3072]{1,0:T(8,128)(2,1)S(1)}, u32[]{:S(2)}, u32[]{:S(2)}) collective-permute-start(bf16[8,3072]{1,0:T(8,128)(2,1)S(1)} %get-tuple-element.19), channel_id=1, source_target_pairs={{1,0},{2,1},{3,2},{4,3},{5,4},{6,5},{7,6},{8,7},{9,8},{10,9},{11,1... | collective-permute-start | bytes 147464 | tf_op jit(solution)/shard_map/ppermute | solution.py:21
  52.5 3.4 %copy-start = (bf16[1024,256]{1,0:T(8,128)(2,1)S(1)}, bf16[1024,256]{1,0:T(8,128)(2,1)}, u32[]{:S(2)}) copy-start(bf16[1024,256]{1,0:T(8,128)(2,1)} %get-tuple-element.28.s_ref._) | copy-start | bytes 1572868
  52.5 3.4 %copy-start.6 = (bf16[256,256]{1,0:T(8,128)(2,1)S(1)}, bf16[256,256]{1,0:T(8,128)(2,1)}, u32[]{:S(2)}) copy-start(bf16[256,256]{1,0:T(8,128)(2,1)} %constant.25.third_ref) | copy-start | bytes 393220
  52.5 3.4 %copy-start.10 = (bf16[64,256]{1,0:T(8,128)(2,1)S(1)}, bf16[64,256]{1,0:T(8,128)(2,1)}, u32[]{:S(2)}) copy-start(bf16[64,256]{1,0:T(8,128)(2,1)} %constant.26.fourth_ref) | copy-start | bytes 98308
  52.5 31.8 %all-to-all-start.1 = ((bf16[32,136,128]{2,1,0:T(8,128)(2,1)}), bf16[32,136,128]{2,1,0:T(8,128)(2,1)S(1)}, u32[]{:S(2)}, u32[]{:S(2)}) async-start(bf16[32,136,128]{2,1,0:T(8,128)(2,1)} %get-tuple-element.27), calls=%async_computation.1 | async-start | bytes 2228224 | tf_op jit(solution)/shard_map/all_to_all | solution.py:759
